TPU v7x, 32 devices: a whole 2x2x4 slice. The times are simulated.
32 devices in a mesh: seq: 8 (over z, y), kvh: 4 (over x, core).
Axes of the slice: x: 2, y: 2, z: 4, core: 2. Of those that a mesh axis runs over, the one named last changes fastest.
Arguments:
- queries: bfloat16 [4096, 4096], P(('seq', 'kvh')), may hold values from -5 to 5
- key_rows: bfloat16 [4096, 2048], P(('seq', 'kvh')), may hold values from -6 to 6
- value_rows: bfloat16 [4096, 2048], P(('seq', 'kvh')), may hold values from -6 to 6
- grad_out: bfloat16 [4096, 4096], P(('seq', 'kvh')), may hold values from -6 to 6
Outputs:
- attended: bfloat16 [4096, 4096], P(('seq', 'kvh'))
- grad_queries: bfloat16 [4096, 4096], P(('seq', 'kvh'))
- grad_keys: bfloat16 [4096, 2048], P(('seq', 'kvh'))
- grad_values: bfloat16 [4096, 2048], P(('seq', 'kvh'))
All inputs are finite; a program needn't handle non-finite values.
Results may differ from a plain program's by a relative error of at most 0.012.
Values may be sent and summed in bfloat16 or wider, within the bound.
No kernel may reach another device: no remote copies, remote signals or barrier semaphores. Data moves between devices by JAX's collectives and lax.ppermute only.
A program may use at most 128 MiB of HBM per device.

v0:
```python
import math

import jax
import jax.numpy as jnp
from jax import lax
from jax.sharding import PartitionSpec as P

HEAD_DIM = 128
WINDOW = 1024


score_scale = 168.0 ** (-0.5)


def as_sent(shard):

    def short(part):
        return part.astype(jnp.bfloat16) if part.dtype == jnp.float32 else part

    return jax.tree.map(short, shard)


def passed_along(value, axis, steps):
    count = lax.axis_size(axis)
    first, last = (max(0, -steps), min(count, count - steps))
    return lax.ppermute(value, axis, [(source, source + steps) for source in range(first, last)])


def head_loop(queries, grad_out, window_keys, window_values, query_pos, key_pos):
    row_count = queries.shape[0]
    key_count = window_keys.shape[0]
    kv_count = window_keys.shape[1] // HEAD_DIM
    allowed = (
        (key_pos[None, :] <= query_pos[:, None])
        & (query_pos[:, None] - key_pos[None, :] < WINDOW)
        & (key_pos[None, :] >= 0)
    )

    def one_head(kv_head, totals):
        attended, grad_q, grad_k, grad_v = totals
        q_cols = kv_head * (2 * HEAD_DIM)
        k_cols = kv_head * HEAD_DIM
        q_head = lax.dynamic_slice_in_dim(queries, q_cols, 2 * HEAD_DIM, 1).reshape(
            row_count, 2, HEAD_DIM
        )
        o_head = lax.dynamic_slice_in_dim(grad_out, q_cols, 2 * HEAD_DIM, 1).reshape(
            row_count, 2, HEAD_DIM
        )
        k_head = lax.dynamic_slice_in_dim(window_keys, k_cols, HEAD_DIM, 1)
        v_head = lax.dynamic_slice_in_dim(window_values, k_cols, HEAD_DIM, 1)
        scores = (
            jnp.einsum("rhd,kd->hrk", q_head, k_head, preferred_element_type=jnp.float32)
            * score_scale
        )
        scores = jnp.where(allowed[None], scores, -jnp.inf)
        row_max = jnp.max(scores, axis=-1, keepdims=True)
        exponent = jnp.exp(scores - row_max)
        weights = exponent / jnp.sum(exponent, axis=-1, keepdims=True)
        weights_low = weights.astype(jnp.bfloat16)
        out_head = jnp.einsum(
            "hrk,kd->rhd", weights_low, v_head, preferred_element_type=jnp.float32
        )
        grad_weights = jnp.einsum("rhd,kd->hrk", o_head, v_head, preferred_element_type=jnp.float32)
        row_delta = jnp.sum(weights * grad_weights, axis=-1, keepdims=True)
        grad_scores = (weights * (grad_weights - row_delta)).astype(jnp.bfloat16)
        dq_head = (
            jnp.einsum("hrk,kd->rhd", grad_scores, k_head, preferred_element_type=jnp.float32)
            * score_scale
        )
        dk_head = (
            jnp.einsum("hrk,rhd->kd", grad_scores, q_head, preferred_element_type=jnp.float32)
            * score_scale
        )
        dv_head = jnp.einsum("hrk,rhd->kd", weights_low, o_head, preferred_element_type=jnp.float32)
        attended = lax.dynamic_update_slice_in_dim(
            attended, out_head.reshape(row_count, 2 * HEAD_DIM).astype(jnp.bfloat16), q_cols, 1
        )
        grad_q = lax.dynamic_update_slice_in_dim(
            grad_q, dq_head.reshape(row_count, 2 * HEAD_DIM).astype(jnp.bfloat16), q_cols, 1
        )
        grad_k = lax.dynamic_update_slice_in_dim(grad_k, dk_head, k_cols, 1)
        grad_v = lax.dynamic_update_slice_in_dim(grad_v, dv_head, k_cols, 1)
        return (attended, grad_q, grad_k, grad_v)

    initial = (
        jnp.zeros(queries.shape, jnp.bfloat16),
        jnp.zeros(queries.shape, jnp.bfloat16),
        jnp.zeros((key_count, window_keys.shape[1]), jnp.float32),
        jnp.zeros((key_count, window_keys.shape[1]), jnp.float32),
    )
    return lax.fori_loop(0, kv_count, one_head, initial)


def window_core(queries, key_rows, value_rows, grad_out, shard_index, fetch_pair, give_back):
    row_count = queries.shape[0]
    back_count = -(-WINDOW // row_count)
    pieces = [fetch_pair((key_rows, value_rows), offset) for offset in range(back_count, 0, -1)]
    window_keys = jnp.concatenate([piece[0] for piece in pieces] + [key_rows], axis=0)
    window_values = jnp.concatenate([piece[1] for piece in pieces] + [value_rows], axis=0)
    query_pos = shard_index * row_count + jnp.arange(row_count, dtype=jnp.int32)
    key_pos = (
        shard_index * row_count
        - back_count * row_count
        + jnp.arange((back_count + 1) * row_count, dtype=jnp.int32)
    )
    own_start = back_count * row_count
    block_rows = math.gcd(row_count, WINDOW // 8)
    key_span = WINDOW + block_rows
    grad_kwin = jnp.zeros(window_keys.shape, jnp.float32)
    grad_vwin = jnp.zeros(window_values.shape, jnp.float32)
    attended_parts = []
    grad_q_parts = []
    for number in range(row_count // block_rows):
        first = number * block_rows
        key_first = own_start + first - WINDOW
        result = head_loop(
            queries[first : first + block_rows],
            grad_out[first : first + block_rows],
            window_keys[key_first : key_first + key_span],
            window_values[key_first : key_first + key_span],
            query_pos[first : first + block_rows],
            key_pos[key_first : key_first + key_span],
        )
        attended_parts.append(result[0])
        grad_q_parts.append(result[1])
        grad_kwin = grad_kwin.at[key_first : key_first + key_span].add(result[2])
        grad_vwin = grad_vwin.at[key_first : key_first + key_span].add(result[3])
    attended = jnp.concatenate(attended_parts, axis=0)
    grad_q = jnp.concatenate(grad_q_parts, axis=0)
    grad_k = grad_kwin[own_start:]
    grad_v = grad_vwin[own_start:]
    for offset in range(1, back_count + 1):
        start_row = (back_count - offset) * row_count
        returned = give_back(
            (
                grad_kwin[start_row : start_row + row_count],
                grad_vwin[start_row : start_row + row_count],
            ),
            -offset,
        )
        grad_k = grad_k + returned[0]
        grad_v = grad_v + returned[1]
    return (attended, grad_q, grad_k.astype(jnp.bfloat16), grad_v.astype(jnp.bfloat16))


def body(queries, key_rows, value_rows, grad_out):
    local_rows = (
        lax.all_to_all(queries, "kvh", split_axis=1, concat_axis=0, tiled=True),
        lax.all_to_all(key_rows, "kvh", split_axis=1, concat_axis=0, tiled=True),
        lax.all_to_all(value_rows, "kvh", split_axis=1, concat_axis=0, tiled=True),
        lax.all_to_all(grad_out, "kvh", split_axis=1, concat_axis=0, tiled=True),
    )

    def fetch_seq(pair, offset):
        return jax.tree.map(
            lambda part, own: part.astype(own.dtype),
            passed_along(as_sent(pair), "seq", offset),
            pair,
        )

    def return_seq(pair, offset):
        return passed_along(pair, "seq", offset)

    shard_index = lax.axis_index("seq")
    results = window_core(
        local_rows[0],
        local_rows[1],
        local_rows[2],
        local_rows[3],
        shard_index,
        fetch_seq,
        return_seq,
    )
    finished = (
        lax.all_to_all(results[0], "kvh", split_axis=0, concat_axis=1, tiled=True),
        lax.all_to_all(results[1], "kvh", split_axis=0, concat_axis=1, tiled=True),
        lax.all_to_all(results[2], "kvh", split_axis=0, concat_axis=1, tiled=True),
        lax.all_to_all(results[3], "kvh", split_axis=0, concat_axis=1, tiled=True),
    )
    return (finished[0], finished[1], finished[2], finished[3])


def solution(mesh):
    return jax.shard_map(
        body,
        mesh=mesh,
        in_specs=(
            P(("seq", "kvh"), None),
            P(("seq", "kvh"), None),
            P(("seq", "kvh"), None),
            P(("seq", "kvh"), None),
        ),
        out_specs=(
            P(("seq", "kvh"), None),
            P(("seq", "kvh"), None),
            P(("seq", "kvh"), None),
            P(("seq", "kvh"), None),
        ),
        check_vma=False,
    )
```

profile of v0, /device:TPU:0, one launch (start us, length us, event | category | flops | bytes accessed | tf_op | source)
XLA Modules:
  0.0 464.0 jit_solution(3501850391550508046)
XLA Ops:
  0.6 2.1 copy.140
  2.7 4.2 all-to-all-start
  7.8 8.0 %all-to-all-done = bf16[128,4,512]{0,2,1:T(8,128)(2,1)S(1)} async-done(((bf16[128,4,512]{0,2,1:T(8,128)(2,1)}), bf16[128,4,512]{0,2,1:T(8,128)(2,1)S(1)}, u32[]{:S(2)}, u32[]{:S(2)}) %all-to-all-start) | async-done | bytes 524320 | tf_op jit(solution)/shard_map/all_to_all | solution.py:150
  15.8 3.5 all-to-all-start.1
  20.6 7.5 %all-to-all-done.1 = bf16[128,4,512]{2,0,1:T(8,128)(2,1)S(1)} async-done(((bf16[128,4,512]{2,0,1:T(8,128)(2,1)}), bf16[128,4,512]{2,0,1:T(8,128)(2,1)S(1)}, u32[]{:S(2)}, u32[]{:S(2)}) %all-to-all-start.1) | async-done | bytes 524320 | tf_op jit(solution)/shard_map/all_to_all | solution.py:149
  28.1 3.5 all-to-all-start.2
  33.0 13.1 %all-to-all-done.2 = bf16[128,4,1024]{0,2,1:T(8,128)(2,1)S(1)} async-done(((bf16[128,4,1024]{0,2,1:T(8,128)(2,1)}), bf16[128,4,1024]{0,2,1:T(8,128)(2,1)S(1)}, u32[]{:S(2)}, u32[]{:S(2)}) %all-to-all-start.2) | async-done | bytes 1048608 | tf_op jit(solution)/shard_map/all_to_all | solution.py:148
  46.0 3.5 all-to-all-start.3
  50.6 5.0 %collective-permute-start = (bf16[512,512]{1,0:T(8,128)(2,1)}, bf16[512,512]{1,0:T(8,128)(2,1)}, u32[]{:S(2)}, u32[]{:S(2)}) collective-permute-start(bf16[512,512]{1,0:T(8,128)(2,1)} %bitcast.567), channel_id=1, source_target_pairs={{0,8},{4,12},{8,16},{12,20},{16,24},{20,28},{1,9},{5,13},{9,17},{1... | collective-permute-start | bytes 1572872 | tf_op jit(solution)/shard_map/ppermute | solution.py:26
  55.6 4.2 collective-permute-start.1
  60.3 2.7 collective-permute-start.2
  63.0 4.2 collective-permute-start.3
  69.2 2.4 collective-permute-done.1
  72.9 2.3 fusion.195
  75.2 2.8 collective-permute-done.2
  78.0 4.0 collective-permute-done.3
  83.3 2.0 fusion.194
  90.2 56.7 %while.88 = (s32[]{:T(128)}, bf16[128,1024]{0,1:T(8,128)(2,1)}, bf16[128,1024]{0,1:T(8,128)(2,1)}, f32[1152,512]{1,0:T(8,128)}, f32[1152,512]{1,0:T(8,128)}, /*i...) while((s32[]{:T(128)}, bf16[128,1024]{0,1:T(8,128)(2,1)}, ...), condition=%wide.region_4.5_spmd.clone, body=%wide.region_0.4_spmd.clone.sunk | while | flops 611159680 | bytes 12271005 | solution.py:91
  97.7 2.8 fusion.329
  111.9 2.8 fusion.329
  126.0 2.8 fusion.329
  140.2 2.8 fusion.329
  151.8 54.1 %while.89 = (s32[]{:T(128)}, bf16[128,1024]{0,1:T(8,128)(2,1)}, bf16[128,1024]{0,1:T(8,128)(2,1)}, f32[1152,512]{1,0:T(8,128)}, f32[1152,512]{1,0:T(8,128)}, /*i...) while((s32[]{:T(128)}, bf16[128,1024]{0,1:T(8,128)(2,1)}, ...), condition=%wide.region_9.0_spmd.clone, body=%wide.region_5.9_spmd.clone.sunk | while | flops 611159680 | bytes 12271005 | solution.py:91
  158.7 2.8 fusion.349
  172.2 2.8 fusion.349
  185.7 2.8 fusion.349
  199.3 2.8 fusion.349
  210.9 54.0 %while.90 = (s32[]{:T(128)}, bf16[128,1024]{0,1:T(8,128)(2,1)}, bf16[128,1024]{0,1:T(8,128)(2,1)}, f32[1152,512]{1,0:T(8,128)}, f32[1152,512]{1,0:T(8,128)}, /*i...) while((s32[]{:T(128)}, bf16[128,1024]{0,1:T(8,128)(2,1)}, ...), condition=%wide.region_14.15_spmd.clone, body=%wide.region_10.14_spmd.clone.sunk | while | flops 611159680 | bytes 12271005 | solution.py:91
  217.7 2.8 fusion.369
  231.2 2.8 fusion.369
  244.7 2.8 fusion.369
  258.2 2.8 fusion.369
  269.8 38.8 %while.91 = (s32[]{:T(128)}, bf16[128,1024]{0,1:T(8,128)(2,1)}, bf16[128,1024]{0,1:T(8,128)(2,1)}, f32[1152,512]{1,0:T(8,128)}, f32[1152,512]{1,0:T(8,128)}, /*i...) while((s32[]{:T(128)}, bf16[128,1024]{0,1:T(8,128)(2,1)}, ...), condition=%wide.region_19.20_spmd.clone, body=%wide.region_15.19_spmd.clone.sunk | while | flops 611159680 | bytes 12271005 | solution.py:91
  308.6 2.7 pad_maximum_fusion.2
  312.6 3.5 all-to-all-start.4
  316.2 2.0 scatter-add.26
  318.2 2.3 add_dynamic-update-slice_fusion.1
  320.5 2.4 fusion.177
  327.9 3.3 constant_dynamic-update-slice_fusion.8
  340.6 2.3 copy.151
  342.9 4.3 all-to-all-start.5
  347.1 31.4 %collective-permute-done.6 = f32[512,512]{1,0:T(8,128)} collective-permute-done((f32[512,512]{1,0:T(8,128)}, f32[512,512]{1,0:T(8,128)}, u32[]{:S(2)}, u32[]{:S(2)}) %collective-permute-start.6) | collective-permute-done | bytes 1048608 | tf_op jit(solution)/shard_map/ppermute | solution.py:26
  378.5 24.5 %collective-permute-done.7 = f32[512,512]{1,0:T(8,128)} collective-permute-done((f32[512,512]{1,0:T(8,128)}, f32[512,512]{1,0:T(8,128)}, u32[]{:S(2)}, u32[]{:S(2)}) %collective-permute-start.7) | collective-permute-done | bytes 1048608 | tf_op jit(solution)/shard_map/ppermute | solution.py:26
  403.0 2.9 fusion.179
  406.0 4.1 all-to-all-start.7
  410.1 37.6 %collective-permute-done.5 = f32[512,512]{1,0:T(8,128)} collective-permute-done((f32[512,512]{1,0:T(8,128)}, f32[512,512]{1,0:T(8,128)}, u32[]{:S(2)}, u32[]{:S(2)}) %collective-permute-start.5) | collective-permute-done | bytes 1048608 | tf_op jit(solution)/shard_map/ppermute | solution.py:26
  447.8 2.6 fusion.181
  450.4 3.5 all-to-all-start.6
  (238 shorter events, 224.4 us)
Async XLA Ops:
  0.6 6.3 %copy-start.8 = (bf16[128,2048]{1,0:T(8,128)(2,1)S(1)}, bf16[128,2048]{1,0:T(8,128)(2,1)}, u32[]{:S(2)}) copy-start(bf16[128,2048]{1,0:T(8,128)(2,1)} %param.29) | copy-start | bytes 1572868
  2.7 13.1 %all-to-all-start = ((bf16[128,4,512]{0,2,1:T(8,128)(2,1)}), bf16[128,4,512]{0,2,1:T(8,128)(2,1)S(1)}, u32[]{:S(2)}, u32[]{:S(2)}) async-start(bf16[128,4,512]{0,2,1:T(8,128)(2,1)} %bitcast), calls=%async_computation | async-start | bytes 1048576 | tf_op jit(solution)/shard_map/all_to_all | solution.py:150
  6.9 12.3 %copy-start.6 = (bf16[128,4096]{1,0:T(8,128)(2,1)S(1)}, bf16[128,4096]{1,0:T(8,128)(2,1)}, u32[]{:S(2)}) copy-start(bf16[128,4096]{1,0:T(8,128)(2,1)} %param.28) | copy-start | bytes 3145732
  15.8 12.3 %all-to-all-start.1 = ((bf16[128,4,512]{2,0,1:T(8,128)(2,1)}), bf16[128,4,512]{2,0,1:T(8,128)(2,1)S(1)}, u32[]{:S(2)}, u32[]{:S(2)}) async-start(bf16[128,4,512]{2,0,1:T(8,128)(2,1)} %bitcast.350), calls=%async_computation.1 | async-start | bytes 1048576 | tf_op jit(solution)/shard_map/all_to_all | solution.py:149
  20.6 11.0 %copy-start.7 = (bf16[128,4096]{1,0:T(8,128)(2,1)S(1)}, bf16[128,4096]{1,0:T(8,128)(2,1)}, u32[]{:S(2)}) copy-start(bf16[128,4096]{1,0:T(8,128)(2,1)} %param.31) | copy-start | bytes 3145732
  28.1 18.0 %all-to-all-start.2 = ((bf16[128,4,1024]{0,2,1:T(8,128)(2,1)}), bf16[128,4,1024]{0,2,1:T(8,128)(2,1)S(1)}, u32[]{:S(2)}, u32[]{:S(2)}) async-start(bf16[128,4,1024]{0,2,1:T(8,128)(2,1)} %bitcast.7), calls=%async_computation.2 | async-start | bytes 2097152 | tf_op jit(solution)/shard_map/all_to_all | solution.py:148
  46.0 22.1 %all-to-all-start.3 = ((bf16[128,4,1024]{0,2,1:T(8,128)(2,1)}), bf16[128,4,1024]{0,2,1:T(8,128)(2,1)S(1)}, u32[]{:S(2)}, u32[]{:S(2)}) async-start(bf16[128,4,1024]{0,2,1:T(8,128)(2,1)} %bitcast.10), calls=%async_computation.3 | async-start | bytes 2097152 | tf_op jit(solution)/shard_map/all_to_all | solution.py:151
  50.6 18.6 %collective-permute-start = (bf16[512,512]{1,0:T(8,128)(2,1)}, bf16[512,512]{1,0:T(8,128)(2,1)}, u32[]{:S(2)}, u32[]{:S(2)}) collective-permute-start(bf16[512,512]{1,0:T(8,128)(2,1)} %bitcast.567), channel_id=1, source_target_pairs={{0,8},{4,12},{8,16},{12,20},{16,24},{20,28},{1,9},{5,13},{9,17},{1... | collective-permute-start | bytes 1572872 | tf_op jit(solution)/shard_map/ppermute | solution.py:26
  55.6 16.0 %collective-permute-start.1 = (bf16[512,512]{1,0:T(8,128)(2,1)}, bf16[512,512]{1,0:T(8,128)(2,1)}, u32[]{:S(2)}, u32[]{:S(2)}) collective-permute-start(bf16[512,512]{1,0:T(8,128)(2,1)} %bitcast.568), channel_id=1, source_target_pairs={{0,4},{4,8},{8,12},{12,16},{16,20},{20,24},{24,28},{1,5},{5,9},{9,... | collective-permute-start | bytes 1572872 | tf_op jit(solution)/shard_map/ppermute | solution.py:26
  60.3 17.6 %collective-permute-start.2 = (bf16[512,512]{1,0:T(8,128)(2,1)S(1)}, bf16[512,512]{1,0:T(8,128)(2,1)}, u32[]{:S(2)}, u32[]{:S(2)}) collective-permute-start(bf16[512,512]{1,0:T(8,128)(2,1)S(1)} %bitcast.564), channel_id=1, source_target_pairs={{0,8},{4,12},{8,16},{12,20},{16,24},{20,28},{1,9},{5,13},{9,17},{1... | collective-permute-start | bytes 1572872 | tf_op jit(solution)/shard_map/ppermute | solution.py:26
  63.0 18.9 %collective-permute-start.3 = (bf16[512,512]{1,0:T(8,128)(2,1)S(1)}, bf16[512,512]{1,0:T(8,128)(2,1)}, u32[]{:S(2)}, u32[]{:S(2)}) collective-permute-start(bf16[512,512]{1,0:T(8,128)(2,1)S(1)} %bitcast.565), channel_id=1, source_target_pairs={{0,4},{4,8},{8,12},{12,16},{16,20},{20,24},{24,28},{1,5},{5,9},{9,... | collective-permute-start | bytes 1572872 | tf_op jit(solution)/shard_map/ppermute | solution.py:26
  68.2 3.4 copy-start.5
  312.6 30.2 %all-to-all-start.4 = ((bf16[4,128,1024]{2,1,0:T(8,128)(2,1)}), bf16[4,128,1024]{2,1,0:T(8,128)(2,1)S(1)}, u32[]{:S(2)}, u32[]{:S(2)}) async-start(bf16[4,128,1024]{2,1,0:T(8,128)(2,1)} %bitcast.19), calls=%async_computation.4 | async-start | bytes 2097152 | tf_op jit(solution)/shard_map/all_to_all | solution.py:175
  320.4 2.4 copy-start.3
  322.9 1.7 copy-start.1
  324.6 1.7 copy-start.2
  326.2 1.7 copy-start
  331.2 3.5 copy-start.4
  332.3 46.3 %collective-permute-start.6 = (f32[512,512]{1,0:T(8,128)}, f32[512,512]{1,0:T(8,128)}, u32[]{:S(2)}, u32[]{:S(2)}) collective-permute-start(f32[512,512]{1,0:T(8,128)} %slice.336), channel_id=1, source_target_pairs={{4,0},{8,4},{12,8},{16,12},{20,16},{24,20},{28,24},{5,1},{9,5},{13... | collective-permute-start | bytes 3145736 | tf_op jit(solution)/shard_map/ppermute | solution.py:26
  334.6 68.4 %collective-permute-start.7 = (f32[512,512]{1,0:T(8,128)}, f32[512,512]{1,0:T(8,128)}, u32[]{:S(2)}, u32[]{:S(2)}) collective-permute-start(f32[512,512]{1,0:T(8,128)} %slice.337), channel_id=1, source_target_pairs={{8,0},{12,4},{16,8},{20,12},{24,16},{28,20},{9,1},{13,5},{17,9},{2... | collective-permute-start | bytes 3145736 | tf_op jit(solution)/shard_map/ppermute | solution.py:26
  336.9 73.2 %collective-permute-start.4 = (f32[512,512]{1,0:T(8,128)}, f32[512,512]{1,0:T(8,128)}, u32[]{:S(2)}, u32[]{:S(2)}) collective-permute-start(f32[512,512]{1,0:T(8,128)} %slice.331), channel_id=1, source_target_pairs={{4,0},{8,4},{12,8},{16,12},{20,16},{24,20},{28,24},{5,1},{9,5},{13... | collective-permute-start | bytes 3145736 | tf_op jit(solution)/shard_map/ppermute | solution.py:26
  339.3 108.5 %collective-permute-start.5 = (f32[512,512]{1,0:T(8,128)}, f32[512,512]{1,0:T(8,128)}, u32[]{:S(2)}, u32[]{:S(2)}) collective-permute-start(f32[512,512]{1,0:T(8,128)} %slice.332), channel_id=1, source_target_pairs={{8,0},{12,4},{16,8},{20,12},{24,16},{28,20},{9,1},{13,5},{17,9},{2... | collective-permute-start | bytes 3145736 | tf_op jit(solution)/shard_map/ppermute | solution.py:26
  342.9 63.1 %all-to-all-start.5 = ((bf16[4,128,1024]{2,1,0:T(8,128)(2,1)}), bf16[4,128,1024]{2,1,0:T(8,128)(2,1)}, u32[]{:S(2)}, u32[]{:S(2)}) async-start(bf16[4,128,1024]{2,1,0:T(8,128)(2,1)} %bitcast.557), calls=%async_computation.5 | async-start | bytes 2097152 | tf_op jit(solution)/shard_map/all_to_all | solution.py:176
  406.0 44.4 %all-to-all-start.7 = ((bf16[4,128,512]{2,1,0:T(8,128)(2,1)}), bf16[4,128,512]{2,1,0:T(8,128)(2,1)}, u32[]{:S(2)}, u32[]{:S(2)}) async-start(bf16[4,128,512]{2,1,0:T(8,128)(2,1)} %bitcast.560), calls=%async_computation.7 | async-start | bytes 1048576 | tf_op jit(solution)/shard_map/all_to_all | solution.py:178
  450.4 12.3 %all-to-all-start.6 = ((bf16[4,128,512]{2,1,0:T(8,128)(2,1)}), bf16[4,128,512]{2,1,0:T(8,128)(2,1)S(1)}, u32[]{:S(2)}, u32[]{:S(2)}) async-start(bf16[4,128,512]{2,1,0:T(8,128)(2,1)} %bitcast.561), calls=%async_computation.6 | async-start | bytes 1048576 | tf_op jit(solution)/shard_map/all_to_all | solution.py:177
where the time goes:
time: 469 us; the launch traced here: 464 us
  matrix products  150 us (32%)
  waiting for transfers between devices  133 us (28%)
  local copies, waits for them, and re-layouts  89.5 us (19%)
  starting transfers between devices  51.3 us (11%)
  other arithmetic  38.9 us (8%)
    ppermute x8, waiting for transfers between devices, passed_along(): lax.ppermute(value, axis, [(source, source + steps) for source in range(f...  103 us
    dot_general x16, matrix products, one_head(): jnp.einsum('hrk,rhd->kd', weights_low, o_head, preferred_element_type=jnp...  41.2 us
    dot_general x16, matrix products, one_head(): jnp.einsum('hrk,kd->rhd', weights_low, v_head, preferred_element_type=jnp...  30.6 us
    dot_general x16, matrix products, one_head(): jnp.einsum('rhd,kd->hrk', o_head, v_head, preferred_element_type=jnp.floa...  21.6 us
    sub x16, matrix products, one_head(): exponent = jnp.exp(scores - row_max)  21.2 us
    ppermute x8, starting transfers between devices, passed_along(): lax.ppermute(value, axis, [(source, source + steps) for source in range(f...  21.2 us
    another operation x16, local copies, waits for them, and re-layouts  19.7 us
    dot_general x16, matrix products, one_head(): jnp.einsum('hrk,rhd->kd', grad_scores, q_head, preferred_element_type=jnp...  19.1 us
  transfers between devices with their start and end apart: 16, of which 10 were waited for; matrix products, arithmetic and copies ran while one was open for 9% of the time, Pallas kernels for 0%

commit v1 on v0

v1 whole, which is shorter than its diff:
```python
import functools

import jax
import jax.numpy as jnp
from jax import lax
from jax.experimental import pallas as pl
from jax.experimental.pallas import tpu as pltpu
from jax.sharding import PartitionSpec as P

HEAD_DIM = 128
WINDOW = 1024
BLOCK = 128
CHUNKS = WINDOW // BLOCK + 1
SCORE_SCALE = 168.0 ** (-0.5)
EXP2_SCALE = SCORE_SCALE * 1.4426950408889634
EXCLUDED = -1e30
VMEM_BYTES = 56 * 2**20

NN = (((1,), (0,)), ((), ()))
NT = (((1,), (1,)), ((), ()))
TN = (((0,), (0,)), ((), ()))

VMEM = pl.BlockSpec(memory_space=pltpu.VMEM)
SMEM = pl.BlockSpec(memory_space=pltpu.SMEM)


def dot(left, right, dims):
    return lax.dot_general(left, right, dims, preferred_element_type=jnp.float32)


def attention_kernel(
    heads, first_ref, qo_ref, halo_ref, own_ref, ao_ref, dhalo_ref, down_ref, keys, values, acc_k, acc_v
):
    rows = own_ref.shape[0]
    width = heads * HEAD_DIM
    for h in range(heads):
        cols = slice(h * HEAD_DIM, (h + 1) * HEAD_DIM)
        vcols = slice(width + h * HEAD_DIM, width + (h + 1) * HEAD_DIM)
        keys[h, :WINDOW] = halo_ref[:, cols]
        keys[h, WINDOW:] = own_ref[:, cols]
        values[h, :WINDOW] = halo_ref[:, vcols]
        values[h, WINDOW:] = own_ref[:, vcols]
    acc_k[...] = jnp.zeros_like(acc_k)
    acc_v[...] = jnp.zeros_like(acc_v)
    key_at = lax.broadcasted_iota(jnp.int32, (BLOCK, 2 * BLOCK), 0)
    query_at = lax.broadcasted_iota(jnp.int32, (BLOCK, 2 * BLOCK), 1) & (BLOCK - 1)
    first = first_ref[0]

    def unit(h, i):
        start = pl.multiple_of(i * BLOCK, BLOCK)
        span = pl.ds(start, CHUNKS * BLOCK)
        here = pl.ds(start, BLOCK)
        qcol = 2 * h * HEAD_DIM
        ocol = 2 * width + qcol

        def both(col):
            return jnp.concatenate(
                [qo_ref[here, col : col + HEAD_DIM], qo_ref[here, col + HEAD_DIM : col + 2 * HEAD_DIM]], 0
            )

        q_rows, o_rows = both(qcol), both(ocol)
        k_rows, v_rows = keys[h, span, :], values[h, span, :]
        scores = dot(k_rows, q_rows, NT)
        parts = [scores[c * BLOCK : (c + 1) * BLOCK] for c in range(CHUNKS)]
        parts[0] = jnp.where(key_at > query_at, parts[0], EXCLUDED)
        parts[-1] = jnp.where(key_at <= query_at, parts[-1], EXCLUDED)
        bias = [
            jnp.where((first > 0) & (i + c < WINDOW // BLOCK), EXCLUDED, 0.0).astype(jnp.float32)
            for c in range(CHUNKS - 1)
        ]
        top = jnp.max(parts[-1], axis=0, keepdims=True)
        for c in range(CHUNKS - 1):
            top = jnp.maximum(top, jnp.max(parts[c], axis=0, keepdims=True) + bias[c])
        top = top * EXP2_SCALE
        total = jnp.zeros_like(top)
        exps = []
        for c in range(CHUNKS):
            shift = top if c == CHUNKS - 1 else top - bias[c]
            exps.append(jnp.exp2(parts[c] * EXP2_SCALE - shift))
            total = total + jnp.sum(exps[c], axis=0, keepdims=True)
        inverse = 1.0 / total
        weights = [e * inverse for e in exps]
        weights_low = jnp.concatenate([w.astype(jnp.bfloat16) for w in weights], 0)
        grad_weights = dot(v_rows, o_rows, NT)
        delta = jnp.zeros_like(total)
        for c in range(CHUNKS):
            delta = delta + jnp.sum(weights[c] * grad_weights[c * BLOCK : (c + 1) * BLOCK], axis=0, keepdims=True)
        grad_scores = jnp.concatenate(
            [
                (weights[c] * (grad_weights[c * BLOCK : (c + 1) * BLOCK] - delta)).astype(jnp.bfloat16)
                for c in range(CHUNKS)
            ],
            0,
        )
        attended = dot(weights_low, v_rows, TN).astype(jnp.bfloat16)
        grad_q = (dot(grad_scores, k_rows, TN) * SCORE_SCALE).astype(jnp.bfloat16)
        for j in range(2):
            part = slice(j * BLOCK, (j + 1) * BLOCK)
            ao_ref[here, qcol + j * HEAD_DIM : qcol + (j + 1) * HEAD_DIM] = attended[part]
            ao_ref[here, ocol + j * HEAD_DIM : ocol + (j + 1) * HEAD_DIM] = grad_q[part]
        acc_v[h, span, :] += dot(weights_low, o_rows, NN)
        acc_k[h, span, :] += dot(grad_scores, q_rows, NN)

    def step(i, carry):
        for h in range(heads):
            unit(h, i)
        return carry

    lax.fori_loop(0, rows // BLOCK, step, 0)
    for h in range(heads):
        cols = slice(h * HEAD_DIM, (h + 1) * HEAD_DIM)
        vcols = slice(width + h * HEAD_DIM, width + (h + 1) * HEAD_DIM)
        dhalo_ref[:, cols] = (acc_k[h, :WINDOW] * SCORE_SCALE).astype(jnp.bfloat16)
        dhalo_ref[:, vcols] = acc_v[h, :WINDOW].astype(jnp.bfloat16)
        down_ref[:, cols] = acc_k[h, WINDOW:] * SCORE_SCALE
        down_ref[:, vcols] = acc_v[h, WINDOW:]


def attention(first, qo, halo, own):
    rows = own.shape[0]
    heads = own.shape[1] // (2 * HEAD_DIM)
    window = (heads, WINDOW + rows, HEAD_DIM)
    return pl.pallas_call(
        functools.partial(attention_kernel, heads),
        out_shape=(
            jax.ShapeDtypeStruct(qo.shape, jnp.bfloat16),
            jax.ShapeDtypeStruct(halo.shape, jnp.bfloat16),
            jax.ShapeDtypeStruct(own.shape, jnp.float32),
        ),
        in_specs=[SMEM, VMEM, VMEM, VMEM],
        out_specs=(VMEM, VMEM, VMEM),
        scratch_shapes=[
            pltpu.VMEM(window, jnp.bfloat16),
            pltpu.VMEM(window, jnp.bfloat16),
            pltpu.VMEM(window, jnp.float32),
            pltpu.VMEM(window, jnp.float32),
        ],
        compiler_params=pltpu.CompilerParams(vmem_limit_bytes=VMEM_BYTES),
        name="attention",
    )(first, qo, halo, own)


def pack_kernel(a_ref, b_ref, out_ref):
    groups, _, width = out_ref.shape
    half = width // 2
    for g in range(groups):
        out_ref[g, :, :half] = a_ref[:, g * half : (g + 1) * half]
        out_ref[g, :, half:] = b_ref[:, g * half : (g + 1) * half]


def pack(a, b, groups):
    rows, cols = a.shape
    return pl.pallas_call(
        pack_kernel,
        out_shape=jax.ShapeDtypeStruct((groups, rows, 2 * cols // groups), a.dtype),
        in_specs=[VMEM, VMEM],
        out_specs=VMEM,
        compiler_params=pltpu.CompilerParams(vmem_limit_bytes=VMEM_BYTES),
        name="pack",
    )(a, b)


def unpack_kernel(x_ref, a_ref, b_ref):
    groups, _, width = x_ref.shape
    half = width // 2
    for g in range(groups):
        a_ref[:, g * half : (g + 1) * half] = x_ref[g, :, :half]
        b_ref[:, g * half : (g + 1) * half] = x_ref[g, :, half:]


def unpack(x):
    groups, rows, width = x.shape
    shape = jax.ShapeDtypeStruct((rows, groups * width // 2), x.dtype)
    return pl.pallas_call(
        unpack_kernel,
        out_shape=(shape, shape),
        in_specs=[VMEM],
        out_specs=(VMEM, VMEM),
        compiler_params=pltpu.CompilerParams(vmem_limit_bytes=VMEM_BYTES),
        name="unpack",
    )(x)


def body(queries, key_rows, value_rows, grad_out):
    shards, split = lax.axis_size("seq"), lax.axis_size("kvh")
    rows = queries.shape[0]
    span = WINDOW // (rows * split)
    members = span * split
    groups = [[g * members + i for i in range(members)] for g in range(shards // span)]
    first = (lax.axis_index("seq") < span).astype(jnp.int32).reshape(1)

    def exchange(x):
        return lax.all_to_all(x, ("seq", "kvh"), 0, 0, tiled=True, axis_index_groups=groups)

    own = exchange(pack(key_rows, value_rows, members)).reshape(WINDOW, -1)
    halo = lax.ppermute(own, "seq", [(i, i + span) for i in range(shards - span)])
    qo = exchange(pack(queries, grad_out, members)).reshape(WINDOW, -1)
    outs, dhalo, down = attention(first, qo, halo, own)
    back = lax.ppermute(dhalo, "seq", [(i + span, i) for i in range(shards - span)])
    attended, grad_q = unpack(exchange(outs.reshape(members, rows, -1)))
    total = (down + back.astype(jnp.float32)).astype(jnp.bfloat16)
    grad_k, grad_v = unpack(exchange(total.reshape(members, rows, -1)))
    return (attended, grad_q, grad_k, grad_v)


def solution(mesh):
    placed = P(("seq", "kvh"), None)
    return jax.shard_map(
        body, mesh=mesh, in_specs=(placed,) * 4, out_specs=(placed,) * 4, check_vma=False
    )
```

time: 469 us -> 143 us (0.30)
  matrix products: 150 us -> 0 us
  local copies, waits for them, and re-layouts: 89.5 us -> 2.34 us
  waiting for transfers between devices: 133 us -> 72.8 us
  Pallas kernels: 0 us -> 41.7 us
  other arithmetic: 38.9 us -> 2.92 us
  starting transfers between devices: 51.3 us -> 22.2 us
    dot_general x80 -> x0, matrix products: 129 us -> none  [the longest x16 41.2 us: one_head(): jnp.einsum('hrk,rhd->kd', weights_low, o_head, preferred_element_type=jnp...]
    ppermute x8 -> x2, waiting for transfers between devices: 103 us -> 26 us  [the longest x1 26 us: body(): lax.ppermute(dhalo, 'seq', [(i + span, i) for i in range(shards - span)])]
    pallas_call x0 -> x5, Pallas kernels: none -> 41.7 us  [the longest x1 31 us: attention(): pl.pallas_call(functools.partial(attention_kernel, heads), out_shape=(jax...]
    dynamic_slice x32 -> x0, local copies, waits for them, and re-layouts: 23.7 us -> none  [the longest x16 13.6 us: one_head(): lax.dynamic_slice_in_dim(grad_out, q_cols, 2 * HEAD_DIM, 1)]
    sub x16 -> x0, matrix products: 21.2 us -> none  [one_head(): exponent = jnp.exp(scores - row_max)]
    another operation x16 -> x0, local copies, waits for them, and re-layouts: 19.7 us -> none
    all_to_all x8 -> x4, waiting for transfers between devices: 30.2 us -> 46.8 us  [exchange(): lax.all_to_all(x, ('seq', 'kvh'), 0, 0, tiled=True, axis_index_groups=gro...]
    and x16 -> x0, other arithmetic: 16.1 us -> none  [head_loop(): (key_pos[None, :] <= query_pos[:, None]) & (query_pos[:, None] - key_pos[...]
  transfers between devices with their start and end apart: 16 -> 6, of which waited for: 10 -> 4; matrix products, arithmetic and copies ran while one was open for 9% -> 2% of each run, Pallas kernels for 0% -> 4%
where the time goes in v1:
time: 143 us
  waiting for transfers between devices  72.8 us (51%)
  Pallas kernels  41.7 us (29%)
  starting transfers between devices  22.2 us (16%)
  other arithmetic  2.92 us (2%)
  local copies, waits for them, and re-layouts  2.34 us (2%)
    all_to_all x4, waiting for transfers between devices, exchange(): lax.all_to_all(x, ('seq', 'kvh'), 0, 0, tiled=True, axis_index_groups=gro...  46.8 us
    pallas_call x1, Pallas kernels, attention(): pl.pallas_call(functools.partial(attention_kernel, heads), out_shape=(jax...  31 us
    ppermute x1, waiting for transfers between devices, body(): lax.ppermute(dhalo, 'seq', [(i + span, i) for i in range(shards - span)])  26 us
    all_to_all x4, starting transfers between devices, exchange(): lax.all_to_all(x, ('seq', 'kvh'), 0, 0, tiled=True, axis_index_groups=gro...  16.4 us
    pallas_call x2, Pallas kernels, unpack(): pl.pallas_call(unpack_kernel, out_shape=(shape, shape), in_specs=[VMEM],...  5.36 us
    pallas_call x2, Pallas kernels, pack(): pl.pallas_call(pack_kernel, out_shape=jax.ShapeDtypeStruct((groups, rows,...  5.3 us
    ppermute x1, starting transfers between devices, body(): lax.ppermute(own, 'seq', [(i, i + span) for i in range(shards - span)])  4.51 us
    convert_element_type x1, other arithmetic, body(): total = (down + back.astype(jnp.float32)).astype(jnp.bfloat16)  2.92 us
  transfers between devices with their start and end apart: 6, of which 4 were waited for; matrix products, arithmetic and copies ran while one was open for 2% of the time, Pallas kernels for 4%

profile of v1, /device:TPU:0, one launch (start us, length us, event | category | flops | bytes accessed | tf_op | source)
XLA Modules:
  0.0 142.6 jit_solution(14061419985038256755)
XLA Ops:
  0.6 2.3 %pack.3 = bf16[8,128,512]{2,1,0:T(8,128)(2,1)} custom-call(bf16[128,2048]{1,0:T(8,128)(2,1)} %a_ref.3, bf16[128,2048]{1,0:T(8,128)(2,1)} %b_ref.3), custom_call_target="tpu_custom_call" | custom-call | tf_op jit(solution)/shard_map/pack/pallas_call | solution.py:153
  2.9 5.2 %all-to-all-start.1 = ((bf16[8,128,512]{2,1,0:T(8,128)(2,1)}), bf16[8,128,512]{2,1,0:T(8,128)(2,1)S(1)}, u32[]{:S(2)}, u32[]{:S(2)}) async-start(bf16[8,128,512]{2,1,0:T(8,128)(2,1)} %pack.3), calls=%async_computation.1 | async-start | bytes 2097152 | tf_op jit(solution)/shard_map/all_to_all | solution.py:193
  8.1 3.0 %pack.2 = bf16[8,128,1024]{2,1,0:T(8,128)(2,1)} custom-call(bf16[128,4096]{1,0:T(8,128)(2,1)} %a_ref.2, bf16[128,4096]{1,0:T(8,128)(2,1)} %b_ref.2), custom_call_target="tpu_custom_call" | custom-call | tf_op jit(solution)/shard_map/pack/pallas_call | solution.py:153
  11.1 12.4 %all-to-all-done.1 = bf16[8,128,512]{2,1,0:T(8,128)(2,1)S(1)} async-done(((bf16[8,128,512]{2,1,0:T(8,128)(2,1)}), bf16[8,128,512]{2,1,0:T(8,128)(2,1)S(1)}, u32[]{:S(2)}, u32[]{:S(2)}) %all-to-all-start.1) | async-done | bytes 1048608 | tf_op jit(solution)/shard_map/all_to_all | solution.py:193
  23.5 0.0 copy-start.2
  23.5 3.6 %all-to-all-start = ((bf16[8,128,1024]{2,1,0:T(8,128)(2,1)}), bf16[8,128,1024]{2,1,0:T(8,128)(2,1)S(1)}, u32[]{:S(2)}, u32[]{:S(2)}) async-start(bf16[8,128,1024]{2,1,0:T(8,128)(2,1)} %pack.2), calls=%async_computation | async-start | bytes 4194304 | tf_op jit(solution)/shard_map/all_to_all | solution.py:193
  27.1 0.0 copy-done.2
  27.1 4.5 %collective-permute-start = (bf16[1024,512]{1,0:T(8,128)(2,1)S(1)}, bf16[1024,512]{1,0:T(8,128)(2,1)}, u32[]{:S(2)}, u32[]{:S(2)}) collective-permute-start(bf16[1024,512]{1,0:T(8,128)(2,1)S(1)} %bitcast.6), channel_id=1, source_target_pairs={{0,8},{4,12},{8,16},{12,20},{16,24},{20,28},{1,9},{5,13},{9,17},{1... | collective-permute-start | bytes 3145736 | tf_op jit(solution)/shard_map/ppermute | solution.py:196
  31.6 22.1 %all-to-all-done = bf16[8,128,1024]{2,1,0:T(8,128)(2,1)S(1)} async-done(((bf16[8,128,1024]{2,1,0:T(8,128)(2,1)}), bf16[8,128,1024]{2,1,0:T(8,128)(2,1)S(1)}, u32[]{:S(2)}, u32[]{:S(2)}) %all-to-all-start) | async-done | bytes 2097184 | tf_op jit(solution)/shard_map/all_to_all | solution.py:193
  53.7 0.0 copy-start
  53.7 0.0 collective-permute-done.halo_ref
  53.7 1.3 copy-done
  55.0 31.0 %attention.1 = (bf16[1024,1024]{1,0:T(8,128)(2,1)}, bf16[1024,512]{1,0:T(8,128)(2,1)}, f32[1024,512]{1,0:T(8,128)}) custom-call(s32[1]{0:T(128)} %bitcast.first_ref, bf16[1024,1024]{1,0:T(8,128)(2,1)} %bitcast.5, bf16[1024,512]{1,0:T(8,128)(2,1)} %collective-permute-done.halo_ref, bf16[1024,512]{1,0:T(8,128)(2,1)} %bitcast.7), custom_call_target="tpu_custom_call" | custom-call | tf_op jit(solution)/shard_map/attention/pallas_call | solution.py:123
  86.0 0.0 copy-start.4
  86.0 3.7 %all-to-all-start.2 = ((bf16[8,128,1024]{2,1,0:T(8,128)(2,1)}), bf16[8,128,1024]{2,1,0:T(8,128)(2,1)S(1)}, u32[]{:S(2)}, u32[]{:S(2)}) async-start(bf16[8,128,1024]{2,1,0:T(8,128)(2,1)} %bitcast.9), calls=%async_computation.2 | async-start | bytes 4194304 | tf_op jit(solution)/shard_map/all_to_all | solution.py:193
  89.8 0.0 copy-done.4
  89.8 1.3 collective-permute-start.1
  91.1 26.0 %collective-permute-done.1 = bf16[1024,512]{1,0:T(8,128)(2,1)S(1)} collective-permute-done((bf16[1024,512]{1,0:T(8,128)(2,1)S(1)}, bf16[1024,512]{1,0:T(8,128)(2,1)S(1)}, u32[]{:S(2)}, u32[]{:S(2)}) %collective-permute-start.1) | collective-permute-done | bytes 1048608 | tf_op jit(solution)/shard_map/ppermute | solution.py:199
  117.1 2.9 %add_convert_fusion = bf16[1024,512]{1,0:T(8,128)(2,1)} fusion(f32[1024,512]{1,0:T(8,128)} %get-tuple-element.14, bf16[1024,512]{1,0:T(8,128)(2,1)S(1)} %collective-permute-done.1), kind=kLoop, calls=%fused_computation | loop fusion | flops 1572864 | bytes 4194304 | tf_op jit(solution)/shard_map/convert_element_type | solution.py:201
  120.0 0.0 all-to-all-done.2.x_ref
  120.0 0.0 copy-start.1
  120.0 3.9 %all-to-all-start.3 = ((bf16[8,128,512]{2,1,0:T(8,128)(2,1)}), bf16[8,128,512]{2,1,0:T(8,128)(2,1)S(1)}, u32[]{:S(2)}, u32[]{:S(2)}) async-start(bf16[8,128,512]{2,1,0:T(8,128)(2,1)} %bitcast.8), calls=%async_computation.3 | async-start | bytes 2097152 | tf_op jit(solution)/shard_map/all_to_all | solution.py:193
  123.9 0.0 copy-done.1
  123.9 3.0 %unpack.2 = (bf16[128,4096]{1,0:T(8,128)(2,1)}, bf16[128,4096]{1,0:T(8,128)(2,1)}) custom-call(bf16[8,128,1024]{2,1,0:T(8,128)(2,1)} %copy-done.1), custom_call_target="tpu_custom_call" | custom-call | tf_op jit(solution)/shard_map/unpack/pallas_call | solution.py:174
  127.0 12.4 %all-to-all-done.3.x_ref = bf16[8,128,512]{2,1,0:T(8,128)(2,1)S(1)} async-done(((bf16[8,128,512]{2,1,0:T(8,128)(2,1)}), bf16[8,128,512]{2,1,0:T(8,128)(2,1)S(1)}, u32[]{:S(2)}, u32[]{:S(2)}) %all-to-all-start.3) | async-done | bytes 1048608 | tf_op jit(solution)/shard_map/all_to_all | solution.py:193
  139.3 0.0 copy-start.3
  139.3 1.0 copy-done.3
  140.3 2.3 %unpack.3 = (bf16[128,2048]{1,0:T(8,128)(2,1)}, bf16[128,2048]{1,0:T(8,128)(2,1)}) custom-call(bf16[8,128,512]{2,1,0:T(8,128)(2,1)} %copy-done.3), custom_call_target="tpu_custom_call" | custom-call | tf_op jit(solution)/shard_map/unpack/pallas_call | solution.py:174
Async XLA Ops:
  2.9 20.6 %all-to-all-start.1 = ((bf16[8,128,512]{2,1,0:T(8,128)(2,1)}), bf16[8,128,512]{2,1,0:T(8,128)(2,1)S(1)}, u32[]{:S(2)}, u32[]{:S(2)}) async-start(bf16[8,128,512]{2,1,0:T(8,128)(2,1)} %pack.3), calls=%async_computation.1 | async-start | bytes 2097152 | tf_op jit(solution)/shard_map/all_to_all | solution.py:193
  23.5 3.6 %copy-start.2 = (bf16[8,128,512]{2,1,0:T(8,128)(2,1)}, bf16[8,128,512]{2,1,0:T(8,128)(2,1)S(1)}, u32[]{:S(2)}) copy-start(bf16[8,128,512]{2,1,0:T(8,128)(2,1)S(1)} %all-to-all-done.1) | copy-start | bytes 3145732
  23.5 30.2 %all-to-all-start = ((bf16[8,128,1024]{2,1,0:T(8,128)(2,1)}), bf16[8,128,1024]{2,1,0:T(8,128)(2,1)S(1)}, u32[]{:S(2)}, u32[]{:S(2)}) async-start(bf16[8,128,1024]{2,1,0:T(8,128)(2,1)} %pack.2), calls=%async_computation | async-start | bytes 4194304 | tf_op jit(solution)/shard_map/all_to_all | solution.py:193
  27.1 26.6 %collective-permute-start = (bf16[1024,512]{1,0:T(8,128)(2,1)S(1)}, bf16[1024,512]{1,0:T(8,128)(2,1)}, u32[]{:S(2)}, u32[]{:S(2)}) collective-permute-start(bf16[1024,512]{1,0:T(8,128)(2,1)S(1)} %bitcast.6), channel_id=1, source_target_pairs={{0,8},{4,12},{8,16},{12,20},{16,24},{20,28},{1,9},{5,13},{9,17},{1... | collective-permute-start | bytes 3145736 | tf_op jit(solution)/shard_map/ppermute | solution.py:196
  53.7 1.4 copy-start
  86.0 3.7 %copy-start.4 = (bf16[1024,512]{1,0:T(8,128)(2,1)S(1)}, bf16[1024,512]{1,0:T(8,128)(2,1)}, u32[]{:S(2)}) copy-start(bf16[1024,512]{1,0:T(8,128)(2,1)} %get-tuple-element.15) | copy-start | bytes 3145732
  86.0 34.0 %all-to-all-start.2 = ((bf16[8,128,1024]{2,1,0:T(8,128)(2,1)}), bf16[8,128,1024]{2,1,0:T(8,128)(2,1)S(1)}, u32[]{:S(2)}, u32[]{:S(2)}) async-start(bf16[8,128,1024]{2,1,0:T(8,128)(2,1)} %bitcast.9), calls=%async_computation.2 | async-start | bytes 4194304 | tf_op jit(solution)/shard_map/all_to_all | solution.py:193
  89.8 27.3 %collective-permute-start.1 = (bf16[1024,512]{1,0:T(8,128)(2,1)S(1)}, bf16[1024,512]{1,0:T(8,128)(2,1)S(1)}, u32[]{:S(2)}, u32[]{:S(2)}) collective-permute-start(bf16[1024,512]{1,0:T(8,128)(2,1)S(1)} %copy-done.4), channel_id=1, source_target_pairs={{8,0},{12,4},{16,8},{20,12},{24,16},{28,20},{9,1},{13,5},{17,9},{2... | collective-permute-start | bytes 3145736 | tf_op jit(solution)/shard_map/ppermute | solution.py:199
  120.0 3.9 %copy-start.1 = (bf16[8,128,1024]{2,1,0:T(8,128)(2,1)}, bf16[8,128,1024]{2,1,0:T(8,128)(2,1)S(1)}, u32[]{:S(2)}) copy-start(bf16[8,128,1024]{2,1,0:T(8,128)(2,1)S(1)} %all-to-all-done.2.x_ref) | copy-start | bytes 6291460
  120.0 19.3 %all-to-all-start.3 = ((bf16[8,128,512]{2,1,0:T(8,128)(2,1)}), bf16[8,128,512]{2,1,0:T(8,128)(2,1)S(1)}, u32[]{:S(2)}, u32[]{:S(2)}) async-start(bf16[8,128,512]{2,1,0:T(8,128)(2,1)} %bitcast.8), calls=%async_computation.3 | async-start | bytes 2097152 | tf_op jit(solution)/shard_map/all_to_all | solution.py:193
  139.3 1.0 copy-start.3

commit v2 on v1

v2 whole, which is shorter than its diff:
```python
import functools

import jax
import jax.numpy as jnp
from jax import lax
from jax.experimental import pallas as pl
from jax.experimental.pallas import tpu as pltpu
from jax.sharding import PartitionSpec as P

HEAD_DIM = 128
PAIR = 2 * HEAD_DIM
WINDOW = 1024
BLOCK = 128
CHUNKS = WINDOW // BLOCK + 1
SCORE_SCALE = 168.0 ** (-0.5)
EXP2_SCALE = SCORE_SCALE * 1.4426950408889634
EXCLUDED = -1e30
ONES = 16

NN = (((1,), (0,)), ((), ()))
NT = (((1,), (1,)), ((), ()))

VMEM = pl.BlockSpec(memory_space=pltpu.VMEM)
SMEM = pl.BlockSpec(memory_space=pltpu.SMEM)
ANY = pl.BlockSpec(memory_space=pl.ANY)
HBM = pl.BlockSpec(memory_space=pltpu.HBM)


def dot(left, right, dims):
    return lax.dot_general(left, right, dims, preferred_element_type=jnp.float32)


def side_by_side(x):
    return jnp.concatenate([x[:, :HEAD_DIM].T, x[:, HEAD_DIM:].T], 1)


def attention_kernel(
    head, first_ref, qo_hbm, halo_hbm, own_hbm, ao_hbm, dhalo_hbm, down_hbm,
    kv, qo, ao, dhalo, keys_t, values_t, acc_k, acc_v, exps0, exps1, q_turned, o_turned, in_sem, q_sem, out_sem,
):
    rows = qo.shape[0]
    blocks = rows // BLOCK
    whole = WINDOW // BLOCK
    exps = (exps0, exps1)

    def at(i):
        return pl.ds(pl.multiple_of(i * BLOCK, BLOCK), BLOCK)

    def span(i):
        return pl.ds(pl.multiple_of(i * BLOCK, BLOCK), CHUNKS * BLOCK)

    def qo_copy(i):
        return pltpu.make_async_copy(qo_hbm.at[at(i)], qo.at[at(i)], q_sem.at[i])

    def ao_copy(i):
        return pltpu.make_async_copy(ao.at[at(i)], ao_hbm.at[at(i)], out_sem.at[0, i])

    def dhalo_copy(i):
        return pltpu.make_async_copy(dhalo.at[at(i)], dhalo_hbm.at[at(i)], out_sem.at[1, i])

    halo_copy = pltpu.make_async_copy(halo_hbm, kv.at[pl.ds(0, WINDOW)], in_sem.at[0])
    own_copy = pltpu.make_async_copy(
        own_hbm.at[:, pl.ds(head * PAIR, PAIR)], kv.at[pl.ds(WINDOW, rows)], in_sem.at[1]
    )
    halo_copy.start()
    own_copy.start()
    for i in range(blocks):
        qo_copy(i).start()

    ones_row = lax.broadcasted_iota(jnp.int32, (ONES, values_t.shape[1]), 0) == 0
    values_t[HEAD_DIM:, :] = jnp.where(ones_row, 1.0, 0.0).astype(jnp.bfloat16)
    acc_k[:, : WINDOW + BLOCK] = jnp.zeros((HEAD_DIM, WINDOW + BLOCK), jnp.float32)
    acc_v[:, : WINDOW + BLOCK] = jnp.zeros((HEAD_DIM, WINDOW + BLOCK), jnp.float32)
    exps1[...] = jnp.ones_like(exps1)
    q_turned[...] = jnp.zeros_like(q_turned)
    o_turned[...] = jnp.zeros_like(o_turned)
    key_at = lax.broadcasted_iota(jnp.int32, (BLOCK, 2 * BLOCK), 0)
    query_at = lax.broadcasted_iota(jnp.int32, (BLOCK, 2 * BLOCK), 1) & (BLOCK - 1)
    first = first_ref[0]

    def turn(target, source):
        keys_t[:, at(target)] = kv[at(source), :HEAD_DIM].T
        values_t[:HEAD_DIM, at(target)] = kv[at(source), HEAD_DIM:].T

    halo_copy.wait()
    own_copy.wait()
    for c in range(whole + 1):
        turn(c, c)

    def scores_of(slot, i):
        q_t, o_t = side_by_side(qo[at(i), :PAIR]), side_by_side(qo[at(i), PAIR:])
        q_turned[slot] = q_t
        o_turned[slot] = o_t
        bias = [
            jnp.where((first > 0) & (i + c < whole), EXCLUDED, 0.0).astype(jnp.float32) for c in range(CHUNKS - 1)
        ]
        scores = dot(kv[span(i), :HEAD_DIM], q_t, NN)
        parts = [scores[c * BLOCK : (c + 1) * BLOCK] for c in range(CHUNKS)]
        parts[0] = jnp.where(key_at > query_at, parts[0], EXCLUDED)
        parts[-1] = jnp.where(key_at <= query_at, parts[-1], EXCLUDED)
        top = jnp.max(parts[-1], axis=0, keepdims=True)
        for c in range(CHUNKS - 1):
            top = jnp.maximum(top, jnp.max(parts[c], axis=0, keepdims=True) + bias[c])
        top = top * EXP2_SCALE
        return parts, [top - b for b in bias] + [top]

    def exponentials(slot, parts, shifts):
        for c in range(CHUNKS):
            exps[slot][c * BLOCK : (c + 1) * BLOCK] = jnp.exp2(parts[c] * EXP2_SCALE - shifts[c]).astype(jnp.bfloat16)

    def attended_of(slot, i):
        out = dot(values_t[:, span(i)], exps[slot][...], NN)
        inverse = 1.0 / out[HEAD_DIM : HEAD_DIM + 1]
        out = out[:HEAD_DIM] * inverse
        grad_out = o_turned[slot].astype(jnp.float32)
        delta = jnp.sum(out * grad_out, axis=0, keepdims=True)
        out = out.astype(jnp.bfloat16)
        ao[at(i), :HEAD_DIM] = out[:, :BLOCK].T
        ao[at(i), HEAD_DIM:PAIR] = out[:, BLOCK:].T
        o_scaled = (grad_out * inverse).astype(jnp.bfloat16)
        q_scaled = (q_turned[slot].astype(jnp.float32) * inverse).astype(jnp.bfloat16)
        return inverse, delta, o_scaled, q_scaled

    def gradients(slot, i, inverse, delta, o_scaled, q_scaled):
        grad_weights = dot(kv[span(i), HEAD_DIM:], o_turned[slot], NN)
        grad_scores = []
        for c in range(CHUNKS):
            part = slice(c * BLOCK, (c + 1) * BLOCK)
            grad_scores.append(
                (exps[slot][part].astype(jnp.float32) * (grad_weights[part] - delta)).astype(jnp.bfloat16)
            )
        grad_scores = jnp.concatenate(grad_scores, 0)
        acc_v[:, span(i)] += dot(o_scaled, exps[slot][...], NT)
        grad_q = (dot(keys_t[:, span(i)], grad_scores, NN) * (inverse * SCORE_SCALE)).astype(jnp.bfloat16)
        ao[at(i), PAIR : PAIR + HEAD_DIM] = grad_q[:, :BLOCK].T
        ao[at(i), PAIR + HEAD_DIM :] = grad_q[:, BLOCK:].T
        acc_k[:, span(i)] += dot(q_scaled, grad_scores, NT)

    def flush(i):
        dhalo[at(i), :HEAD_DIM] = (acc_k[:, at(i)] * SCORE_SCALE).astype(jnp.bfloat16).T
        dhalo[at(i), HEAD_DIM:] = acc_v[:, at(i)].astype(jnp.bfloat16).T

    def both(slot, i, before):
        known = attended_of(1 - slot, before)
        parts, shifts = scores_of(slot, i)
        exponentials(slot, parts, shifts)
        gradients(1 - slot, before, *known)
        flush(before)
        turn(i + whole + 1, jnp.minimum(i + whole + 1, whole + blocks - 1))
        acc_k[:, at(i + whole + 1)] = jnp.zeros((HEAD_DIM, BLOCK), jnp.float32)
        acc_v[:, at(i + whole + 1)] = jnp.zeros((HEAD_DIM, BLOCK), jnp.float32)

    def step(j, carry):
        i = 2 * j
        qo_copy(i).wait()
        qo_copy(i + 1).wait()
        both(0, i, jnp.maximum(i - 1, 0))
        both(1, i + 1, i)

        @pl.when(j > 0)
        def _():
            ao_copy(i - 1).start()
            dhalo_copy(i - 1).start()

        ao_copy(i).start()
        dhalo_copy(i).start()
        return carry

    lax.fori_loop(0, blocks // 2, step, 0)
    gradients(1, blocks - 1, *attended_of(1, blocks - 1))
    flush(blocks - 1)
    ao_copy(blocks - 1).start()
    dhalo_copy(blocks - 1).start()
    own_k = pltpu.make_async_copy(acc_k.at[:, pl.ds(WINDOW, rows)], down_hbm.at[0], in_sem.at[0])
    own_v = pltpu.make_async_copy(acc_v.at[:, pl.ds(WINDOW, rows)], down_hbm.at[1], in_sem.at[1])
    own_k.start()
    own_v.start()
    for i in range(blocks):
        ao_copy(i).wait()
        dhalo_copy(i).wait()
    own_k.wait()
    own_v.wait()


def attention(head, first, qo, halo, own):
    rows = own.shape[0]
    blocks = rows // BLOCK
    reach = WINDOW + rows
    bf16, f32 = jnp.bfloat16, jnp.float32
    return pl.pallas_call(
        functools.partial(attention_kernel, head),
        out_shape=(
            jax.ShapeDtypeStruct(qo.shape, bf16),
            jax.ShapeDtypeStruct(halo.shape, bf16),
            jax.ShapeDtypeStruct((2, HEAD_DIM, rows), f32),
        ),
        in_specs=[SMEM, ANY, ANY, ANY],
        out_specs=(HBM, HBM, HBM),
        scratch_shapes=[
            pltpu.VMEM((reach, PAIR), bf16),
            pltpu.VMEM(qo.shape, bf16),
            pltpu.VMEM(qo.shape, bf16),
            pltpu.VMEM(halo.shape, bf16),
            pltpu.VMEM((HEAD_DIM, reach + BLOCK), bf16),
            pltpu.VMEM((HEAD_DIM + ONES, reach + BLOCK), bf16),
            pltpu.VMEM((HEAD_DIM, reach + BLOCK), f32),
            pltpu.VMEM((HEAD_DIM, reach + BLOCK), f32),
            pltpu.VMEM((CHUNKS * BLOCK, 2 * BLOCK), bf16),
            pltpu.VMEM((CHUNKS * BLOCK, 2 * BLOCK), bf16),
            pltpu.VMEM((2, HEAD_DIM, 2 * BLOCK), bf16),
            pltpu.VMEM((2, HEAD_DIM, 2 * BLOCK), bf16),
            pltpu.SemaphoreType.DMA((2,)),
            pltpu.SemaphoreType.DMA((blocks,)),
            pltpu.SemaphoreType.DMA((2, blocks)),
        ],
        compiler_params=pltpu.CompilerParams(vmem_limit_bytes=32 * 2**20),
        cost_estimate=pl.CostEstimate(flops=10**10, bytes_accessed=4 * 2**20, transcendentals=0),
        name="attention",
    )(first, qo, halo, own)


def interleave_kernel(width, parts, *refs):
    *arrays, out = refs
    for g in range(out.shape[0]):
        for n, (which, start, stride) in enumerate(parts):
            first = g * stride + start
            out[g, :, n * width : (n + 1) * width] = arrays[which][:, first : first + width]


def interleave(arrays, groups, width, parts):
    rows = arrays[0].shape[0]
    return pl.pallas_call(
        functools.partial(interleave_kernel, width, parts),
        out_shape=jax.ShapeDtypeStruct((groups, rows, width * len(parts)), arrays[0].dtype),
        in_specs=[VMEM] * len(arrays),
        out_specs=VMEM,
        compiler_params=pltpu.CompilerParams(vmem_limit_bytes=16 * 2**20),
        name="interleave",
    )(*arrays)


def spread_kernel(x_ref, y_ref, a_ref, b_ref):
    groups, _, width = x_ref.shape
    half = width // 2
    for g in range(groups):
        for n, ref in enumerate((x_ref, y_ref)):
            cols = slice(g * width + n * half, g * width + (n + 1) * half)
            a_ref[:, cols] = ref[g, :, :half]
            b_ref[:, cols] = ref[g, :, half:]


def spread(x, y):
    groups, rows, width = x.shape
    shape = jax.ShapeDtypeStruct((rows, groups * width), x.dtype)
    return pl.pallas_call(
        spread_kernel,
        out_shape=(shape, shape),
        in_specs=[VMEM, VMEM],
        out_specs=(VMEM, VMEM),
        compiler_params=pltpu.CompilerParams(vmem_limit_bytes=16 * 2**20),
        name="spread",
    )(x, y)


def add_kernel(own0_ref, own1_ref, back0_ref, back1_ref, out_ref):
    for h, (own, back) in enumerate(((own0_ref, back0_ref), (own1_ref, back1_ref))):
        for i in range(out_ref.shape[0] // BLOCK):
            rows = slice(i * BLOCK, (i + 1) * BLOCK)
            for n, scale in enumerate((SCORE_SCALE, 1.0)):
                total = (own[n, :, rows] * scale).T + back[rows, n * HEAD_DIM : (n + 1) * HEAD_DIM].astype(jnp.float32)
                cols = slice((2 * n + h) * HEAD_DIM, (2 * n + h + 1) * HEAD_DIM)
                out_ref[rows, cols] = total.astype(jnp.bfloat16)


def add(own, back):
    rows, width = back[0].shape
    return pl.pallas_call(
        add_kernel,
        out_shape=jax.ShapeDtypeStruct((rows, 2 * width), jnp.bfloat16),
        in_specs=[VMEM] * 4,
        out_specs=VMEM,
        compiler_params=pltpu.CompilerParams(vmem_limit_bytes=16 * 2**20),
        name="add",
    )(*own, *back)


def unpack_kernel(x_ref, a_ref, b_ref):
    groups, _, width = x_ref.shape
    half = width // 2
    for g in range(groups):
        a_ref[:, g * half : (g + 1) * half] = x_ref[g, :, :half]
        b_ref[:, g * half : (g + 1) * half] = x_ref[g, :, half:]


def unpack(x):
    groups, rows, width = x.shape
    shape = jax.ShapeDtypeStruct((rows, groups * width // 2), x.dtype)
    return pl.pallas_call(
        unpack_kernel,
        out_shape=(shape, shape),
        in_specs=[VMEM],
        out_specs=(VMEM, VMEM),
        compiler_params=pltpu.CompilerParams(vmem_limit_bytes=16 * 2**20),
        name="unpack",
    )(x)


def body(queries, key_rows, value_rows, grad_out):
    shards, split = lax.axis_size("seq"), lax.axis_size("kvh")
    rows = queries.shape[0]
    apart = WINDOW // (rows * split)
    members = apart * split
    heads = key_rows.shape[1] // (members * HEAD_DIM)
    groups = [[g * members + i for i in range(members)] for g in range(shards // apart)]
    first = (lax.axis_index("seq") < apart).astype(jnp.int32).reshape(1)

    def exchange(x):
        return lax.all_to_all(x, ("seq", "kvh"), 0, 0, tiled=True, axis_index_groups=groups)

    def onward(x):
        return lax.ppermute(x, "seq", [(i, i + apart) for i in range(shards - apart)])

    def backward(x):
        return lax.ppermute(x, "seq", [(i + apart, i) for i in range(shards - apart)])

    stride = heads * HEAD_DIM
    kv_parts = [(n, h * HEAD_DIM, stride) for h in range(heads) for n in range(2)]
    own = exchange(interleave((key_rows, value_rows), members, HEAD_DIM, kv_parts)).reshape(WINDOW, -1)
    halos = [onward(own[:, h * PAIR : (h + 1) * PAIR]) for h in range(heads)]
    outs, down, back = [], [], []
    for h in range(heads):
        qo_parts = [(n, h * PAIR, 2 * stride) for n in range(2)]
        qo = exchange(interleave((queries, grad_out), members, PAIR, qo_parts)).reshape(WINDOW, -1)
        ao, dhalo, mine = attention(h, first, qo, halos[h], own)
        if h > 0:
            ao, back[h - 1] = lax.optimization_barrier((ao, back[h - 1]))
        back.append(backward(dhalo))
        outs.append(exchange(ao.reshape(members, rows, -1)))
        down.append(mine)
    *outs, total = lax.optimization_barrier((*outs, add(down, back)))
    grad_k, grad_v = unpack(exchange(total.reshape(members, rows, -1)))
    attended, grad_q = spread(*outs)
    return (attended, grad_q, grad_k, grad_v)


def solution(mesh):
    placed = P(("seq", "kvh"), None)
    return jax.shard_map(
        body, mesh=mesh, in_specs=(placed,) * 4, out_specs=(placed,) * 4, check_vma=False
    )
```

time: 143 us -> 129 us (0.902)
  waiting for transfers between devices: 72.8 us -> 51.3 us
  starting transfers between devices: 22.2 us -> 35.8 us
  Pallas kernels: 41.7 us -> 31.4 us
  local copies, waits for them, and re-layouts: 2.34 us -> 9.02 us
  other arithmetic: 2.92 us -> 0 us
    ppermute x2 -> x4, waiting for transfers between devices: 26 us -> 15.1 us  [the longest x2 15.1 us: backward(): lax.ppermute(x, 'seq', [(i + apart, i) for i in range(shards - apart)])]
    all_to_all x4 -> x6, waiting for transfers between devices: 46.8 us -> 36.2 us  [exchange(): lax.all_to_all(x, ('seq', 'kvh'), 0, 0, tiled=True, axis_index_groups=gro...]
    all_to_all x4 -> x6, starting transfers between devices: 16.4 us -> 25.5 us  [exchange(): lax.all_to_all(x, ('seq', 'kvh'), 0, 0, tiled=True, axis_index_groups=gro...]
    pallas_call x3 -> x7, Pallas kernels: 36.3 us -> 30.3 us  [the longest x2 24.8 us: attention(): pl.pallas_call(functools.partial(attention_kernel, head), out_shape=(jax....]
    unnamed x10 -> x24, local copies, waits for them, and re-layouts: 2.34 us -> 7.99 us
    ppermute x2 -> x4, starting transfers between devices: 5.8 us -> 10.4 us  [the longest x2 7.79 us: onward(): lax.ppermute(x, 'seq', [(i, i + apart) for i in range(shards - apart)])]
    pallas_call x2 -> x1, Pallas kernels: 5.36 us -> 1.1 us  [unpack(): pl.pallas_call(unpack_kernel, out_shape=(shape, shape), in_specs=[VMEM],...]
    convert_element_type x1 -> x0, other arithmetic: 2.92 us -> none  [body(): total = (down + back.astype(jnp.float32)).astype(jnp.bfloat16)]
  transfers between devices with their start and end apart: 6 -> 10, of which waited for: 4 -> 5; matrix products, arithmetic and copies ran while one was open for 2% -> 1% of each run, Pallas kernels for 4% -> 23%
where the time goes in v2:
time: 129 us; the launch traced here: 128 us
  waiting for transfers between devices  51.3 us (40%)
  starting transfers between devices  35.8 us (28%)
  Pallas kernels  31.4 us (24%)
  local copies, waits for them, and re-layouts  9.02 us (7%)
    all_to_all x6, waiting for transfers between devices, exchange(): lax.all_to_all(x, ('seq', 'kvh'), 0, 0, tiled=True, axis_index_groups=gro...  36.2 us
    all_to_all x6, starting transfers between devices, exchange(): lax.all_to_all(x, ('seq', 'kvh'), 0, 0, tiled=True, axis_index_groups=gro...  25.5 us
    pallas_call x2, Pallas kernels, attention(): pl.pallas_call(functools.partial(attention_kernel, head), out_shape=(jax....  24.8 us
    ppermute x2, waiting for transfers between devices, backward(): lax.ppermute(x, 'seq', [(i + apart, i) for i in range(shards - apart)])  15.1 us
    unnamed x24, local copies, waits for them, and re-layouts  7.99 us
    ppermute x2, starting transfers between devices, onward(): lax.ppermute(x, 'seq', [(i, i + apart) for i in range(shards - apart)])  7.79 us
  transfers between devices with their start and end apart: 10, of which 5 were waited for; matrix products, arithmetic and copies ran while one was open for 1% of the time, Pallas kernels for 23%

profile of v2, /device:TPU:0, one launch (start us, length us, event | category | flops | bytes accessed | tf_op | source)
XLA Modules:
  0.0 128.3 jit_solution(11502171159517661760)
XLA Ops:
  0.6 0.0 copy-start.9
  0.6 1.0 copy-done.9
  1.7 0.0 copy-start.10
  1.7 1.0 copy-done.10
  2.7 0.2 interleave.4
  2.9 0.0 copy-start.2
  2.9 1.0 copy-done.2
  3.9 0.0 copy-start
  3.9 5.3 %all-to-all-start.1 = ((bf16[8,128,512]{2,1,0:T(8,128)(2,1)}), bf16[8,128,512]{2,1,0:T(8,128)(2,1)S(1)}, u32[]{:S(2)}, u32[]{:S(2)}) async-start(bf16[8,128,512]{2,1,0:T(8,128)(2,1)} %copy-done.2), calls=%async_computation.1 | async-start | bytes 2097152 | tf_op jit(solution)/shard_map/all_to_all | solution.py:318
  9.2 0.0 copy-done
  9.2 0.0 copy-done.1
  9.2 1.1 interleave.3
  10.3 14.3 %all-to-all-done.1 = bf16[8,128,512]{2,1,0:T(8,128)(2,1)S(1)} async-done(((bf16[8,128,512]{2,1,0:T(8,128)(2,1)}), bf16[8,128,512]{2,1,0:T(8,128)(2,1)S(1)}, u32[]{:S(2)}, u32[]{:S(2)}) %all-to-all-start.1) | async-done | bytes 1048608 | tf_op jit(solution)/shard_map/all_to_all | solution.py:318
  24.6 4.2 %all-to-all-start = ((bf16[8,128,512]{2,1,0:T(8,128)(2,1)}), bf16[8,128,512]{2,1,0:T(8,128)(2,1)}, u32[]{:S(2)}, u32[]{:S(2)}) async-start(bf16[8,128,512]{2,1,0:T(8,128)(2,1)} %interleave.3), calls=%async_computation | async-start | bytes 2097152 | tf_op jit(solution)/shard_map/all_to_all | solution.py:318
  28.8 1.0 fusion
  29.9 4.3 %collective-permute-start = (bf16[1024,256]{1,0:T(8,128)(2,1)}, bf16[1024,256]{1,0:T(8,128)(2,1)}, u32[]{:S(2)}, u32[]{:S(2)}) collective-permute-start(bf16[1024,256]{1,0:T(8,128)(2,1)} %get-tuple-element.35), channel_id=1, source_target_pairs={{0,8},{4,12},{8,16},{12,20},{16,24},{20,28},{1,9},{5,13},{9,17},{1... | collective-permute-start | bytes 1572872 | tf_op jit(solution)/shard_map/ppermute | solution.py:321
  34.2 1.1 interleave.5
  35.2 3.5 %collective-permute-start.1 = (bf16[1024,256]{1,0:T(8,128)(2,1)}, bf16[1024,256]{1,0:T(8,128)(2,1)}, u32[]{:S(2)}, u32[]{:S(2)}) collective-permute-start(bf16[1024,256]{1,0:T(8,128)(2,1)} %get-tuple-element.34), channel_id=1, source_target_pairs={{0,8},{4,12},{8,16},{12,20},{16,24},{20,28},{1,9},{5,13},{9,17},{1... | collective-permute-start | bytes 1572872 | tf_op jit(solution)/shard_map/ppermute | solution.py:321
  38.7 5.5 %all-to-all-done = bf16[8,128,512]{2,1,0:T(8,128)(2,1)} async-done(((bf16[8,128,512]{2,1,0:T(8,128)(2,1)}), bf16[8,128,512]{2,1,0:T(8,128)(2,1)}, u32[]{:S(2)}, u32[]{:S(2)}) %all-to-all-start) | async-done | bytes 1048608 | tf_op jit(solution)/shard_map/all_to_all | solution.py:318
  44.3 4.2 %all-to-all-start.3 = ((bf16[8,128,512]{2,1,0:T(8,128)(2,1)}), bf16[8,128,512]{2,1,0:T(8,128)(2,1)}, u32[]{:S(2)}, u32[]{:S(2)}) async-start(bf16[8,128,512]{2,1,0:T(8,128)(2,1)} %interleave.5), calls=%async_computation.3 | async-start | bytes 2097152 | tf_op jit(solution)/shard_map/all_to_all | solution.py:318
  48.5 0.0 collective-permute-done.halo_hbm
  48.5 11.6 %attention.2 = (bf16[1024,512]{1,0:T(8,128)(2,1)}, bf16[1024,256]{1,0:T(8,128)(2,1)}, f32[2,128,1024]{2,1,0:T(8,128)S(1)}) custom-call(s32[1]{0:T(128)} %bitcast.first_ref, bf16[1024,512]{1,0:T(8,128)(2,1)} %bitcast.1.qo_hbm, bf16[1024,256]{1,0:T(8,128)(2,1)} %collective-permute-done.halo_hbm, bf16[1024,512]{1,0:T(8,128)(2,1)S(1)} %bitcast.8), custom_call_target="tpu_custom_call" | custom-call | flops 10000000000 | bytes 4194304 | tf_op jit(solution)/shard_map/attention/pallas_call | solution.py:190
  60.2 0.0 copy-start.5
  60.2 1.3 %collective-permute-start.2 = (bf16[1024,256]{1,0:T(8,128)(2,1)}, bf16[1024,256]{1,0:T(8,128)(2,1)}, u32[]{:S(2)}, u32[]{:S(2)}) collective-permute-start(bf16[1024,256]{1,0:T(8,128)(2,1)} %get-tuple-element.21), channel_id=1, source_target_pairs={{8,0},{12,4},{16,8},{20,12},{24,16},{28,20},{9,1},{13,5},{17,9},{2... | collective-permute-start | bytes 1572872 | tf_op jit(solution)/shard_map/ppermute | solution.py:324
  61.5 2.5 %all-to-all-done.3 = bf16[8,128,512]{2,1,0:T(8,128)(2,1)} async-done(((bf16[8,128,512]{2,1,0:T(8,128)(2,1)}), bf16[8,128,512]{2,1,0:T(8,128)(2,1)}, u32[]{:S(2)}, u32[]{:S(2)}) %all-to-all-start.3) | async-done | bytes 1048608 | tf_op jit(solution)/shard_map/all_to_all | solution.py:318
  63.9 0.0 copy-done.5
  63.9 3.6 %all-to-all-start.2 = ((bf16[8,128,512]{2,1,0:T(8,128)(2,1)}), bf16[8,128,512]{2,1,0:T(8,128)(2,1)S(1)}, u32[]{:S(2)}, u32[]{:S(2)}) async-start(bf16[8,128,512]{2,1,0:T(8,128)(2,1)} %bitcast.3), calls=%async_computation.2 | async-start | bytes 2097152 | tf_op jit(solution)/shard_map/all_to_all | solution.py:318
  67.5 0.0 collective-permute-done.1.halo_hbm
  67.5 13.2 %attention.3 = (bf16[1024,512]{1,0:T(8,128)(2,1)S(1)}, bf16[1024,256]{1,0:T(8,128)(2,1)S(1)}, f32[2,128,1024]{2,1,0:T(8,128)S(1)}) custom-call(s32[1]{0:T(128)} %bitcast.first_ref, bf16[1024,512]{1,0:T(8,128)(2,1)} %bitcast.4.qo_hbm, bf16[1024,256]{1,0:T(8,128)(2,1)} %collective-permute-done.1.halo_hbm, bf16[1024,512]{1,0:T(8,128)(2,1)S(1)} %bitcast.9), custom_call_target="tpu_custom_call" | custom-call | flops 10000000000 | bytes 4194304 | tf_op jit(solution)/shard_map/attention/pallas_call | solution.py:190
  80.7 0.0 copy-start.4
  80.7 1.0 copy-done.4
  81.7 1.0 copy-done.7
  82.6 0.8 copy-done.11
  83.4 0.0 collective-permute-done.2.back0_ref
  83.4 0.0 all-to-all-done.2.x_ref
  83.4 4.3 %all-to-all-start.4 = ((bf16[8,128,512]{2,1,0:T(8,128)(2,1)}), bf16[8,128,512]{2,1,0:T(8,128)(2,1)S(1)}, u32[]{:S(2)}, u32[]{:S(2)}) async-start(bf16[8,128,512]{2,1,0:T(8,128)(2,1)} %bitcast.11), calls=%async_computation.4 | async-start | bytes 2097152 | tf_op jit(solution)/shard_map/all_to_all | solution.py:318
  87.7 1.3 collective-permute-start.3
  89.0 15.1 %collective-permute-done.3.back1_ref = bf16[1024,256]{1,0:T(8,128)(2,1)S(1)} collective-permute-done((bf16[1024,256]{1,0:T(8,128)(2,1)}, bf16[1024,256]{1,0:T(8,128)(2,1)S(1)}, u32[]{:S(2)}, u32[]{:S(2)}) %collective-permute-start.3) | collective-permute-done | bytes 524320 | tf_op jit(solution)/shard_map/ppermute | solution.py:324
  104.1 0.0 copy-done.6
  104.1 1.2 copy-done.8
  105.4 1.6 %add.1 = bf16[1024,512]{1,0:T(8,128)(2,1)S(1)} custom-call(f32[2,128,1024]{2,1,0:T(8,128)S(1)} %copy-done.6, f32[2,128,1024]{2,1,0:T(8,128)S(1)} %copy-done.8, bf16[1024,256]{1,0:T(8,128)(2,1)} %collective-permute-done.2.back0_ref, bf16[1024,256]{1,0:T(8,128)(2,1)S(1)} %collective-permute-done.3.back1_ref), custom_call_target="tpu_custom_call" | custom-call | tf_op jit(solution)/shard_map/add/pallas_call | solution.py:277
  107.0 0.0 copy-start.3
  107.0 1.0 copy-done.3
  108.0 0.0 all-to-all-done.4.y_ref
  108.0 3.8 %all-to-all-start.5 = ((bf16[8,128,512]{2,1,0:T(8,128)(2,1)}), bf16[8,128,512]{2,1,0:T(8,128)(2,1)S(1)}, u32[]{:S(2)}, u32[]{:S(2)}) async-start(bf16[8,128,512]{2,1,0:T(8,128)(2,1)} %bitcast.10), calls=%async_computation.5 | async-start | bytes 2097152 | tf_op jit(solution)/shard_map/all_to_all | solution.py:318
  111.8 1.6 %spread.1 = (bf16[128,4096]{1,0:T(8,128)(2,1)}, bf16[128,4096]{1,0:T(8,128)(2,1)}) custom-call(bf16[8,128,512]{2,1,0:T(8,128)(2,1)S(1)} %all-to-all-done.2.x_ref, bf16[8,128,512]{2,1,0:T(8,128)(2,1)S(1)} %all-to-all-done.4.y_ref), custom_call_target="tpu_custom_call" | custom-call | tf_op jit(solution)/shard_map/spread/pallas_call | solution.py:255
  113.4 13.8 %all-to-all-done.5.x_ref = bf16[8,128,512]{2,1,0:T(8,128)(2,1)S(1)} async-done(((bf16[8,128,512]{2,1,0:T(8,128)(2,1)}), bf16[8,128,512]{2,1,0:T(8,128)(2,1)S(1)}, u32[]{:S(2)}, u32[]{:S(2)}) %all-to-all-start.5) | async-done | bytes 1048608 | tf_op jit(solution)/shard_map/all_to_all | solution.py:318
  127.2 1.1 unpack.1
  (5 shorter events, 0.0 us)
Async XLA Ops:
  0.6 1.0 copy-start.9
  1.7 1.0 copy-start.10
  2.9 1.0 copy-start.2
  3.9 5.3 %copy-start = (bf16[128,4096]{1,0:T(8,128)(2,1)S(1)}, bf16[128,4096]{1,0:T(8,128)(2,1)}, u32[]{:S(2)}) copy-start(bf16[128,4096]{1,0:T(8,128)(2,1)} %refs_0_.5) | copy-start | bytes 3145732
  3.9 5.3 %copy-start.1 = (bf16[128,4096]{1,0:T(8,128)(2,1)S(1)}, bf16[128,4096]{1,0:T(8,128)(2,1)}, u32[]{:S(2)}) copy-start(bf16[128,4096]{1,0:T(8,128)(2,1)} %refs_1_.5) | copy-start | bytes 3145732
  3.9 20.7 %all-to-all-start.1 = ((bf16[8,128,512]{2,1,0:T(8,128)(2,1)}), bf16[8,128,512]{2,1,0:T(8,128)(2,1)S(1)}, u32[]{:S(2)}, u32[]{:S(2)}) async-start(bf16[8,128,512]{2,1,0:T(8,128)(2,1)} %copy-done.2), calls=%async_computation.1 | async-start | bytes 2097152 | tf_op jit(solution)/shard_map/all_to_all | solution.py:318
  24.6 19.7 %all-to-all-start = ((bf16[8,128,512]{2,1,0:T(8,128)(2,1)}), bf16[8,128,512]{2,1,0:T(8,128)(2,1)}, u32[]{:S(2)}, u32[]{:S(2)}) async-start(bf16[8,128,512]{2,1,0:T(8,128)(2,1)} %interleave.3), calls=%async_computation | async-start | bytes 2097152 | tf_op jit(solution)/shard_map/all_to_all | solution.py:318
  29.9 18.6 %collective-permute-start = (bf16[1024,256]{1,0:T(8,128)(2,1)}, bf16[1024,256]{1,0:T(8,128)(2,1)}, u32[]{:S(2)}, u32[]{:S(2)}) collective-permute-start(bf16[1024,256]{1,0:T(8,128)(2,1)} %get-tuple-element.35), channel_id=1, source_target_pairs={{0,8},{4,12},{8,16},{12,20},{16,24},{20,28},{1,9},{5,13},{9,17},{1... | collective-permute-start | bytes 1572872 | tf_op jit(solution)/shard_map/ppermute | solution.py:321
  35.2 32.3 %collective-permute-start.1 = (bf16[1024,256]{1,0:T(8,128)(2,1)}, bf16[1024,256]{1,0:T(8,128)(2,1)}, u32[]{:S(2)}, u32[]{:S(2)}) collective-permute-start(bf16[1024,256]{1,0:T(8,128)(2,1)} %get-tuple-element.34), channel_id=1, source_target_pairs={{0,8},{4,12},{8,16},{12,20},{16,24},{20,28},{1,9},{5,13},{9,17},{1... | collective-permute-start | bytes 1572872 | tf_op jit(solution)/shard_map/ppermute | solution.py:321
  44.3 19.7 %all-to-all-start.3 = ((bf16[8,128,512]{2,1,0:T(8,128)(2,1)}), bf16[8,128,512]{2,1,0:T(8,128)(2,1)}, u32[]{:S(2)}, u32[]{:S(2)}) async-start(bf16[8,128,512]{2,1,0:T(8,128)(2,1)} %interleave.5), calls=%async_computation.3 | async-start | bytes 2097152 | tf_op jit(solution)/shard_map/all_to_all | solution.py:318
  60.2 3.8 %copy-start.5 = (f32[2,128,1024]{2,1,0:T(8,128)}, f32[2,128,1024]{2,1,0:T(8,128)S(1)}, u32[]{:S(2)}) copy-start(f32[2,128,1024]{2,1,0:T(8,128)S(1)} %get-tuple-element.23.own0_ref) | copy-start | bytes 3145732
  60.2 23.3 %collective-permute-start.2 = (bf16[1024,256]{1,0:T(8,128)(2,1)}, bf16[1024,256]{1,0:T(8,128)(2,1)}, u32[]{:S(2)}, u32[]{:S(2)}) collective-permute-start(bf16[1024,256]{1,0:T(8,128)(2,1)} %get-tuple-element.21), channel_id=1, source_target_pairs={{8,0},{12,4},{16,8},{20,12},{24,16},{28,20},{9,1},{13,5},{17,9},{2... | collective-permute-start | bytes 1572872 | tf_op jit(solution)/shard_map/ppermute | solution.py:324
  63.9 19.5 %all-to-all-start.2 = ((bf16[8,128,512]{2,1,0:T(8,128)(2,1)}), bf16[8,128,512]{2,1,0:T(8,128)(2,1)S(1)}, u32[]{:S(2)}, u32[]{:S(2)}) async-start(bf16[8,128,512]{2,1,0:T(8,128)(2,1)} %bitcast.3), calls=%async_computation.2 | async-start | bytes 2097152 | tf_op jit(solution)/shard_map/all_to_all | solution.py:318
  80.7 1.0 copy-start.4
  81.7 1.0 copy-start.7
  82.6 0.8 copy-start.11
  83.4 20.7 %copy-start.6 = (f32[2,128,1024]{2,1,0:T(8,128)S(1)}, f32[2,128,1024]{2,1,0:T(8,128)}, u32[]{:S(2)}) copy-start(f32[2,128,1024]{2,1,0:T(8,128)} %copy-done.5) | copy-start | bytes 3145732
  83.4 24.6 %all-to-all-start.4 = ((bf16[8,128,512]{2,1,0:T(8,128)(2,1)}), bf16[8,128,512]{2,1,0:T(8,128)(2,1)S(1)}, u32[]{:S(2)}, u32[]{:S(2)}) async-start(bf16[8,128,512]{2,1,0:T(8,128)(2,1)} %bitcast.11), calls=%async_computation.4 | async-start | bytes 2097152 | tf_op jit(solution)/shard_map/all_to_all | solution.py:318
  87.7 16.4 %collective-permute-start.3 = (bf16[1024,256]{1,0:T(8,128)(2,1)}, bf16[1024,256]{1,0:T(8,128)(2,1)S(1)}, u32[]{:S(2)}, u32[]{:S(2)}) collective-permute-start(bf16[1024,256]{1,0:T(8,128)(2,1)} %copy-done.11), channel_id=1, source_target_pairs={{8,0},{12,4},{16,8},{20,12},{24,16},{28,20},{9,1},{13,5},{17,9},{2... | collective-permute-start | bytes 1572872 | tf_op jit(solution)/shard_map/ppermute | solution.py:324
  104.1 1.2 copy-start.8
  107.0 1.0 copy-start.3
  108.0 19.3 %all-to-all-start.5 = ((bf16[8,128,512]{2,1,0:T(8,128)(2,1)}), bf16[8,128,512]{2,1,0:T(8,128)(2,1)S(1)}, u32[]{:S(2)}, u32[]{:S(2)}) async-start(bf16[8,128,512]{2,1,0:T(8,128)(2,1)} %bitcast.10), calls=%async_computation.5 | async-start | bytes 2097152 | tf_op jit(solution)/shard_map/all_to_all | solution.py:318

commit v3 on v2

--- a/solution.py
+++ b/solution.py
@@ -16,6 +16,7 @@
 EXP2_SCALE = SCORE_SCALE * 1.4426950408889634
 EXCLUDED = -1e30
 ONES = 16
+IN_FLIGHT = 4
 
 NN = (((1,), (0,)), ((), ()))
 NT = (((1,), (1,)), ((), ()))
@@ -35,9 +36,10 @@
 
 
 def attention_kernel(
-    head, first_ref, qo_hbm, halo_hbm, own_hbm, ao_hbm, dhalo_hbm, down_hbm,
-    kv, qo, ao, dhalo, keys_t, values_t, acc_k, acc_v, exps0, exps1, q_turned, o_turned, in_sem, q_sem, out_sem,
+    head, pieces, place_ref, qo_hbm, halo_hbm, own_hbm, *refs
 ):
+    ao_hbm, (dhalo_hbm, down_hbm, *refs) = refs[:pieces], refs[pieces:]
+    (kv, qo, ao, dhalo, keys_t, values_t, acc_k, acc_v, exps0, exps1, q_turned, o_turned, in_sem, q_sem, out_sem) = refs
     rows = qo.shape[0]
     blocks = rows // BLOCK
     whole = WINDOW // BLOCK
@@ -53,7 +55,10 @@
         return pltpu.make_async_copy(qo_hbm.at[at(i)], qo.at[at(i)], q_sem.at[i])
 
     def ao_copy(i):
-        return pltpu.make_async_copy(ao.at[at(i)], ao_hbm.at[at(i)], out_sem.at[0, i])
+        return pltpu.make_async_copy(ao.at[at(i)], ao_hbm[0].at[at(i)], out_sem.at[0, i])
+
+    def piece_copy(j):
+        return pltpu.make_async_copy(ao.at[at(place_ref[1] ^ j)], ao_hbm[j], out_sem.at[0, j])
 
     def dhalo_copy(i):
         return pltpu.make_async_copy(dhalo.at[at(i)], dhalo_hbm.at[at(i)], out_sem.at[1, i])
@@ -76,7 +81,7 @@
     o_turned[...] = jnp.zeros_like(o_turned)
     key_at = lax.broadcasted_iota(jnp.int32, (BLOCK, 2 * BLOCK), 0)
     query_at = lax.broadcasted_iota(jnp.int32, (BLOCK, 2 * BLOCK), 1) & (BLOCK - 1)
-    first = first_ref[0]
+    first = place_ref[0]
 
     def turn(target, source):
         keys_t[:, at(target)] = kv[at(source), :HEAD_DIM].T
@@ -159,43 +164,49 @@
 
         @pl.when(j > 0)
         def _():
-            ao_copy(i - 1).start()
+            if pieces == 1:
+                ao_copy(i - 1).start()
             dhalo_copy(i - 1).start()
 
-        ao_copy(i).start()
+        if pieces == 1:
+            ao_copy(i).start()
         dhalo_copy(i).start()
         return carry
 
     lax.fori_loop(0, blocks // 2, step, 0)
     gradients(1, blocks - 1, *attended_of(1, blocks - 1))
     flush(blocks - 1)
-    ao_copy(blocks - 1).start()
     dhalo_copy(blocks - 1).start()
+    if pieces == 1:
+        ao_copy(blocks - 1).start()
+    else:
+        for j in range(pieces):
+            piece_copy(j).start()
     own_k = pltpu.make_async_copy(acc_k.at[:, pl.ds(WINDOW, rows)], down_hbm.at[0], in_sem.at[0])
     own_v = pltpu.make_async_copy(acc_v.at[:, pl.ds(WINDOW, rows)], down_hbm.at[1], in_sem.at[1])
     own_k.start()
     own_v.start()
     for i in range(blocks):
-        ao_copy(i).wait()
+        (ao_copy(i) if pieces == 1 else piece_copy(i)).wait()
         dhalo_copy(i).wait()
     own_k.wait()
     own_v.wait()
 
 
-def attention(head, first, qo, halo, own):
+def attention(head, place, qo, halo, own, pieces):
     rows = own.shape[0]
     blocks = rows // BLOCK
     reach = WINDOW + rows
     bf16, f32 = jnp.bfloat16, jnp.float32
     return pl.pallas_call(
-        functools.partial(attention_kernel, head),
+        functools.partial(attention_kernel, head, pieces),
         out_shape=(
-            jax.ShapeDtypeStruct(qo.shape, bf16),
+            *[jax.ShapeDtypeStruct((rows // pieces, qo.shape[1]), bf16)] * pieces,
             jax.ShapeDtypeStruct(halo.shape, bf16),
             jax.ShapeDtypeStruct((2, HEAD_DIM, rows), f32),
         ),
         in_specs=[SMEM, ANY, ANY, ANY],
-        out_specs=(HBM, HBM, HBM),
+        out_specs=(HBM,) * (pieces + 2),
         scratch_shapes=[
             pltpu.VMEM((reach, PAIR), bf16),
             pltpu.VMEM(qo.shape, bf16),
@@ -213,96 +224,140 @@
             pltpu.SemaphoreType.DMA((blocks,)),
             pltpu.SemaphoreType.DMA((2, blocks)),
         ],
-        compiler_params=pltpu.CompilerParams(vmem_limit_bytes=32 * 2**20),
+        compiler_params=pltpu.CompilerParams(vmem_limit_bytes=58 * 2**20),
         cost_estimate=pl.CostEstimate(flops=10**10, bytes_accessed=4 * 2**20, transcendentals=0),
         name="attention",
-    )(first, qo, halo, own)
-
-
-def interleave_kernel(width, parts, *refs):
-    *arrays, out = refs
-    for g in range(out.shape[0]):
+    )(place, qo, halo, own)
+
+
+def interleave_kernel(width, parts, split, place_ref, *refs):
+    arrays, refs = refs[:2], refs[2:]
+    groups = arrays[0].shape[1] // parts[0][2]
+    outs, (first, second, staged, in_sem, out_sem) = refs[: groups if split else 1], refs[groups if split else 1 :]
+    half = arrays[0].shape[1] // 2
+    fetched = (first, second)
+    loads = []
+    for n in range(2):
+        for h in range(2):
+            cols = pl.ds(h * half, half)
+            loads.append(pltpu.make_async_copy(arrays[n].at[:, cols], fetched[n].at[:, cols], in_sem.at[2 * n + h]))
+    for load in loads:
+        load.start()
+    if split:
+        for load in loads:
+            load.wait()
+    stores = []
+    for g in range(groups):
+        if not split and g % (groups // 2) == 0:
+            loads[g // (groups // 2)].wait()
+            loads[2 + g // (groups // 2)].wait()
+        source = place_ref[1] ^ g if split else g
         for n, (which, start, stride) in enumerate(parts):
-            first = g * stride + start
-            out[g, :, n * width : (n + 1) * width] = arrays[which][:, first : first + width]
-
-
-def interleave(arrays, groups, width, parts):
-    rows = arrays[0].shape[0]
+            at = source * stride + start
+            if split:
+                at = pl.multiple_of(at, HEAD_DIM)
+            staged[g, :, n * width : (n + 1) * width] = fetched[which][:, pl.ds(at, width)]
+        stores.append(pltpu.make_async_copy(staged.at[g], outs[g] if split else outs[0].at[g], out_sem.at[g]))
+        stores[g].start()
+    for store in stores:
+        store.wait()
+
+
+def interleave(place, arrays, groups, width, parts, split=False):
+    rows, cols = arrays[0].shape
+    dtype = arrays[0].dtype
+    out = (rows, width * len(parts))
+    whole = (groups, *out)
     return pl.pallas_call(
-        functools.partial(interleave_kernel, width, parts),
-        out_shape=jax.ShapeDtypeStruct((groups, rows, width * len(parts)), arrays[0].dtype),
-        in_specs=[VMEM] * len(arrays),
-        out_specs=VMEM,
-        compiler_params=pltpu.CompilerParams(vmem_limit_bytes=16 * 2**20),
+        functools.partial(interleave_kernel, width, parts, split),
+        out_shape=(jax.ShapeDtypeStruct(out, dtype),) * groups if split else (jax.ShapeDtypeStruct(whole, dtype),),
+        in_specs=[SMEM, HBM, HBM],
+        out_specs=(HBM,) * (groups if split else 1),
+        scratch_shapes=[
+            pltpu.VMEM((rows, cols), dtype),
+            pltpu.VMEM((rows, cols), dtype),
+            pltpu.VMEM(whole, dtype),
+            pltpu.SemaphoreType.DMA((4,)),
+            pltpu.SemaphoreType.DMA((groups,)),
+        ],
+        compiler_params=pltpu.CompilerParams(vmem_limit_bytes=58 * 2**20),
         name="interleave",
-    )(*arrays)
-
-
-def spread_kernel(x_ref, y_ref, a_ref, b_ref):
+    )(place, *arrays)
+
+
+def group_at(place_ref, j, width):
+    return pl.multiple_of((place_ref[1] ^ j) * width, HEAD_DIM)
+
+
+def spread_kernel(place_ref, x_ref, *refs):
+    *pieces, a_ref, b_ref = refs
     groups, _, width = x_ref.shape
     half = width // 2
     for g in range(groups):
-        for n, ref in enumerate((x_ref, y_ref)):
-            cols = slice(g * width + n * half, g * width + (n + 1) * half)
-            a_ref[:, cols] = ref[g, :, :half]
-            b_ref[:, cols] = ref[g, :, half:]
-
-
-def spread(x, y):
+        a_ref[:, g * width : g * width + half] = x_ref[g, :, :half]
+        b_ref[:, g * width : g * width + half] = x_ref[g, :, half:]
+        cols = pl.ds(group_at(place_ref, g, width) + half, half)
+        a_ref[:, cols] = pieces[g][:, :half]
+        b_ref[:, cols] = pieces[g][:, half:]
+
+
+def spread(place, x, pieces):
     groups, rows, width = x.shape
     shape = jax.ShapeDtypeStruct((rows, groups * width), x.dtype)
     return pl.pallas_call(
         spread_kernel,
         out_shape=(shape, shape),
-        in_specs=[VMEM, VMEM],
+        in_specs=[SMEM] + [VMEM] * (groups + 1),
         out_specs=(VMEM, VMEM),
         compiler_params=pltpu.CompilerParams(vmem_limit_bytes=16 * 2**20),
         name="spread",
-    )(x, y)
-
-
-def add_kernel(own0_ref, own1_ref, back0_ref, back1_ref, out_ref):
-    for h, (own, back) in enumerate(((own0_ref, back0_ref), (own1_ref, back1_ref))):
-        for i in range(out_ref.shape[0] // BLOCK):
-            rows = slice(i * BLOCK, (i + 1) * BLOCK)
+    )(place, x, *pieces)
+
+
+def add_kernel(place_ref, own0_ref, own1_ref, back0_ref, back1_ref, *out_refs):
+    rows = out_refs[0].shape[0]
+    for j, out_ref in enumerate(out_refs):
+        at = pl.ds(group_at(place_ref, j, rows), rows)
+        for h, (own, back) in enumerate(((own0_ref, back0_ref), (own1_ref, back1_ref))):
             for n, scale in enumerate((SCORE_SCALE, 1.0)):
-                total = (own[n, :, rows] * scale).T + back[rows, n * HEAD_DIM : (n + 1) * HEAD_DIM].astype(jnp.float32)
+                total = (own[n, :, at] * scale).T + back[at, n * HEAD_DIM : (n + 1) * HEAD_DIM].astype(jnp.float32)
                 cols = slice((2 * n + h) * HEAD_DIM, (2 * n + h + 1) * HEAD_DIM)
-                out_ref[rows, cols] = total.astype(jnp.bfloat16)
-
-
-def add(own, back):
+                out_ref[:, cols] = total.astype(jnp.bfloat16)
+
+
+def add(place, own, back, groups):
     rows, width = back[0].shape
+    shape = jax.ShapeDtypeStruct((rows // groups, 2 * width), jnp.bfloat16)
     return pl.pallas_call(
         add_kernel,
-        out_shape=jax.ShapeDtypeStruct((rows, 2 * width), jnp.bfloat16),
-        in_specs=[VMEM] * 4,
-        out_specs=VMEM,
+        out_shape=(shape,) * groups,
+        in_specs=[SMEM] + [VMEM] * 4,
+        out_specs=(VMEM,) * groups,
         compiler_params=pltpu.CompilerParams(vmem_limit_bytes=16 * 2**20),
         name="add",
-    )(*own, *back)
-
-
-def unpack_kernel(x_ref, a_ref, b_ref):
-    groups, _, width = x_ref.shape
-    half = width // 2
-    for g in range(groups):
-        a_ref[:, g * half : (g + 1) * half] = x_ref[g, :, :half]
-        b_ref[:, g * half : (g + 1) * half] = x_ref[g, :, half:]
-
-
-def unpack(x):
-    groups, rows, width = x.shape
-    shape = jax.ShapeDtypeStruct((rows, groups * width // 2), x.dtype)
+    )(place, *own, *back)
+
+
+def unpack_kernel(place_ref, *refs):
+    *pieces, a_ref, b_ref = refs
+    half = pieces[0].shape[1] // 2
+    for j, piece in enumerate(pieces):
+        cols = pl.ds(group_at(place_ref, j, half), half)
+        a_ref[:, cols] = piece[:, :half]
+        b_ref[:, cols] = piece[:, half:]
+
+
+def unpack(place, pieces):
+    rows, width = pieces[0].shape
+    shape = jax.ShapeDtypeStruct((rows, len(pieces) * width // 2), pieces[0].dtype)
     return pl.pallas_call(
         unpack_kernel,
         out_shape=(shape, shape),
-        in_specs=[VMEM],
+        in_specs=[SMEM] + [VMEM] * len(pieces),
         out_specs=(VMEM, VMEM),
         compiler_params=pltpu.CompilerParams(vmem_limit_bytes=16 * 2**20),
         name="unpack",
-    )(x)
+    )(place, *pieces)
 
 
 def body(queries, key_rows, value_rows, grad_out):
@@ -312,11 +367,24 @@
     members = apart * split
     heads = key_rows.shape[1] // (members * HEAD_DIM)
     groups = [[g * members + i for i in range(members)] for g in range(shards // apart)]
-    first = (lax.axis_index("seq") < apart).astype(jnp.int32).reshape(1)
+    spot = lax.axis_index(("seq", "kvh"))
+    place = jnp.stack([lax.axis_index("seq") < apart, spot % members]).astype(jnp.int32)
 
     def exchange(x):
         return lax.all_to_all(x, ("seq", "kvh"), 0, 0, tiled=True, axis_index_groups=groups)
 
+    def swap(pieces):
+        every = range(shards * split)
+        out = [pieces[0]] * members
+        order = sorted(range(1, members), key=lambda j: j == 1)
+        for n, j in enumerate(order):
+            piece = pieces[j]
+            if n >= IN_FLIGHT:
+                before = order[n - IN_FLIGHT]
+                piece, out[before] = lax.optimization_barrier((piece, out[before]))
+            out[j] = lax.ppermute(piece, ("seq", "kvh"), [(i, i ^ j) for i in every])
+        return out
+
     def onward(x):
         return lax.ppermute(x, "seq", [(i, i + apart) for i in range(shards - apart)])
 
@@ -325,21 +393,25 @@
 
     stride = heads * HEAD_DIM
     kv_parts = [(n, h * HEAD_DIM, stride) for h in range(heads) for n in range(2)]
-    own = exchange(interleave((key_rows, value_rows), members, HEAD_DIM, kv_parts)).reshape(WINDOW, -1)
+    (own,) = interleave(place, (key_rows, value_rows), members, HEAD_DIM, kv_parts)
+    own = exchange(own).reshape(WINDOW, -1)
     halos = [onward(own[:, h * PAIR : (h + 1) * PAIR]) for h in range(heads)]
     outs, down, back = [], [], []
     for h in range(heads):
         qo_parts = [(n, h * PAIR, 2 * stride) for n in range(2)]
-        qo = exchange(interleave((queries, grad_out), members, PAIR, qo_parts)).reshape(WINDOW, -1)
-        ao, dhalo, mine = attention(h, first, qo, halos[h], own)
+        (qo,) = interleave(place, (queries, grad_out), members, PAIR, qo_parts)
+        qo = exchange(qo).reshape(WINDOW, -1)
+        last = h == heads - 1
+        *ao, dhalo, mine = attention(h, place, qo, halos[h], own, members if last else 1)
         if h > 0:
             ao, back[h - 1] = lax.optimization_barrier((ao, back[h - 1]))
         back.append(backward(dhalo))
-        outs.append(exchange(ao.reshape(members, rows, -1)))
+        outs.append(swap(ao) if last else exchange(ao[0].reshape(members, rows, -1)))
         down.append(mine)
-    *outs, total = lax.optimization_barrier((*outs, add(down, back)))
-    grad_k, grad_v = unpack(exchange(total.reshape(members, rows, -1)))
-    attended, grad_q = spread(*outs)
+    total = add(place, down, back, members)
+    outs[-1], total = lax.optimization_barrier((outs[-1], total))
+    grad_k, grad_v = unpack(place, swap(total))
+    attended, grad_q = spread(place, *outs)
     return (attended, grad_q, grad_k, grad_v)
 
 

time: 129 us -> 121 us (0.938)
  waiting for transfers between devices: 51.3 us -> 31.7 us
  Pallas kernels: 31.4 us -> 41.3 us
  starting transfers between devices: 35.8 us -> 40.6 us
  local copies, waits for them, and re-layouts: 9.02 us -> 5.43 us
    all_to_all x6 -> x4, waiting for transfers between devices: 36.2 us -> 15.9 us  [exchange(): lax.all_to_all(x, ('seq', 'kvh'), 0, 0, tiled=True, axis_index_groups=gro...]
    ppermute x0 -> x14, starting transfers between devices: none -> 13.9 us  [swap(): out[j] = lax.ppermute(piece, ('seq', 'kvh'), [(i, i ^ j) for i in every])]
    ppermute x0 -> x14, waiting for transfers between devices: none -> 11.3 us  [swap(): out[j] = lax.ppermute(piece, ('seq', 'kvh'), [(i, i ^ j) for i in every])]
    ppermute x2, waiting for transfers between devices: 15.1 us -> 4.47 us  [backward(): lax.ppermute(x, 'seq', [(i + apart, i) for i in range(shards - apart)])]
    pallas_call x8, Pallas kernels: 31.4 us -> 41.3 us  [the longest x2 26.8 us: attention(): pl.pallas_call(functools.partial(attention_kernel, head, pieces), out_sha...]
    all_to_all x6 -> x4, starting transfers between devices: 25.5 us -> 16.4 us  [exchange(): lax.all_to_all(x, ('seq', 'kvh'), 0, 0, tiled=True, axis_index_groups=gro...]
    unnamed x24 -> x16, local copies, waits for them, and re-layouts: 7.99 us -> 4.57 us
  transfers between devices with their start and end apart: 10 -> 22, of which waited for: 5 -> 9; matrix products, arithmetic and copies ran while one was open for 1% -> 1% of each run, Pallas kernels for 23% -> 31%
where the time goes in v3:
time: 121 us
  Pallas kernels  41.3 us (34%)
  starting transfers between devices  40.6 us (34%)
  waiting for transfers between devices  31.7 us (26%)
  local copies, waits for them, and re-layouts  5.43 us (4%)
    pallas_call x2, Pallas kernels, attention(): pl.pallas_call(functools.partial(attention_kernel, head, pieces), out_sha...  26.8 us
    all_to_all x4, starting transfers between devices, exchange(): lax.all_to_all(x, ('seq', 'kvh'), 0, 0, tiled=True, axis_index_groups=gro...  16.4 us
    all_to_all x4, waiting for transfers between devices, exchange(): lax.all_to_all(x, ('seq', 'kvh'), 0, 0, tiled=True, axis_index_groups=gro...  15.9 us
    ppermute x14, starting transfers between devices, swap(): out[j] = lax.ppermute(piece, ('seq', 'kvh'), [(i, i ^ j) for i in every])  13.9 us
    ppermute x14, waiting for transfers between devices, swap(): out[j] = lax.ppermute(piece, ('seq', 'kvh'), [(i, i ^ j) for i in every])  11.3 us
    pallas_call x3, Pallas kernels, interleave(): pl.pallas_call(functools.partial(interleave_kernel, width, parts, split),...  9.08 us
    ppermute x2, starting transfers between devices, onward(): lax.ppermute(x, 'seq', [(i, i + apart) for i in range(shards - apart)])  7.74 us
    unnamed x16, local copies, waits for them, and re-layouts  4.57 us
  transfers between devices with their start and end apart: 22, of which 9 were waited for; matrix products, arithmetic and copies ran while one was open for 1% of the time, Pallas kernels for 31%

profile of v3, /device:TPU:0, one launch (start us, length us, event | category | flops | bytes accessed | tf_op | source)
XLA Modules:
  0.0 120.5 jit_solution(11778288160768061717)
XLA Ops:
  0.6 0.6 pad_add_fusion.place_ref
  1.2 2.9 %interleave.4 = bf16[8,128,512]{2,1,0:T(8,128)(2,1)} custom-call(s32[2]{0:T(128)} %pad_add_fusion.place_ref, bf16[128,2048]{1,0:T(8,128)(2,1)} %refs_0_.4, bf16[128,2048]{1,0:T(8,128)(2,1)} %refs_1_.4), custom_call_target="tpu_custom_call" | custom-call | tf_op jit(solution)/shard_map/interleave/pallas_call | solution.py:271
  4.1 5.2 %all-to-all-start.1 = ((bf16[8,128,512]{2,1,0:T(8,128)(2,1)}), bf16[8,128,512]{2,1,0:T(8,128)(2,1)S(1)}, u32[]{:S(2)}, u32[]{:S(2)}) async-start(bf16[8,128,512]{2,1,0:T(8,128)(2,1)} %interleave.4), calls=%async_computation.1 | async-start | bytes 2097152 | tf_op jit(solution)/shard_map/all_to_all | solution.py:374
  9.3 3.1 %interleave.3 = bf16[8,128,512]{2,1,0:T(8,128)(2,1)} custom-call(s32[2]{0:T(128)} %pad_add_fusion.place_ref, bf16[128,4096]{1,0:T(8,128)(2,1)} %refs_0_.5, bf16[128,4096]{1,0:T(8,128)(2,1)} %refs_1_.5), custom_call_target="tpu_custom_call" | custom-call | tf_op jit(solution)/shard_map/interleave/pallas_call | solution.py:271
  12.4 12.3 %all-to-all-done.1 = bf16[8,128,512]{2,1,0:T(8,128)(2,1)S(1)} async-done(((bf16[8,128,512]{2,1,0:T(8,128)(2,1)}), bf16[8,128,512]{2,1,0:T(8,128)(2,1)S(1)}, u32[]{:S(2)}, u32[]{:S(2)}) %all-to-all-start.1) | async-done | bytes 1048608 | tf_op jit(solution)/shard_map/all_to_all | solution.py:374
  24.7 3.6 %all-to-all-start = ((bf16[8,128,512]{2,1,0:T(8,128)(2,1)}), bf16[8,128,512]{2,1,0:T(8,128)(2,1)S(1)}, u32[]{:S(2)}, u32[]{:S(2)}) async-start(bf16[8,128,512]{2,1,0:T(8,128)(2,1)} %interleave.3), calls=%async_computation | async-start | bytes 2097152 | tf_op jit(solution)/shard_map/all_to_all | solution.py:374
  28.3 0.9 fusion
  29.1 3.5 %collective-permute-start = (bf16[1024,256]{1,0:T(8,128)(2,1)}, bf16[1024,256]{1,0:T(8,128)(2,1)S(1)}, u32[]{:S(2)}, u32[]{:S(2)}) collective-permute-start(bf16[1024,256]{1,0:T(8,128)(2,1)} %get-tuple-element.129), channel_id=1, source_target_pairs={{0,8},{4,12},{8,16},{12,20},{16,24},{20,28},{1,9},{5,13},{9,17},{1... | collective-permute-start | bytes 1572872 | tf_op jit(solution)/shard_map/ppermute | solution.py:389
  32.6 3.1 %interleave.5 = bf16[8,128,512]{2,1,0:T(8,128)(2,1)} custom-call(s32[2]{0:T(128)} %pad_add_fusion.place_ref, bf16[128,4096]{1,0:T(8,128)(2,1)} %refs_0_.5, bf16[128,4096]{1,0:T(8,128)(2,1)} %refs_1_.5), custom_call_target="tpu_custom_call" | custom-call | tf_op jit(solution)/shard_map/interleave/pallas_call | solution.py:271
  35.8 4.2 %collective-permute-start.1 = (bf16[1024,256]{1,0:T(8,128)(2,1)S(1)}, bf16[1024,256]{1,0:T(8,128)(2,1)}, u32[]{:S(2)}, u32[]{:S(2)}) collective-permute-start(bf16[1024,256]{1,0:T(8,128)(2,1)S(1)} %get-tuple-element.128), channel_id=1, source_target_pairs={{0,8},{4,12},{8,16},{12,20},{16,24},{20,28},{1,9},{5,13},{9,17},{1... | collective-permute-start | bytes 1572872 | tf_op jit(solution)/shard_map/ppermute | solution.py:389
  40.0 3.6 %all-to-all-done = bf16[8,128,512]{2,1,0:T(8,128)(2,1)S(1)} async-done(((bf16[8,128,512]{2,1,0:T(8,128)(2,1)}), bf16[8,128,512]{2,1,0:T(8,128)(2,1)S(1)}, u32[]{:S(2)}, u32[]{:S(2)}) %all-to-all-start) | async-done | bytes 1048608 | tf_op jit(solution)/shard_map/all_to_all | solution.py:374
  43.6 1.0 copy-done.6
  44.6 3.6 %all-to-all-start.3 = ((bf16[8,128,512]{2,1,0:T(8,128)(2,1)}), bf16[8,128,512]{2,1,0:T(8,128)(2,1)S(1)}, u32[]{:S(2)}, u32[]{:S(2)}) async-start(bf16[8,128,512]{2,1,0:T(8,128)(2,1)} %interleave.5), calls=%async_computation.3 | async-start | bytes 2097152 | tf_op jit(solution)/shard_map/all_to_all | solution.py:374
  48.1 0.0 collective-permute-done.halo_hbm
  48.1 0.0 copy-start.7
  48.2 0.8 copy-done.7
  48.9 13.2 %attention.2 = (bf16[1024,512]{1,0:T(8,128)(2,1)}, bf16[1024,256]{1,0:T(8,128)(2,1)}, f32[2,128,1024]{2,1,0:T(8,128)}) custom-call(s32[2]{0:T(128)} %pad_add_fusion.place_ref, bf16[1024,512]{1,0:T(8,128)(2,1)} %bitcast.11, bf16[1024,256]{1,0:T(8,128)(2,1)} %copy-done.7, bf16[1024,512]{1,0:T(8,128)(2,1)} %bitcast.7), custom_call_target="tpu_custom_call" | custom-call | flops 10000000000 | bytes 4194304 | tf_op jit(solution)/shard_map/attention/pallas_call | solution.py:201
  62.2 1.3 %collective-permute-start.2 = (bf16[1024,256]{1,0:T(8,128)(2,1)}, bf16[1024,256]{1,0:T(8,128)(2,1)S(1)}, u32[]{:S(2)}, u32[]{:S(2)}) collective-permute-start(bf16[1024,256]{1,0:T(8,128)(2,1)} %get-tuple-element.75), channel_id=1, source_target_pairs={{8,0},{12,4},{16,8},{20,12},{24,16},{28,20},{9,1},{13,5},{17,9},{2... | collective-permute-start | bytes 1572872 | tf_op jit(solution)/shard_map/ppermute | solution.py:392
  63.5 0.0 all-to-all-done.3
  63.5 1.0 copy-done.5
  64.4 4.1 %all-to-all-start.2 = ((bf16[8,128,512]{2,1,0:T(8,128)(2,1)}), bf16[8,128,512]{2,1,0:T(8,128)(2,1)S(1)}, u32[]{:S(2)}, u32[]{:S(2)}) async-start(bf16[8,128,512]{2,1,0:T(8,128)(2,1)} %bitcast.9), calls=%async_computation.2 | async-start | bytes 2097152 | tf_op jit(solution)/shard_map/all_to_all | solution.py:374
  68.6 0.0 collective-permute-done.1.halo_hbm
  68.6 13.6 %attention.3 = (bf16[128,512]{1,0:T(8,128)(2,1)}, bf16[128,512]{1,0:T(8,128)(2,1)}, bf16[128,512]{1,0:T(8,128)(2,1)}, bf16[128,512]{1,0:T(8,128)(2,1)}, bf16[128...) custom-call(s32[2]{0:T(128)} %pad_add_fusion.place_ref, ...), custom_call_target="tpu_custom_call" | custom-call | flops 10000000000 | bytes 4194304 | tf_op jit(solution)/shard_map/attention/pallas_call | solution.py:201
  82.2 1.3 %collective-permute-start.10 = (bf16[1024,256]{1,0:T(8,128)(2,1)}, bf16[1024,256]{1,0:T(8,128)(2,1)S(1)}, u32[]{:S(2)}, u32[]{:S(2)}) collective-permute-start(bf16[1024,256]{1,0:T(8,128)(2,1)} %get-tuple-element.93), channel_id=1, source_target_pairs={{8,0},{12,4},{16,8},{20,12},{24,16},{28,20},{9,1},{13,5},{17,9},{2... | collective-permute-start | bytes 1572872 | tf_op jit(solution)/shard_map/ppermute | solution.py:392
  83.5 2.1 %collective-permute-start.3 = (bf16[128,512]{1,0:T(8,128)(2,1)}, bf16[128,512]{1,0:T(8,128)(2,1)S(1)}, u32[]{:S(2)}, u32[]{:S(2)}) collective-permute-start(bf16[128,512]{1,0:T(8,128)(2,1)} %get-tuple-element.78), channel_id=1, source_target_pairs={{0,4},{1,5},{2,6},{3,7},{4,0},{5,1},{6,2},{7,3},{8,12},{9,13},{10,... | collective-permute-start | bytes 393224 | tf_op jit(solution)/shard_map/ppermute | solution.py:385
  85.6 1.5 %collective-permute-start.5 = (bf16[128,512]{1,0:T(8,128)(2,1)}, bf16[128,512]{1,0:T(8,128)(2,1)S(1)}, u32[]{:S(2)}, u32[]{:S(2)}) collective-permute-start(bf16[128,512]{1,0:T(8,128)(2,1)} %get-tuple-element.81), channel_id=1, source_target_pairs={{0,2},{1,3},{2,0},{3,1},{4,6},{5,7},{6,4},{7,5},{8,10},{9,11},{10,... | collective-permute-start | bytes 393224 | tf_op jit(solution)/shard_map/ppermute | solution.py:385
  87.0 0.0 collective-permute-start.6
  87.0 0.4 collective-permute-start.7
  87.4 2.3 %collective-permute-done.3.refs_4_ = bf16[128,512]{1,0:T(8,128)(2,1)S(1)} collective-permute-done((bf16[128,512]{1,0:T(8,128)(2,1)}, bf16[128,512]{1,0:T(8,128)(2,1)S(1)}, u32[]{:S(2)}, u32[]{:S(2)}) %collective-permute-start.3) | collective-permute-done | bytes 131104 | tf_op jit(solution)/shard_map/ppermute | solution.py:385
  89.7 2.2 %collective-permute-done.5.refs_2_ = bf16[128,512]{1,0:T(8,128)(2,1)S(1)} collective-permute-done((bf16[128,512]{1,0:T(8,128)(2,1)}, bf16[128,512]{1,0:T(8,128)(2,1)S(1)}, u32[]{:S(2)}, u32[]{:S(2)}) %collective-permute-start.5) | collective-permute-done | bytes 131104 | tf_op jit(solution)/shard_map/ppermute | solution.py:385
  91.9 1.7 %collective-permute-start.8 = (bf16[128,512]{1,0:T(8,128)(2,1)}, bf16[128,512]{1,0:T(8,128)(2,1)S(1)}, u32[]{:S(2)}, u32[]{:S(2)}) collective-permute-start(bf16[128,512]{1,0:T(8,128)(2,1)} %get-tuple-element.88), channel_id=1, source_target_pairs={{0,6},{1,7},{2,4},{3,5},{4,2},{5,3},{6,0},{7,1},{8,14},{9,15},{10,... | collective-permute-start | bytes 393224 | tf_op jit(solution)/shard_map/ppermute | solution.py:385
  93.6 0.0 collective-permute-done.6.refs_3_
  93.6 1.4 %collective-permute-start.9 = (bf16[128,512]{1,0:T(8,128)(2,1)}, bf16[128,512]{1,0:T(8,128)(2,1)S(1)}, u32[]{:S(2)}, u32[]{:S(2)}) collective-permute-start(bf16[128,512]{1,0:T(8,128)(2,1)} %get-tuple-element.89), channel_id=1, source_target_pairs={{0,7},{1,6},{2,5},{3,4},{4,3},{5,2},{6,1},{7,0},{8,15},{9,14},{10,... | collective-permute-start | bytes 393224 | tf_op jit(solution)/shard_map/ppermute | solution.py:385
  95.1 4.5 %collective-permute-done.10.back1_ref = bf16[1024,256]{1,0:T(8,128)(2,1)S(1)} collective-permute-done((bf16[1024,256]{1,0:T(8,128)(2,1)}, bf16[1024,256]{1,0:T(8,128)(2,1)S(1)}, u32[]{:S(2)}, u32[]{:S(2)}) %collective-permute-start.10) | collective-permute-done | bytes 524320 | tf_op jit(solution)/shard_map/ppermute | solution.py:392
  99.5 0.6 copy-done.3
  100.1 1.2 %copy-done.1 = f32[2,128,1024]{2,1,0:T(8,128)S(1)} copy-done((f32[2,128,1024]{2,1,0:T(8,128)S(1)}, f32[2,128,1024]{2,1,0:T(8,128)}, u32[]{:S(2)}) %copy-start.1) | copy-done | bytes 1048600
  101.4 1.7 %add.12 = (bf16[128,512]{1,0:T(8,128)(2,1)S(1)}, bf16[128,512]{1,0:T(8,128)(2,1)S(1)}, bf16[128,512]{1,0:T(8,128)(2,1)S(1)}, bf16[128,512]{1,0:T(8,128)(2,1)S(1)...) custom-call(s32[2]{0:T(128)S(1)} %copy-done.3, ...), custom_call_target="tpu_custom_call" | custom-call | tf_op jit(solution)/shard_map/add/pallas_call | solution.py:331
  103.1 1.7 %collective-permute-start.11 = (bf16[128,512]{1,0:T(8,128)(2,1)S(1)}, bf16[128,512]{1,0:T(8,128)(2,1)S(1)}, u32[]{:S(2)}, u32[]{:S(2)}) collective-permute-start(bf16[128,512]{1,0:T(8,128)(2,1)S(1)} %get-tuple-element.114), channel_id=1, source_target_pairs={{0,4},{1,5},{2,6},{3,7},{4,0},{5,1},{6,2},{7,3},{8,12},{9,13},{10,... | collective-permute-start | bytes 393224 | tf_op jit(solution)/shard_map/ppermute | solution.py:385
  104.8 1.5 %collective-permute-start.13 = (bf16[128,512]{1,0:T(8,128)(2,1)S(1)}, bf16[128,512]{1,0:T(8,128)(2,1)S(1)}, u32[]{:S(2)}, u32[]{:S(2)}) collective-permute-start(bf16[128,512]{1,0:T(8,128)(2,1)S(1)} %get-tuple-element.117), channel_id=1, source_target_pairs={{0,2},{1,3},{2,0},{3,1},{4,6},{5,7},{6,4},{7,5},{8,10},{9,11},{10,... | collective-permute-start | bytes 393224 | tf_op jit(solution)/shard_map/ppermute | solution.py:385
  106.3 0.6 collective-permute-start.15
  106.9 1.5 %collective-permute-done.11.refs_4_ = bf16[128,512]{1,0:T(8,128)(2,1)S(1)} collective-permute-done((bf16[128,512]{1,0:T(8,128)(2,1)S(1)}, bf16[128,512]{1,0:T(8,128)(2,1)S(1)}, u32[]{:S(2)}, u32[]{:S(2)}) %collective-permute-start.11) | collective-permute-done | bytes 131104 | tf_op jit(solution)/shard_map/ppermute | solution.py:385
  108.5 1.9 %collective-permute-done.13.refs_2_ = bf16[128,512]{1,0:T(8,128)(2,1)S(1)} collective-permute-done((bf16[128,512]{1,0:T(8,128)(2,1)S(1)}, bf16[128,512]{1,0:T(8,128)(2,1)S(1)}, u32[]{:S(2)}, u32[]{:S(2)}) %collective-permute-start.13) | collective-permute-done | bytes 131104 | tf_op jit(solution)/shard_map/ppermute | solution.py:385
  110.3 2.1 %collective-permute-start.16 = (bf16[128,512]{1,0:T(8,128)(2,1)S(1)}, bf16[128,512]{1,0:T(8,128)(2,1)S(1)}, u32[]{:S(2)}, u32[]{:S(2)}) collective-permute-start(bf16[128,512]{1,0:T(8,128)(2,1)S(1)} %get-tuple-element.124), channel_id=1, source_target_pairs={{0,6},{1,7},{2,4},{3,5},{4,2},{5,3},{6,0},{7,1},{8,14},{9,15},{10,... | collective-permute-start | bytes 393224 | tf_op jit(solution)/shard_map/ppermute | solution.py:385
  112.5 0.8 collective-permute-start.17
  113.3 2.1 %spread.1 = (bf16[128,4096]{1,0:T(8,128)(2,1)}, bf16[128,4096]{1,0:T(8,128)(2,1)}) custom-call(s32[2]{0:T(128)S(1)} %copy-done.3, bf16[8,128,512]{2,1,0:T(8,128)(2,1)S(1)} %all-to-all-done.2.x_ref, bf16[128,512]{1,0:T(8,128)(2,1)S(1)} %copy-done.2, bf16[128,512]{1,0:T(8,128)(2,1)S(1)} %collective-permute-done.4.refs_1_, ...), custom_call_target="tpu_custom_call" | custom-call | tf_op jit(solution)/shard_map/spread/pallas_call | solution.py:307
  115.4 0.8 collective-permute-done.16.refs_6_
  116.2 2.7 %collective-permute-done.17.refs_7_ = bf16[128,512]{1,0:T(8,128)(2,1)S(1)} collective-permute-done((bf16[128,512]{1,0:T(8,128)(2,1)S(1)}, bf16[128,512]{1,0:T(8,128)(2,1)S(1)}, u32[]{:S(2)}, u32[]{:S(2)}) %collective-permute-start.17) | collective-permute-done | bytes 131104 | tf_op jit(solution)/shard_map/ppermute | solution.py:385
  118.9 1.6 %unpack.1 = (bf16[128,2048]{1,0:T(8,128)(2,1)}, bf16[128,2048]{1,0:T(8,128)(2,1)}) custom-call(s32[2]{0:T(128)S(1)} %copy-done.3, bf16[128,512]{1,0:T(8,128)(2,1)S(1)} %get-tuple-element.112.refs_0_, bf16[128,512]{1,0:T(8,128)(2,1)S(1)} %collective-permute-done.12.refs_1_, bf16[128,512]{1,0:T(8,128)(2,1)S(1)} %collective-permute-done.13.refs_2_, ...), custom_call_target="tpu_custom_call" | custom-call | tf_op jit(solution)/shard_map/unpack/pallas_call | solution.py:353
  (22 shorter events, 0.0 us)
Async XLA Ops:
  4.1 20.6 %all-to-all-start.1 = ((bf16[8,128,512]{2,1,0:T(8,128)(2,1)}), bf16[8,128,512]{2,1,0:T(8,128)(2,1)S(1)}, u32[]{:S(2)}, u32[]{:S(2)}) async-start(bf16[8,128,512]{2,1,0:T(8,128)(2,1)} %interleave.4), calls=%async_computation.1 | async-start | bytes 2097152 | tf_op jit(solution)/shard_map/all_to_all | solution.py:374
  24.7 3.6 %copy-start.4 = (bf16[8,128,512]{2,1,0:T(8,128)(2,1)}, bf16[8,128,512]{2,1,0:T(8,128)(2,1)S(1)}, u32[]{:S(2)}) copy-start(bf16[8,128,512]{2,1,0:T(8,128)(2,1)S(1)} %all-to-all-done.1) | copy-start | bytes 3145732
  24.7 18.9 %all-to-all-start = ((bf16[8,128,512]{2,1,0:T(8,128)(2,1)}), bf16[8,128,512]{2,1,0:T(8,128)(2,1)S(1)}, u32[]{:S(2)}, u32[]{:S(2)}) async-start(bf16[8,128,512]{2,1,0:T(8,128)(2,1)} %interleave.3), calls=%async_computation | async-start | bytes 2097152 | tf_op jit(solution)/shard_map/all_to_all | solution.py:374
  29.1 19.0 %collective-permute-start = (bf16[1024,256]{1,0:T(8,128)(2,1)}, bf16[1024,256]{1,0:T(8,128)(2,1)S(1)}, u32[]{:S(2)}, u32[]{:S(2)}) collective-permute-start(bf16[1024,256]{1,0:T(8,128)(2,1)} %get-tuple-element.129), channel_id=1, source_target_pairs={{0,8},{4,12},{8,16},{12,20},{16,24},{20,28},{1,9},{5,13},{9,17},{1... | collective-permute-start | bytes 1572872 | tf_op jit(solution)/shard_map/ppermute | solution.py:389
  35.8 32.8 %collective-permute-start.1 = (bf16[1024,256]{1,0:T(8,128)(2,1)S(1)}, bf16[1024,256]{1,0:T(8,128)(2,1)}, u32[]{:S(2)}, u32[]{:S(2)}) collective-permute-start(bf16[1024,256]{1,0:T(8,128)(2,1)S(1)} %get-tuple-element.128), channel_id=1, source_target_pairs={{0,8},{4,12},{8,16},{12,20},{16,24},{20,28},{1,9},{5,13},{9,17},{1... | collective-permute-start | bytes 1572872 | tf_op jit(solution)/shard_map/ppermute | solution.py:389
  43.6 1.0 copy-start.6
  44.6 18.9 %all-to-all-start.3 = ((bf16[8,128,512]{2,1,0:T(8,128)(2,1)}), bf16[8,128,512]{2,1,0:T(8,128)(2,1)S(1)}, u32[]{:S(2)}, u32[]{:S(2)}) async-start(bf16[8,128,512]{2,1,0:T(8,128)(2,1)} %interleave.5), calls=%async_computation.3 | async-start | bytes 2097152 | tf_op jit(solution)/shard_map/all_to_all | solution.py:374
  48.1 0.8 copy-start.7
  62.2 21.3 %collective-permute-start.2 = (bf16[1024,256]{1,0:T(8,128)(2,1)}, bf16[1024,256]{1,0:T(8,128)(2,1)S(1)}, u32[]{:S(2)}, u32[]{:S(2)}) collective-permute-start(bf16[1024,256]{1,0:T(8,128)(2,1)} %get-tuple-element.75), channel_id=1, source_target_pairs={{8,0},{12,4},{16,8},{20,12},{24,16},{28,20},{9,1},{13,5},{17,9},{2... | collective-permute-start | bytes 1572872 | tf_op jit(solution)/shard_map/ppermute | solution.py:392
  63.5 1.0 copy-start.5
  64.4 48.9 %all-to-all-start.2 = ((bf16[8,128,512]{2,1,0:T(8,128)(2,1)}), bf16[8,128,512]{2,1,0:T(8,128)(2,1)S(1)}, u32[]{:S(2)}, u32[]{:S(2)}) async-start(bf16[8,128,512]{2,1,0:T(8,128)(2,1)} %bitcast.9), calls=%async_computation.2 | async-start | bytes 2097152 | tf_op jit(solution)/shard_map/all_to_all | solution.py:374
  68.6 31.0 %copy-start = (f32[2,128,1024]{2,1,0:T(8,128)S(1)}, f32[2,128,1024]{2,1,0:T(8,128)}, u32[]{:S(2)}) copy-start(f32[2,128,1024]{2,1,0:T(8,128)} %get-tuple-element.90.own0_ref) | copy-start | bytes 3145732
  82.2 17.3 %collective-permute-start.10 = (bf16[1024,256]{1,0:T(8,128)(2,1)}, bf16[1024,256]{1,0:T(8,128)(2,1)S(1)}, u32[]{:S(2)}, u32[]{:S(2)}) collective-permute-start(bf16[1024,256]{1,0:T(8,128)(2,1)} %get-tuple-element.93), channel_id=1, source_target_pairs={{8,0},{12,4},{16,8},{20,12},{24,16},{28,20},{9,1},{13,5},{17,9},{2... | collective-permute-start | bytes 1572872 | tf_op jit(solution)/shard_map/ppermute | solution.py:392
  83.5 6.2 %collective-permute-start.3 = (bf16[128,512]{1,0:T(8,128)(2,1)}, bf16[128,512]{1,0:T(8,128)(2,1)S(1)}, u32[]{:S(2)}, u32[]{:S(2)}) collective-permute-start(bf16[128,512]{1,0:T(8,128)(2,1)} %get-tuple-element.78), channel_id=1, source_target_pairs={{0,4},{1,5},{2,6},{3,7},{4,0},{5,1},{6,2},{7,3},{8,12},{9,13},{10,... | collective-permute-start | bytes 393224 | tf_op jit(solution)/shard_map/ppermute | solution.py:385
  85.6 6.3 %collective-permute-start.5 = (bf16[128,512]{1,0:T(8,128)(2,1)}, bf16[128,512]{1,0:T(8,128)(2,1)S(1)}, u32[]{:S(2)}, u32[]{:S(2)}) collective-permute-start(bf16[128,512]{1,0:T(8,128)(2,1)} %get-tuple-element.81), channel_id=1, source_target_pairs={{0,2},{1,3},{2,0},{3,1},{4,6},{5,7},{6,4},{7,5},{8,10},{9,11},{10,... | collective-permute-start | bytes 393224 | tf_op jit(solution)/shard_map/ppermute | solution.py:385
  87.0 6.6 %collective-permute-start.6 = (bf16[128,512]{1,0:T(8,128)(2,1)}, bf16[128,512]{1,0:T(8,128)(2,1)S(1)}, u32[]{:S(2)}, u32[]{:S(2)}) collective-permute-start(bf16[128,512]{1,0:T(8,128)(2,1)} %get-tuple-element.84), channel_id=1, source_target_pairs={{0,3},{1,2},{2,1},{3,0},{4,7},{5,6},{6,5},{7,4},{8,11},{9,10},{10,... | collective-permute-start | bytes 393224 | tf_op jit(solution)/shard_map/ppermute | solution.py:385
  87.0 16.0 %collective-permute-start.7 = (bf16[128,512]{1,0:T(8,128)(2,1)}, bf16[128,512]{1,0:T(8,128)(2,1)S(1)}, u32[]{:S(2)}, u32[]{:S(2)}) collective-permute-start(bf16[128,512]{1,0:T(8,128)(2,1)} %get-tuple-element.87), channel_id=1, source_target_pairs={{0,5},{1,4},{2,7},{3,6},{4,1},{5,0},{6,3},{7,2},{8,13},{9,12},{10,... | collective-permute-start | bytes 393224 | tf_op jit(solution)/shard_map/ppermute | solution.py:385
  89.7 13.4 %collective-permute-start.4 = (bf16[128,512]{1,0:T(8,128)(2,1)}, bf16[128,512]{1,0:T(8,128)(2,1)S(1)}, u32[]{:S(2)}, u32[]{:S(2)}) collective-permute-start(bf16[128,512]{1,0:T(8,128)(2,1)} %get-tuple-element.79), channel_id=1, source_target_pairs={{0,1},{1,0},{2,3},{3,2},{4,5},{5,4},{6,7},{7,6},{8,9},{9,8},{10,11... | collective-permute-start | bytes 393224 | tf_op jit(solution)/shard_map/ppermute | solution.py:385
  91.9 11.2 %collective-permute-start.8 = (bf16[128,512]{1,0:T(8,128)(2,1)}, bf16[128,512]{1,0:T(8,128)(2,1)S(1)}, u32[]{:S(2)}, u32[]{:S(2)}) collective-permute-start(bf16[128,512]{1,0:T(8,128)(2,1)} %get-tuple-element.88), channel_id=1, source_target_pairs={{0,6},{1,7},{2,4},{3,5},{4,2},{5,3},{6,0},{7,1},{8,14},{9,15},{10,... | collective-permute-start | bytes 393224 | tf_op jit(solution)/shard_map/ppermute | solution.py:385
  93.6 9.5 %collective-permute-start.9 = (bf16[128,512]{1,0:T(8,128)(2,1)}, bf16[128,512]{1,0:T(8,128)(2,1)S(1)}, u32[]{:S(2)}, u32[]{:S(2)}) collective-permute-start(bf16[128,512]{1,0:T(8,128)(2,1)} %get-tuple-element.89), channel_id=1, source_target_pairs={{0,7},{1,6},{2,5},{3,4},{4,3},{5,2},{6,1},{7,0},{8,15},{9,14},{10,... | collective-permute-start | bytes 393224 | tf_op jit(solution)/shard_map/ppermute | solution.py:385
  99.5 0.6 copy-start.3
  100.1 1.2 %copy-start.1 = (f32[2,128,1024]{2,1,0:T(8,128)S(1)}, f32[2,128,1024]{2,1,0:T(8,128)}, u32[]{:S(2)}) copy-start(f32[2,128,1024]{2,1,0:T(8,128)} %get-tuple-element.91.own1_ref) | copy-start | bytes 3145732
  101.4 12.0 %copy-start.2 = (bf16[128,512]{1,0:T(8,128)(2,1)S(1)}, bf16[128,512]{1,0:T(8,128)(2,1)}, u32[]{:S(2)}) copy-start(bf16[128,512]{1,0:T(8,128)(2,1)} %get-tuple-element.102.refs_0_) | copy-start | bytes 393220
  103.1 5.4 %collective-permute-start.11 = (bf16[128,512]{1,0:T(8,128)(2,1)S(1)}, bf16[128,512]{1,0:T(8,128)(2,1)S(1)}, u32[]{:S(2)}, u32[]{:S(2)}) collective-permute-start(bf16[128,512]{1,0:T(8,128)(2,1)S(1)} %get-tuple-element.114), channel_id=1, source_target_pairs={{0,4},{1,5},{2,6},{3,7},{4,0},{5,1},{6,2},{7,3},{8,12},{9,13},{10,... | collective-permute-start | bytes 393224 | tf_op jit(solution)/shard_map/ppermute | solution.py:385
  104.8 5.5 %collective-permute-start.13 = (bf16[128,512]{1,0:T(8,128)(2,1)S(1)}, bf16[128,512]{1,0:T(8,128)(2,1)S(1)}, u32[]{:S(2)}, u32[]{:S(2)}) collective-permute-start(bf16[128,512]{1,0:T(8,128)(2,1)S(1)} %get-tuple-element.117), channel_id=1, source_target_pairs={{0,2},{1,3},{2,0},{3,1},{4,6},{5,7},{6,4},{7,5},{8,10},{9,11},{10,... | collective-permute-start | bytes 393224 | tf_op jit(solution)/shard_map/ppermute | solution.py:385
  106.3 6.2 %collective-permute-start.14 = (bf16[128,512]{1,0:T(8,128)(2,1)S(1)}, bf16[128,512]{1,0:T(8,128)(2,1)S(1)}, u32[]{:S(2)}, u32[]{:S(2)}) collective-permute-start(bf16[128,512]{1,0:T(8,128)(2,1)S(1)} %get-tuple-element.120), channel_id=1, source_target_pairs={{0,3},{1,2},{2,1},{3,0},{4,7},{5,6},{6,5},{7,4},{8,11},{9,10},{10,... | collective-permute-start | bytes 393224 | tf_op jit(solution)/shard_map/ppermute | solution.py:385
  106.3 9.1 %collective-permute-start.15 = (bf16[128,512]{1,0:T(8,128)(2,1)}, bf16[128,512]{1,0:T(8,128)(2,1)S(1)}, u32[]{:S(2)}, u32[]{:S(2)}) collective-permute-start(bf16[128,512]{1,0:T(8,128)(2,1)} %get-tuple-element.123), channel_id=1, source_target_pairs={{0,5},{1,4},{2,7},{3,6},{4,1},{5,0},{6,3},{7,2},{8,13},{9,12},{10,... | collective-permute-start | bytes 393224 | tf_op jit(solution)/shard_map/ppermute | solution.py:385
  108.5 6.9 %collective-permute-start.12 = (bf16[128,512]{1,0:T(8,128)(2,1)S(1)}, bf16[128,512]{1,0:T(8,128)(2,1)S(1)}, u32[]{:S(2)}, u32[]{:S(2)}) collective-permute-start(bf16[128,512]{1,0:T(8,128)(2,1)S(1)} %get-tuple-element.115), channel_id=1, source_target_pairs={{0,1},{1,0},{2,3},{3,2},{4,5},{5,4},{6,7},{7,6},{8,9},{9,8},{10,11... | collective-permute-start | bytes 393224 | tf_op jit(solution)/shard_map/ppermute | solution.py:385
  110.3 5.9 %collective-permute-start.16 = (bf16[128,512]{1,0:T(8,128)(2,1)S(1)}, bf16[128,512]{1,0:T(8,128)(2,1)S(1)}, u32[]{:S(2)}, u32[]{:S(2)}) collective-permute-start(bf16[128,512]{1,0:T(8,128)(2,1)S(1)} %get-tuple-element.124), channel_id=1, source_target_pairs={{0,6},{1,7},{2,4},{3,5},{4,2},{5,3},{6,0},{7,1},{8,14},{9,15},{10,... | collective-permute-start | bytes 393224 | tf_op jit(solution)/shard_map/ppermute | solution.py:385
  112.5 6.4 %collective-permute-start.17 = (bf16[128,512]{1,0:T(8,128)(2,1)S(1)}, bf16[128,512]{1,0:T(8,128)(2,1)S(1)}, u32[]{:S(2)}, u32[]{:S(2)}) collective-permute-start(bf16[128,512]{1,0:T(8,128)(2,1)S(1)} %get-tuple-element.125), channel_id=1, source_target_pairs={{0,7},{1,6},{2,5},{3,4},{4,3},{5,2},{6,1},{7,0},{8,15},{9,14},{10,... | collective-permute-start | bytes 393224 | tf_op jit(solution)/shard_map/ppermute | solution.py:385

commit v4 on v3

--- a/solution.py
+++ b/solution.py
@@ -17,6 +17,8 @@
 EXCLUDED = -1e30
 ONES = 16
 IN_FLIGHT = 4
+HOLD = 3
+EARLY = 4
 
 NN = (((1,), (0,)), ((), ()))
 NT = (((1,), (1,)), ((), ()))
@@ -36,8 +38,9 @@
 
 
 def attention_kernel(
-    head, pieces, place_ref, qo_hbm, halo_hbm, own_hbm, *refs
+    taken, pieces, place_ref, *refs
 ):
+    qo_hbm, (halo_hbm, own_hbm, *refs) = refs[:taken], refs[taken:]
     ao_hbm, (dhalo_hbm, down_hbm, *refs) = refs[:pieces], refs[pieces:]
     (kv, qo, ao, dhalo, keys_t, values_t, acc_k, acc_v, exps0, exps1, q_turned, o_turned, in_sem, q_sem, out_sem) = refs
     rows = qo.shape[0]
@@ -51,8 +54,9 @@
     def span(i):
         return pl.ds(pl.multiple_of(i * BLOCK, BLOCK), CHUNKS * BLOCK)
 
-    def qo_copy(i):
-        return pltpu.make_async_copy(qo_hbm.at[at(i)], qo.at[at(i)], q_sem.at[i])
+    def qo_copy(i, piece=0):
+        source = qo_hbm[0].at[at(i)] if taken == 1 else qo_hbm[piece]
+        return pltpu.make_async_copy(source, qo.at[at(i)], q_sem.at[i])
 
     def ao_copy(i):
         return pltpu.make_async_copy(ao.at[at(i)], ao_hbm[0].at[at(i)], out_sem.at[0, i])
@@ -64,13 +68,11 @@
         return pltpu.make_async_copy(dhalo.at[at(i)], dhalo_hbm.at[at(i)], out_sem.at[1, i])
 
     halo_copy = pltpu.make_async_copy(halo_hbm, kv.at[pl.ds(0, WINDOW)], in_sem.at[0])
-    own_copy = pltpu.make_async_copy(
-        own_hbm.at[:, pl.ds(head * PAIR, PAIR)], kv.at[pl.ds(WINDOW, rows)], in_sem.at[1]
-    )
+    own_copy = pltpu.make_async_copy(own_hbm, kv.at[pl.ds(WINDOW, rows)], in_sem.at[1])
     halo_copy.start()
     own_copy.start()
     for i in range(blocks):
-        qo_copy(i).start()
+        (qo_copy(i) if taken == 1 else qo_copy(place_ref[1] ^ i, i)).start()
 
     ones_row = lax.broadcasted_iota(jnp.int32, (ONES, values_t.shape[1]), 0) == 0
     values_t[HEAD_DIM:, :] = jnp.where(ones_row, 1.0, 0.0).astype(jnp.bfloat16)
@@ -193,24 +195,24 @@
     own_v.wait()
 
 
-def attention(head, place, qo, halo, own, pieces):
+def attention(place, qo, halo, own, pieces):
     rows = own.shape[0]
     blocks = rows // BLOCK
     reach = WINDOW + rows
     bf16, f32 = jnp.bfloat16, jnp.float32
     return pl.pallas_call(
-        functools.partial(attention_kernel, head, pieces),
+        functools.partial(attention_kernel, len(qo), pieces),
         out_shape=(
-            *[jax.ShapeDtypeStruct((rows // pieces, qo.shape[1]), bf16)] * pieces,
+            *[jax.ShapeDtypeStruct((rows // pieces, 2 * PAIR), bf16)] * pieces,
             jax.ShapeDtypeStruct(halo.shape, bf16),
             jax.ShapeDtypeStruct((2, HEAD_DIM, rows), f32),
         ),
-        in_specs=[SMEM, ANY, ANY, ANY],
+        in_specs=[SMEM] + [ANY] * (len(qo) + 2),
         out_specs=(HBM,) * (pieces + 2),
         scratch_shapes=[
             pltpu.VMEM((reach, PAIR), bf16),
-            pltpu.VMEM(qo.shape, bf16),
-            pltpu.VMEM(qo.shape, bf16),
+            pltpu.VMEM((rows, 2 * PAIR), bf16),
+            pltpu.VMEM((rows, 2 * PAIR), bf16),
             pltpu.VMEM(halo.shape, bf16),
             pltpu.VMEM((HEAD_DIM, reach + BLOCK), bf16),
             pltpu.VMEM((HEAD_DIM + ONES, reach + BLOCK), bf16),
@@ -227,62 +229,91 @@
         compiler_params=pltpu.CompilerParams(vmem_limit_bytes=58 * 2**20),
         cost_estimate=pl.CostEstimate(flops=10**10, bytes_accessed=4 * 2**20, transcendentals=0),
         name="attention",
-    )(place, qo, halo, own)
-
-
-def interleave_kernel(width, parts, split, place_ref, *refs):
+    )(place, *qo, halo, own)
+
+
+def interleave_kernel(width, sets, place_ref, *refs):
     arrays, refs = refs[:2], refs[2:]
-    groups = arrays[0].shape[1] // parts[0][2]
-    outs, (first, second, staged, in_sem, out_sem) = refs[: groups if split else 1], refs[groups if split else 1 :]
-    half = arrays[0].shape[1] // 2
-    fetched = (first, second)
-    loads = []
-    for n in range(2):
-        for h in range(2):
-            cols = pl.ds(h * half, half)
-            loads.append(pltpu.make_async_copy(arrays[n].at[:, cols], fetched[n].at[:, cols], in_sem.at[2 * n + h]))
+    groups = arrays[0].shape[1] // sets[0][1][0][2]
+    outs, refs = refs[: -(4 + len(sets))], refs[-(4 + len(sets)) :]
+    fetched, staged, (in_sem, out_sem) = refs[:2], refs[2:-2], refs[-2:]
+    loads = [pltpu.make_async_copy(arrays[n], fetched[n], in_sem.at[n]) for n in range(2)]
     for load in loads:
         load.start()
-    if split:
-        for load in loads:
-            load.wait()
+    for load in loads:
+        load.wait()
     stores = []
-    for g in range(groups):
-        if not split and g % (groups // 2) == 0:
-            loads[g // (groups // 2)].wait()
-            loads[2 + g // (groups // 2)].wait()
-        source = place_ref[1] ^ g if split else g
-        for n, (which, start, stride) in enumerate(parts):
-            at = source * stride + start
-            if split:
-                at = pl.multiple_of(at, HEAD_DIM)
-            staged[g, :, n * width : (n + 1) * width] = fetched[which][:, pl.ds(at, width)]
-        stores.append(pltpu.make_async_copy(staged.at[g], outs[g] if split else outs[0].at[g], out_sem.at[g]))
-        stores[g].start()
+    taken = 0
+    for k, (split, parts) in enumerate(sets):
+        for g in range(groups):
+            source = place_ref[1] ^ g if split else g
+            for n, (which, start, stride) in enumerate(parts):
+                at = source * stride + start
+                if split:
+                    at = pl.multiple_of(at, HEAD_DIM)
+                staged[k][g, :, n * width : (n + 1) * width] = fetched[which][:, pl.ds(at, width)]
+            out = outs[taken + g] if split else outs[taken].at[g]
+            stores.append(pltpu.make_async_copy(staged[k].at[g], out, out_sem.at[k, g]))
+            stores[-1].start()
+        taken += groups if split else 1
     for store in stores:
         store.wait()
 
 
-def interleave(place, arrays, groups, width, parts, split=False):
+def interleave(place, arrays, groups, width, sets):
     rows, cols = arrays[0].shape
     dtype = arrays[0].dtype
-    out = (rows, width * len(parts))
-    whole = (groups, *out)
-    return pl.pallas_call(
-        functools.partial(interleave_kernel, width, parts, split),
-        out_shape=(jax.ShapeDtypeStruct(out, dtype),) * groups if split else (jax.ShapeDtypeStruct(whole, dtype),),
+    shapes, staged = [], []
+    for split, parts in sets:
+        whole = (groups, rows, width * len(parts))
+        staged.append(pltpu.VMEM(whole, dtype))
+        shapes += [jax.ShapeDtypeStruct(whole[1:], dtype)] * groups if split else [jax.ShapeDtypeStruct(whole, dtype)]
+    return pl.pallas_call(
+        functools.partial(interleave_kernel, width, sets),
+        out_shape=tuple(shapes),
         in_specs=[SMEM, HBM, HBM],
-        out_specs=(HBM,) * (groups if split else 1),
+        out_specs=(HBM,) * len(shapes),
         scratch_shapes=[
             pltpu.VMEM((rows, cols), dtype),
             pltpu.VMEM((rows, cols), dtype),
-            pltpu.VMEM(whole, dtype),
-            pltpu.SemaphoreType.DMA((4,)),
-            pltpu.SemaphoreType.DMA((groups,)),
+            *staged,
+            pltpu.SemaphoreType.DMA((2,)),
+            pltpu.SemaphoreType.DMA((len(sets), groups)),
         ],
         compiler_params=pltpu.CompilerParams(vmem_limit_bytes=58 * 2**20),
         name="interleave",
     )(place, *arrays)
+
+
+def assemble_kernel(place_ref, *refs):
+    *arrays, sem = refs
+    count, heads = sem.shape
+    pieces, outs = arrays[:count], arrays[count:]
+    rows, width = pieces[0].shape[0], outs[0].shape[1]
+    copies = []
+    for j in range(count):
+        at = pl.ds(pl.multiple_of((place_ref[1] ^ j) * rows, BLOCK), rows)
+        for h in range(heads):
+            source = pieces[j].at[:, pl.ds(h * width, width)]
+            copies.append(pltpu.make_async_copy(source, outs[h].at[at], sem.at[j, h]))
+    for copy in copies:
+        copy.start()
+    for copy in copies:
+        copy.wait()
+
+
+def assemble(place, pieces, heads):
+    rows, width = pieces[0].shape
+    shape = jax.ShapeDtypeStruct((len(pieces) * rows, width // heads), pieces[0].dtype)
+    return pl.pallas_call(
+        assemble_kernel,
+        out_shape=(shape,) * heads,
+        in_specs=[SMEM] + [ANY] * len(pieces),
+        out_specs=(VMEM,) * heads,
+        scratch_shapes=[pltpu.SemaphoreType.DMA((len(pieces), heads))],
+        compiler_params=pltpu.CompilerParams(vmem_limit_bytes=8 * 2**20),
+        name="assemble",
+    )(place, *pieces)
 
 
 def group_at(place_ref, j, width):
@@ -373,36 +404,48 @@
     def exchange(x):
         return lax.all_to_all(x, ("seq", "kvh"), 0, 0, tiled=True, axis_index_groups=groups)
 
-    def swap(pieces):
+    order = sorted(range(1, members), key=lambda j: j == 1)
+
+    def swap(pieces, before=None, limit=IN_FLIGHT):
         every = range(shards * split)
         out = [pieces[0]] * members
-        order = sorted(range(1, members), key=lambda j: j == 1)
-        for n, j in enumerate(order):
+        sent = [] if before is None else [(before, j) for j in order]
+        for j in order:
             piece = pieces[j]
-            if n >= IN_FLIGHT:
-                before = order[n - IN_FLIGHT]
-                piece, out[before] = lax.optimization_barrier((piece, out[before]))
+            if len(sent) >= limit:
+                box, k = sent[-limit]
+                piece, box[k] = lax.optimization_barrier((piece, box[k]))
             out[j] = lax.ppermute(piece, ("seq", "kvh"), [(i, i ^ j) for i in every])
+            sent.append((out, j))
         return out
 
     def onward(x):
-        return lax.ppermute(x, "seq", [(i, i + apart) for i in range(shards - apart)])
+        return lax.ppermute(x, "seq", [(i, (i + apart) % shards) for i in range(shards)])
 
     def backward(x):
-        return lax.ppermute(x, "seq", [(i + apart, i) for i in range(shards - apart)])
+        return lax.ppermute(x, "seq", [((i + apart) % shards, i) for i in range(shards)])
 
     stride = heads * HEAD_DIM
     kv_parts = [(n, h * HEAD_DIM, stride) for h in range(heads) for n in range(2)]
-    (own,) = interleave(place, (key_rows, value_rows), members, HEAD_DIM, kv_parts)
-    own = exchange(own).reshape(WINDOW, -1)
-    halos = [onward(own[:, h * PAIR : (h + 1) * PAIR]) for h in range(heads)]
+    def qo_parts(h):
+        return [(n, h * PAIR, 2 * stride) for n in range(2)]
+
+    kv = list(interleave(place, (key_rows, value_rows), members, HEAD_DIM, [(True, kv_parts)]))
+    sets = [(h == 0, qo_parts(h)) for h in range(heads)]
+    packed = interleave(place, (queries, grad_out), members, PAIR, sets)
+    late = order[EARLY]
+    kv[late], (*first, second) = lax.optimization_barrier((kv[late], packed))
+    kv = swap(kv, None, 5)
+    first = swap(first, kv, 5)
+    own = assemble(place, kv, heads)
+    second, first[order[HOLD]] = lax.optimization_barrier((second, first[order[HOLD]]))
+    qos = [first, [exchange(second).reshape(WINDOW, -1)]]
+    held, first[order[-2]] = lax.optimization_barrier((own[1], first[order[-2]]))
+    halos = [onward(own[0]), onward(held)]
     outs, down, back = [], [], []
     for h in range(heads):
-        qo_parts = [(n, h * PAIR, 2 * stride) for n in range(2)]
-        (qo,) = interleave(place, (queries, grad_out), members, PAIR, qo_parts)
-        qo = exchange(qo).reshape(WINDOW, -1)
         last = h == heads - 1
-        *ao, dhalo, mine = attention(h, place, qo, halos[h], own, members if last else 1)
+        *ao, dhalo, mine = attention(place, qos[h], halos[h], own[h], members if last else 1)
         if h > 0:
             ao, back[h - 1] = lax.optimization_barrier((ao, back[h - 1]))
         back.append(backward(dhalo))

time: 121 us -> 112 us (0.926)
  waiting for transfers between devices: 31.7 us -> 21.8 us
  starting transfers between devices: 40.6 us -> 43.7 us
  Pallas kernels: 41.3 us -> 39.5 us
    all_to_all x4 -> x2, waiting for transfers between devices: 15.9 us -> 0.01 us  [exchange(): lax.all_to_all(x, ('seq', 'kvh'), 0, 0, tiled=True, axis_index_groups=gro...]
    ppermute x14 -> x28, starting transfers between devices: 13.9 us -> 29.8 us  [swap(): out[j] = lax.ppermute(piece, ('seq', 'kvh'), [(i, i ^ j) for i in every])]
    all_to_all x4 -> x2, starting transfers between devices: 16.4 us -> 7.77 us  [exchange(): lax.all_to_all(x, ('seq', 'kvh'), 0, 0, tiled=True, axis_index_groups=gro...]
    ppermute x14 -> x28, waiting for transfers between devices: 11.3 us -> 19.1 us  [swap(): out[j] = lax.ppermute(piece, ('seq', 'kvh'), [(i, i ^ j) for i in every])]
    ppermute x4, starting transfers between devices: 10.3 us -> 6.2 us  [the longest x2 3.26 us: onward(): lax.ppermute(x, 'seq', [(i, (i + apart) % shards) for i in range(shards)])]
    pallas_call x5, Pallas kernels: 35.9 us -> 34 us  [the longest x2 26.4 us: attention(): pl.pallas_call(functools.partial(attention_kernel, len(qo), pieces), out_...]
    ppermute x4, waiting for transfers between devices: 4.48 us -> 2.77 us  [the longest x2 2.76 us: backward(): lax.ppermute(x, 'seq', [((i + apart) % shards, i) for i in range(shards)])]
    unnamed x16 -> x52, local copies, waits for them, and re-layouts: 4.57 us -> 4.98 us
  transfers between devices with their start and end apart: 22 -> 34, of which waited for: 9 -> 10; matrix products, arithmetic and copies ran while one was open for 1% -> 0% of each run, Pallas kernels for 31% -> 31%
where the time goes in v4:
time: 112 us
  starting transfers between devices  43.7 us (39%)
  Pallas kernels  39.5 us (35%)
  waiting for transfers between devices  21.8 us (19%)
  local copies, waits for them, and re-layouts  4.98 us (4%)
    ppermute x28, starting transfers between devices, swap(): out[j] = lax.ppermute(piece, ('seq', 'kvh'), [(i, i ^ j) for i in every])  29.8 us
    pallas_call x2, Pallas kernels, attention(): pl.pallas_call(functools.partial(attention_kernel, len(qo), pieces), out_...  26.4 us
    ppermute x28, waiting for transfers between devices, swap(): out[j] = lax.ppermute(piece, ('seq', 'kvh'), [(i, i ^ j) for i in every])  19.1 us
    all_to_all x2, starting transfers between devices, exchange(): lax.all_to_all(x, ('seq', 'kvh'), 0, 0, tiled=True, axis_index_groups=gro...  7.77 us
    pallas_call x2, Pallas kernels, interleave(): pl.pallas_call(functools.partial(interleave_kernel, width, sets), out_sha...  6.74 us
    unnamed x52, local copies, waits for them, and re-layouts  4.98 us
    ppermute x2, starting transfers between devices, onward(): lax.ppermute(x, 'seq', [(i, (i + apart) % shards) for i in range(shards)])  3.26 us
    ppermute x2, starting transfers between devices, backward(): lax.ppermute(x, 'seq', [((i + apart) % shards, i) for i in range(shards)])  2.94 us
  transfers between devices with their start and end apart: 34, of which 10 were waited for; matrix products, arithmetic and copies ran while one was open for 0% of the time, Pallas kernels for 31%

profile of v4, /device:TPU:0, one launch (start us, length us, event | category | flops | bytes accessed | tf_op | source)
XLA Modules:
  0.0 111.6 jit_solution(4592453322955390116)
XLA Ops:
  0.6 0.6 pad_add_fusion.place_ref
  1.2 2.9 %interleave.2 = (bf16[128,512]{1,0:T(8,128)(2,1)}, bf16[128,512]{1,0:T(8,128)(2,1)}, bf16[128,512]{1,0:T(8,128)(2,1)}, bf16[128,512]{1,0:T(8,128)(2,1)}, bf16[12...) custom-call(s32[2]{0:T(128)} %pad_add_fusion.place_ref, ...), custom_call_target="tpu_custom_call" | custom-call | tf_op jit(solution)/shard_map/interleave/pallas_call | solution.py:271
  4.2 3.0 %collective-permute-start.7 = (bf16[128,512]{1,0:T(8,128)(2,1)}, bf16[128,512]{1,0:T(8,128)(2,1)S(1)}, u32[]{:S(2)}, u32[]{:S(2)}) collective-permute-start(bf16[128,512]{1,0:T(8,128)(2,1)} %get-tuple-element.145), channel_id=1, source_target_pairs={{0,2},{1,3},{2,0},{3,1},{4,6},{5,7},{6,4},{7,5},{8,10},{9,11},{10,... | collective-permute-start | bytes 393224 | tf_op jit(solution)/shard_map/ppermute | solution.py:418
  7.2 1.8 %collective-permute-start = (bf16[128,512]{1,0:T(8,128)(2,1)}, bf16[128,512]{1,0:T(8,128)(2,1)S(1)}, u32[]{:S(2)}, u32[]{:S(2)}) collective-permute-start(bf16[128,512]{1,0:T(8,128)(2,1)} %get-tuple-element.130), channel_id=1, source_target_pairs={{0,5},{1,4},{2,7},{3,6},{4,1},{5,0},{6,3},{7,2},{8,13},{9,12},{10,... | collective-permute-start | bytes 393224 | tf_op jit(solution)/shard_map/ppermute | solution.py:418
  9.1 3.8 %interleave.3 = (bf16[128,512]{1,0:T(8,128)(2,1)}, bf16[128,512]{1,0:T(8,128)(2,1)}, bf16[128,512]{1,0:T(8,128)(2,1)}, bf16[128,512]{1,0:T(8,128)(2,1)}, bf16[12...) custom-call(s32[2]{0:T(128)} %pad_add_fusion.place_ref, ...), custom_call_target="tpu_custom_call" | custom-call | tf_op jit(solution)/shard_map/interleave/pallas_call | solution.py:271
  12.9 2.8 %collective-permute-start.5 = (bf16[128,512]{1,0:T(8,128)(2,1)S(1)}, bf16[128,512]{1,0:T(8,128)(2,1)S(1)}, u32[]{:S(2)}, u32[]{:S(2)}) collective-permute-start(bf16[128,512]{1,0:T(8,128)(2,1)S(1)} %copy-done.22), channel_id=1, source_target_pairs={{0,6},{1,7},{2,4},{3,5},{4,2},{5,3},{6,0},{7,1},{8,14},{9,15},{10,... | collective-permute-start | bytes 393224 | tf_op jit(solution)/shard_map/ppermute | solution.py:418
  16.1 3.2 %collective-permute-done.5.refs_6_ = bf16[128,512]{1,0:T(8,128)(2,1)S(1)} collective-permute-done((bf16[128,512]{1,0:T(8,128)(2,1)S(1)}, bf16[128,512]{1,0:T(8,128)(2,1)S(1)}, u32[]{:S(2)}, u32[]{:S(2)}) %collective-permute-start.5) | collective-permute-done | bytes 131104 | tf_op jit(solution)/shard_map/ppermute | solution.py:418
  19.4 2.7 %collective-permute-done.8.refs_7_ = bf16[128,512]{1,0:T(8,128)(2,1)S(1)} collective-permute-done((bf16[128,512]{1,0:T(8,128)(2,1)S(1)}, bf16[128,512]{1,0:T(8,128)(2,1)S(1)}, u32[]{:S(2)}, u32[]{:S(2)}) %collective-permute-start.8) | collective-permute-done | bytes 131104 | tf_op jit(solution)/shard_map/ppermute | solution.py:418
  22.1 0.8 assemble.1
  23.0 1.6 %collective-permute-start.14 = (bf16[1024,256]{1,0:T(8,128)(2,1)S(1)}, bf16[1024,256]{1,0:T(8,128)(2,1)S(1)}, u32[]{:S(2)}, u32[]{:S(2)}) collective-permute-start(bf16[1024,256]{1,0:T(8,128)(2,1)S(1)} %get-tuple-element.165.refs_9_), channel_id=1, source_target_pairs={{0,8},{4,12},{8,16},{12,20},{16,24},{20,28},{24,0},{28,4},{1,9},{5... | collective-permute-start | bytes 1572872 | tf_op jit(solution)/shard_map/ppermute | solution.py:423
  24.6 1.0 collective-permute-start.4
  25.6 1.7 %collective-permute-start.9 = (bf16[128,512]{1,0:T(8,128)(2,1)S(1)}, bf16[128,512]{1,0:T(8,128)(2,1)S(1)}, u32[]{:S(2)}, u32[]{:S(2)}) collective-permute-start(bf16[128,512]{1,0:T(8,128)(2,1)S(1)} %copy-done.14), channel_id=1, source_target_pairs={{0,5},{1,4},{2,7},{3,6},{4,1},{5,0},{6,3},{7,2},{8,13},{9,12},{10,... | collective-permute-start | bytes 393224 | tf_op jit(solution)/shard_map/ppermute | solution.py:418
  27.3 1.1 %collective-permute-start.6 = (bf16[128,512]{1,0:T(8,128)(2,1)S(1)}, bf16[128,512]{1,0:T(8,128)(2,1)}, u32[]{:S(2)}, u32[]{:S(2)}) collective-permute-start(bf16[128,512]{1,0:T(8,128)(2,1)S(1)} %copy-done.12), channel_id=1, source_target_pairs={{0,4},{1,5},{2,6},{3,7},{4,0},{5,1},{6,2},{7,3},{8,12},{9,13},{10,... | collective-permute-start | bytes 393224 | tf_op jit(solution)/shard_map/ppermute | solution.py:418
  28.4 2.3 %collective-permute-done.4.refs_2_ = bf16[128,512]{1,0:T(8,128)(2,1)S(1)} collective-permute-done((bf16[128,512]{1,0:T(8,128)(2,1)S(1)}, bf16[128,512]{1,0:T(8,128)(2,1)S(1)}, u32[]{:S(2)}, u32[]{:S(2)}) %collective-permute-start.4) | collective-permute-done | bytes 131104 | tf_op jit(solution)/shard_map/ppermute | solution.py:418
  30.7 0.9 collective-permute-start.13
  31.6 3.1 %collective-permute-start.12 = (bf16[128,512]{1,0:T(8,128)(2,1)S(1)}, bf16[128,512]{1,0:T(8,128)(2,1)S(1)}, u32[]{:S(2)}, u32[]{:S(2)}) collective-permute-start(bf16[128,512]{1,0:T(8,128)(2,1)S(1)} %copy-done.11), channel_id=1, source_target_pairs={{0,6},{1,7},{2,4},{3,5},{4,2},{5,3},{6,0},{7,1},{8,14},{9,15},{10,... | collective-permute-start | bytes 393224 | tf_op jit(solution)/shard_map/ppermute | solution.py:418
  34.7 0.6 copy-done.19
  35.3 3.6 %all-to-all-start.1 = ((bf16[8,128,512]{2,1,0:T(8,128)(2,1)}), bf16[8,128,512]{2,1,0:T(8,128)(2,1)S(1)}, u32[]{:S(2)}, u32[]{:S(2)}) async-start(bf16[8,128,512]{2,1,0:T(8,128)(2,1)} %get-tuple-element.167), calls=%async_computation.1 | async-start | bytes 2097152 | tf_op jit(solution)/shard_map/all_to_all | solution.py:405
  38.9 1.6 %collective-permute-start.15 = (bf16[1024,256]{1,0:T(8,128)(2,1)S(1)}, bf16[1024,256]{1,0:T(8,128)(2,1)}, u32[]{:S(2)}, u32[]{:S(2)}) collective-permute-start(bf16[1024,256]{1,0:T(8,128)(2,1)S(1)} %get-tuple-element.168.refs_2_), channel_id=1, source_target_pairs={{0,8},{4,12},{8,16},{12,20},{16,24},{20,28},{24,0},{28,4},{1,9},{5... | collective-permute-start | bytes 1572872 | tf_op jit(solution)/shard_map/ppermute | solution.py:423
  40.6 0.6 copy-done.24
  41.3 0.8 copy-done.9
  42.1 12.8 %attention.2 = (bf16[1024,512]{1,0:T(8,128)(2,1)}, bf16[1024,256]{1,0:T(8,128)(2,1)}, f32[2,128,1024]{2,1,0:T(8,128)}) custom-call(s32[2]{0:T(128)} %pad_add_fusion.place_ref, bf16[128,512]{1,0:T(8,128)(2,1)} %get-tuple-element.127.refs_0_, bf16[128,512]{1,0:T(8,128)(2,1)} %copy-done.25, bf16[128,512]{1,0:T(8,128)(2,1)} %copy-done.17, ...), custom_call_target="tpu_custom_call" | custom-call | flops 10000000000 | bytes 4194304 | tf_op jit(solution)/shard_map/attention/pallas_call | solution.py:203
  54.9 2.3 %collective-permute-start.16 = (bf16[1024,256]{1,0:T(8,128)(2,1)}, bf16[1024,256]{1,0:T(8,128)(2,1)S(1)}, u32[]{:S(2)}, u32[]{:S(2)}) collective-permute-start(bf16[1024,256]{1,0:T(8,128)(2,1)} %get-tuple-element.177), channel_id=1, source_target_pairs={{8,0},{12,4},{16,8},{20,12},{24,16},{28,20},{0,24},{4,28},{9,1},{1... | collective-permute-start | bytes 1572872 | tf_op jit(solution)/shard_map/ppermute | solution.py:426
  57.2 1.0 copy-done.8
  58.1 4.2 %all-to-all-start = ((bf16[8,128,512]{2,1,0:T(8,128)(2,1)}), bf16[8,128,512]{2,1,0:T(8,128)(2,1)S(1)}, u32[]{:S(2)}, u32[]{:S(2)}) async-start(bf16[8,128,512]{2,1,0:T(8,128)(2,1)} %bitcast.4), calls=%async_computation | async-start | bytes 2097152 | tf_op jit(solution)/shard_map/all_to_all | solution.py:405
  62.4 13.6 %attention.3 = (bf16[128,512]{1,0:T(8,128)(2,1)}, bf16[128,512]{1,0:T(8,128)(2,1)}, bf16[128,512]{1,0:T(8,128)(2,1)}, bf16[128,512]{1,0:T(8,128)(2,1)}, bf16[128...) custom-call(s32[2]{0:T(128)} %pad_add_fusion.place_ref, ...), custom_call_target="tpu_custom_call" | custom-call | flops 10000000000 | bytes 4194304 | tf_op jit(solution)/shard_map/attention/pallas_call | solution.py:203
  76.0 0.7 collective-permute-start.24
  76.7 2.0 %collective-permute-start.17 = (bf16[128,512]{1,0:T(8,128)(2,1)}, bf16[128,512]{1,0:T(8,128)(2,1)S(1)}, u32[]{:S(2)}, u32[]{:S(2)}) collective-permute-start(bf16[128,512]{1,0:T(8,128)(2,1)} %get-tuple-element.180), channel_id=1, source_target_pairs={{0,4},{1,5},{2,6},{3,7},{4,0},{5,1},{6,2},{7,3},{8,12},{9,13},{10,... | collective-permute-start | bytes 393224 | tf_op jit(solution)/shard_map/ppermute | solution.py:418
  78.6 1.5 %collective-permute-start.19 = (bf16[128,512]{1,0:T(8,128)(2,1)}, bf16[128,512]{1,0:T(8,128)(2,1)S(1)}, u32[]{:S(2)}, u32[]{:S(2)}) collective-permute-start(bf16[128,512]{1,0:T(8,128)(2,1)} %get-tuple-element.183), channel_id=1, source_target_pairs={{0,2},{1,3},{2,0},{3,1},{4,6},{5,7},{6,4},{7,5},{8,10},{9,11},{10,... | collective-permute-start | bytes 393224 | tf_op jit(solution)/shard_map/ppermute | solution.py:418
  80.4 2.0 %collective-permute-done.17.refs_4_ = bf16[128,512]{1,0:T(8,128)(2,1)S(1)} collective-permute-done((bf16[128,512]{1,0:T(8,128)(2,1)}, bf16[128,512]{1,0:T(8,128)(2,1)S(1)}, u32[]{:S(2)}, u32[]{:S(2)}) %collective-permute-start.17) | collective-permute-done | bytes 131104 | tf_op jit(solution)/shard_map/ppermute | solution.py:418
  82.4 1.9 %collective-permute-done.19.refs_2_ = bf16[128,512]{1,0:T(8,128)(2,1)S(1)} collective-permute-done((bf16[128,512]{1,0:T(8,128)(2,1)}, bf16[128,512]{1,0:T(8,128)(2,1)S(1)}, u32[]{:S(2)}, u32[]{:S(2)}) %collective-permute-start.19) | collective-permute-done | bytes 131104 | tf_op jit(solution)/shard_map/ppermute | solution.py:418
  84.4 2.3 %collective-permute-start.22 = (bf16[128,512]{1,0:T(8,128)(2,1)}, bf16[128,512]{1,0:T(8,128)(2,1)S(1)}, u32[]{:S(2)}, u32[]{:S(2)}) collective-permute-start(bf16[128,512]{1,0:T(8,128)(2,1)} %get-tuple-element.190), channel_id=1, source_target_pairs={{0,6},{1,7},{2,4},{3,5},{4,2},{5,3},{6,0},{7,1},{8,14},{9,15},{10,... | collective-permute-start | bytes 393224 | tf_op jit(solution)/shard_map/ppermute | solution.py:418
  86.7 1.1 %collective-permute-start.23 = (bf16[128,512]{1,0:T(8,128)(2,1)}, bf16[128,512]{1,0:T(8,128)(2,1)S(1)}, u32[]{:S(2)}, u32[]{:S(2)}) collective-permute-start(bf16[128,512]{1,0:T(8,128)(2,1)} %get-tuple-element.191), channel_id=1, source_target_pairs={{0,7},{1,6},{2,5},{3,4},{4,3},{5,2},{6,1},{7,0},{8,15},{9,14},{10,... | collective-permute-start | bytes 393224 | tf_op jit(solution)/shard_map/ppermute | solution.py:418
  87.8 2.8 %collective-permute-done.24.back1_ref = bf16[1024,256]{1,0:T(8,128)(2,1)S(1)} collective-permute-done((bf16[1024,256]{1,0:T(8,128)(2,1)}, bf16[1024,256]{1,0:T(8,128)(2,1)S(1)}, u32[]{:S(2)}, u32[]{:S(2)}) %collective-permute-start.24) | collective-permute-done | bytes 524320 | tf_op jit(solution)/shard_map/ppermute | solution.py:426
  90.6 0.6 copy-done.5
  91.2 1.2 %copy-done.1 = f32[2,128,1024]{2,1,0:T(8,128)S(1)} copy-done((f32[2,128,1024]{2,1,0:T(8,128)S(1)}, f32[2,128,1024]{2,1,0:T(8,128)}, u32[]{:S(2)}) %copy-start.1) | copy-done | bytes 1048600
  92.4 1.7 %add.12 = (bf16[128,512]{1,0:T(8,128)(2,1)S(1)}, bf16[128,512]{1,0:T(8,128)(2,1)S(1)}, bf16[128,512]{1,0:T(8,128)(2,1)S(1)}, bf16[128,512]{1,0:T(8,128)(2,1)S(1)...) custom-call(s32[2]{0:T(128)S(1)} %copy-done.5, ...), custom_call_target="tpu_custom_call" | custom-call | tf_op jit(solution)/shard_map/add/pallas_call | solution.py:362
  94.2 1.7 %collective-permute-start.25 = (bf16[128,512]{1,0:T(8,128)(2,1)S(1)}, bf16[128,512]{1,0:T(8,128)(2,1)S(1)}, u32[]{:S(2)}, u32[]{:S(2)}) collective-permute-start(bf16[128,512]{1,0:T(8,128)(2,1)S(1)} %get-tuple-element.216), channel_id=1, source_target_pairs={{0,4},{1,5},{2,6},{3,7},{4,0},{5,1},{6,2},{7,3},{8,12},{9,13},{10,... | collective-permute-start | bytes 393224 | tf_op jit(solution)/shard_map/ppermute | solution.py:418
  95.9 1.5 %collective-permute-start.27 = (bf16[128,512]{1,0:T(8,128)(2,1)S(1)}, bf16[128,512]{1,0:T(8,128)(2,1)S(1)}, u32[]{:S(2)}, u32[]{:S(2)}) collective-permute-start(bf16[128,512]{1,0:T(8,128)(2,1)S(1)} %get-tuple-element.219), channel_id=1, source_target_pairs={{0,2},{1,3},{2,0},{3,1},{4,6},{5,7},{6,4},{7,5},{8,10},{9,11},{10,... | collective-permute-start | bytes 393224 | tf_op jit(solution)/shard_map/ppermute | solution.py:418
  97.4 0.6 collective-permute-start.29
  98.0 1.3 %collective-permute-done.25.refs_4_ = bf16[128,512]{1,0:T(8,128)(2,1)S(1)} collective-permute-done((bf16[128,512]{1,0:T(8,128)(2,1)S(1)}, bf16[128,512]{1,0:T(8,128)(2,1)S(1)}, u32[]{:S(2)}, u32[]{:S(2)}) %collective-permute-start.25) | collective-permute-done | bytes 131104 | tf_op jit(solution)/shard_map/ppermute | solution.py:418
  99.3 2.1 %collective-permute-done.27.refs_2_ = bf16[128,512]{1,0:T(8,128)(2,1)S(1)} collective-permute-done((bf16[128,512]{1,0:T(8,128)(2,1)S(1)}, bf16[128,512]{1,0:T(8,128)(2,1)S(1)}, u32[]{:S(2)}, u32[]{:S(2)}) %collective-permute-start.27) | collective-permute-done | bytes 131104 | tf_op jit(solution)/shard_map/ppermute | solution.py:418
  101.4 2.1 %collective-permute-start.30 = (bf16[128,512]{1,0:T(8,128)(2,1)S(1)}, bf16[128,512]{1,0:T(8,128)(2,1)S(1)}, u32[]{:S(2)}, u32[]{:S(2)}) collective-permute-start(bf16[128,512]{1,0:T(8,128)(2,1)S(1)} %get-tuple-element.226), channel_id=1, source_target_pairs={{0,6},{1,7},{2,4},{3,5},{4,2},{5,3},{6,0},{7,1},{8,14},{9,15},{10,... | collective-permute-start | bytes 393224 | tf_op jit(solution)/shard_map/ppermute | solution.py:418
  103.5 0.8 collective-permute-start.31
  104.4 2.1 %spread.1 = (bf16[128,4096]{1,0:T(8,128)(2,1)}, bf16[128,4096]{1,0:T(8,128)(2,1)}) custom-call(s32[2]{0:T(128)S(1)} %copy-done.5, bf16[8,128,512]{2,1,0:T(8,128)(2,1)S(1)} %all-to-all-done.x_ref, bf16[128,512]{1,0:T(8,128)(2,1)S(1)} %copy-done.2, bf16[128,512]{1,0:T(8,128)(2,1)S(1)} %collective-permute-done.18.refs_1_, ...), custom_call_target="tpu_custom_call" | custom-call | tf_op jit(solution)/shard_map/spread/pallas_call | solution.py:338
  106.5 0.8 collective-permute-done.30.refs_6_
  107.3 2.7 %collective-permute-done.31.refs_7_ = bf16[128,512]{1,0:T(8,128)(2,1)S(1)} collective-permute-done((bf16[128,512]{1,0:T(8,128)(2,1)S(1)}, bf16[128,512]{1,0:T(8,128)(2,1)S(1)}, u32[]{:S(2)}, u32[]{:S(2)}) %collective-permute-start.31) | collective-permute-done | bytes 131104 | tf_op jit(solution)/shard_map/ppermute | solution.py:418
  109.9 1.6 %unpack.1 = (bf16[128,2048]{1,0:T(8,128)(2,1)}, bf16[128,2048]{1,0:T(8,128)(2,1)}) custom-call(s32[2]{0:T(128)S(1)} %copy-done.5, bf16[128,512]{1,0:T(8,128)(2,1)S(1)} %get-tuple-element.214.refs_0_, bf16[128,512]{1,0:T(8,128)(2,1)S(1)} %collective-permute-done.26.refs_1_, bf16[128,512]{1,0:T(8,128)(2,1)S(1)} %collective-permute-done.27.refs_2_, ...), custom_call_target="tpu_custom_call" | custom-call | tf_op jit(solution)/shard_map/unpack/pallas_call | solution.py:384
  (81 shorter events, 1.0 us)
Async XLA Ops:
  4.2 11.6 %collective-permute-start.7 = (bf16[128,512]{1,0:T(8,128)(2,1)}, bf16[128,512]{1,0:T(8,128)(2,1)S(1)}, u32[]{:S(2)}, u32[]{:S(2)}) collective-permute-start(bf16[128,512]{1,0:T(8,128)(2,1)} %get-tuple-element.145), channel_id=1, source_target_pairs={{0,2},{1,3},{2,0},{3,1},{4,6},{5,7},{6,4},{7,5},{8,10},{9,11},{10,... | collective-permute-start | bytes 393224 | tf_op jit(solution)/shard_map/ppermute | solution.py:418
  7.2 8.6 %collective-permute-start.10 = (bf16[128,512]{1,0:T(8,128)(2,1)}, bf16[128,512]{1,0:T(8,128)(2,1)S(1)}, u32[]{:S(2)}, u32[]{:S(2)}) collective-permute-start(bf16[128,512]{1,0:T(8,128)(2,1)} %get-tuple-element.151), channel_id=1, source_target_pairs={{0,3},{1,2},{2,1},{3,0},{4,7},{5,6},{6,5},{7,4},{8,11},{9,10},{10,... | collective-permute-start | bytes 393224 | tf_op jit(solution)/shard_map/ppermute | solution.py:418
  7.2 8.9 %collective-permute-start = (bf16[128,512]{1,0:T(8,128)(2,1)}, bf16[128,512]{1,0:T(8,128)(2,1)S(1)}, u32[]{:S(2)}, u32[]{:S(2)}) collective-permute-start(bf16[128,512]{1,0:T(8,128)(2,1)} %get-tuple-element.130), channel_id=1, source_target_pairs={{0,5},{1,4},{2,7},{3,6},{4,1},{5,0},{6,3},{7,2},{8,13},{9,12},{10,... | collective-permute-start | bytes 393224 | tf_op jit(solution)/shard_map/ppermute | solution.py:418
  9.0 4.0 %copy-start.22 = (bf16[128,512]{1,0:T(8,128)(2,1)S(1)}, bf16[128,512]{1,0:T(8,128)(2,1)}, u32[]{:S(2)}) copy-start(bf16[128,512]{1,0:T(8,128)(2,1)} %get-tuple-element.140) | copy-start | bytes 393220
  9.0 6.8 %copy-start.21 = (bf16[128,512]{1,0:T(8,128)(2,1)S(1)}, bf16[128,512]{1,0:T(8,128)(2,1)}, u32[]{:S(2)}) copy-start(bf16[128,512]{1,0:T(8,128)(2,1)} %get-tuple-element.146) | copy-start | bytes 393220
  9.0 6.8 %copy-start.20 = (bf16[128,512]{1,0:T(8,128)(2,1)S(1)}, bf16[128,512]{1,0:T(8,128)(2,1)}, u32[]{:S(2)}) copy-start(bf16[128,512]{1,0:T(8,128)(2,1)} %get-tuple-element.152) | copy-start | bytes 393220
  9.0 13.1 %copy-start.3 = (bf16[128,512]{1,0:T(8,128)(2,1)S(1)}, bf16[128,512]{1,0:T(8,128)(2,1)}, u32[]{:S(2)}) copy-start(bf16[128,512]{1,0:T(8,128)(2,1)} %get-tuple-element.154.refs_0_) | copy-start | bytes 393220
  9.0 7.1 %collective-permute-start.3 = (bf16[128,512]{1,0:T(8,128)(2,1)}, bf16[128,512]{1,0:T(8,128)(2,1)S(1)}, u32[]{:S(2)}, u32[]{:S(2)}) collective-permute-start(bf16[128,512]{1,0:T(8,128)(2,1)} %get-tuple-element.135), channel_id=1, source_target_pairs={{0,4},{1,5},{2,6},{3,7},{4,0},{5,1},{6,2},{7,3},{8,12},{9,13},{10,... | collective-permute-start | bytes 393224 | tf_op jit(solution)/shard_map/ppermute | solution.py:418
  12.9 6.4 %collective-permute-start.5 = (bf16[128,512]{1,0:T(8,128)(2,1)S(1)}, bf16[128,512]{1,0:T(8,128)(2,1)S(1)}, u32[]{:S(2)}, u32[]{:S(2)}) collective-permute-start(bf16[128,512]{1,0:T(8,128)(2,1)S(1)} %copy-done.22), channel_id=1, source_target_pairs={{0,6},{1,7},{2,4},{3,5},{4,2},{5,3},{6,0},{7,1},{8,14},{9,15},{10,... | collective-permute-start | bytes 393224 | tf_op jit(solution)/shard_map/ppermute | solution.py:418
  15.8 6.3 %collective-permute-start.8 = (bf16[128,512]{1,0:T(8,128)(2,1)S(1)}, bf16[128,512]{1,0:T(8,128)(2,1)S(1)}, u32[]{:S(2)}, u32[]{:S(2)}) collective-permute-start(bf16[128,512]{1,0:T(8,128)(2,1)S(1)} %copy-done.21), channel_id=1, source_target_pairs={{0,7},{1,6},{2,5},{3,4},{4,3},{5,2},{6,1},{7,0},{8,15},{9,14},{10,... | collective-permute-start | bytes 393224 | tf_op jit(solution)/shard_map/ppermute | solution.py:418
  15.8 6.3 %copy-start.4 = (s32[2]{0:T(128)S(1)}, s32[2]{0:T(128)}, u32[]{:S(2)}) copy-start(s32[2]{0:T(128)} %pad_add_fusion.place_ref) | copy-start | bytes 28
  15.8 6.2 %collective-permute-start.11 = (bf16[128,512]{1,0:T(8,128)(2,1)S(1)}, bf16[128,512]{1,0:T(8,128)(2,1)S(1)}, u32[]{:S(2)}, u32[]{:S(2)}) collective-permute-start(bf16[128,512]{1,0:T(8,128)(2,1)S(1)} %copy-done.20), channel_id=1, source_target_pairs={{0,1},{1,0},{2,3},{3,2},{4,5},{5,4},{6,7},{7,6},{8,9},{9,8},{10,11... | collective-permute-start | bytes 393224 | tf_op jit(solution)/shard_map/ppermute | solution.py:418
  22.1 5.2 %copy-start.12 = (bf16[128,512]{1,0:T(8,128)(2,1)S(1)}, bf16[128,512]{1,0:T(8,128)(2,1)}, u32[]{:S(2)}) copy-start(bf16[128,512]{1,0:T(8,128)(2,1)} %get-tuple-element.141) | copy-start | bytes 393220
  22.1 8.6 %copy-start.13 = (bf16[128,512]{1,0:T(8,128)(2,1)S(1)}, bf16[128,512]{1,0:T(8,128)(2,1)}, u32[]{:S(2)}) copy-start(bf16[128,512]{1,0:T(8,128)(2,1)} %get-tuple-element.163) | copy-start | bytes 393220
  22.1 9.5 %copy-start.11 = (bf16[128,512]{1,0:T(8,128)(2,1)S(1)}, bf16[128,512]{1,0:T(8,128)(2,1)}, u32[]{:S(2)}) copy-start(bf16[128,512]{1,0:T(8,128)(2,1)} %get-tuple-element.153) | copy-start | bytes 393220
  22.1 13.2 %copy-start.10 = (bf16[128,512]{1,0:T(8,128)(2,1)S(1)}, bf16[128,512]{1,0:T(8,128)(2,1)}, u32[]{:S(2)}) copy-start(bf16[128,512]{1,0:T(8,128)(2,1)} %get-tuple-element.132) | copy-start | bytes 393220
  23.0 12.3 %copy-start.7 = (bf16[1024,256]{1,0:T(8,128)(2,1)}, bf16[1024,256]{1,0:T(8,128)(2,1)S(1)}, u32[]{:S(2)}) copy-start(bf16[1024,256]{1,0:T(8,128)(2,1)S(1)} %get-tuple-element.165.refs_9_) | copy-start | bytes 1572868
  23.0 15.9 %copy-start.6 = (bf16[1024,256]{1,0:T(8,128)(2,1)}, bf16[1024,256]{1,0:T(8,128)(2,1)S(1)}, u32[]{:S(2)}) copy-start(bf16[1024,256]{1,0:T(8,128)(2,1)S(1)} %get-tuple-element.168.refs_2_) | copy-start | bytes 1572868
  23.0 17.6 %collective-permute-start.14 = (bf16[1024,256]{1,0:T(8,128)(2,1)S(1)}, bf16[1024,256]{1,0:T(8,128)(2,1)S(1)}, u32[]{:S(2)}, u32[]{:S(2)}) collective-permute-start(bf16[1024,256]{1,0:T(8,128)(2,1)S(1)} %get-tuple-element.165.refs_9_), channel_id=1, source_target_pairs={{0,8},{4,12},{8,16},{12,20},{16,24},{20,28},{24,0},{28,4},{1,9},{5... | collective-permute-start | bytes 1572872 | tf_op jit(solution)/shard_map/ppermute | solution.py:423
  24.6 6.1 %collective-permute-start.4 = (bf16[128,512]{1,0:T(8,128)(2,1)S(1)}, bf16[128,512]{1,0:T(8,128)(2,1)S(1)}, u32[]{:S(2)}, u32[]{:S(2)}) collective-permute-start(bf16[128,512]{1,0:T(8,128)(2,1)S(1)} %copy-done.16), channel_id=1, source_target_pairs={{0,2},{1,3},{2,0},{3,1},{4,6},{5,7},{6,4},{7,5},{8,10},{9,11},{10,... | collective-permute-start | bytes 393224 | tf_op jit(solution)/shard_map/ppermute | solution.py:418
  25.6 6.0 %collective-permute-start.1 = (bf16[128,512]{1,0:T(8,128)(2,1)S(1)}, bf16[128,512]{1,0:T(8,128)(2,1)S(1)}, u32[]{:S(2)}, u32[]{:S(2)}) collective-permute-start(bf16[128,512]{1,0:T(8,128)(2,1)S(1)} %copy-done.15), channel_id=1, source_target_pairs={{0,3},{1,2},{2,1},{3,0},{4,7},{5,6},{6,5},{7,4},{8,11},{9,10},{10,... | collective-permute-start | bytes 393224 | tf_op jit(solution)/shard_map/ppermute | solution.py:418
  25.6 9.1 %collective-permute-start.9 = (bf16[128,512]{1,0:T(8,128)(2,1)S(1)}, bf16[128,512]{1,0:T(8,128)(2,1)S(1)}, u32[]{:S(2)}, u32[]{:S(2)}) collective-permute-start(bf16[128,512]{1,0:T(8,128)(2,1)S(1)} %copy-done.14), channel_id=1, source_target_pairs={{0,5},{1,4},{2,7},{3,6},{4,1},{5,0},{6,3},{7,2},{8,13},{9,12},{10,... | collective-permute-start | bytes 393224 | tf_op jit(solution)/shard_map/ppermute | solution.py:418
  27.3 13.3 %collective-permute-start.6 = (bf16[128,512]{1,0:T(8,128)(2,1)S(1)}, bf16[128,512]{1,0:T(8,128)(2,1)}, u32[]{:S(2)}, u32[]{:S(2)}) collective-permute-start(bf16[128,512]{1,0:T(8,128)(2,1)S(1)} %copy-done.12), channel_id=1, source_target_pairs={{0,4},{1,5},{2,6},{3,7},{4,0},{5,1},{6,2},{7,3},{8,12},{9,13},{10,... | collective-permute-start | bytes 393224 | tf_op jit(solution)/shard_map/ppermute | solution.py:418
  30.7 4.0 %copy-start.17 = (bf16[128,512]{1,0:T(8,128)(2,1)}, bf16[128,512]{1,0:T(8,128)(2,1)S(1)}, u32[]{:S(2)}) copy-start(bf16[128,512]{1,0:T(8,128)(2,1)S(1)} %collective-permute-done.4.refs_2_) | copy-start | bytes 393220
  30.7 8.2 %collective-permute-start.13 = (bf16[128,512]{1,0:T(8,128)(2,1)S(1)}, bf16[128,512]{1,0:T(8,128)(2,1)S(1)}, u32[]{:S(2)}, u32[]{:S(2)}) collective-permute-start(bf16[128,512]{1,0:T(8,128)(2,1)S(1)} %copy-done.13), channel_id=1, source_target_pairs={{0,7},{1,6},{2,5},{3,4},{4,3},{5,2},{6,1},{7,0},{8,15},{9,14},{10,... | collective-permute-start | bytes 393224 | tf_op jit(solution)/shard_map/ppermute | solution.py:418
  31.6 9.0 %collective-permute-start.12 = (bf16[128,512]{1,0:T(8,128)(2,1)S(1)}, bf16[128,512]{1,0:T(8,128)(2,1)S(1)}, u32[]{:S(2)}, u32[]{:S(2)}) collective-permute-start(bf16[128,512]{1,0:T(8,128)(2,1)S(1)} %copy-done.11), channel_id=1, source_target_pairs={{0,6},{1,7},{2,4},{3,5},{4,2},{5,3},{6,0},{7,1},{8,14},{9,15},{10,... | collective-permute-start | bytes 393224 | tf_op jit(solution)/shard_map/ppermute | solution.py:418
  35.3 5.3 %collective-permute-start.2 = (bf16[128,512]{1,0:T(8,128)(2,1)S(1)}, bf16[128,512]{1,0:T(8,128)(2,1)S(1)}, u32[]{:S(2)}, u32[]{:S(2)}) collective-permute-start(bf16[128,512]{1,0:T(8,128)(2,1)S(1)} %copy-done.10), channel_id=1, source_target_pairs={{0,1},{1,0},{2,3},{3,2},{4,5},{5,4},{6,7},{7,6},{8,9},{9,8},{10,11... | collective-permute-start | bytes 393224 | tf_op jit(solution)/shard_map/ppermute | solution.py:418
  35.3 21.9 %all-to-all-start.1 = ((bf16[8,128,512]{2,1,0:T(8,128)(2,1)}), bf16[8,128,512]{2,1,0:T(8,128)(2,1)S(1)}, u32[]{:S(2)}, u32[]{:S(2)}) async-start(bf16[8,128,512]{2,1,0:T(8,128)(2,1)} %get-tuple-element.167), calls=%async_computation.1 | async-start | bytes 2097152 | tf_op jit(solution)/shard_map/all_to_all | solution.py:405
  38.9 23.4 %collective-permute-start.15 = (bf16[1024,256]{1,0:T(8,128)(2,1)S(1)}, bf16[1024,256]{1,0:T(8,128)(2,1)}, u32[]{:S(2)}, u32[]{:S(2)}) collective-permute-start(bf16[1024,256]{1,0:T(8,128)(2,1)S(1)} %get-tuple-element.168.refs_2_), channel_id=1, source_target_pairs={{0,8},{4,12},{8,16},{12,20},{16,24},{20,28},{24,0},{28,4},{1,9},{5... | collective-permute-start | bytes 1572872 | tf_op jit(solution)/shard_map/ppermute | solution.py:423
  54.9 21.8 %collective-permute-start.16 = (bf16[1024,256]{1,0:T(8,128)(2,1)}, bf16[1024,256]{1,0:T(8,128)(2,1)S(1)}, u32[]{:S(2)}, u32[]{:S(2)}) collective-permute-start(bf16[1024,256]{1,0:T(8,128)(2,1)} %get-tuple-element.177), channel_id=1, source_target_pairs={{8,0},{12,4},{16,8},{20,12},{24,16},{28,20},{0,24},{4,28},{9,1},{1... | collective-permute-start | bytes 1572872 | tf_op jit(solution)/shard_map/ppermute | solution.py:426
  58.1 46.2 %all-to-all-start = ((bf16[8,128,512]{2,1,0:T(8,128)(2,1)}), bf16[8,128,512]{2,1,0:T(8,128)(2,1)S(1)}, u32[]{:S(2)}, u32[]{:S(2)}) async-start(bf16[8,128,512]{2,1,0:T(8,128)(2,1)} %bitcast.4), calls=%async_computation | async-start | bytes 2097152 | tf_op jit(solution)/shard_map/all_to_all | solution.py:405
  62.4 28.2 %copy-start = (f32[2,128,1024]{2,1,0:T(8,128)S(1)}, f32[2,128,1024]{2,1,0:T(8,128)}, u32[]{:S(2)}) copy-start(f32[2,128,1024]{2,1,0:T(8,128)} %get-tuple-element.192.own0_ref) | copy-start | bytes 3145732
  76.0 14.6 %collective-permute-start.24 = (bf16[1024,256]{1,0:T(8,128)(2,1)}, bf16[1024,256]{1,0:T(8,128)(2,1)S(1)}, u32[]{:S(2)}, u32[]{:S(2)}) collective-permute-start(bf16[1024,256]{1,0:T(8,128)(2,1)} %get-tuple-element.195), channel_id=1, source_target_pairs={{8,0},{12,4},{16,8},{20,12},{24,16},{28,20},{0,24},{4,28},{9,1},{1... | collective-permute-start | bytes 1572872 | tf_op jit(solution)/shard_map/ppermute | solution.py:426
  76.7 5.8 %collective-permute-start.17 = (bf16[128,512]{1,0:T(8,128)(2,1)}, bf16[128,512]{1,0:T(8,128)(2,1)S(1)}, u32[]{:S(2)}, u32[]{:S(2)}) collective-permute-start(bf16[128,512]{1,0:T(8,128)(2,1)} %get-tuple-element.180), channel_id=1, source_target_pairs={{0,4},{1,5},{2,6},{3,7},{4,0},{5,1},{6,2},{7,3},{8,12},{9,13},{10,... | collective-permute-start | bytes 393224 | tf_op jit(solution)/shard_map/ppermute | solution.py:418
  78.6 5.7 %collective-permute-start.19 = (bf16[128,512]{1,0:T(8,128)(2,1)}, bf16[128,512]{1,0:T(8,128)(2,1)S(1)}, u32[]{:S(2)}, u32[]{:S(2)}) collective-permute-start(bf16[128,512]{1,0:T(8,128)(2,1)} %get-tuple-element.183), channel_id=1, source_target_pairs={{0,2},{1,3},{2,0},{3,1},{4,6},{5,7},{6,4},{7,5},{8,10},{9,11},{10,... | collective-permute-start | bytes 393224 | tf_op jit(solution)/shard_map/ppermute | solution.py:418
  80.1 6.6 %collective-permute-start.20 = (bf16[128,512]{1,0:T(8,128)(2,1)}, bf16[128,512]{1,0:T(8,128)(2,1)S(1)}, u32[]{:S(2)}, u32[]{:S(2)}) collective-permute-start(bf16[128,512]{1,0:T(8,128)(2,1)} %get-tuple-element.186), channel_id=1, source_target_pairs={{0,3},{1,2},{2,1},{3,0},{4,7},{5,6},{6,5},{7,4},{8,11},{9,10},{10,... | collective-permute-start | bytes 393224 | tf_op jit(solution)/shard_map/ppermute | solution.py:418
  80.1 14.0 %collective-permute-start.21 = (bf16[128,512]{1,0:T(8,128)(2,1)}, bf16[128,512]{1,0:T(8,128)(2,1)S(1)}, u32[]{:S(2)}, u32[]{:S(2)}) collective-permute-start(bf16[128,512]{1,0:T(8,128)(2,1)} %get-tuple-element.189), channel_id=1, source_target_pairs={{0,5},{1,4},{2,7},{3,6},{4,1},{5,0},{6,3},{7,2},{8,13},{9,12},{10,... | collective-permute-start | bytes 393224 | tf_op jit(solution)/shard_map/ppermute | solution.py:418
  82.4 11.7 %collective-permute-start.18 = (bf16[128,512]{1,0:T(8,128)(2,1)}, bf16[128,512]{1,0:T(8,128)(2,1)S(1)}, u32[]{:S(2)}, u32[]{:S(2)}) collective-permute-start(bf16[128,512]{1,0:T(8,128)(2,1)} %get-tuple-element.181), channel_id=1, source_target_pairs={{0,1},{1,0},{2,3},{3,2},{4,5},{5,4},{6,7},{7,6},{8,9},{9,8},{10,11... | collective-permute-start | bytes 393224 | tf_op jit(solution)/shard_map/ppermute | solution.py:418
  84.4 9.8 %collective-permute-start.22 = (bf16[128,512]{1,0:T(8,128)(2,1)}, bf16[128,512]{1,0:T(8,128)(2,1)S(1)}, u32[]{:S(2)}, u32[]{:S(2)}) collective-permute-start(bf16[128,512]{1,0:T(8,128)(2,1)} %get-tuple-element.190), channel_id=1, source_target_pairs={{0,6},{1,7},{2,4},{3,5},{4,2},{5,3},{6,0},{7,1},{8,14},{9,15},{10,... | collective-permute-start | bytes 393224 | tf_op jit(solution)/shard_map/ppermute | solution.py:418
  86.7 7.4 %collective-permute-start.23 = (bf16[128,512]{1,0:T(8,128)(2,1)}, bf16[128,512]{1,0:T(8,128)(2,1)S(1)}, u32[]{:S(2)}, u32[]{:S(2)}) collective-permute-start(bf16[128,512]{1,0:T(8,128)(2,1)} %get-tuple-element.191), channel_id=1, source_target_pairs={{0,7},{1,6},{2,5},{3,4},{4,3},{5,2},{6,1},{7,0},{8,15},{9,14},{10,... | collective-permute-start | bytes 393224 | tf_op jit(solution)/shard_map/ppermute | solution.py:418
  92.4 12.0 %copy-start.2 = (bf16[128,512]{1,0:T(8,128)(2,1)S(1)}, bf16[128,512]{1,0:T(8,128)(2,1)}, u32[]{:S(2)}) copy-start(bf16[128,512]{1,0:T(8,128)(2,1)} %get-tuple-element.204.refs_0_) | copy-start | bytes 393220
  94.2 5.2 %collective-permute-start.25 = (bf16[128,512]{1,0:T(8,128)(2,1)S(1)}, bf16[128,512]{1,0:T(8,128)(2,1)S(1)}, u32[]{:S(2)}, u32[]{:S(2)}) collective-permute-start(bf16[128,512]{1,0:T(8,128)(2,1)S(1)} %get-tuple-element.216), channel_id=1, source_target_pairs={{0,4},{1,5},{2,6},{3,7},{4,0},{5,1},{6,2},{7,3},{8,12},{9,13},{10,... | collective-permute-start | bytes 393224 | tf_op jit(solution)/shard_map/ppermute | solution.py:418
  95.9 5.5 %collective-permute-start.27 = (bf16[128,512]{1,0:T(8,128)(2,1)S(1)}, bf16[128,512]{1,0:T(8,128)(2,1)S(1)}, u32[]{:S(2)}, u32[]{:S(2)}) collective-permute-start(bf16[128,512]{1,0:T(8,128)(2,1)S(1)} %get-tuple-element.219), channel_id=1, source_target_pairs={{0,2},{1,3},{2,0},{3,1},{4,6},{5,7},{6,4},{7,5},{8,10},{9,11},{10,... | collective-permute-start | bytes 393224 | tf_op jit(solution)/shard_map/ppermute | solution.py:418
  97.4 6.2 %collective-permute-start.28 = (bf16[128,512]{1,0:T(8,128)(2,1)S(1)}, bf16[128,512]{1,0:T(8,128)(2,1)S(1)}, u32[]{:S(2)}, u32[]{:S(2)}) collective-permute-start(bf16[128,512]{1,0:T(8,128)(2,1)S(1)} %get-tuple-element.222), channel_id=1, source_target_pairs={{0,3},{1,2},{2,1},{3,0},{4,7},{5,6},{6,5},{7,4},{8,11},{9,10},{10,... | collective-permute-start | bytes 393224 | tf_op jit(solution)/shard_map/ppermute | solution.py:418
  97.4 9.1 %collective-permute-start.29 = (bf16[128,512]{1,0:T(8,128)(2,1)}, bf16[128,512]{1,0:T(8,128)(2,1)S(1)}, u32[]{:S(2)}, u32[]{:S(2)}) collective-permute-start(bf16[128,512]{1,0:T(8,128)(2,1)} %get-tuple-element.225), channel_id=1, source_target_pairs={{0,5},{1,4},{2,7},{3,6},{4,1},{5,0},{6,3},{7,2},{8,13},{9,12},{10,... | collective-permute-start | bytes 393224 | tf_op jit(solution)/shard_map/ppermute | solution.py:418
  99.3 7.1 %collective-permute-start.26 = (bf16[128,512]{1,0:T(8,128)(2,1)S(1)}, bf16[128,512]{1,0:T(8,128)(2,1)S(1)}, u32[]{:S(2)}, u32[]{:S(2)}) collective-permute-start(bf16[128,512]{1,0:T(8,128)(2,1)S(1)} %get-tuple-element.217), channel_id=1, source_target_pairs={{0,1},{1,0},{2,3},{3,2},{4,5},{5,4},{6,7},{7,6},{8,9},{9,8},{10,11... | collective-permute-start | bytes 393224 | tf_op jit(solution)/shard_map/ppermute | solution.py:418
  101.4 5.9 %collective-permute-start.30 = (bf16[128,512]{1,0:T(8,128)(2,1)S(1)}, bf16[128,512]{1,0:T(8,128)(2,1)S(1)}, u32[]{:S(2)}, u32[]{:S(2)}) collective-permute-start(bf16[128,512]{1,0:T(8,128)(2,1)S(1)} %get-tuple-element.226), channel_id=1, source_target_pairs={{0,6},{1,7},{2,4},{3,5},{4,2},{5,3},{6,0},{7,1},{8,14},{9,15},{10,... | collective-permute-start | bytes 393224 | tf_op jit(solution)/shard_map/ppermute | solution.py:418
  103.5 6.4 %collective-permute-start.31 = (bf16[128,512]{1,0:T(8,128)(2,1)S(1)}, bf16[128,512]{1,0:T(8,128)(2,1)S(1)}, u32[]{:S(2)}, u32[]{:S(2)}) collective-permute-start(bf16[128,512]{1,0:T(8,128)(2,1)S(1)} %get-tuple-element.227), channel_id=1, source_target_pairs={{0,7},{1,6},{2,5},{3,4},{4,3},{5,2},{6,1},{7,0},{8,15},{9,14},{10,... | collective-permute-start | bytes 393224 | tf_op jit(solution)/shard_map/ppermute | solution.py:418
  (12 other events, 20.0 us)

commit v5 on v4

--- a/solution.py
+++ b/solution.py
@@ -33,16 +33,26 @@
     return lax.dot_general(left, right, dims, preferred_element_type=jnp.float32)
 
 
+class Place:
+    def __init__(self, apart):
+        split = lax.axis_size("kvh")
+        self.shard = lax.axis_index("seq")
+        self.first = self.shard < apart
+        self.member = lax.rem(self.shard, apart) * split + lax.axis_index("kvh")
+
+
 def side_by_side(x):
     return jnp.concatenate([x[:, :HEAD_DIM].T, x[:, HEAD_DIM:].T], 1)
 
 
 def attention_kernel(
-    taken, pieces, place_ref, *refs
+    apart, taken, pieces, joins, *refs
 ):
+    place = Place(apart)
     qo_hbm, (halo_hbm, own_hbm, *refs) = refs[:taken], refs[taken:]
+    (mine_hbm, back_hbm), refs = refs[:2] if joins else (None, None), refs[2 * joins :]
     ao_hbm, (dhalo_hbm, down_hbm, *refs) = refs[:pieces], refs[pieces:]
-    (kv, qo, ao, dhalo, keys_t, values_t, acc_k, acc_v, exps0, exps1, q_turned, o_turned, in_sem, q_sem, out_sem) = refs
+    (kv, qo, ao, dhalo, keys_t, values_t, acc_k, acc_v, exps0, exps1, q_turned, o_turned, mine, back, in_sem, q_sem, out_sem) = refs
     rows = qo.shape[0]
     blocks = rows // BLOCK
     whole = WINDOW // BLOCK
@@ -62,7 +72,7 @@
         return pltpu.make_async_copy(ao.at[at(i)], ao_hbm[0].at[at(i)], out_sem.at[0, i])
 
     def piece_copy(j):
-        return pltpu.make_async_copy(ao.at[at(place_ref[1] ^ j)], ao_hbm[j], out_sem.at[0, j])
+        return pltpu.make_async_copy(ao.at[at(place.member ^ j)], ao_hbm[j], out_sem.at[0, j])
 
     def dhalo_copy(i):
         return pltpu.make_async_copy(dhalo.at[at(i)], dhalo_hbm.at[at(i)], out_sem.at[1, i])
@@ -71,8 +81,15 @@
     own_copy = pltpu.make_async_copy(own_hbm, kv.at[pl.ds(WINDOW, rows)], in_sem.at[1])
     halo_copy.start()
     own_copy.start()
+    if joins:
+        mine_copy = pltpu.make_async_copy(mine_hbm, mine, in_sem.at[2])
+        back_copy = pltpu.make_async_copy(back_hbm, back, in_sem.at[3])
     for i in range(blocks):
-        (qo_copy(i) if taken == 1 else qo_copy(place_ref[1] ^ i, i)).start()
+        (qo_copy(i) if taken == 1 else qo_copy(place.member ^ i, i)).start()
+
+    if joins:
+        mine_copy.start()
+        back_copy.start()
 
     ones_row = lax.broadcasted_iota(jnp.int32, (ONES, values_t.shape[1]), 0) == 0
     values_t[HEAD_DIM:, :] = jnp.where(ones_row, 1.0, 0.0).astype(jnp.bfloat16)
@@ -83,7 +100,7 @@
     o_turned[...] = jnp.zeros_like(o_turned)
     key_at = lax.broadcasted_iota(jnp.int32, (BLOCK, 2 * BLOCK), 0)
     query_at = lax.broadcasted_iota(jnp.int32, (BLOCK, 2 * BLOCK), 1) & (BLOCK - 1)
-    first = place_ref[0]
+    first = place.first
 
     def turn(target, source):
         keys_t[:, at(target)] = kv[at(source), :HEAD_DIM].T
@@ -91,6 +108,9 @@
 
     halo_copy.wait()
     own_copy.wait()
+    if joins:
+        mine_copy.wait()
+        back_copy.wait()
     for c in range(whole + 1):
         turn(c, c)
 
@@ -99,7 +119,7 @@
         q_turned[slot] = q_t
         o_turned[slot] = o_t
         bias = [
-            jnp.where((first > 0) & (i + c < whole), EXCLUDED, 0.0).astype(jnp.float32) for c in range(CHUNKS - 1)
+            jnp.where(first & (i + c < whole), EXCLUDED, 0.0).astype(jnp.float32) for c in range(CHUNKS - 1)
         ]
         scores = dot(kv[span(i), :HEAD_DIM], q_t, NN)
         parts = [scores[c * BLOCK : (c + 1) * BLOCK] for c in range(CHUNKS)]
@@ -140,12 +160,18 @@
         acc_v[:, span(i)] += dot(o_scaled, exps[slot][...], NT)
         grad_q = (dot(keys_t[:, span(i)], grad_scores, NN) * (inverse * SCORE_SCALE)).astype(jnp.bfloat16)
         ao[at(i), PAIR : PAIR + HEAD_DIM] = grad_q[:, :BLOCK].T
-        ao[at(i), PAIR + HEAD_DIM :] = grad_q[:, BLOCK:].T
+        ao[at(i), PAIR + HEAD_DIM : 2 * PAIR] = grad_q[:, BLOCK:].T
         acc_k[:, span(i)] += dot(q_scaled, grad_scores, NT)
 
     def flush(i):
         dhalo[at(i), :HEAD_DIM] = (acc_k[:, at(i)] * SCORE_SCALE).astype(jnp.bfloat16).T
         dhalo[at(i), HEAD_DIM:] = acc_v[:, at(i)].astype(jnp.bfloat16).T
+
+    def join(i):
+        for n, scale in enumerate((SCORE_SCALE, 1.0)):
+            cols = slice(n * HEAD_DIM, (n + 1) * HEAD_DIM)
+            total = (mine[n, :, at(i)] * scale).T + back[at(i), cols].astype(jnp.float32)
+            ao[at(i), 2 * PAIR + n * HEAD_DIM : 2 * PAIR + (n + 1) * HEAD_DIM] = total.astype(jnp.bfloat16)
 
     def both(slot, i, before):
         known = attended_of(1 - slot, before)
@@ -153,6 +179,8 @@
         exponentials(slot, parts, shifts)
         gradients(1 - slot, before, *known)
         flush(before)
+        if joins:
+            join(i)
         turn(i + whole + 1, jnp.minimum(i + whole + 1, whole + blocks - 1))
         acc_k[:, at(i + whole + 1)] = jnp.zeros((HEAD_DIM, BLOCK), jnp.float32)
         acc_v[:, at(i + whole + 1)] = jnp.zeros((HEAD_DIM, BLOCK), jnp.float32)
@@ -195,24 +223,26 @@
     own_v.wait()
 
 
-def attention(place, qo, halo, own, pieces):
+def attention(apart, qo, halo, own, pieces, joined=()):
     rows = own.shape[0]
     blocks = rows // BLOCK
     reach = WINDOW + rows
     bf16, f32 = jnp.bfloat16, jnp.float32
-    return pl.pallas_call(
-        functools.partial(attention_kernel, len(qo), pieces),
+    width = 2 * PAIR + (PAIR if joined else 0)
+    small = (8, HEAD_DIM)
+    return pl.pallas_call(
+        functools.partial(attention_kernel, apart, len(qo), pieces, len(joined) > 0),
         out_shape=(
-            *[jax.ShapeDtypeStruct((rows // pieces, 2 * PAIR), bf16)] * pieces,
+            *[jax.ShapeDtypeStruct((rows // pieces, width), bf16)] * pieces,
             jax.ShapeDtypeStruct(halo.shape, bf16),
             jax.ShapeDtypeStruct((2, HEAD_DIM, rows), f32),
         ),
-        in_specs=[SMEM] + [ANY] * (len(qo) + 2),
+        in_specs=[ANY] * (len(qo) + 2 + len(joined)),
         out_specs=(HBM,) * (pieces + 2),
         scratch_shapes=[
             pltpu.VMEM((reach, PAIR), bf16),
             pltpu.VMEM((rows, 2 * PAIR), bf16),
-            pltpu.VMEM((rows, 2 * PAIR), bf16),
+            pltpu.VMEM((rows, width), bf16),
             pltpu.VMEM(halo.shape, bf16),
             pltpu.VMEM((HEAD_DIM, reach + BLOCK), bf16),
             pltpu.VMEM((HEAD_DIM + ONES, reach + BLOCK), bf16),
@@ -222,17 +252,20 @@
             pltpu.VMEM((CHUNKS * BLOCK, 2 * BLOCK), bf16),
             pltpu.VMEM((2, HEAD_DIM, 2 * BLOCK), bf16),
             pltpu.VMEM((2, HEAD_DIM, 2 * BLOCK), bf16),
-            pltpu.SemaphoreType.DMA((2,)),
+            pltpu.VMEM((2, HEAD_DIM, rows) if joined else small, f32),
+            pltpu.VMEM((rows, PAIR) if joined else small, bf16),
+            pltpu.SemaphoreType.DMA((4,)),
             pltpu.SemaphoreType.DMA((blocks,)),
             pltpu.SemaphoreType.DMA((2, blocks)),
         ],
         compiler_params=pltpu.CompilerParams(vmem_limit_bytes=58 * 2**20),
         cost_estimate=pl.CostEstimate(flops=10**10, bytes_accessed=4 * 2**20, transcendentals=0),
         name="attention",
-    )(place, *qo, halo, own)
-
-
-def interleave_kernel(width, sets, place_ref, *refs):
+    )(*qo, halo, own, *joined)
+
+
+def interleave_kernel(apart, width, sets, *refs):
+    place = Place(apart)
     arrays, refs = refs[:2], refs[2:]
     groups = arrays[0].shape[1] // sets[0][1][0][2]
     outs, refs = refs[: -(4 + len(sets))], refs[-(4 + len(sets)) :]
@@ -246,7 +279,7 @@
     taken = 0
     for k, (split, parts) in enumerate(sets):
         for g in range(groups):
-            source = place_ref[1] ^ g if split else g
+            source = place.member ^ g if split else g
             for n, (which, start, stride) in enumerate(parts):
                 at = source * stride + start
                 if split:
@@ -260,7 +293,7 @@
         store.wait()
 
 
-def interleave(place, arrays, groups, width, sets):
+def interleave(apart, arrays, groups, width, sets):
     rows, cols = arrays[0].shape
     dtype = arrays[0].dtype
     shapes, staged = [], []
@@ -269,9 +302,9 @@
         staged.append(pltpu.VMEM(whole, dtype))
         shapes += [jax.ShapeDtypeStruct(whole[1:], dtype)] * groups if split else [jax.ShapeDtypeStruct(whole, dtype)]
     return pl.pallas_call(
-        functools.partial(interleave_kernel, width, sets),
+        functools.partial(interleave_kernel, apart, width, sets),
         out_shape=tuple(shapes),
-        in_specs=[SMEM, HBM, HBM],
+        in_specs=[HBM, HBM],
         out_specs=(HBM,) * len(shapes),
         scratch_shapes=[
             pltpu.VMEM((rows, cols), dtype),
@@ -282,17 +315,18 @@
         ],
         compiler_params=pltpu.CompilerParams(vmem_limit_bytes=58 * 2**20),
         name="interleave",
-    )(place, *arrays)
-
-
-def assemble_kernel(place_ref, *refs):
+    )(*arrays)
+
+
+def assemble_kernel(apart, *refs):
+    place = Place(apart)
     *arrays, sem = refs
     count, heads = sem.shape
     pieces, outs = arrays[:count], arrays[count:]
     rows, width = pieces[0].shape[0], outs[0].shape[1]
     copies = []
     for j in range(count):
-        at = pl.ds(pl.multiple_of((place_ref[1] ^ j) * rows, BLOCK), rows)
+        at = pl.ds(pl.multiple_of((place.member ^ j) * rows, BLOCK), rows)
         for h in range(heads):
             source = pieces[j].at[:, pl.ds(h * width, width)]
             copies.append(pltpu.make_async_copy(source, outs[h].at[at], sem.at[j, h]))
@@ -302,93 +336,119 @@
         copy.wait()
 
 
-def assemble(place, pieces, heads):
+def assemble(apart, pieces, heads):
     rows, width = pieces[0].shape
     shape = jax.ShapeDtypeStruct((len(pieces) * rows, width // heads), pieces[0].dtype)
     return pl.pallas_call(
-        assemble_kernel,
+        functools.partial(assemble_kernel, apart),
         out_shape=(shape,) * heads,
-        in_specs=[SMEM] + [ANY] * len(pieces),
+        in_specs=[ANY] * len(pieces),
         out_specs=(VMEM,) * heads,
         scratch_shapes=[pltpu.SemaphoreType.DMA((len(pieces), heads))],
         compiler_params=pltpu.CompilerParams(vmem_limit_bytes=8 * 2**20),
         name="assemble",
-    )(place, *pieces)
-
-
-def group_at(place_ref, j, width):
-    return pl.multiple_of((place_ref[1] ^ j) * width, HEAD_DIM)
-
-
-def spread_kernel(place_ref, x_ref, *refs):
+    )(*pieces)
+
+
+def group_at(place, j, width):
+    return pl.multiple_of((place.member ^ j) * width, HEAD_DIM)
+
+
+def spread_kernel(apart, x_ref, *refs):
+    place = Place(apart)
     *pieces, a_ref, b_ref = refs
     groups, _, width = x_ref.shape
     half = width // 2
     for g in range(groups):
         a_ref[:, g * width : g * width + half] = x_ref[g, :, :half]
         b_ref[:, g * width : g * width + half] = x_ref[g, :, half:]
-        cols = pl.ds(group_at(place_ref, g, width) + half, half)
+        cols = pl.ds(group_at(place, g, width) + half, half)
         a_ref[:, cols] = pieces[g][:, :half]
         b_ref[:, cols] = pieces[g][:, half:]
 
 
-def spread(place, x, pieces):
+def spread(apart, x, pieces):
     groups, rows, width = x.shape
     shape = jax.ShapeDtypeStruct((rows, groups * width), x.dtype)
     return pl.pallas_call(
-        spread_kernel,
+        functools.partial(spread_kernel, apart),
         out_shape=(shape, shape),
-        in_specs=[SMEM] + [VMEM] * (groups + 1),
+        in_specs=[VMEM] * (groups + 1),
         out_specs=(VMEM, VMEM),
         compiler_params=pltpu.CompilerParams(vmem_limit_bytes=16 * 2**20),
         name="spread",
-    )(place, x, *pieces)
-
-
-def add_kernel(place_ref, own0_ref, own1_ref, back0_ref, back1_ref, *out_refs):
+    )(x, *pieces)
+
+
+def settle_kernel(own0, own1, back0, done_ref, open_ref):
+    for n, scale in enumerate((SCORE_SCALE, 1.0)):
+        cols = slice(n * HEAD_DIM, (n + 1) * HEAD_DIM)
+        for i in range(done_ref.shape[0] // BLOCK):
+            at = slice(i * BLOCK, (i + 1) * BLOCK)
+            total = (own0[n, :, at] * scale).T + back0[at, cols].astype(jnp.float32)
+            done_ref[at, cols] = total.astype(jnp.bfloat16)
+            open_ref[at, cols] = (own1[n, :, at] * scale).T
+
+
+def settle(own, back):
+    return pl.pallas_call(
+        settle_kernel,
+        out_shape=(
+            jax.ShapeDtypeStruct(back.shape, jnp.bfloat16),
+            jax.ShapeDtypeStruct(back.shape, jnp.float32),
+        ),
+        in_specs=[VMEM] * 3,
+        out_specs=(VMEM,) * 2,
+        compiler_params=pltpu.CompilerParams(vmem_limit_bytes=16 * 2**20),
+        name="settle",
+    )(*own, back)
+
+
+def add_kernel(apart, done_ref, open_ref, back_ref, *out_refs):
+    place = Place(apart)
     rows = out_refs[0].shape[0]
     for j, out_ref in enumerate(out_refs):
-        at = pl.ds(group_at(place_ref, j, rows), rows)
-        for h, (own, back) in enumerate(((own0_ref, back0_ref), (own1_ref, back1_ref))):
-            for n, scale in enumerate((SCORE_SCALE, 1.0)):
-                total = (own[n, :, at] * scale).T + back[at, n * HEAD_DIM : (n + 1) * HEAD_DIM].astype(jnp.float32)
-                cols = slice((2 * n + h) * HEAD_DIM, (2 * n + h + 1) * HEAD_DIM)
-                out_ref[:, cols] = total.astype(jnp.bfloat16)
-
-
-def add(place, own, back, groups):
-    rows, width = back[0].shape
+        at = pl.ds(group_at(place, j, rows), rows)
+        out_ref[:, :PAIR] = done_ref[at, :]
+        out_ref[:, PAIR:] = (open_ref[at, :] + back_ref[at, :].astype(jnp.float32)).astype(jnp.bfloat16)
+
+
+def add(apart, done, started, back, groups):
+    rows, width = back.shape
     shape = jax.ShapeDtypeStruct((rows // groups, 2 * width), jnp.bfloat16)
     return pl.pallas_call(
-        add_kernel,
+        functools.partial(add_kernel, apart),
         out_shape=(shape,) * groups,
-        in_specs=[SMEM] + [VMEM] * 4,
+        in_specs=[VMEM] * 3,
         out_specs=(VMEM,) * groups,
         compiler_params=pltpu.CompilerParams(vmem_limit_bytes=16 * 2**20),
         name="add",
-    )(place, *own, *back)
-
-
-def unpack_kernel(place_ref, *refs):
+    )(done, started, back)
+
+
+def unpack_kernel(apart, *refs):
+    place = Place(apart)
     *pieces, a_ref, b_ref = refs
-    half = pieces[0].shape[1] // 2
+    heads = pieces[0].shape[1] // PAIR
     for j, piece in enumerate(pieces):
-        cols = pl.ds(group_at(place_ref, j, half), half)
-        a_ref[:, cols] = piece[:, :half]
-        b_ref[:, cols] = piece[:, half:]
-
-
-def unpack(place, pieces):
+        start = group_at(place, j, heads * HEAD_DIM)
+        for h in range(heads):
+            cols = pl.ds(start + h * HEAD_DIM, HEAD_DIM)
+            a_ref[:, cols] = piece[:, h * PAIR : h * PAIR + HEAD_DIM]
+            b_ref[:, cols] = piece[:, h * PAIR + HEAD_DIM : (h + 1) * PAIR]
+
+
+def unpack(apart, pieces):
     rows, width = pieces[0].shape
     shape = jax.ShapeDtypeStruct((rows, len(pieces) * width // 2), pieces[0].dtype)
     return pl.pallas_call(
-        unpack_kernel,
+        functools.partial(unpack_kernel, apart),
         out_shape=(shape, shape),
-        in_specs=[SMEM] + [VMEM] * len(pieces),
+        in_specs=[VMEM] * len(pieces),
         out_specs=(VMEM, VMEM),
         compiler_params=pltpu.CompilerParams(vmem_limit_bytes=16 * 2**20),
         name="unpack",
-    )(place, *pieces)
+    )(*pieces)
 
 
 def body(queries, key_rows, value_rows, grad_out):
@@ -398,9 +458,6 @@
     members = apart * split
     heads = key_rows.shape[1] // (members * HEAD_DIM)
     groups = [[g * members + i for i in range(members)] for g in range(shards // apart)]
-    spot = lax.axis_index(("seq", "kvh"))
-    place = jnp.stack([lax.axis_index("seq") < apart, spot % members]).astype(jnp.int32)
-
     def exchange(x):
         return lax.all_to_all(x, ("seq", "kvh"), 0, 0, tiled=True, axis_index_groups=groups)
 
@@ -430,31 +487,31 @@
     def qo_parts(h):
         return [(n, h * PAIR, 2 * stride) for n in range(2)]
 
-    kv = list(interleave(place, (key_rows, value_rows), members, HEAD_DIM, [(True, kv_parts)]))
+    kv = list(interleave(apart, (key_rows, value_rows), members, HEAD_DIM, [(True, kv_parts)]))
     sets = [(h == 0, qo_parts(h)) for h in range(heads)]
-    packed = interleave(place, (queries, grad_out), members, PAIR, sets)
+    packed = interleave(apart, (queries, grad_out), members, PAIR, sets)
     late = order[EARLY]
     kv[late], (*first, second) = lax.optimization_barrier((kv[late], packed))
     kv = swap(kv, None, 5)
     first = swap(first, kv, 5)
-    own = assemble(place, kv, heads)
+    own = assemble(apart, kv, heads)
     second, first[order[HOLD]] = lax.optimization_barrier((second, first[order[HOLD]]))
     qos = [first, [exchange(second).reshape(WINDOW, -1)]]
     held, first[order[-2]] = lax.optimization_barrier((own[1], first[order[-2]]))
     halos = [onward(own[0]), onward(held)]
-    outs, down, back = [], [], []
+    outs, mine, back = [], [], []
     for h in range(heads):
         last = h == heads - 1
-        *ao, dhalo, mine = attention(place, qos[h], halos[h], own[h], members if last else 1)
-        if h > 0:
+        *ao, dhalo, down = attention(apart, qos[h], halos[h], own[h], members if last else 1)
+        if last:
             ao, back[h - 1] = lax.optimization_barrier((ao, back[h - 1]))
         back.append(backward(dhalo))
         outs.append(swap(ao) if last else exchange(ao[0].reshape(members, rows, -1)))
-        down.append(mine)
-    total = add(place, down, back, members)
-    outs[-1], total = lax.optimization_barrier((outs[-1], total))
-    grad_k, grad_v = unpack(place, swap(total))
-    attended, grad_q = spread(place, *outs)
+        mine.append(down)
+    total = add(apart, *settle(mine, back[0]), back[1], members)
+    outs[0], total = lax.optimization_barrier((outs[0], total))
+    grad_k, grad_v = unpack(apart, swap(total, outs[-1], 5))
+    attended, grad_q = spread(apart, *outs)
     return (attended, grad_q, grad_k, grad_v)
 
 

time: 112 us -> 106 us (0.946)
  Pallas kernels: 39.5 us -> 34.3 us
  waiting for transfers between devices: 21.8 us -> 24 us
  local copies, waits for them, and re-layouts: 4.98 us -> 3.28 us
    pallas_call x8 -> x9, Pallas kernels: 39.5 us -> 34.3 us  [the longest x2 25.1 us: attention(): pl.pallas_call(functools.partial(attention_kernel, apart, len(qo), pieces...]
    ppermute x28, waiting for transfers between devices: 19.1 us -> 22.3 us  [swap(): out[j] = lax.ppermute(piece, ('seq', 'kvh'), [(i, i ^ j) for i in every])]
    unnamed x52 -> x48, local copies, waits for them, and re-layouts: 4.98 us -> 3.28 us
    ppermute x28, starting transfers between devices: 29.8 us -> 28.2 us  [swap(): out[j] = lax.ppermute(piece, ('seq', 'kvh'), [(i, i ^ j) for i in every])]
    ppermute x2, starting transfers between devices: 2.94 us -> 4.19 us  [backward(): lax.ppermute(x, 'seq', [((i + apart) % shards, i) for i in range(shards)])]
  transfers between devices with their start and end apart: 34 -> 34, of which waited for: 10 -> 12; matrix products, arithmetic and copies ran while one was open for 0% -> 0% of each run, Pallas kernels for 31% -> 29%
where the time goes in v5:
time: 106 us; the launch traced here: 105 us
  starting transfers between devices  42.8 us (40%)
  Pallas kernels  34.3 us (32%)
  waiting for transfers between devices  24 us (23%)
  local copies, waits for them, and re-layouts  3.28 us (3%)
    ppermute x28, starting transfers between devices, swap(): out[j] = lax.ppermute(piece, ('seq', 'kvh'), [(i, i ^ j) for i in every])  28.2 us
    pallas_call x2, Pallas kernels, attention(): pl.pallas_call(functools.partial(attention_kernel, apart, len(qo), pieces...  25.1 us
    ppermute x28, waiting for transfers between devices, swap(): out[j] = lax.ppermute(piece, ('seq', 'kvh'), [(i, i ^ j) for i in every])  22.3 us
    all_to_all x2, starting transfers between devices, exchange(): lax.all_to_all(x, ('seq', 'kvh'), 0, 0, tiled=True, axis_index_groups=gro...  7.13 us
    pallas_call x2, Pallas kernels, interleave(): pl.pallas_call(functools.partial(interleave_kernel, apart, width, sets),...  5.41 us
    ppermute x2, starting transfers between devices, backward(): lax.ppermute(x, 'seq', [((i + apart) % shards, i) for i in range(shards)])  4.19 us
    unnamed x48, local copies, waits for them, and re-layouts  3.28 us
    ppermute x2, starting transfers between devices, onward(): lax.ppermute(x, 'seq', [(i, (i + apart) % shards) for i in range(shards)])  3.26 us
  transfers between devices with their start and end apart: 34, of which 12 were waited for; matrix products, arithmetic and copies ran while one was open for 0% of the time, Pallas kernels for 29%

profile of v5, /device:TPU:0, one launch (start us, length us, event | category | flops | bytes accessed | tf_op | source)
XLA Modules:
  0.0 105.4 jit_solution(3528889636232029753)
XLA Ops:
  0.6 2.3 %interleave.2 = (bf16[128,512]{1,0:T(8,128)(2,1)}, bf16[128,512]{1,0:T(8,128)(2,1)}, bf16[128,512]{1,0:T(8,128)(2,1)}, bf16[128,512]{1,0:T(8,128)(2,1)}, bf16[12...) custom-call(bf16[128,2048]{1,0:T(8,128)(2,1)} %refs_0_.2, ...), custom_call_target="tpu_custom_call" | custom-call | tf_op jit(solution)/shard_map/interleave/pallas_call | solution.py:304
  2.9 3.0 %collective-permute-start.7 = (bf16[128,512]{1,0:T(8,128)(2,1)}, bf16[128,512]{1,0:T(8,128)(2,1)S(1)}, u32[]{:S(2)}, u32[]{:S(2)}) collective-permute-start(bf16[128,512]{1,0:T(8,128)(2,1)} %get-tuple-element.148), channel_id=1, source_target_pairs={{0,2},{1,3},{2,0},{3,1},{4,6},{5,7},{6,4},{7,5},{8,10},{9,11},{10,... | collective-permute-start | bytes 393224 | tf_op jit(solution)/shard_map/ppermute | solution.py:475
  5.9 1.8 %collective-permute-start = (bf16[128,512]{1,0:T(8,128)(2,1)}, bf16[128,512]{1,0:T(8,128)(2,1)S(1)}, u32[]{:S(2)}, u32[]{:S(2)}) collective-permute-start(bf16[128,512]{1,0:T(8,128)(2,1)} %get-tuple-element.133), channel_id=1, source_target_pairs={{0,5},{1,4},{2,7},{3,6},{4,1},{5,0},{6,3},{7,2},{8,13},{9,12},{10,... | collective-permute-start | bytes 393224 | tf_op jit(solution)/shard_map/ppermute | solution.py:475
  7.8 3.1 %interleave.3 = (bf16[128,512]{1,0:T(8,128)(2,1)}, bf16[128,512]{1,0:T(8,128)(2,1)}, bf16[128,512]{1,0:T(8,128)(2,1)}, bf16[128,512]{1,0:T(8,128)(2,1)}, bf16[12...) custom-call(bf16[128,4096]{1,0:T(8,128)(2,1)} %refs_0_.3, ...), custom_call_target="tpu_custom_call" | custom-call | tf_op jit(solution)/shard_map/interleave/pallas_call | solution.py:304
  11.0 2.8 %collective-permute-start.5 = (bf16[128,512]{1,0:T(8,128)(2,1)S(1)}, bf16[128,512]{1,0:T(8,128)(2,1)S(1)}, u32[]{:S(2)}, u32[]{:S(2)}) collective-permute-start(bf16[128,512]{1,0:T(8,128)(2,1)S(1)} %copy-done.23), channel_id=1, source_target_pairs={{0,6},{1,7},{2,4},{3,5},{4,2},{5,3},{6,0},{7,1},{8,14},{9,15},{10,... | collective-permute-start | bytes 393224 | tf_op jit(solution)/shard_map/ppermute | solution.py:475
  13.9 0.2 collective-permute-start.11
  14.1 6.3 %collective-permute-done.3.refs_4_ = bf16[128,512]{1,0:T(8,128)(2,1)S(1)} collective-permute-done((bf16[128,512]{1,0:T(8,128)(2,1)}, bf16[128,512]{1,0:T(8,128)(2,1)S(1)}, u32[]{:S(2)}, u32[]{:S(2)}) %collective-permute-start.3) | collective-permute-done | bytes 131104 | tf_op jit(solution)/shard_map/ppermute | solution.py:475
  20.5 0.3 assemble.1
  20.8 1.6 %collective-permute-start.14 = (bf16[1024,256]{1,0:T(8,128)(2,1)S(1)}, bf16[1024,256]{1,0:T(8,128)(2,1)S(1)}, u32[]{:S(2)}, u32[]{:S(2)}) collective-permute-start(bf16[1024,256]{1,0:T(8,128)(2,1)S(1)} %get-tuple-element.168.refs_9_), channel_id=1, source_target_pairs={{0,8},{4,12},{8,16},{12,20},{16,24},{20,28},{24,0},{28,4},{1,9},{5... | collective-permute-start | bytes 1572872 | tf_op jit(solution)/shard_map/ppermute | solution.py:480
  22.5 1.5 %collective-permute-start.4 = (bf16[128,512]{1,0:T(8,128)(2,1)S(1)}, bf16[128,512]{1,0:T(8,128)(2,1)S(1)}, u32[]{:S(2)}, u32[]{:S(2)}) collective-permute-start(bf16[128,512]{1,0:T(8,128)(2,1)S(1)} %copy-done.17), channel_id=1, source_target_pairs={{0,2},{1,3},{2,0},{3,1},{4,6},{5,7},{6,4},{7,5},{8,10},{9,11},{10,... | collective-permute-start | bytes 393224 | tf_op jit(solution)/shard_map/ppermute | solution.py:475
  24.0 1.8 %collective-permute-start.9 = (bf16[128,512]{1,0:T(8,128)(2,1)S(1)}, bf16[128,512]{1,0:T(8,128)(2,1)S(1)}, u32[]{:S(2)}, u32[]{:S(2)}) collective-permute-start(bf16[128,512]{1,0:T(8,128)(2,1)S(1)} %copy-done.15), channel_id=1, source_target_pairs={{0,5},{1,4},{2,7},{3,6},{4,1},{5,0},{6,3},{7,2},{8,13},{9,12},{10,... | collective-permute-start | bytes 393224 | tf_op jit(solution)/shard_map/ppermute | solution.py:475
  25.7 0.5 collective-permute-start.6
  26.2 1.7 %collective-permute-done.4.refs_2_ = bf16[128,512]{1,0:T(8,128)(2,1)S(1)} collective-permute-done((bf16[128,512]{1,0:T(8,128)(2,1)S(1)}, bf16[128,512]{1,0:T(8,128)(2,1)S(1)}, u32[]{:S(2)}, u32[]{:S(2)}) %collective-permute-start.4) | collective-permute-done | bytes 131104 | tf_op jit(solution)/shard_map/ppermute | solution.py:475
  27.9 1.8 %collective-permute-done.1.refs_3_ = bf16[128,512]{1,0:T(8,128)(2,1)S(1)} collective-permute-done((bf16[128,512]{1,0:T(8,128)(2,1)S(1)}, bf16[128,512]{1,0:T(8,128)(2,1)S(1)}, u32[]{:S(2)}, u32[]{:S(2)}) %collective-permute-start.1) | collective-permute-done | bytes 131104 | tf_op jit(solution)/shard_map/ppermute | solution.py:475
  29.7 1.5 %collective-permute-start.12 = (bf16[128,512]{1,0:T(8,128)(2,1)S(1)}, bf16[128,512]{1,0:T(8,128)(2,1)}, u32[]{:S(2)}, u32[]{:S(2)}) collective-permute-start(bf16[128,512]{1,0:T(8,128)(2,1)S(1)} %copy-done.9), channel_id=1, source_target_pairs={{0,6},{1,7},{2,4},{3,5},{4,2},{5,3},{6,0},{7,1},{8,14},{9,15},{10,... | collective-permute-start | bytes 393224 | tf_op jit(solution)/shard_map/ppermute | solution.py:475
  31.2 1.0 collective-permute-start.2
  32.3 3.6 %all-to-all-start.1 = ((bf16[8,128,512]{2,1,0:T(8,128)(2,1)}), bf16[8,128,512]{2,1,0:T(8,128)(2,1)S(1)}, u32[]{:S(2)}, u32[]{:S(2)}) async-start(bf16[8,128,512]{2,1,0:T(8,128)(2,1)} %get-tuple-element.171), calls=%async_computation.1 | async-start | bytes 2097152 | tf_op jit(solution)/shard_map/all_to_all | solution.py:462
  35.9 1.6 %collective-permute-start.15 = (bf16[1024,256]{1,0:T(8,128)(2,1)S(1)}, bf16[1024,256]{1,0:T(8,128)(2,1)}, u32[]{:S(2)}, u32[]{:S(2)}) collective-permute-start(bf16[1024,256]{1,0:T(8,128)(2,1)S(1)} %get-tuple-element.172.refs_2_), channel_id=1, source_target_pairs={{0,8},{4,12},{8,16},{12,20},{16,24},{20,28},{24,0},{28,4},{1,9},{5... | collective-permute-start | bytes 1572872 | tf_op jit(solution)/shard_map/ppermute | solution.py:480
  37.5 0.9 collective-permute-done.6.refs_4_
  38.4 0.8 copy-done.7
  39.2 12.2 %attention.2 = (bf16[1024,512]{1,0:T(8,128)(2,1)}, bf16[1024,256]{1,0:T(8,128)(2,1)}, f32[2,128,1024]{2,1,0:T(8,128)}) custom-call(bf16[128,512]{1,0:T(8,128)(2,1)} %get-tuple-element.130.refs_0_, bf16[128,512]{1,0:T(8,128)(2,1)} %collective-permute-done.2.refs_1_, bf16[128,512]{1,0:T(8,128)(2,1)} %copy-done.18, bf16[128,512]{1,0:T(8,128)(2,1)} %copy-done.19, ...), custom_call_target="tpu_custom_call" | custom-call | flops 10000000000 | bytes 4194304 | tf_op jit(solution)/shard_map/attention/pallas_call | solution.py:233
  51.3 2.5 %collective-permute-start.16 = (bf16[1024,256]{1,0:T(8,128)(2,1)}, bf16[1024,256]{1,0:T(8,128)(2,1)S(1)}, u32[]{:S(2)}, u32[]{:S(2)}) collective-permute-start(bf16[1024,256]{1,0:T(8,128)(2,1)} %get-tuple-element.182), channel_id=1, source_target_pairs={{8,0},{12,4},{16,8},{20,12},{24,16},{28,20},{0,24},{4,28},{9,1},{1... | collective-permute-start | bytes 1572872 | tf_op jit(solution)/shard_map/ppermute | solution.py:483
  53.9 1.0 copy-done.6
  54.8 3.6 %all-to-all-start = ((bf16[8,128,512]{2,1,0:T(8,128)(2,1)}), bf16[8,128,512]{2,1,0:T(8,128)(2,1)S(1)}, u32[]{:S(2)}, u32[]{:S(2)}) async-start(bf16[8,128,512]{2,1,0:T(8,128)(2,1)} %bitcast.2), calls=%async_computation | async-start | bytes 2097152 | tf_op jit(solution)/shard_map/all_to_all | solution.py:462
  58.4 12.9 %attention.3 = (bf16[128,512]{1,0:T(8,128)(2,1)}, bf16[128,512]{1,0:T(8,128)(2,1)}, bf16[128,512]{1,0:T(8,128)(2,1)}, bf16[128,512]{1,0:T(8,128)(2,1)}, bf16[128...) custom-call(bf16[1024,512]{1,0:T(8,128)(2,1)} %bitcast.3, ...), custom_call_target="tpu_custom_call" | custom-call | flops 10000000000 | bytes 4194304 | tf_op jit(solution)/shard_map/attention/pallas_call | solution.py:233
  71.4 1.7 %collective-permute-start.17 = (bf16[1024,256]{1,0:T(8,128)(2,1)}, bf16[1024,256]{1,0:T(8,128)(2,1)S(1)}, u32[]{:S(2)}, u32[]{:S(2)}) collective-permute-start(bf16[1024,256]{1,0:T(8,128)(2,1)} %get-tuple-element.186), channel_id=1, source_target_pairs={{8,0},{12,4},{16,8},{20,12},{24,16},{28,20},{0,24},{4,28},{9,1},{1... | collective-permute-start | bytes 1572872 | tf_op jit(solution)/shard_map/ppermute | solution.py:483
  73.0 1.9 %collective-permute-start.18 = (bf16[128,512]{1,0:T(8,128)(2,1)}, bf16[128,512]{1,0:T(8,128)(2,1)S(1)}, u32[]{:S(2)}, u32[]{:S(2)}) collective-permute-start(bf16[128,512]{1,0:T(8,128)(2,1)} %get-tuple-element.199), channel_id=1, source_target_pairs={{0,4},{1,5},{2,6},{3,7},{4,0},{5,1},{6,2},{7,3},{8,12},{9,13},{10,... | collective-permute-start | bytes 393224 | tf_op jit(solution)/shard_map/ppermute | solution.py:475
  74.9 1.5 %collective-permute-start.20 = (bf16[128,512]{1,0:T(8,128)(2,1)}, bf16[128,512]{1,0:T(8,128)(2,1)S(1)}, u32[]{:S(2)}, u32[]{:S(2)}) collective-permute-start(bf16[128,512]{1,0:T(8,128)(2,1)} %get-tuple-element.203), channel_id=1, source_target_pairs={{0,2},{1,3},{2,0},{3,1},{4,6},{5,7},{6,4},{7,5},{8,10},{9,11},{10,... | collective-permute-start | bytes 393224 | tf_op jit(solution)/shard_map/ppermute | solution.py:475
  76.4 0.4 collective-permute-start.22
  76.8 1.2 %copy-done.1 = f32[2,128,1024]{2,1,0:T(8,128)S(1)} copy-done((f32[2,128,1024]{2,1,0:T(8,128)S(1)}, f32[2,128,1024]{2,1,0:T(8,128)}, u32[]{:S(2)}) %copy-start.1) | copy-done | bytes 1048600
  78.0 0.6 settle.1
  78.9 0.3 collective-permute-start.19
  79.2 1.5 %collective-permute-done.20.refs_2_ = bf16[128,512]{1,0:T(8,128)(2,1)S(1)} collective-permute-done((bf16[128,512]{1,0:T(8,128)(2,1)}, bf16[128,512]{1,0:T(8,128)(2,1)S(1)}, u32[]{:S(2)}, u32[]{:S(2)}) %collective-permute-start.20) | collective-permute-done | bytes 131104 | tf_op jit(solution)/shard_map/ppermute | solution.py:475
  80.7 2.3 %collective-permute-start.23 = (bf16[128,512]{1,0:T(8,128)(2,1)S(1)}, bf16[128,512]{1,0:T(8,128)(2,1)S(1)}, u32[]{:S(2)}, u32[]{:S(2)}) collective-permute-start(bf16[128,512]{1,0:T(8,128)(2,1)S(1)} %copy-done.13), channel_id=1, source_target_pairs={{0,6},{1,7},{2,4},{3,5},{4,2},{5,3},{6,0},{7,1},{8,14},{9,15},{10,... | collective-permute-start | bytes 393224 | tf_op jit(solution)/shard_map/ppermute | solution.py:475
  83.0 1.1 %collective-permute-start.24 = (bf16[128,512]{1,0:T(8,128)(2,1)S(1)}, bf16[128,512]{1,0:T(8,128)(2,1)S(1)}, u32[]{:S(2)}, u32[]{:S(2)}) collective-permute-start(bf16[128,512]{1,0:T(8,128)(2,1)S(1)} %copy-done.11), channel_id=1, source_target_pairs={{0,7},{1,6},{2,5},{3,4},{4,3},{5,2},{6,1},{7,0},{8,15},{9,14},{10,... | collective-permute-start | bytes 393224 | tf_op jit(solution)/shard_map/ppermute | solution.py:475
  84.1 1.7 %collective-permute-done.17.back_ref = bf16[1024,256]{1,0:T(8,128)(2,1)S(1)} collective-permute-done((bf16[1024,256]{1,0:T(8,128)(2,1)}, bf16[1024,256]{1,0:T(8,128)(2,1)S(1)}, u32[]{:S(2)}, u32[]{:S(2)}) %collective-permute-start.17) | collective-permute-done | bytes 524320 | tf_op jit(solution)/shard_map/ppermute | solution.py:483
  86.0 1.7 %collective-permute-start.27 = (bf16[128,512]{1,0:T(8,128)(2,1)S(1)}, bf16[128,512]{1,0:T(8,128)(2,1)S(1)}, u32[]{:S(2)}, u32[]{:S(2)}) collective-permute-start(bf16[128,512]{1,0:T(8,128)(2,1)S(1)} %get-tuple-element.227), channel_id=1, source_target_pairs={{0,2},{1,3},{2,0},{3,1},{4,6},{5,7},{6,4},{7,5},{8,10},{9,11},{10,... | collective-permute-start | bytes 393224 | tf_op jit(solution)/shard_map/ppermute | solution.py:475
  87.7 1.6 %collective-permute-start.30 = (bf16[128,512]{1,0:T(8,128)(2,1)S(1)}, bf16[128,512]{1,0:T(8,128)(2,1)S(1)}, u32[]{:S(2)}, u32[]{:S(2)}) collective-permute-start(bf16[128,512]{1,0:T(8,128)(2,1)S(1)} %get-tuple-element.232), channel_id=1, source_target_pairs={{0,6},{1,7},{2,4},{3,5},{4,2},{5,3},{6,0},{7,1},{8,14},{9,15},{10,... | collective-permute-start | bytes 393224 | tf_op jit(solution)/shard_map/ppermute | solution.py:475
  89.3 0.5 collective-permute-start.28
  89.9 2.0 %collective-permute-start.29 = (bf16[128,512]{1,0:T(8,128)(2,1)S(1)}, bf16[128,512]{1,0:T(8,128)(2,1)S(1)}, u32[]{:S(2)}, u32[]{:S(2)}) collective-permute-start(bf16[128,512]{1,0:T(8,128)(2,1)S(1)} %get-tuple-element.231), channel_id=1, source_target_pairs={{0,5},{1,4},{2,7},{3,6},{4,1},{5,0},{6,3},{7,2},{8,13},{9,12},{10,... | collective-permute-start | bytes 393224 | tf_op jit(solution)/shard_map/ppermute | solution.py:475
  91.9 0.6 collective-permute-done.27.refs_2_
  92.6 2.3 %collective-permute-done.25.refs_3_ = bf16[128,512]{1,0:T(8,128)(2,1)S(1)} collective-permute-done((bf16[128,512]{1,0:T(8,128)(2,1)S(1)}, bf16[128,512]{1,0:T(8,128)(2,1)S(1)}, u32[]{:S(2)}, u32[]{:S(2)}) %collective-permute-start.25) | collective-permute-done | bytes 131104 | tf_op jit(solution)/shard_map/ppermute | solution.py:475
  95.0 0.4 collective-permute-start.26
  95.4 1.6 %spread.1 = (bf16[128,4096]{1,0:T(8,128)(2,1)}, bf16[128,4096]{1,0:T(8,128)(2,1)}) custom-call(bf16[8,128,512]{2,1,0:T(8,128)(2,1)S(1)} %all-to-all-done.x_ref, bf16[128,512]{1,0:T(8,128)(2,1)S(1)} %copy-done.2, bf16[128,512]{1,0:T(8,128)(2,1)S(1)} %collective-permute-done.19.refs_1_, bf16[128,512]{1,0:T(8,128)(2,1)S(1)} %collective-permute-done.20.refs_2_, ...), custom_call_target="tpu_custom_call" | custom-call | tf_op jit(solution)/shard_map/spread/pallas_call | solution.py:373
  97.0 2.1 %collective-permute-done.30.refs_6_ = bf16[128,512]{1,0:T(8,128)(2,1)S(1)} collective-permute-done((bf16[128,512]{1,0:T(8,128)(2,1)S(1)}, bf16[128,512]{1,0:T(8,128)(2,1)S(1)}, u32[]{:S(2)}, u32[]{:S(2)}) %collective-permute-start.30) | collective-permute-done | bytes 131104 | tf_op jit(solution)/shard_map/ppermute | solution.py:475
  99.1 2.0 %collective-permute-done.28.refs_4_ = bf16[128,512]{1,0:T(8,128)(2,1)S(1)} collective-permute-done((bf16[128,512]{1,0:T(8,128)(2,1)S(1)}, bf16[128,512]{1,0:T(8,128)(2,1)S(1)}, u32[]{:S(2)}, u32[]{:S(2)}) %collective-permute-start.28) | collective-permute-done | bytes 131104 | tf_op jit(solution)/shard_map/ppermute | solution.py:475
  101.1 3.0 %collective-permute-done.29.refs_5_ = bf16[128,512]{1,0:T(8,128)(2,1)S(1)} collective-permute-done((bf16[128,512]{1,0:T(8,128)(2,1)S(1)}, bf16[128,512]{1,0:T(8,128)(2,1)S(1)}, u32[]{:S(2)}, u32[]{:S(2)}) %collective-permute-start.29) | collective-permute-done | bytes 131104 | tf_op jit(solution)/shard_map/ppermute | solution.py:475
  104.1 1.3 %unpack.1 = (bf16[128,2048]{1,0:T(8,128)(2,1)}, bf16[128,2048]{1,0:T(8,128)(2,1)}) custom-call(bf16[128,512]{1,0:T(8,128)(2,1)S(1)} %get-tuple-element.222.refs_0_, bf16[128,512]{1,0:T(8,128)(2,1)S(1)} %collective-permute-done.26.refs_1_, bf16[128,512]{1,0:T(8,128)(2,1)S(1)} %collective-permute-done.27.refs_2_, ...), custom_call_target="tpu_custom_call" | custom-call | tf_op jit(solution)/shard_map/unpack/pallas_call | solution.py:444
  (77 shorter events, 0.9 us)
Async XLA Ops:
  2.9 10.9 %collective-permute-start.7 = (bf16[128,512]{1,0:T(8,128)(2,1)}, bf16[128,512]{1,0:T(8,128)(2,1)S(1)}, u32[]{:S(2)}, u32[]{:S(2)}) collective-permute-start(bf16[128,512]{1,0:T(8,128)(2,1)} %get-tuple-element.148), channel_id=1, source_target_pairs={{0,2},{1,3},{2,0},{3,1},{4,6},{5,7},{6,4},{7,5},{8,10},{9,11},{10,... | collective-permute-start | bytes 393224 | tf_op jit(solution)/shard_map/ppermute | solution.py:475
  5.9 7.9 %collective-permute-start.10 = (bf16[128,512]{1,0:T(8,128)(2,1)}, bf16[128,512]{1,0:T(8,128)(2,1)S(1)}, u32[]{:S(2)}, u32[]{:S(2)}) collective-permute-start(bf16[128,512]{1,0:T(8,128)(2,1)} %get-tuple-element.154), channel_id=1, source_target_pairs={{0,3},{1,2},{2,1},{3,0},{4,7},{5,6},{6,5},{7,4},{8,11},{9,10},{10,... | collective-permute-start | bytes 393224 | tf_op jit(solution)/shard_map/ppermute | solution.py:475
  5.9 8.2 %collective-permute-start = (bf16[128,512]{1,0:T(8,128)(2,1)}, bf16[128,512]{1,0:T(8,128)(2,1)S(1)}, u32[]{:S(2)}, u32[]{:S(2)}) collective-permute-start(bf16[128,512]{1,0:T(8,128)(2,1)} %get-tuple-element.133), channel_id=1, source_target_pairs={{0,5},{1,4},{2,7},{3,6},{4,1},{5,0},{6,3},{7,2},{8,13},{9,12},{10,... | collective-permute-start | bytes 393224 | tf_op jit(solution)/shard_map/ppermute | solution.py:475
  7.7 6.1 %copy-start.22 = (bf16[128,512]{1,0:T(8,128)(2,1)S(1)}, bf16[128,512]{1,0:T(8,128)(2,1)}, u32[]{:S(2)}) copy-start(bf16[128,512]{1,0:T(8,128)(2,1)} %get-tuple-element.149) | copy-start | bytes 393220
  7.7 6.1 %copy-start.21 = (bf16[128,512]{1,0:T(8,128)(2,1)S(1)}, bf16[128,512]{1,0:T(8,128)(2,1)}, u32[]{:S(2)}) copy-start(bf16[128,512]{1,0:T(8,128)(2,1)} %get-tuple-element.155) | copy-start | bytes 393220
  7.7 12.7 %copy-start.3 = (bf16[128,512]{1,0:T(8,128)(2,1)S(1)}, bf16[128,512]{1,0:T(8,128)(2,1)}, u32[]{:S(2)}) copy-start(bf16[128,512]{1,0:T(8,128)(2,1)} %get-tuple-element.157.refs_0_) | copy-start | bytes 393220
  7.7 12.7 %collective-permute-start.3 = (bf16[128,512]{1,0:T(8,128)(2,1)}, bf16[128,512]{1,0:T(8,128)(2,1)S(1)}, u32[]{:S(2)}, u32[]{:S(2)}) collective-permute-start(bf16[128,512]{1,0:T(8,128)(2,1)} %get-tuple-element.138), channel_id=1, source_target_pairs={{0,4},{1,5},{2,6},{3,7},{4,0},{5,1},{6,2},{7,3},{8,12},{9,13},{10,... | collective-permute-start | bytes 393224 | tf_op jit(solution)/shard_map/ppermute | solution.py:475
  11.0 9.4 %collective-permute-start.5 = (bf16[128,512]{1,0:T(8,128)(2,1)S(1)}, bf16[128,512]{1,0:T(8,128)(2,1)S(1)}, u32[]{:S(2)}, u32[]{:S(2)}) collective-permute-start(bf16[128,512]{1,0:T(8,128)(2,1)S(1)} %copy-done.23), channel_id=1, source_target_pairs={{0,6},{1,7},{2,4},{3,5},{4,2},{5,3},{6,0},{7,1},{8,14},{9,15},{10,... | collective-permute-start | bytes 393224 | tf_op jit(solution)/shard_map/ppermute | solution.py:475
  13.8 6.6 %collective-permute-start.8 = (bf16[128,512]{1,0:T(8,128)(2,1)S(1)}, bf16[128,512]{1,0:T(8,128)(2,1)S(1)}, u32[]{:S(2)}, u32[]{:S(2)}) collective-permute-start(bf16[128,512]{1,0:T(8,128)(2,1)S(1)} %copy-done.22), channel_id=1, source_target_pairs={{0,7},{1,6},{2,5},{3,4},{4,3},{5,2},{6,1},{7,0},{8,15},{9,14},{10,... | collective-permute-start | bytes 393224 | tf_op jit(solution)/shard_map/ppermute | solution.py:475
  13.9 6.5 %collective-permute-start.11 = (bf16[128,512]{1,0:T(8,128)(2,1)S(1)}, bf16[128,512]{1,0:T(8,128)(2,1)S(1)}, u32[]{:S(2)}, u32[]{:S(2)}) collective-permute-start(bf16[128,512]{1,0:T(8,128)(2,1)S(1)} %copy-done.21), channel_id=1, source_target_pairs={{0,1},{1,0},{2,3},{3,2},{4,5},{5,4},{6,7},{7,6},{8,9},{9,8},{10,11... | collective-permute-start | bytes 393224 | tf_op jit(solution)/shard_map/ppermute | solution.py:475
  20.4 3.5 %copy-start.16 = (bf16[128,512]{1,0:T(8,128)(2,1)S(1)}, bf16[128,512]{1,0:T(8,128)(2,1)}, u32[]{:S(2)}) copy-start(bf16[128,512]{1,0:T(8,128)(2,1)} %get-tuple-element.134) | copy-start | bytes 393220
  20.5 5.3 %copy-start.10 = (bf16[128,512]{1,0:T(8,128)(2,1)S(1)}, bf16[128,512]{1,0:T(8,128)(2,1)}, u32[]{:S(2)}) copy-start(bf16[128,512]{1,0:T(8,128)(2,1)} %get-tuple-element.144) | copy-start | bytes 393220
  20.5 7.5 %copy-start.12 = (bf16[128,512]{1,0:T(8,128)(2,1)S(1)}, bf16[128,512]{1,0:T(8,128)(2,1)}, u32[]{:S(2)}) copy-start(bf16[128,512]{1,0:T(8,128)(2,1)} %get-tuple-element.166) | copy-start | bytes 393220
  20.5 9.3 %copy-start.9 = (bf16[128,512]{1,0:T(8,128)(2,1)S(1)}, bf16[128,512]{1,0:T(8,128)(2,1)}, u32[]{:S(2)}) copy-start(bf16[128,512]{1,0:T(8,128)(2,1)} %get-tuple-element.156) | copy-start | bytes 393220
  20.5 10.8 %copy-start.8 = (bf16[128,512]{1,0:T(8,128)(2,1)S(1)}, bf16[128,512]{1,0:T(8,128)(2,1)}, u32[]{:S(2)}) copy-start(bf16[128,512]{1,0:T(8,128)(2,1)} %get-tuple-element.135) | copy-start | bytes 393220
  20.8 11.5 %copy-start.5 = (bf16[1024,256]{1,0:T(8,128)(2,1)}, bf16[1024,256]{1,0:T(8,128)(2,1)S(1)}, u32[]{:S(2)}) copy-start(bf16[1024,256]{1,0:T(8,128)(2,1)S(1)} %get-tuple-element.168.refs_9_) | copy-start | bytes 1572868
  20.8 15.0 %copy-start.4 = (bf16[1024,256]{1,0:T(8,128)(2,1)}, bf16[1024,256]{1,0:T(8,128)(2,1)S(1)}, u32[]{:S(2)}) copy-start(bf16[1024,256]{1,0:T(8,128)(2,1)S(1)} %get-tuple-element.172.refs_2_) | copy-start | bytes 1572868
  20.8 17.5 %collective-permute-start.14 = (bf16[1024,256]{1,0:T(8,128)(2,1)S(1)}, bf16[1024,256]{1,0:T(8,128)(2,1)S(1)}, u32[]{:S(2)}, u32[]{:S(2)}) collective-permute-start(bf16[1024,256]{1,0:T(8,128)(2,1)S(1)} %get-tuple-element.168.refs_9_), channel_id=1, source_target_pairs={{0,8},{4,12},{8,16},{12,20},{16,24},{20,28},{24,0},{28,4},{1,9},{5... | collective-permute-start | bytes 1572872 | tf_op jit(solution)/shard_map/ppermute | solution.py:480
  22.5 5.5 %collective-permute-start.4 = (bf16[128,512]{1,0:T(8,128)(2,1)S(1)}, bf16[128,512]{1,0:T(8,128)(2,1)S(1)}, u32[]{:S(2)}, u32[]{:S(2)}) collective-permute-start(bf16[128,512]{1,0:T(8,128)(2,1)S(1)} %copy-done.17), channel_id=1, source_target_pairs={{0,2},{1,3},{2,0},{3,1},{4,6},{5,7},{6,4},{7,5},{8,10},{9,11},{10,... | collective-permute-start | bytes 393224 | tf_op jit(solution)/shard_map/ppermute | solution.py:475
  24.0 5.8 %collective-permute-start.1 = (bf16[128,512]{1,0:T(8,128)(2,1)S(1)}, bf16[128,512]{1,0:T(8,128)(2,1)S(1)}, u32[]{:S(2)}, u32[]{:S(2)}) collective-permute-start(bf16[128,512]{1,0:T(8,128)(2,1)S(1)} %copy-done.16), channel_id=1, source_target_pairs={{0,3},{1,2},{2,1},{3,0},{4,7},{5,6},{6,5},{7,4},{8,11},{9,10},{10,... | collective-permute-start | bytes 393224 | tf_op jit(solution)/shard_map/ppermute | solution.py:475
  24.0 7.3 %collective-permute-start.9 = (bf16[128,512]{1,0:T(8,128)(2,1)S(1)}, bf16[128,512]{1,0:T(8,128)(2,1)S(1)}, u32[]{:S(2)}, u32[]{:S(2)}) collective-permute-start(bf16[128,512]{1,0:T(8,128)(2,1)S(1)} %copy-done.15), channel_id=1, source_target_pairs={{0,5},{1,4},{2,7},{3,6},{4,1},{5,0},{6,3},{7,2},{8,13},{9,12},{10,... | collective-permute-start | bytes 393224 | tf_op jit(solution)/shard_map/ppermute | solution.py:475
  25.7 12.6 %collective-permute-start.6 = (bf16[128,512]{1,0:T(8,128)(2,1)S(1)}, bf16[128,512]{1,0:T(8,128)(2,1)}, u32[]{:S(2)}, u32[]{:S(2)}) collective-permute-start(bf16[128,512]{1,0:T(8,128)(2,1)S(1)} %copy-done.10), channel_id=1, source_target_pairs={{0,4},{1,5},{2,6},{3,7},{4,0},{5,1},{6,2},{7,3},{8,12},{9,13},{10,... | collective-permute-start | bytes 393224 | tf_op jit(solution)/shard_map/ppermute | solution.py:475
  27.9 4.3 %copy-start.18 = (bf16[128,512]{1,0:T(8,128)(2,1)}, bf16[128,512]{1,0:T(8,128)(2,1)S(1)}, u32[]{:S(2)}) copy-start(bf16[128,512]{1,0:T(8,128)(2,1)S(1)} %collective-permute-done.4.refs_2_) | copy-start | bytes 393220
  27.9 7.9 %collective-permute-start.13 = (bf16[128,512]{1,0:T(8,128)(2,1)S(1)}, bf16[128,512]{1,0:T(8,128)(2,1)}, u32[]{:S(2)}, u32[]{:S(2)}) collective-permute-start(bf16[128,512]{1,0:T(8,128)(2,1)S(1)} %copy-done.12), channel_id=1, source_target_pairs={{0,7},{1,6},{2,5},{3,4},{4,3},{5,2},{6,1},{7,0},{8,15},{9,14},{10,... | collective-permute-start | bytes 393224 | tf_op jit(solution)/shard_map/ppermute | solution.py:475
  29.7 8.6 %collective-permute-start.12 = (bf16[128,512]{1,0:T(8,128)(2,1)S(1)}, bf16[128,512]{1,0:T(8,128)(2,1)}, u32[]{:S(2)}, u32[]{:S(2)}) collective-permute-start(bf16[128,512]{1,0:T(8,128)(2,1)S(1)} %copy-done.9), channel_id=1, source_target_pairs={{0,6},{1,7},{2,4},{3,5},{4,2},{5,3},{6,0},{7,1},{8,14},{9,15},{10,... | collective-permute-start | bytes 393224 | tf_op jit(solution)/shard_map/ppermute | solution.py:475
  31.2 7.1 %collective-permute-start.2 = (bf16[128,512]{1,0:T(8,128)(2,1)S(1)}, bf16[128,512]{1,0:T(8,128)(2,1)}, u32[]{:S(2)}, u32[]{:S(2)}) collective-permute-start(bf16[128,512]{1,0:T(8,128)(2,1)S(1)} %copy-done.8), channel_id=1, source_target_pairs={{0,1},{1,0},{2,3},{3,2},{4,5},{5,4},{6,7},{7,6},{8,9},{9,8},{10,11... | collective-permute-start | bytes 393224 | tf_op jit(solution)/shard_map/ppermute | solution.py:475
  32.3 21.6 %all-to-all-start.1 = ((bf16[8,128,512]{2,1,0:T(8,128)(2,1)}), bf16[8,128,512]{2,1,0:T(8,128)(2,1)S(1)}, u32[]{:S(2)}, u32[]{:S(2)}) async-start(bf16[8,128,512]{2,1,0:T(8,128)(2,1)} %get-tuple-element.171), calls=%async_computation.1 | async-start | bytes 2097152 | tf_op jit(solution)/shard_map/all_to_all | solution.py:462
  35.9 22.5 %collective-permute-start.15 = (bf16[1024,256]{1,0:T(8,128)(2,1)S(1)}, bf16[1024,256]{1,0:T(8,128)(2,1)}, u32[]{:S(2)}, u32[]{:S(2)}) collective-permute-start(bf16[1024,256]{1,0:T(8,128)(2,1)S(1)} %get-tuple-element.172.refs_2_), channel_id=1, source_target_pairs={{0,8},{4,12},{8,16},{12,20},{16,24},{20,28},{24,0},{28,4},{1,9},{5... | collective-permute-start | bytes 1572872 | tf_op jit(solution)/shard_map/ppermute | solution.py:480
  51.3 21.7 %collective-permute-start.16 = (bf16[1024,256]{1,0:T(8,128)(2,1)}, bf16[1024,256]{1,0:T(8,128)(2,1)S(1)}, u32[]{:S(2)}, u32[]{:S(2)}) collective-permute-start(bf16[1024,256]{1,0:T(8,128)(2,1)} %get-tuple-element.182), channel_id=1, source_target_pairs={{8,0},{12,4},{16,8},{20,12},{24,16},{28,20},{0,24},{4,28},{9,1},{1... | collective-permute-start | bytes 1572872 | tf_op jit(solution)/shard_map/ppermute | solution.py:483
  54.8 31.1 %all-to-all-start = ((bf16[8,128,512]{2,1,0:T(8,128)(2,1)}), bf16[8,128,512]{2,1,0:T(8,128)(2,1)S(1)}, u32[]{:S(2)}, u32[]{:S(2)}) async-start(bf16[8,128,512]{2,1,0:T(8,128)(2,1)} %bitcast.2), calls=%async_computation | async-start | bytes 2097152 | tf_op jit(solution)/shard_map/all_to_all | solution.py:462
  58.4 18.4 %copy-start = (f32[2,128,1024]{2,1,0:T(8,128)S(1)}, f32[2,128,1024]{2,1,0:T(8,128)}, u32[]{:S(2)}) copy-start(f32[2,128,1024]{2,1,0:T(8,128)} %get-tuple-element.170.own0) | copy-start | bytes 3145732
  71.4 14.5 %collective-permute-start.17 = (bf16[1024,256]{1,0:T(8,128)(2,1)}, bf16[1024,256]{1,0:T(8,128)(2,1)S(1)}, u32[]{:S(2)}, u32[]{:S(2)}) collective-permute-start(bf16[1024,256]{1,0:T(8,128)(2,1)} %get-tuple-element.186), channel_id=1, source_target_pairs={{8,0},{12,4},{16,8},{20,12},{24,16},{28,20},{0,24},{4,28},{9,1},{1... | collective-permute-start | bytes 1572872 | tf_op jit(solution)/shard_map/ppermute | solution.py:483
  73.0 5.7 %collective-permute-start.18 = (bf16[128,512]{1,0:T(8,128)(2,1)}, bf16[128,512]{1,0:T(8,128)(2,1)S(1)}, u32[]{:S(2)}, u32[]{:S(2)}) collective-permute-start(bf16[128,512]{1,0:T(8,128)(2,1)} %get-tuple-element.199), channel_id=1, source_target_pairs={{0,4},{1,5},{2,6},{3,7},{4,0},{5,1},{6,2},{7,3},{8,12},{9,13},{10,... | collective-permute-start | bytes 393224 | tf_op jit(solution)/shard_map/ppermute | solution.py:475
  74.9 5.7 %collective-permute-start.20 = (bf16[128,512]{1,0:T(8,128)(2,1)}, bf16[128,512]{1,0:T(8,128)(2,1)S(1)}, u32[]{:S(2)}, u32[]{:S(2)}) collective-permute-start(bf16[128,512]{1,0:T(8,128)(2,1)} %get-tuple-element.203), channel_id=1, source_target_pairs={{0,2},{1,3},{2,0},{3,1},{4,6},{5,7},{6,4},{7,5},{8,10},{9,11},{10,... | collective-permute-start | bytes 393224 | tf_op jit(solution)/shard_map/ppermute | solution.py:475
  76.4 6.6 %collective-permute-start.21 = (bf16[128,512]{1,0:T(8,128)(2,1)}, bf16[128,512]{1,0:T(8,128)(2,1)S(1)}, u32[]{:S(2)}, u32[]{:S(2)}) collective-permute-start(bf16[128,512]{1,0:T(8,128)(2,1)} %get-tuple-element.206), channel_id=1, source_target_pairs={{0,3},{1,2},{2,1},{3,0},{4,7},{5,6},{6,5},{7,4},{8,11},{9,10},{10,... | collective-permute-start | bytes 393224 | tf_op jit(solution)/shard_map/ppermute | solution.py:475
  76.4 11.3 %collective-permute-start.22 = (bf16[128,512]{1,0:T(8,128)(2,1)}, bf16[128,512]{1,0:T(8,128)(2,1)S(1)}, u32[]{:S(2)}, u32[]{:S(2)}) collective-permute-start(bf16[128,512]{1,0:T(8,128)(2,1)} %get-tuple-element.212), channel_id=1, source_target_pairs={{0,5},{1,4},{2,7},{3,6},{4,1},{5,0},{6,3},{7,2},{8,13},{9,12},{10,... | collective-permute-start | bytes 393224 | tf_op jit(solution)/shard_map/ppermute | solution.py:475
  78.0 5.0 %copy-start.11 = (bf16[128,512]{1,0:T(8,128)(2,1)S(1)}, bf16[128,512]{1,0:T(8,128)(2,1)}, u32[]{:S(2)}) copy-start(bf16[128,512]{1,0:T(8,128)(2,1)} %get-tuple-element.218) | copy-start | bytes 393220
  78.9 8.8 %collective-permute-start.19 = (bf16[128,512]{1,0:T(8,128)(2,1)S(1)}, bf16[128,512]{1,0:T(8,128)(2,1)S(1)}, u32[]{:S(2)}, u32[]{:S(2)}) collective-permute-start(bf16[128,512]{1,0:T(8,128)(2,1)S(1)} %copy-done.14), channel_id=1, source_target_pairs={{0,1},{1,0},{2,3},{3,2},{4,5},{5,4},{6,7},{7,6},{8,9},{9,8},{10,11... | collective-permute-start | bytes 393224 | tf_op jit(solution)/shard_map/ppermute | solution.py:475
  80.7 8.6 %collective-permute-start.23 = (bf16[128,512]{1,0:T(8,128)(2,1)S(1)}, bf16[128,512]{1,0:T(8,128)(2,1)S(1)}, u32[]{:S(2)}, u32[]{:S(2)}) collective-permute-start(bf16[128,512]{1,0:T(8,128)(2,1)S(1)} %copy-done.13), channel_id=1, source_target_pairs={{0,6},{1,7},{2,4},{3,5},{4,2},{5,3},{6,0},{7,1},{8,14},{9,15},{10,... | collective-permute-start | bytes 393224 | tf_op jit(solution)/shard_map/ppermute | solution.py:475
  83.0 6.9 %collective-permute-start.24 = (bf16[128,512]{1,0:T(8,128)(2,1)S(1)}, bf16[128,512]{1,0:T(8,128)(2,1)S(1)}, u32[]{:S(2)}, u32[]{:S(2)}) collective-permute-start(bf16[128,512]{1,0:T(8,128)(2,1)S(1)} %copy-done.11), channel_id=1, source_target_pairs={{0,7},{1,6},{2,5},{3,4},{4,3},{5,2},{6,1},{7,0},{8,15},{9,14},{10,... | collective-permute-start | bytes 393224 | tf_op jit(solution)/shard_map/ppermute | solution.py:475
  85.8 9.6 %copy-start.2 = (bf16[128,512]{1,0:T(8,128)(2,1)S(1)}, bf16[128,512]{1,0:T(8,128)(2,1)}, u32[]{:S(2)}) copy-start(bf16[128,512]{1,0:T(8,128)(2,1)} %get-tuple-element.196.refs_0_) | copy-start | bytes 393220
  86.0 6.5 %collective-permute-start.27 = (bf16[128,512]{1,0:T(8,128)(2,1)S(1)}, bf16[128,512]{1,0:T(8,128)(2,1)S(1)}, u32[]{:S(2)}, u32[]{:S(2)}) collective-permute-start(bf16[128,512]{1,0:T(8,128)(2,1)S(1)} %get-tuple-element.227), channel_id=1, source_target_pairs={{0,2},{1,3},{2,0},{3,1},{4,6},{5,7},{6,4},{7,5},{8,10},{9,11},{10,... | collective-permute-start | bytes 393224 | tf_op jit(solution)/shard_map/ppermute | solution.py:475
  87.7 7.3 %collective-permute-start.25 = (bf16[128,512]{1,0:T(8,128)(2,1)S(1)}, bf16[128,512]{1,0:T(8,128)(2,1)S(1)}, u32[]{:S(2)}, u32[]{:S(2)}) collective-permute-start(bf16[128,512]{1,0:T(8,128)(2,1)S(1)} %get-tuple-element.224), channel_id=1, source_target_pairs={{0,3},{1,2},{2,1},{3,0},{4,7},{5,6},{6,5},{7,4},{8,11},{9,10},{10,... | collective-permute-start | bytes 393224 | tf_op jit(solution)/shard_map/ppermute | solution.py:475
  87.7 11.4 %collective-permute-start.30 = (bf16[128,512]{1,0:T(8,128)(2,1)S(1)}, bf16[128,512]{1,0:T(8,128)(2,1)S(1)}, u32[]{:S(2)}, u32[]{:S(2)}) collective-permute-start(bf16[128,512]{1,0:T(8,128)(2,1)S(1)} %get-tuple-element.232), channel_id=1, source_target_pairs={{0,6},{1,7},{2,4},{3,5},{4,2},{5,3},{6,0},{7,1},{8,14},{9,15},{10,... | collective-permute-start | bytes 393224 | tf_op jit(solution)/shard_map/ppermute | solution.py:475
  89.3 11.8 %collective-permute-start.28 = (bf16[128,512]{1,0:T(8,128)(2,1)S(1)}, bf16[128,512]{1,0:T(8,128)(2,1)S(1)}, u32[]{:S(2)}, u32[]{:S(2)}) collective-permute-start(bf16[128,512]{1,0:T(8,128)(2,1)S(1)} %get-tuple-element.230), channel_id=1, source_target_pairs={{0,4},{1,5},{2,6},{3,7},{4,0},{5,1},{6,2},{7,3},{8,12},{9,13},{10,... | collective-permute-start | bytes 393224 | tf_op jit(solution)/shard_map/ppermute | solution.py:475
  89.9 14.3 %collective-permute-start.29 = (bf16[128,512]{1,0:T(8,128)(2,1)S(1)}, bf16[128,512]{1,0:T(8,128)(2,1)S(1)}, u32[]{:S(2)}, u32[]{:S(2)}) collective-permute-start(bf16[128,512]{1,0:T(8,128)(2,1)S(1)} %get-tuple-element.231), channel_id=1, source_target_pairs={{0,5},{1,4},{2,7},{3,6},{4,1},{5,0},{6,3},{7,2},{8,13},{9,12},{10,... | collective-permute-start | bytes 393224 | tf_op jit(solution)/shard_map/ppermute | solution.py:475
  92.5 11.6 %collective-permute-start.31 = (bf16[128,512]{1,0:T(8,128)(2,1)S(1)}, bf16[128,512]{1,0:T(8,128)(2,1)S(1)}, u32[]{:S(2)}, u32[]{:S(2)}) collective-permute-start(bf16[128,512]{1,0:T(8,128)(2,1)S(1)} %get-tuple-element.233), channel_id=1, source_target_pairs={{0,7},{1,6},{2,5},{3,4},{4,3},{5,2},{6,1},{7,0},{8,15},{9,14},{10,... | collective-permute-start | bytes 393224 | tf_op jit(solution)/shard_map/ppermute | solution.py:475
  95.0 9.2 %collective-permute-start.26 = (bf16[128,512]{1,0:T(8,128)(2,1)S(1)}, bf16[128,512]{1,0:T(8,128)(2,1)S(1)}, u32[]{:S(2)}, u32[]{:S(2)}) collective-permute-start(bf16[128,512]{1,0:T(8,128)(2,1)S(1)} %get-tuple-element.225), channel_id=1, source_target_pairs={{0,1},{1,0},{2,3},{3,2},{4,5},{5,4},{6,7},{7,6},{8,9},{9,8},{10,11... | collective-permute-start | bytes 393224 | tf_op jit(solution)/shard_map/ppermute | solution.py:475
  (10 other events, 18.9 us)

commit v6 on v5

--- a/solution.py
+++ b/solution.py
@@ -24,7 +24,6 @@
 NT = (((1,), (1,)), ((), ()))
 
 VMEM = pl.BlockSpec(memory_space=pltpu.VMEM)
-SMEM = pl.BlockSpec(memory_space=pltpu.SMEM)
 ANY = pl.BlockSpec(memory_space=pl.ANY)
 HBM = pl.BlockSpec(memory_space=pltpu.HBM)
 
@@ -46,17 +45,16 @@
 
 
 def attention_kernel(
-    apart, taken, pieces, joins, *refs
+    apart, taken, pieces, *refs
 ):
     place = Place(apart)
     qo_hbm, (halo_hbm, own_hbm, *refs) = refs[:taken], refs[taken:]
-    (mine_hbm, back_hbm), refs = refs[:2] if joins else (None, None), refs[2 * joins :]
     ao_hbm, (dhalo_hbm, down_hbm, *refs) = refs[:pieces], refs[pieces:]
-    (kv, qo, ao, dhalo, keys_t, values_t, acc_k, acc_v, exps0, exps1, q_turned, o_turned, mine, back, in_sem, q_sem, out_sem) = refs
+    (kv, qo, ao, dhalo, keys_t, values_t, acc_k, acc_v, exps0, exps1, scores0, scores1, tops, in_sem, q_sem, out_sem) = refs
     rows = qo.shape[0]
     blocks = rows // BLOCK
     whole = WINDOW // BLOCK
-    exps = (exps0, exps1)
+    exps, scores = (exps0, exps1), (scores0, scores1)
 
     def at(i):
         return pl.ds(pl.multiple_of(i * BLOCK, BLOCK), BLOCK)
@@ -81,135 +79,137 @@
     own_copy = pltpu.make_async_copy(own_hbm, kv.at[pl.ds(WINDOW, rows)], in_sem.at[1])
     halo_copy.start()
     own_copy.start()
-    if joins:
-        mine_copy = pltpu.make_async_copy(mine_hbm, mine, in_sem.at[2])
-        back_copy = pltpu.make_async_copy(back_hbm, back, in_sem.at[3])
     for i in range(blocks):
         (qo_copy(i) if taken == 1 else qo_copy(place.member ^ i, i)).start()
-
-    if joins:
-        mine_copy.start()
-        back_copy.start()
 
     ones_row = lax.broadcasted_iota(jnp.int32, (ONES, values_t.shape[1]), 0) == 0
     values_t[HEAD_DIM:, :] = jnp.where(ones_row, 1.0, 0.0).astype(jnp.bfloat16)
     acc_k[:, : WINDOW + BLOCK] = jnp.zeros((HEAD_DIM, WINDOW + BLOCK), jnp.float32)
     acc_v[:, : WINDOW + BLOCK] = jnp.zeros((HEAD_DIM, WINDOW + BLOCK), jnp.float32)
-    exps1[...] = jnp.ones_like(exps1)
-    q_turned[...] = jnp.zeros_like(q_turned)
-    o_turned[...] = jnp.zeros_like(o_turned)
     key_at = lax.broadcasted_iota(jnp.int32, (BLOCK, 2 * BLOCK), 0)
     query_at = lax.broadcasted_iota(jnp.int32, (BLOCK, 2 * BLOCK), 1) & (BLOCK - 1)
     first = place.first
 
-    def turn(target, source):
-        keys_t[:, at(target)] = kv[at(source), :HEAD_DIM].T
-        values_t[:HEAD_DIM, at(target)] = kv[at(source), HEAD_DIM:].T
-
-    halo_copy.wait()
-    own_copy.wait()
-    if joins:
-        mine_copy.wait()
-        back_copy.wait()
-    for c in range(whole + 1):
-        turn(c, c)
-
-    def scores_of(slot, i):
-        q_t, o_t = side_by_side(qo[at(i), :PAIR]), side_by_side(qo[at(i), PAIR:])
-        q_turned[slot] = q_t
-        o_turned[slot] = o_t
-        bias = [
-            jnp.where(first & (i + c < whole), EXCLUDED, 0.0).astype(jnp.float32) for c in range(CHUNKS - 1)
-        ]
-        scores = dot(kv[span(i), :HEAD_DIM], q_t, NN)
-        parts = [scores[c * BLOCK : (c + 1) * BLOCK] for c in range(CHUNKS)]
-        parts[0] = jnp.where(key_at > query_at, parts[0], EXCLUDED)
-        parts[-1] = jnp.where(key_at <= query_at, parts[-1], EXCLUDED)
-        top = jnp.max(parts[-1], axis=0, keepdims=True)
-        for c in range(CHUNKS - 1):
-            top = jnp.maximum(top, jnp.max(parts[c], axis=0, keepdims=True) + bias[c])
-        top = top * EXP2_SCALE
-        return parts, [top - b for b in bias] + [top]
-
-    def exponentials(slot, parts, shifts):
+    def turn(c):
+        keys_t[:, at(c)] = kv[at(c), :HEAD_DIM].T
+        values_t[:HEAD_DIM, at(c)] = kv[at(c), HEAD_DIM:].T
+
+    def bias(i, c):
+        return jnp.where(first & (i + c < whole), EXCLUDED, 0.0).astype(jnp.float32)
+
+    def score_dot(i):
+        return dot(kv[span(i), :HEAD_DIM], side_by_side(qo[at(i), :PAIR]), NN)
+
+    def keep_scores(slot, i, found):
+        top = None
         for c in range(CHUNKS):
-            exps[slot][c * BLOCK : (c + 1) * BLOCK] = jnp.exp2(parts[c] * EXP2_SCALE - shifts[c]).astype(jnp.bfloat16)
-
-    def attended_of(slot, i):
+            part = found[c * BLOCK : (c + 1) * BLOCK]
+            if c == 0:
+                part = jnp.where(key_at > query_at, part, EXCLUDED)
+            if c == CHUNKS - 1:
+                part = jnp.where(key_at <= query_at, part, EXCLUDED)
+            scores[slot][c * BLOCK : (c + 1) * BLOCK] = part
+            high = jnp.max(part, axis=0, keepdims=True)
+            if c < CHUNKS - 1:
+                high = high + bias(i, c)
+            top = high if top is None else jnp.maximum(top, high)
+        tops[slot, :1] = top * EXP2_SCALE
+
+    def exponentials(slot, i):
+        top = tops[slot, :1]
+        for c in range(CHUNKS):
+            part = slice(c * BLOCK, (c + 1) * BLOCK)
+            shift = top - bias(i, c) if c < CHUNKS - 1 else top
+            exps[slot][part] = jnp.exp2(scores[slot][part] * EXP2_SCALE - shift).astype(jnp.bfloat16)
+
+    def attended_of(slot, i, o_t):
         out = dot(values_t[:, span(i)], exps[slot][...], NN)
         inverse = 1.0 / out[HEAD_DIM : HEAD_DIM + 1]
         out = out[:HEAD_DIM] * inverse
-        grad_out = o_turned[slot].astype(jnp.float32)
+        grad_out = o_t.astype(jnp.float32)
         delta = jnp.sum(out * grad_out, axis=0, keepdims=True)
         out = out.astype(jnp.bfloat16)
         ao[at(i), :HEAD_DIM] = out[:, :BLOCK].T
         ao[at(i), HEAD_DIM:PAIR] = out[:, BLOCK:].T
-        o_scaled = (grad_out * inverse).astype(jnp.bfloat16)
-        q_scaled = (q_turned[slot].astype(jnp.float32) * inverse).astype(jnp.bfloat16)
-        return inverse, delta, o_scaled, q_scaled
-
-    def gradients(slot, i, inverse, delta, o_scaled, q_scaled):
-        grad_weights = dot(kv[span(i), HEAD_DIM:], o_turned[slot], NN)
+        return inverse, delta, (grad_out * inverse).astype(jnp.bfloat16)
+
+    def score_gradients(slot, grad_weights, delta):
         grad_scores = []
         for c in range(CHUNKS):
             part = slice(c * BLOCK, (c + 1) * BLOCK)
             grad_scores.append(
                 (exps[slot][part].astype(jnp.float32) * (grad_weights[part] - delta)).astype(jnp.bfloat16)
             )
-        grad_scores = jnp.concatenate(grad_scores, 0)
-        acc_v[:, span(i)] += dot(o_scaled, exps[slot][...], NT)
+        return jnp.concatenate(grad_scores, 0)
+
+    def spend(i, grad_scores, inverse):
+        q_t = side_by_side(qo[at(i), :PAIR])
+        q_scaled = (q_t.astype(jnp.float32) * inverse).astype(jnp.bfloat16)
         grad_q = (dot(keys_t[:, span(i)], grad_scores, NN) * (inverse * SCORE_SCALE)).astype(jnp.bfloat16)
         ao[at(i), PAIR : PAIR + HEAD_DIM] = grad_q[:, :BLOCK].T
-        ao[at(i), PAIR + HEAD_DIM : 2 * PAIR] = grad_q[:, BLOCK:].T
+        ao[at(i), PAIR + HEAD_DIM :] = grad_q[:, BLOCK:].T
         acc_k[:, span(i)] += dot(q_scaled, grad_scores, NT)
 
     def flush(i):
         dhalo[at(i), :HEAD_DIM] = (acc_k[:, at(i)] * SCORE_SCALE).astype(jnp.bfloat16).T
         dhalo[at(i), HEAD_DIM:] = acc_v[:, at(i)].astype(jnp.bfloat16).T
 
-    def join(i):
-        for n, scale in enumerate((SCORE_SCALE, 1.0)):
-            cols = slice(n * HEAD_DIM, (n + 1) * HEAD_DIM)
-            total = (mine[n, :, at(i)] * scale).T + back[at(i), cols].astype(jnp.float32)
-            ao[at(i), 2 * PAIR + n * HEAD_DIM : 2 * PAIR + (n + 1) * HEAD_DIM] = total.astype(jnp.bfloat16)
-
-    def both(slot, i, before):
-        known = attended_of(1 - slot, before)
-        parts, shifts = scores_of(slot, i)
-        exponentials(slot, parts, shifts)
-        gradients(1 - slot, before, *known)
-        flush(before)
-        if joins:
-            join(i)
-        turn(i + whole + 1, jnp.minimum(i + whole + 1, whole + blocks - 1))
-        acc_k[:, at(i + whole + 1)] = jnp.zeros((HEAD_DIM, BLOCK), jnp.float32)
-        acc_v[:, at(i + whole + 1)] = jnp.zeros((HEAD_DIM, BLOCK), jnp.float32)
-
-    def step(j, carry):
-        i = 2 * j
-        qo_copy(i).wait()
-        qo_copy(i + 1).wait()
-        both(0, i, jnp.maximum(i - 1, 0))
-        both(1, i + 1, i)
-
-        @pl.when(j > 0)
-        def _():
-            if pieces == 1:
-                ao_copy(i - 1).start()
-            dhalo_copy(i - 1).start()
-
+    def stages(n, slot, begin=True, middle=True, end=True):
+        if end:
+            o_t = side_by_side(qo[at(n - 2), PAIR:])
+            inverse, delta, o_scaled = attended_of(slot, n - 2, o_t)
+            grad_weights = dot(kv[span(n - 2), HEAD_DIM:], o_t, NN)
+        if begin:
+            found = score_dot(n)
+        if end:
+            grad_scores = score_gradients(slot, grad_weights, delta)
+            acc_v[:, span(n - 2)] += dot(o_scaled, exps[slot][...], NT)
+        if middle:
+            exponentials(1 - slot, n - 1)
+        if begin:
+            keep_scores(slot, n, found)
+        if end:
+            spend(n - 2, grad_scores, inverse)
+            flush(n - 2)
+
+    def extend(c):
+        turn(c)
+        acc_k[:, at(c)] = jnp.zeros((HEAD_DIM, BLOCK), jnp.float32)
+        acc_v[:, at(c)] = jnp.zeros((HEAD_DIM, BLOCK), jnp.float32)
+
+    def send(i):
+        dhalo_copy(i).start()
         if pieces == 1:
             ao_copy(i).start()
-        dhalo_copy(i).start()
+
+    halo_copy.wait()
+    own_copy.wait()
+    qo_copy(0).wait()
+    qo_copy(1).wait()
+    stages(0, 0, middle=False, end=False)
+    stages(1, 1, end=False)
+    for c in range(whole + 1):
+        turn(c)
+
+    def step(j, carry):
+        n = 2 * j
+        qo_copy(n).wait()
+        qo_copy(n + 1).wait()
+        stages(n, 0)
+        extend(n + whole - 1)
+        stages(n + 1, 1)
+        extend(n + whole)
+        send(n - 2)
+        send(n - 1)
         return carry
 
-    lax.fori_loop(0, blocks // 2, step, 0)
-    gradients(1, blocks - 1, *attended_of(1, blocks - 1))
-    flush(blocks - 1)
-    dhalo_copy(blocks - 1).start()
-    if pieces == 1:
-        ao_copy(blocks - 1).start()
-    else:
+    lax.fori_loop(1, blocks // 2, step, 0)
+    stages(blocks, 0, begin=False)
+    extend(blocks + whole - 1)
+    send(blocks - 2)
+    stages(blocks + 1, 1, begin=False, middle=False)
+    send(blocks - 1)
+    if pieces > 1:
         for j in range(pieces):
             piece_copy(j).start()
     own_k = pltpu.make_async_copy(acc_k.at[:, pl.ds(WINDOW, rows)], down_hbm.at[0], in_sem.at[0])
@@ -223,21 +223,20 @@
     own_v.wait()
 
 
-def attention(apart, qo, halo, own, pieces, joined=()):
+def attention(apart, qo, halo, own, pieces):
     rows = own.shape[0]
     blocks = rows // BLOCK
     reach = WINDOW + rows
     bf16, f32 = jnp.bfloat16, jnp.float32
-    width = 2 * PAIR + (PAIR if joined else 0)
-    small = (8, HEAD_DIM)
-    return pl.pallas_call(
-        functools.partial(attention_kernel, apart, len(qo), pieces, len(joined) > 0),
+    width = 2 * PAIR
+    return pl.pallas_call(
+        functools.partial(attention_kernel, apart, len(qo), pieces),
         out_shape=(
             *[jax.ShapeDtypeStruct((rows // pieces, width), bf16)] * pieces,
             jax.ShapeDtypeStruct(halo.shape, bf16),
             jax.ShapeDtypeStruct((2, HEAD_DIM, rows), f32),
         ),
-        in_specs=[ANY] * (len(qo) + 2 + len(joined)),
+        in_specs=[ANY] * (len(qo) + 2),
         out_specs=(HBM,) * (pieces + 2),
         scratch_shapes=[
             pltpu.VMEM((reach, PAIR), bf16),
@@ -250,18 +249,17 @@
             pltpu.VMEM((HEAD_DIM, reach + BLOCK), f32),
             pltpu.VMEM((CHUNKS * BLOCK, 2 * BLOCK), bf16),
             pltpu.VMEM((CHUNKS * BLOCK, 2 * BLOCK), bf16),
-            pltpu.VMEM((2, HEAD_DIM, 2 * BLOCK), bf16),
-            pltpu.VMEM((2, HEAD_DIM, 2 * BLOCK), bf16),
-            pltpu.VMEM((2, HEAD_DIM, rows) if joined else small, f32),
-            pltpu.VMEM((rows, PAIR) if joined else small, bf16),
-            pltpu.SemaphoreType.DMA((4,)),
+            pltpu.VMEM((CHUNKS * BLOCK, 2 * BLOCK), f32),
+            pltpu.VMEM((CHUNKS * BLOCK, 2 * BLOCK), f32),
+            pltpu.VMEM((2, 8, 2 * BLOCK), f32),
+            pltpu.SemaphoreType.DMA((2,)),
             pltpu.SemaphoreType.DMA((blocks,)),
             pltpu.SemaphoreType.DMA((2, blocks)),
         ],
         compiler_params=pltpu.CompilerParams(vmem_limit_bytes=58 * 2**20),
         cost_estimate=pl.CostEstimate(flops=10**10, bytes_accessed=4 * 2**20, transcendentals=0),
         name="attention",
-    )(*qo, halo, own, *joined)
+    )(*qo, halo, own)
 
 
 def interleave_kernel(apart, width, sets, *refs):

time: 106 us -> 105 us (level)
  transfers between devices with their start and end apart: 34 -> 34, of which waited for: 12 -> 12; matrix products, arithmetic and copies ran while one was open for 0% -> 0% of each run, Pallas kernels for 29% -> 28%
where the time goes in v6:
time: 105 us
  starting transfers between devices  43 us (41%)
  Pallas kernels  33.6 us (32%)
  waiting for transfers between devices  24 us (23%)
  local copies, waits for them, and re-layouts  3.28 us (3%)
    ppermute x28, starting transfers between devices, swap(): out[j] = lax.ppermute(piece, ('seq', 'kvh'), [(i, i ^ j) for i in every])  28.2 us
    pallas_call x2, Pallas kernels, attention(): pl.pallas_call(functools.partial(attention_kernel, apart, len(qo), pieces...  24.3 us
    ppermute x28, waiting for transfers between devices, swap(): out[j] = lax.ppermute(piece, ('seq', 'kvh'), [(i, i ^ j) for i in every])  22.3 us
    all_to_all x2, starting transfers between devices, exchange(): lax.all_to_all(x, ('seq', 'kvh'), 0, 0, tiled=True, axis_index_groups=gro...  7.13 us
    pallas_call x2, Pallas kernels, interleave(): pl.pallas_call(functools.partial(interleave_kernel, apart, width, sets),...  5.41 us
    ppermute x2, starting transfers between devices, backward(): lax.ppermute(x, 'seq', [((i + apart) % shards, i) for i in range(shards)])  4.36 us
    unnamed x48, local copies, waits for them, and re-layouts  3.28 us
    ppermute x2, starting transfers between devices, onward(): lax.ppermute(x, 'seq', [(i, (i + apart) % shards) for i in range(shards)])  3.26 us
  transfers between devices with their start and end apart: 34, of which 12 were waited for; matrix products, arithmetic and copies ran while one was open for 0% of the time, Pallas kernels for 28%

profile of v6, /device:TPU:0, one launch (start us, length us, event | category | flops | bytes accessed | tf_op | source)
XLA Modules:
  0.0 104.8 jit_solution(10821118139150793581)
XLA Ops:
  0.6 2.3 %interleave.2 = (bf16[128,512]{1,0:T(8,128)(2,1)}, bf16[128,512]{1,0:T(8,128)(2,1)}, bf16[128,512]{1,0:T(8,128)(2,1)}, bf16[128,512]{1,0:T(8,128)(2,1)}, bf16[12...) custom-call(bf16[128,2048]{1,0:T(8,128)(2,1)} %refs_0_.2, ...), custom_call_target="tpu_custom_call" | custom-call | tf_op jit(solution)/shard_map/interleave/pallas_call | solution.py:302
  2.9 3.0 %collective-permute-start.7 = (bf16[128,512]{1,0:T(8,128)(2,1)}, bf16[128,512]{1,0:T(8,128)(2,1)S(1)}, u32[]{:S(2)}, u32[]{:S(2)}) collective-permute-start(bf16[128,512]{1,0:T(8,128)(2,1)} %get-tuple-element.148), channel_id=1, source_target_pairs={{0,2},{1,3},{2,0},{3,1},{4,6},{5,7},{6,4},{7,5},{8,10},{9,11},{10,... | collective-permute-start | bytes 393224 | tf_op jit(solution)/shard_map/ppermute | solution.py:473
  5.9 1.8 %collective-permute-start = (bf16[128,512]{1,0:T(8,128)(2,1)}, bf16[128,512]{1,0:T(8,128)(2,1)S(1)}, u32[]{:S(2)}, u32[]{:S(2)}) collective-permute-start(bf16[128,512]{1,0:T(8,128)(2,1)} %get-tuple-element.133), channel_id=1, source_target_pairs={{0,5},{1,4},{2,7},{3,6},{4,1},{5,0},{6,3},{7,2},{8,13},{9,12},{10,... | collective-permute-start | bytes 393224 | tf_op jit(solution)/shard_map/ppermute | solution.py:473
  7.8 3.1 %interleave.3 = (bf16[128,512]{1,0:T(8,128)(2,1)}, bf16[128,512]{1,0:T(8,128)(2,1)}, bf16[128,512]{1,0:T(8,128)(2,1)}, bf16[128,512]{1,0:T(8,128)(2,1)}, bf16[12...) custom-call(bf16[128,4096]{1,0:T(8,128)(2,1)} %refs_0_.3, ...), custom_call_target="tpu_custom_call" | custom-call | tf_op jit(solution)/shard_map/interleave/pallas_call | solution.py:302
  11.0 2.8 %collective-permute-start.5 = (bf16[128,512]{1,0:T(8,128)(2,1)S(1)}, bf16[128,512]{1,0:T(8,128)(2,1)S(1)}, u32[]{:S(2)}, u32[]{:S(2)}) collective-permute-start(bf16[128,512]{1,0:T(8,128)(2,1)S(1)} %copy-done.23), channel_id=1, source_target_pairs={{0,6},{1,7},{2,4},{3,5},{4,2},{5,3},{6,0},{7,1},{8,14},{9,15},{10,... | collective-permute-start | bytes 393224 | tf_op jit(solution)/shard_map/ppermute | solution.py:473
  13.9 0.2 collective-permute-start.11
  14.1 6.3 %collective-permute-done.3.refs_4_ = bf16[128,512]{1,0:T(8,128)(2,1)S(1)} collective-permute-done((bf16[128,512]{1,0:T(8,128)(2,1)}, bf16[128,512]{1,0:T(8,128)(2,1)S(1)}, u32[]{:S(2)}, u32[]{:S(2)}) %collective-permute-start.3) | collective-permute-done | bytes 131104 | tf_op jit(solution)/shard_map/ppermute | solution.py:473
  20.5 0.3 assemble.1
  20.8 1.6 %collective-permute-start.14 = (bf16[1024,256]{1,0:T(8,128)(2,1)S(1)}, bf16[1024,256]{1,0:T(8,128)(2,1)S(1)}, u32[]{:S(2)}, u32[]{:S(2)}) collective-permute-start(bf16[1024,256]{1,0:T(8,128)(2,1)S(1)} %get-tuple-element.168.refs_9_), channel_id=1, source_target_pairs={{0,8},{4,12},{8,16},{12,20},{16,24},{20,28},{24,0},{28,4},{1,9},{5... | collective-permute-start | bytes 1572872 | tf_op jit(solution)/shard_map/ppermute | solution.py:478
  22.5 1.5 %collective-permute-start.4 = (bf16[128,512]{1,0:T(8,128)(2,1)S(1)}, bf16[128,512]{1,0:T(8,128)(2,1)S(1)}, u32[]{:S(2)}, u32[]{:S(2)}) collective-permute-start(bf16[128,512]{1,0:T(8,128)(2,1)S(1)} %copy-done.17), channel_id=1, source_target_pairs={{0,2},{1,3},{2,0},{3,1},{4,6},{5,7},{6,4},{7,5},{8,10},{9,11},{10,... | collective-permute-start | bytes 393224 | tf_op jit(solution)/shard_map/ppermute | solution.py:473
  24.0 1.8 %collective-permute-start.9 = (bf16[128,512]{1,0:T(8,128)(2,1)S(1)}, bf16[128,512]{1,0:T(8,128)(2,1)S(1)}, u32[]{:S(2)}, u32[]{:S(2)}) collective-permute-start(bf16[128,512]{1,0:T(8,128)(2,1)S(1)} %copy-done.15), channel_id=1, source_target_pairs={{0,5},{1,4},{2,7},{3,6},{4,1},{5,0},{6,3},{7,2},{8,13},{9,12},{10,... | collective-permute-start | bytes 393224 | tf_op jit(solution)/shard_map/ppermute | solution.py:473
  25.7 0.5 collective-permute-start.6
  26.2 1.7 %collective-permute-done.4.refs_2_ = bf16[128,512]{1,0:T(8,128)(2,1)S(1)} collective-permute-done((bf16[128,512]{1,0:T(8,128)(2,1)S(1)}, bf16[128,512]{1,0:T(8,128)(2,1)S(1)}, u32[]{:S(2)}, u32[]{:S(2)}) %collective-permute-start.4) | collective-permute-done | bytes 131104 | tf_op jit(solution)/shard_map/ppermute | solution.py:473
  27.9 1.8 %collective-permute-done.1.refs_3_ = bf16[128,512]{1,0:T(8,128)(2,1)S(1)} collective-permute-done((bf16[128,512]{1,0:T(8,128)(2,1)S(1)}, bf16[128,512]{1,0:T(8,128)(2,1)S(1)}, u32[]{:S(2)}, u32[]{:S(2)}) %collective-permute-start.1) | collective-permute-done | bytes 131104 | tf_op jit(solution)/shard_map/ppermute | solution.py:473
  29.7 1.5 %collective-permute-start.12 = (bf16[128,512]{1,0:T(8,128)(2,1)S(1)}, bf16[128,512]{1,0:T(8,128)(2,1)}, u32[]{:S(2)}, u32[]{:S(2)}) collective-permute-start(bf16[128,512]{1,0:T(8,128)(2,1)S(1)} %copy-done.9), channel_id=1, source_target_pairs={{0,6},{1,7},{2,4},{3,5},{4,2},{5,3},{6,0},{7,1},{8,14},{9,15},{10,... | collective-permute-start | bytes 393224 | tf_op jit(solution)/shard_map/ppermute | solution.py:473
  31.2 1.0 collective-permute-start.2
  32.3 3.6 %all-to-all-start.1 = ((bf16[8,128,512]{2,1,0:T(8,128)(2,1)}), bf16[8,128,512]{2,1,0:T(8,128)(2,1)S(1)}, u32[]{:S(2)}, u32[]{:S(2)}) async-start(bf16[8,128,512]{2,1,0:T(8,128)(2,1)} %get-tuple-element.171), calls=%async_computation.1 | async-start | bytes 2097152 | tf_op jit(solution)/shard_map/all_to_all | solution.py:460
  35.9 1.6 %collective-permute-start.15 = (bf16[1024,256]{1,0:T(8,128)(2,1)S(1)}, bf16[1024,256]{1,0:T(8,128)(2,1)}, u32[]{:S(2)}, u32[]{:S(2)}) collective-permute-start(bf16[1024,256]{1,0:T(8,128)(2,1)S(1)} %get-tuple-element.172.refs_2_), channel_id=1, source_target_pairs={{0,8},{4,12},{8,16},{12,20},{16,24},{20,28},{24,0},{28,4},{1,9},{5... | collective-permute-start | bytes 1572872 | tf_op jit(solution)/shard_map/ppermute | solution.py:478
  37.5 0.9 collective-permute-done.6.refs_4_
  38.4 0.8 copy-done.7
  39.2 11.8 %attention.2 = (bf16[1024,512]{1,0:T(8,128)(2,1)}, bf16[1024,256]{1,0:T(8,128)(2,1)}, f32[2,128,1024]{2,1,0:T(8,128)}) custom-call(bf16[128,512]{1,0:T(8,128)(2,1)} %get-tuple-element.130.refs_0_, bf16[128,512]{1,0:T(8,128)(2,1)} %collective-permute-done.2.refs_1_, bf16[128,512]{1,0:T(8,128)(2,1)} %copy-done.18, bf16[128,512]{1,0:T(8,128)(2,1)} %copy-done.19, ...), custom_call_target="tpu_custom_call" | custom-call | flops 10000000000 | bytes 4194304 | tf_op jit(solution)/shard_map/attention/pallas_call | solution.py:232
  51.0 2.5 %collective-permute-start.16 = (bf16[1024,256]{1,0:T(8,128)(2,1)}, bf16[1024,256]{1,0:T(8,128)(2,1)S(1)}, u32[]{:S(2)}, u32[]{:S(2)}) collective-permute-start(bf16[1024,256]{1,0:T(8,128)(2,1)} %get-tuple-element.182), channel_id=1, source_target_pairs={{8,0},{12,4},{16,8},{20,12},{24,16},{28,20},{0,24},{4,28},{9,1},{1... | collective-permute-start | bytes 1572872 | tf_op jit(solution)/shard_map/ppermute | solution.py:481
  53.5 1.0 copy-done.6
  54.5 3.6 %all-to-all-start = ((bf16[8,128,512]{2,1,0:T(8,128)(2,1)}), bf16[8,128,512]{2,1,0:T(8,128)(2,1)S(1)}, u32[]{:S(2)}, u32[]{:S(2)}) async-start(bf16[8,128,512]{2,1,0:T(8,128)(2,1)} %bitcast.2), calls=%async_computation | async-start | bytes 2097152 | tf_op jit(solution)/shard_map/all_to_all | solution.py:460
  58.1 12.5 %attention.3 = (bf16[128,512]{1,0:T(8,128)(2,1)}, bf16[128,512]{1,0:T(8,128)(2,1)}, bf16[128,512]{1,0:T(8,128)(2,1)}, bf16[128,512]{1,0:T(8,128)(2,1)}, bf16[128...) custom-call(bf16[1024,512]{1,0:T(8,128)(2,1)} %bitcast.3, ...), custom_call_target="tpu_custom_call" | custom-call | flops 10000000000 | bytes 4194304 | tf_op jit(solution)/shard_map/attention/pallas_call | solution.py:232
  70.6 1.8 %collective-permute-start.17 = (bf16[1024,256]{1,0:T(8,128)(2,1)}, bf16[1024,256]{1,0:T(8,128)(2,1)S(1)}, u32[]{:S(2)}, u32[]{:S(2)}) collective-permute-start(bf16[1024,256]{1,0:T(8,128)(2,1)} %get-tuple-element.186), channel_id=1, source_target_pairs={{8,0},{12,4},{16,8},{20,12},{24,16},{28,20},{0,24},{4,28},{9,1},{1... | collective-permute-start | bytes 1572872 | tf_op jit(solution)/shard_map/ppermute | solution.py:481
  72.4 1.9 %collective-permute-start.18 = (bf16[128,512]{1,0:T(8,128)(2,1)}, bf16[128,512]{1,0:T(8,128)(2,1)S(1)}, u32[]{:S(2)}, u32[]{:S(2)}) collective-permute-start(bf16[128,512]{1,0:T(8,128)(2,1)} %get-tuple-element.199), channel_id=1, source_target_pairs={{0,4},{1,5},{2,6},{3,7},{4,0},{5,1},{6,2},{7,3},{8,12},{9,13},{10,... | collective-permute-start | bytes 393224 | tf_op jit(solution)/shard_map/ppermute | solution.py:473
  74.3 1.5 %collective-permute-start.20 = (bf16[128,512]{1,0:T(8,128)(2,1)}, bf16[128,512]{1,0:T(8,128)(2,1)S(1)}, u32[]{:S(2)}, u32[]{:S(2)}) collective-permute-start(bf16[128,512]{1,0:T(8,128)(2,1)} %get-tuple-element.203), channel_id=1, source_target_pairs={{0,2},{1,3},{2,0},{3,1},{4,6},{5,7},{6,4},{7,5},{8,10},{9,11},{10,... | collective-permute-start | bytes 393224 | tf_op jit(solution)/shard_map/ppermute | solution.py:473
  75.8 0.4 collective-permute-start.22
  76.2 1.2 %copy-done.1 = f32[2,128,1024]{2,1,0:T(8,128)S(1)} copy-done((f32[2,128,1024]{2,1,0:T(8,128)S(1)}, f32[2,128,1024]{2,1,0:T(8,128)}, u32[]{:S(2)}) %copy-start.1) | copy-done | bytes 1048600
  77.4 0.6 settle.1
  78.3 0.3 collective-permute-start.19
  78.6 1.5 %collective-permute-done.20.refs_2_ = bf16[128,512]{1,0:T(8,128)(2,1)S(1)} collective-permute-done((bf16[128,512]{1,0:T(8,128)(2,1)}, bf16[128,512]{1,0:T(8,128)(2,1)S(1)}, u32[]{:S(2)}, u32[]{:S(2)}) %collective-permute-start.20) | collective-permute-done | bytes 131104 | tf_op jit(solution)/shard_map/ppermute | solution.py:473
  80.1 2.3 %collective-permute-start.23 = (bf16[128,512]{1,0:T(8,128)(2,1)S(1)}, bf16[128,512]{1,0:T(8,128)(2,1)S(1)}, u32[]{:S(2)}, u32[]{:S(2)}) collective-permute-start(bf16[128,512]{1,0:T(8,128)(2,1)S(1)} %copy-done.13), channel_id=1, source_target_pairs={{0,6},{1,7},{2,4},{3,5},{4,2},{5,3},{6,0},{7,1},{8,14},{9,15},{10,... | collective-permute-start | bytes 393224 | tf_op jit(solution)/shard_map/ppermute | solution.py:473
  82.4 1.1 %collective-permute-start.24 = (bf16[128,512]{1,0:T(8,128)(2,1)S(1)}, bf16[128,512]{1,0:T(8,128)(2,1)S(1)}, u32[]{:S(2)}, u32[]{:S(2)}) collective-permute-start(bf16[128,512]{1,0:T(8,128)(2,1)S(1)} %copy-done.11), channel_id=1, source_target_pairs={{0,7},{1,6},{2,5},{3,4},{4,3},{5,2},{6,1},{7,0},{8,15},{9,14},{10,... | collective-permute-start | bytes 393224 | tf_op jit(solution)/shard_map/ppermute | solution.py:473
  83.5 1.7 %collective-permute-done.17.back_ref = bf16[1024,256]{1,0:T(8,128)(2,1)S(1)} collective-permute-done((bf16[1024,256]{1,0:T(8,128)(2,1)}, bf16[1024,256]{1,0:T(8,128)(2,1)S(1)}, u32[]{:S(2)}, u32[]{:S(2)}) %collective-permute-start.17) | collective-permute-done | bytes 524320 | tf_op jit(solution)/shard_map/ppermute | solution.py:481
  85.4 1.7 %collective-permute-start.27 = (bf16[128,512]{1,0:T(8,128)(2,1)S(1)}, bf16[128,512]{1,0:T(8,128)(2,1)S(1)}, u32[]{:S(2)}, u32[]{:S(2)}) collective-permute-start(bf16[128,512]{1,0:T(8,128)(2,1)S(1)} %get-tuple-element.227), channel_id=1, source_target_pairs={{0,2},{1,3},{2,0},{3,1},{4,6},{5,7},{6,4},{7,5},{8,10},{9,11},{10,... | collective-permute-start | bytes 393224 | tf_op jit(solution)/shard_map/ppermute | solution.py:473
  87.1 1.6 %collective-permute-start.30 = (bf16[128,512]{1,0:T(8,128)(2,1)S(1)}, bf16[128,512]{1,0:T(8,128)(2,1)S(1)}, u32[]{:S(2)}, u32[]{:S(2)}) collective-permute-start(bf16[128,512]{1,0:T(8,128)(2,1)S(1)} %get-tuple-element.232), channel_id=1, source_target_pairs={{0,6},{1,7},{2,4},{3,5},{4,2},{5,3},{6,0},{7,1},{8,14},{9,15},{10,... | collective-permute-start | bytes 393224 | tf_op jit(solution)/shard_map/ppermute | solution.py:473
  88.7 0.5 collective-permute-start.28
  89.3 2.0 %collective-permute-start.29 = (bf16[128,512]{1,0:T(8,128)(2,1)S(1)}, bf16[128,512]{1,0:T(8,128)(2,1)S(1)}, u32[]{:S(2)}, u32[]{:S(2)}) collective-permute-start(bf16[128,512]{1,0:T(8,128)(2,1)S(1)} %get-tuple-element.231), channel_id=1, source_target_pairs={{0,5},{1,4},{2,7},{3,6},{4,1},{5,0},{6,3},{7,2},{8,13},{9,12},{10,... | collective-permute-start | bytes 393224 | tf_op jit(solution)/shard_map/ppermute | solution.py:473
  91.3 0.6 collective-permute-done.27.refs_2_
  92.0 2.3 %collective-permute-done.25.refs_3_ = bf16[128,512]{1,0:T(8,128)(2,1)S(1)} collective-permute-done((bf16[128,512]{1,0:T(8,128)(2,1)S(1)}, bf16[128,512]{1,0:T(8,128)(2,1)S(1)}, u32[]{:S(2)}, u32[]{:S(2)}) %collective-permute-start.25) | collective-permute-done | bytes 131104 | tf_op jit(solution)/shard_map/ppermute | solution.py:473
  94.4 0.4 collective-permute-start.26
  94.8 1.6 %spread.1 = (bf16[128,4096]{1,0:T(8,128)(2,1)}, bf16[128,4096]{1,0:T(8,128)(2,1)}) custom-call(bf16[8,128,512]{2,1,0:T(8,128)(2,1)S(1)} %all-to-all-done.x_ref, bf16[128,512]{1,0:T(8,128)(2,1)S(1)} %copy-done.2, bf16[128,512]{1,0:T(8,128)(2,1)S(1)} %collective-permute-done.19.refs_1_, bf16[128,512]{1,0:T(8,128)(2,1)S(1)} %collective-permute-done.20.refs_2_, ...), custom_call_target="tpu_custom_call" | custom-call | tf_op jit(solution)/shard_map/spread/pallas_call | solution.py:371
  96.4 2.1 %collective-permute-done.30.refs_6_ = bf16[128,512]{1,0:T(8,128)(2,1)S(1)} collective-permute-done((bf16[128,512]{1,0:T(8,128)(2,1)S(1)}, bf16[128,512]{1,0:T(8,128)(2,1)S(1)}, u32[]{:S(2)}, u32[]{:S(2)}) %collective-permute-start.30) | collective-permute-done | bytes 131104 | tf_op jit(solution)/shard_map/ppermute | solution.py:473
  98.5 2.0 %collective-permute-done.28.refs_4_ = bf16[128,512]{1,0:T(8,128)(2,1)S(1)} collective-permute-done((bf16[128,512]{1,0:T(8,128)(2,1)S(1)}, bf16[128,512]{1,0:T(8,128)(2,1)S(1)}, u32[]{:S(2)}, u32[]{:S(2)}) %collective-permute-start.28) | collective-permute-done | bytes 131104 | tf_op jit(solution)/shard_map/ppermute | solution.py:473
  100.5 3.0 %collective-permute-done.29.refs_5_ = bf16[128,512]{1,0:T(8,128)(2,1)S(1)} collective-permute-done((bf16[128,512]{1,0:T(8,128)(2,1)S(1)}, bf16[128,512]{1,0:T(8,128)(2,1)S(1)}, u32[]{:S(2)}, u32[]{:S(2)}) %collective-permute-start.29) | collective-permute-done | bytes 131104 | tf_op jit(solution)/shard_map/ppermute | solution.py:473
  103.5 1.3 %unpack.1 = (bf16[128,2048]{1,0:T(8,128)(2,1)}, bf16[128,2048]{1,0:T(8,128)(2,1)}) custom-call(bf16[128,512]{1,0:T(8,128)(2,1)S(1)} %get-tuple-element.222.refs_0_, bf16[128,512]{1,0:T(8,128)(2,1)S(1)} %collective-permute-done.26.refs_1_, bf16[128,512]{1,0:T(8,128)(2,1)S(1)} %collective-permute-done.27.refs_2_, ...), custom_call_target="tpu_custom_call" | custom-call | tf_op jit(solution)/shard_map/unpack/pallas_call | solution.py:442
  (77 shorter events, 0.9 us)
Async XLA Ops:
  2.9 10.9 %collective-permute-start.7 = (bf16[128,512]{1,0:T(8,128)(2,1)}, bf16[128,512]{1,0:T(8,128)(2,1)S(1)}, u32[]{:S(2)}, u32[]{:S(2)}) collective-permute-start(bf16[128,512]{1,0:T(8,128)(2,1)} %get-tuple-element.148), channel_id=1, source_target_pairs={{0,2},{1,3},{2,0},{3,1},{4,6},{5,7},{6,4},{7,5},{8,10},{9,11},{10,... | collective-permute-start | bytes 393224 | tf_op jit(solution)/shard_map/ppermute | solution.py:473
  5.9 7.9 %collective-permute-start.10 = (bf16[128,512]{1,0:T(8,128)(2,1)}, bf16[128,512]{1,0:T(8,128)(2,1)S(1)}, u32[]{:S(2)}, u32[]{:S(2)}) collective-permute-start(bf16[128,512]{1,0:T(8,128)(2,1)} %get-tuple-element.154), channel_id=1, source_target_pairs={{0,3},{1,2},{2,1},{3,0},{4,7},{5,6},{6,5},{7,4},{8,11},{9,10},{10,... | collective-permute-start | bytes 393224 | tf_op jit(solution)/shard_map/ppermute | solution.py:473
  5.9 8.2 %collective-permute-start = (bf16[128,512]{1,0:T(8,128)(2,1)}, bf16[128,512]{1,0:T(8,128)(2,1)S(1)}, u32[]{:S(2)}, u32[]{:S(2)}) collective-permute-start(bf16[128,512]{1,0:T(8,128)(2,1)} %get-tuple-element.133), channel_id=1, source_target_pairs={{0,5},{1,4},{2,7},{3,6},{4,1},{5,0},{6,3},{7,2},{8,13},{9,12},{10,... | collective-permute-start | bytes 393224 | tf_op jit(solution)/shard_map/ppermute | solution.py:473
  7.7 6.1 %copy-start.22 = (bf16[128,512]{1,0:T(8,128)(2,1)S(1)}, bf16[128,512]{1,0:T(8,128)(2,1)}, u32[]{:S(2)}) copy-start(bf16[128,512]{1,0:T(8,128)(2,1)} %get-tuple-element.149) | copy-start | bytes 393220
  7.7 6.1 %copy-start.21 = (bf16[128,512]{1,0:T(8,128)(2,1)S(1)}, bf16[128,512]{1,0:T(8,128)(2,1)}, u32[]{:S(2)}) copy-start(bf16[128,512]{1,0:T(8,128)(2,1)} %get-tuple-element.155) | copy-start | bytes 393220
  7.7 12.7 %copy-start.3 = (bf16[128,512]{1,0:T(8,128)(2,1)S(1)}, bf16[128,512]{1,0:T(8,128)(2,1)}, u32[]{:S(2)}) copy-start(bf16[128,512]{1,0:T(8,128)(2,1)} %get-tuple-element.157.refs_0_) | copy-start | bytes 393220
  7.7 12.7 %collective-permute-start.3 = (bf16[128,512]{1,0:T(8,128)(2,1)}, bf16[128,512]{1,0:T(8,128)(2,1)S(1)}, u32[]{:S(2)}, u32[]{:S(2)}) collective-permute-start(bf16[128,512]{1,0:T(8,128)(2,1)} %get-tuple-element.138), channel_id=1, source_target_pairs={{0,4},{1,5},{2,6},{3,7},{4,0},{5,1},{6,2},{7,3},{8,12},{9,13},{10,... | collective-permute-start | bytes 393224 | tf_op jit(solution)/shard_map/ppermute | solution.py:473
  11.0 9.4 %collective-permute-start.5 = (bf16[128,512]{1,0:T(8,128)(2,1)S(1)}, bf16[128,512]{1,0:T(8,128)(2,1)S(1)}, u32[]{:S(2)}, u32[]{:S(2)}) collective-permute-start(bf16[128,512]{1,0:T(8,128)(2,1)S(1)} %copy-done.23), channel_id=1, source_target_pairs={{0,6},{1,7},{2,4},{3,5},{4,2},{5,3},{6,0},{7,1},{8,14},{9,15},{10,... | collective-permute-start | bytes 393224 | tf_op jit(solution)/shard_map/ppermute | solution.py:473
  13.8 6.6 %collective-permute-start.8 = (bf16[128,512]{1,0:T(8,128)(2,1)S(1)}, bf16[128,512]{1,0:T(8,128)(2,1)S(1)}, u32[]{:S(2)}, u32[]{:S(2)}) collective-permute-start(bf16[128,512]{1,0:T(8,128)(2,1)S(1)} %copy-done.22), channel_id=1, source_target_pairs={{0,7},{1,6},{2,5},{3,4},{4,3},{5,2},{6,1},{7,0},{8,15},{9,14},{10,... | collective-permute-start | bytes 393224 | tf_op jit(solution)/shard_map/ppermute | solution.py:473
  13.9 6.5 %collective-permute-start.11 = (bf16[128,512]{1,0:T(8,128)(2,1)S(1)}, bf16[128,512]{1,0:T(8,128)(2,1)S(1)}, u32[]{:S(2)}, u32[]{:S(2)}) collective-permute-start(bf16[128,512]{1,0:T(8,128)(2,1)S(1)} %copy-done.21), channel_id=1, source_target_pairs={{0,1},{1,0},{2,3},{3,2},{4,5},{5,4},{6,7},{7,6},{8,9},{9,8},{10,11... | collective-permute-start | bytes 393224 | tf_op jit(solution)/shard_map/ppermute | solution.py:473
  20.4 3.5 %copy-start.16 = (bf16[128,512]{1,0:T(8,128)(2,1)S(1)}, bf16[128,512]{1,0:T(8,128)(2,1)}, u32[]{:S(2)}) copy-start(bf16[128,512]{1,0:T(8,128)(2,1)} %get-tuple-element.134) | copy-start | bytes 393220
  20.5 5.3 %copy-start.10 = (bf16[128,512]{1,0:T(8,128)(2,1)S(1)}, bf16[128,512]{1,0:T(8,128)(2,1)}, u32[]{:S(2)}) copy-start(bf16[128,512]{1,0:T(8,128)(2,1)} %get-tuple-element.144) | copy-start | bytes 393220
  20.5 7.5 %copy-start.12 = (bf16[128,512]{1,0:T(8,128)(2,1)S(1)}, bf16[128,512]{1,0:T(8,128)(2,1)}, u32[]{:S(2)}) copy-start(bf16[128,512]{1,0:T(8,128)(2,1)} %get-tuple-element.166) | copy-start | bytes 393220
  20.5 9.3 %copy-start.9 = (bf16[128,512]{1,0:T(8,128)(2,1)S(1)}, bf16[128,512]{1,0:T(8,128)(2,1)}, u32[]{:S(2)}) copy-start(bf16[128,512]{1,0:T(8,128)(2,1)} %get-tuple-element.156) | copy-start | bytes 393220
  20.5 10.8 %copy-start.8 = (bf16[128,512]{1,0:T(8,128)(2,1)S(1)}, bf16[128,512]{1,0:T(8,128)(2,1)}, u32[]{:S(2)}) copy-start(bf16[128,512]{1,0:T(8,128)(2,1)} %get-tuple-element.135) | copy-start | bytes 393220
  20.8 11.5 %copy-start.5 = (bf16[1024,256]{1,0:T(8,128)(2,1)}, bf16[1024,256]{1,0:T(8,128)(2,1)S(1)}, u32[]{:S(2)}) copy-start(bf16[1024,256]{1,0:T(8,128)(2,1)S(1)} %get-tuple-element.168.refs_9_) | copy-start | bytes 1572868
  20.8 15.0 %copy-start.4 = (bf16[1024,256]{1,0:T(8,128)(2,1)}, bf16[1024,256]{1,0:T(8,128)(2,1)S(1)}, u32[]{:S(2)}) copy-start(bf16[1024,256]{1,0:T(8,128)(2,1)S(1)} %get-tuple-element.172.refs_2_) | copy-start | bytes 1572868
  20.8 17.5 %collective-permute-start.14 = (bf16[1024,256]{1,0:T(8,128)(2,1)S(1)}, bf16[1024,256]{1,0:T(8,128)(2,1)S(1)}, u32[]{:S(2)}, u32[]{:S(2)}) collective-permute-start(bf16[1024,256]{1,0:T(8,128)(2,1)S(1)} %get-tuple-element.168.refs_9_), channel_id=1, source_target_pairs={{0,8},{4,12},{8,16},{12,20},{16,24},{20,28},{24,0},{28,4},{1,9},{5... | collective-permute-start | bytes 1572872 | tf_op jit(solution)/shard_map/ppermute | solution.py:478
  22.5 5.5 %collective-permute-start.4 = (bf16[128,512]{1,0:T(8,128)(2,1)S(1)}, bf16[128,512]{1,0:T(8,128)(2,1)S(1)}, u32[]{:S(2)}, u32[]{:S(2)}) collective-permute-start(bf16[128,512]{1,0:T(8,128)(2,1)S(1)} %copy-done.17), channel_id=1, source_target_pairs={{0,2},{1,3},{2,0},{3,1},{4,6},{5,7},{6,4},{7,5},{8,10},{9,11},{10,... | collective-permute-start | bytes 393224 | tf_op jit(solution)/shard_map/ppermute | solution.py:473
  24.0 5.8 %collective-permute-start.1 = (bf16[128,512]{1,0:T(8,128)(2,1)S(1)}, bf16[128,512]{1,0:T(8,128)(2,1)S(1)}, u32[]{:S(2)}, u32[]{:S(2)}) collective-permute-start(bf16[128,512]{1,0:T(8,128)(2,1)S(1)} %copy-done.16), channel_id=1, source_target_pairs={{0,3},{1,2},{2,1},{3,0},{4,7},{5,6},{6,5},{7,4},{8,11},{9,10},{10,... | collective-permute-start | bytes 393224 | tf_op jit(solution)/shard_map/ppermute | solution.py:473
  24.0 7.3 %collective-permute-start.9 = (bf16[128,512]{1,0:T(8,128)(2,1)S(1)}, bf16[128,512]{1,0:T(8,128)(2,1)S(1)}, u32[]{:S(2)}, u32[]{:S(2)}) collective-permute-start(bf16[128,512]{1,0:T(8,128)(2,1)S(1)} %copy-done.15), channel_id=1, source_target_pairs={{0,5},{1,4},{2,7},{3,6},{4,1},{5,0},{6,3},{7,2},{8,13},{9,12},{10,... | collective-permute-start | bytes 393224 | tf_op jit(solution)/shard_map/ppermute | solution.py:473
  25.7 12.6 %collective-permute-start.6 = (bf16[128,512]{1,0:T(8,128)(2,1)S(1)}, bf16[128,512]{1,0:T(8,128)(2,1)}, u32[]{:S(2)}, u32[]{:S(2)}) collective-permute-start(bf16[128,512]{1,0:T(8,128)(2,1)S(1)} %copy-done.10), channel_id=1, source_target_pairs={{0,4},{1,5},{2,6},{3,7},{4,0},{5,1},{6,2},{7,3},{8,12},{9,13},{10,... | collective-permute-start | bytes 393224 | tf_op jit(solution)/shard_map/ppermute | solution.py:473
  27.9 4.3 %copy-start.18 = (bf16[128,512]{1,0:T(8,128)(2,1)}, bf16[128,512]{1,0:T(8,128)(2,1)S(1)}, u32[]{:S(2)}) copy-start(bf16[128,512]{1,0:T(8,128)(2,1)S(1)} %collective-permute-done.4.refs_2_) | copy-start | bytes 393220
  27.9 7.9 %collective-permute-start.13 = (bf16[128,512]{1,0:T(8,128)(2,1)S(1)}, bf16[128,512]{1,0:T(8,128)(2,1)}, u32[]{:S(2)}, u32[]{:S(2)}) collective-permute-start(bf16[128,512]{1,0:T(8,128)(2,1)S(1)} %copy-done.12), channel_id=1, source_target_pairs={{0,7},{1,6},{2,5},{3,4},{4,3},{5,2},{6,1},{7,0},{8,15},{9,14},{10,... | collective-permute-start | bytes 393224 | tf_op jit(solution)/shard_map/ppermute | solution.py:473
  29.7 8.6 %collective-permute-start.12 = (bf16[128,512]{1,0:T(8,128)(2,1)S(1)}, bf16[128,512]{1,0:T(8,128)(2,1)}, u32[]{:S(2)}, u32[]{:S(2)}) collective-permute-start(bf16[128,512]{1,0:T(8,128)(2,1)S(1)} %copy-done.9), channel_id=1, source_target_pairs={{0,6},{1,7},{2,4},{3,5},{4,2},{5,3},{6,0},{7,1},{8,14},{9,15},{10,... | collective-permute-start | bytes 393224 | tf_op jit(solution)/shard_map/ppermute | solution.py:473
  31.2 7.1 %collective-permute-start.2 = (bf16[128,512]{1,0:T(8,128)(2,1)S(1)}, bf16[128,512]{1,0:T(8,128)(2,1)}, u32[]{:S(2)}, u32[]{:S(2)}) collective-permute-start(bf16[128,512]{1,0:T(8,128)(2,1)S(1)} %copy-done.8), channel_id=1, source_target_pairs={{0,1},{1,0},{2,3},{3,2},{4,5},{5,4},{6,7},{7,6},{8,9},{9,8},{10,11... | collective-permute-start | bytes 393224 | tf_op jit(solution)/shard_map/ppermute | solution.py:473
  32.3 21.2 %all-to-all-start.1 = ((bf16[8,128,512]{2,1,0:T(8,128)(2,1)}), bf16[8,128,512]{2,1,0:T(8,128)(2,1)S(1)}, u32[]{:S(2)}, u32[]{:S(2)}) async-start(bf16[8,128,512]{2,1,0:T(8,128)(2,1)} %get-tuple-element.171), calls=%async_computation.1 | async-start | bytes 2097152 | tf_op jit(solution)/shard_map/all_to_all | solution.py:460
  35.9 22.2 %collective-permute-start.15 = (bf16[1024,256]{1,0:T(8,128)(2,1)S(1)}, bf16[1024,256]{1,0:T(8,128)(2,1)}, u32[]{:S(2)}, u32[]{:S(2)}) collective-permute-start(bf16[1024,256]{1,0:T(8,128)(2,1)S(1)} %get-tuple-element.172.refs_2_), channel_id=1, source_target_pairs={{0,8},{4,12},{8,16},{12,20},{16,24},{20,28},{24,0},{28,4},{1,9},{5... | collective-permute-start | bytes 1572872 | tf_op jit(solution)/shard_map/ppermute | solution.py:478
  51.0 21.5 %collective-permute-start.16 = (bf16[1024,256]{1,0:T(8,128)(2,1)}, bf16[1024,256]{1,0:T(8,128)(2,1)S(1)}, u32[]{:S(2)}, u32[]{:S(2)}) collective-permute-start(bf16[1024,256]{1,0:T(8,128)(2,1)} %get-tuple-element.182), channel_id=1, source_target_pairs={{8,0},{12,4},{16,8},{20,12},{24,16},{28,20},{0,24},{4,28},{9,1},{1... | collective-permute-start | bytes 1572872 | tf_op jit(solution)/shard_map/ppermute | solution.py:481
  54.5 30.9 %all-to-all-start = ((bf16[8,128,512]{2,1,0:T(8,128)(2,1)}), bf16[8,128,512]{2,1,0:T(8,128)(2,1)S(1)}, u32[]{:S(2)}, u32[]{:S(2)}) async-start(bf16[8,128,512]{2,1,0:T(8,128)(2,1)} %bitcast.2), calls=%async_computation | async-start | bytes 2097152 | tf_op jit(solution)/shard_map/all_to_all | solution.py:460
  58.0 18.2 %copy-start = (f32[2,128,1024]{2,1,0:T(8,128)S(1)}, f32[2,128,1024]{2,1,0:T(8,128)}, u32[]{:S(2)}) copy-start(f32[2,128,1024]{2,1,0:T(8,128)} %get-tuple-element.170.own0) | copy-start | bytes 3145732
  70.6 14.7 %collective-permute-start.17 = (bf16[1024,256]{1,0:T(8,128)(2,1)}, bf16[1024,256]{1,0:T(8,128)(2,1)S(1)}, u32[]{:S(2)}, u32[]{:S(2)}) collective-permute-start(bf16[1024,256]{1,0:T(8,128)(2,1)} %get-tuple-element.186), channel_id=1, source_target_pairs={{8,0},{12,4},{16,8},{20,12},{24,16},{28,20},{0,24},{4,28},{9,1},{1... | collective-permute-start | bytes 1572872 | tf_op jit(solution)/shard_map/ppermute | solution.py:481
  72.4 5.7 %collective-permute-start.18 = (bf16[128,512]{1,0:T(8,128)(2,1)}, bf16[128,512]{1,0:T(8,128)(2,1)S(1)}, u32[]{:S(2)}, u32[]{:S(2)}) collective-permute-start(bf16[128,512]{1,0:T(8,128)(2,1)} %get-tuple-element.199), channel_id=1, source_target_pairs={{0,4},{1,5},{2,6},{3,7},{4,0},{5,1},{6,2},{7,3},{8,12},{9,13},{10,... | collective-permute-start | bytes 393224 | tf_op jit(solution)/shard_map/ppermute | solution.py:473
  74.3 5.7 %collective-permute-start.20 = (bf16[128,512]{1,0:T(8,128)(2,1)}, bf16[128,512]{1,0:T(8,128)(2,1)S(1)}, u32[]{:S(2)}, u32[]{:S(2)}) collective-permute-start(bf16[128,512]{1,0:T(8,128)(2,1)} %get-tuple-element.203), channel_id=1, source_target_pairs={{0,2},{1,3},{2,0},{3,1},{4,6},{5,7},{6,4},{7,5},{8,10},{9,11},{10,... | collective-permute-start | bytes 393224 | tf_op jit(solution)/shard_map/ppermute | solution.py:473
  75.8 6.6 %collective-permute-start.21 = (bf16[128,512]{1,0:T(8,128)(2,1)}, bf16[128,512]{1,0:T(8,128)(2,1)S(1)}, u32[]{:S(2)}, u32[]{:S(2)}) collective-permute-start(bf16[128,512]{1,0:T(8,128)(2,1)} %get-tuple-element.206), channel_id=1, source_target_pairs={{0,3},{1,2},{2,1},{3,0},{4,7},{5,6},{6,5},{7,4},{8,11},{9,10},{10,... | collective-permute-start | bytes 393224 | tf_op jit(solution)/shard_map/ppermute | solution.py:473
  75.8 11.3 %collective-permute-start.22 = (bf16[128,512]{1,0:T(8,128)(2,1)}, bf16[128,512]{1,0:T(8,128)(2,1)S(1)}, u32[]{:S(2)}, u32[]{:S(2)}) collective-permute-start(bf16[128,512]{1,0:T(8,128)(2,1)} %get-tuple-element.212), channel_id=1, source_target_pairs={{0,5},{1,4},{2,7},{3,6},{4,1},{5,0},{6,3},{7,2},{8,13},{9,12},{10,... | collective-permute-start | bytes 393224 | tf_op jit(solution)/shard_map/ppermute | solution.py:473
  77.4 5.0 %copy-start.11 = (bf16[128,512]{1,0:T(8,128)(2,1)S(1)}, bf16[128,512]{1,0:T(8,128)(2,1)}, u32[]{:S(2)}) copy-start(bf16[128,512]{1,0:T(8,128)(2,1)} %get-tuple-element.218) | copy-start | bytes 393220
  78.3 8.8 %collective-permute-start.19 = (bf16[128,512]{1,0:T(8,128)(2,1)S(1)}, bf16[128,512]{1,0:T(8,128)(2,1)S(1)}, u32[]{:S(2)}, u32[]{:S(2)}) collective-permute-start(bf16[128,512]{1,0:T(8,128)(2,1)S(1)} %copy-done.14), channel_id=1, source_target_pairs={{0,1},{1,0},{2,3},{3,2},{4,5},{5,4},{6,7},{7,6},{8,9},{9,8},{10,11... | collective-permute-start | bytes 393224 | tf_op jit(solution)/shard_map/ppermute | solution.py:473
  80.1 8.6 %collective-permute-start.23 = (bf16[128,512]{1,0:T(8,128)(2,1)S(1)}, bf16[128,512]{1,0:T(8,128)(2,1)S(1)}, u32[]{:S(2)}, u32[]{:S(2)}) collective-permute-start(bf16[128,512]{1,0:T(8,128)(2,1)S(1)} %copy-done.13), channel_id=1, source_target_pairs={{0,6},{1,7},{2,4},{3,5},{4,2},{5,3},{6,0},{7,1},{8,14},{9,15},{10,... | collective-permute-start | bytes 393224 | tf_op jit(solution)/shard_map/ppermute | solution.py:473
  82.4 6.9 %collective-permute-start.24 = (bf16[128,512]{1,0:T(8,128)(2,1)S(1)}, bf16[128,512]{1,0:T(8,128)(2,1)S(1)}, u32[]{:S(2)}, u32[]{:S(2)}) collective-permute-start(bf16[128,512]{1,0:T(8,128)(2,1)S(1)} %copy-done.11), channel_id=1, source_target_pairs={{0,7},{1,6},{2,5},{3,4},{4,3},{5,2},{6,1},{7,0},{8,15},{9,14},{10,... | collective-permute-start | bytes 393224 | tf_op jit(solution)/shard_map/ppermute | solution.py:473
  85.2 9.6 %copy-start.2 = (bf16[128,512]{1,0:T(8,128)(2,1)S(1)}, bf16[128,512]{1,0:T(8,128)(2,1)}, u32[]{:S(2)}) copy-start(bf16[128,512]{1,0:T(8,128)(2,1)} %get-tuple-element.196.refs_0_) | copy-start | bytes 393220
  85.4 6.5 %collective-permute-start.27 = (bf16[128,512]{1,0:T(8,128)(2,1)S(1)}, bf16[128,512]{1,0:T(8,128)(2,1)S(1)}, u32[]{:S(2)}, u32[]{:S(2)}) collective-permute-start(bf16[128,512]{1,0:T(8,128)(2,1)S(1)} %get-tuple-element.227), channel_id=1, source_target_pairs={{0,2},{1,3},{2,0},{3,1},{4,6},{5,7},{6,4},{7,5},{8,10},{9,11},{10,... | collective-permute-start | bytes 393224 | tf_op jit(solution)/shard_map/ppermute | solution.py:473
  87.1 7.3 %collective-permute-start.25 = (bf16[128,512]{1,0:T(8,128)(2,1)S(1)}, bf16[128,512]{1,0:T(8,128)(2,1)S(1)}, u32[]{:S(2)}, u32[]{:S(2)}) collective-permute-start(bf16[128,512]{1,0:T(8,128)(2,1)S(1)} %get-tuple-element.224), channel_id=1, source_target_pairs={{0,3},{1,2},{2,1},{3,0},{4,7},{5,6},{6,5},{7,4},{8,11},{9,10},{10,... | collective-permute-start | bytes 393224 | tf_op jit(solution)/shard_map/ppermute | solution.py:473
  87.1 11.4 %collective-permute-start.30 = (bf16[128,512]{1,0:T(8,128)(2,1)S(1)}, bf16[128,512]{1,0:T(8,128)(2,1)S(1)}, u32[]{:S(2)}, u32[]{:S(2)}) collective-permute-start(bf16[128,512]{1,0:T(8,128)(2,1)S(1)} %get-tuple-element.232), channel_id=1, source_target_pairs={{0,6},{1,7},{2,4},{3,5},{4,2},{5,3},{6,0},{7,1},{8,14},{9,15},{10,... | collective-permute-start | bytes 393224 | tf_op jit(solution)/shard_map/ppermute | solution.py:473
  88.7 11.8 %collective-permute-start.28 = (bf16[128,512]{1,0:T(8,128)(2,1)S(1)}, bf16[128,512]{1,0:T(8,128)(2,1)S(1)}, u32[]{:S(2)}, u32[]{:S(2)}) collective-permute-start(bf16[128,512]{1,0:T(8,128)(2,1)S(1)} %get-tuple-element.230), channel_id=1, source_target_pairs={{0,4},{1,5},{2,6},{3,7},{4,0},{5,1},{6,2},{7,3},{8,12},{9,13},{10,... | collective-permute-start | bytes 393224 | tf_op jit(solution)/shard_map/ppermute | solution.py:473
  89.3 14.3 %collective-permute-start.29 = (bf16[128,512]{1,0:T(8,128)(2,1)S(1)}, bf16[128,512]{1,0:T(8,128)(2,1)S(1)}, u32[]{:S(2)}, u32[]{:S(2)}) collective-permute-start(bf16[128,512]{1,0:T(8,128)(2,1)S(1)} %get-tuple-element.231), channel_id=1, source_target_pairs={{0,5},{1,4},{2,7},{3,6},{4,1},{5,0},{6,3},{7,2},{8,13},{9,12},{10,... | collective-permute-start | bytes 393224 | tf_op jit(solution)/shard_map/ppermute | solution.py:473
  91.9 11.6 %collective-permute-start.31 = (bf16[128,512]{1,0:T(8,128)(2,1)S(1)}, bf16[128,512]{1,0:T(8,128)(2,1)S(1)}, u32[]{:S(2)}, u32[]{:S(2)}) collective-permute-start(bf16[128,512]{1,0:T(8,128)(2,1)S(1)} %get-tuple-element.233), channel_id=1, source_target_pairs={{0,7},{1,6},{2,5},{3,4},{4,3},{5,2},{6,1},{7,0},{8,15},{9,14},{10,... | collective-permute-start | bytes 393224 | tf_op jit(solution)/shard_map/ppermute | solution.py:473
  94.4 9.2 %collective-permute-start.26 = (bf16[128,512]{1,0:T(8,128)(2,1)S(1)}, bf16[128,512]{1,0:T(8,128)(2,1)S(1)}, u32[]{:S(2)}, u32[]{:S(2)}) collective-permute-start(bf16[128,512]{1,0:T(8,128)(2,1)S(1)} %get-tuple-element.225), channel_id=1, source_target_pairs={{0,1},{1,0},{2,3},{3,2},{4,5},{5,4},{6,7},{7,6},{8,9},{9,8},{10,11... | collective-permute-start | bytes 393224 | tf_op jit(solution)/shard_map/ppermute | solution.py:473
  (10 other events, 18.9 us)

commit v7 on v6

--- a/solution.py
+++ b/solution.py
@@ -18,6 +18,7 @@
 ONES = 16
 IN_FLIGHT = 4
 HOLD = 3
+WAITS = 5
 EARLY = 4
 
 NN = (((1,), (0,)), ((), ()))
@@ -59,8 +60,12 @@
     def at(i):
         return pl.ds(pl.multiple_of(i * BLOCK, BLOCK), BLOCK)
 
-    def span(i):
-        return pl.ds(pl.multiple_of(i * BLOCK, BLOCK), CHUNKS * BLOCK)
+    def chunks_of(i, near):
+        return i + 1 if near else CHUNKS
+
+    def span(i, near):
+        start = WINDOW if near else pl.multiple_of(i * BLOCK, BLOCK)
+        return pl.ds(start, chunks_of(i, near) * BLOCK)
 
     def qo_copy(i, piece=0):
         source = qo_hbm[0].at[at(i)] if taken == 1 else qo_hbm[piece]
@@ -88,42 +93,35 @@
     acc_v[:, : WINDOW + BLOCK] = jnp.zeros((HEAD_DIM, WINDOW + BLOCK), jnp.float32)
     key_at = lax.broadcasted_iota(jnp.int32, (BLOCK, 2 * BLOCK), 0)
     query_at = lax.broadcasted_iota(jnp.int32, (BLOCK, 2 * BLOCK), 1) & (BLOCK - 1)
-    first = place.first
-
     def turn(c):
         keys_t[:, at(c)] = kv[at(c), :HEAD_DIM].T
         values_t[:HEAD_DIM, at(c)] = kv[at(c), HEAD_DIM:].T
 
-    def bias(i, c):
-        return jnp.where(first & (i + c < whole), EXCLUDED, 0.0).astype(jnp.float32)
-
-    def score_dot(i):
-        return dot(kv[span(i), :HEAD_DIM], side_by_side(qo[at(i), :PAIR]), NN)
-
-    def keep_scores(slot, i, found):
+    def score_dot(i, near):
+        return dot(kv[span(i, near), :HEAD_DIM], side_by_side(qo[at(i), :PAIR]), NN)
+
+    def keep_scores(slot, i, found, near):
         top = None
-        for c in range(CHUNKS):
+        count = chunks_of(i, near)
+        for c in range(count):
             part = found[c * BLOCK : (c + 1) * BLOCK]
-            if c == 0:
+            if c == 0 and not near:
                 part = jnp.where(key_at > query_at, part, EXCLUDED)
-            if c == CHUNKS - 1:
+            if c == count - 1:
                 part = jnp.where(key_at <= query_at, part, EXCLUDED)
             scores[slot][c * BLOCK : (c + 1) * BLOCK] = part
             high = jnp.max(part, axis=0, keepdims=True)
-            if c < CHUNKS - 1:
-                high = high + bias(i, c)
             top = high if top is None else jnp.maximum(top, high)
         tops[slot, :1] = top * EXP2_SCALE
 
-    def exponentials(slot, i):
+    def exponentials(slot, i, near):
         top = tops[slot, :1]
-        for c in range(CHUNKS):
+        for c in range(chunks_of(i, near)):
             part = slice(c * BLOCK, (c + 1) * BLOCK)
-            shift = top - bias(i, c) if c < CHUNKS - 1 else top
-            exps[slot][part] = jnp.exp2(scores[slot][part] * EXP2_SCALE - shift).astype(jnp.bfloat16)
-
-    def attended_of(slot, i, o_t):
-        out = dot(values_t[:, span(i)], exps[slot][...], NN)
+            exps[slot][part] = jnp.exp2(scores[slot][part] * EXP2_SCALE - top).astype(jnp.bfloat16)
+
+    def attended_of(slot, i, o_t, low, near):
+        out = dot(values_t[:, span(i, near)], low, NN)
         inverse = 1.0 / out[HEAD_DIM : HEAD_DIM + 1]
         out = out[:HEAD_DIM] * inverse
         grad_out = o_t.astype(jnp.float32)
@@ -133,44 +131,46 @@
         ao[at(i), HEAD_DIM:PAIR] = out[:, BLOCK:].T
         return inverse, delta, (grad_out * inverse).astype(jnp.bfloat16)
 
-    def score_gradients(slot, grad_weights, delta):
+    def score_gradients(slot, i, grad_weights, delta, near):
         grad_scores = []
-        for c in range(CHUNKS):
+        for c in range(chunks_of(i, near)):
             part = slice(c * BLOCK, (c + 1) * BLOCK)
             grad_scores.append(
                 (exps[slot][part].astype(jnp.float32) * (grad_weights[part] - delta)).astype(jnp.bfloat16)
             )
         return jnp.concatenate(grad_scores, 0)
 
-    def spend(i, grad_scores, inverse):
+    def spend(i, grad_scores, inverse, near):
         q_t = side_by_side(qo[at(i), :PAIR])
         q_scaled = (q_t.astype(jnp.float32) * inverse).astype(jnp.bfloat16)
-        grad_q = (dot(keys_t[:, span(i)], grad_scores, NN) * (inverse * SCORE_SCALE)).astype(jnp.bfloat16)
+        grad_q = (dot(keys_t[:, span(i, near)], grad_scores, NN) * (inverse * SCORE_SCALE)).astype(jnp.bfloat16)
         ao[at(i), PAIR : PAIR + HEAD_DIM] = grad_q[:, :BLOCK].T
         ao[at(i), PAIR + HEAD_DIM :] = grad_q[:, BLOCK:].T
-        acc_k[:, span(i)] += dot(q_scaled, grad_scores, NT)
+        acc_k[:, span(i, near)] += dot(q_scaled, grad_scores, NT)
 
     def flush(i):
         dhalo[at(i), :HEAD_DIM] = (acc_k[:, at(i)] * SCORE_SCALE).astype(jnp.bfloat16).T
         dhalo[at(i), HEAD_DIM:] = acc_v[:, at(i)].astype(jnp.bfloat16).T
 
-    def stages(n, slot, begin=True, middle=True, end=True):
+    def stages(n, slot, begin=True, middle=True, end=True, near=False):
         if end:
             o_t = side_by_side(qo[at(n - 2), PAIR:])
-            inverse, delta, o_scaled = attended_of(slot, n - 2, o_t)
-            grad_weights = dot(kv[span(n - 2), HEAD_DIM:], o_t, NN)
+            low = exps[slot][: chunks_of(n - 2, near) * BLOCK]
+            inverse, delta, o_scaled = attended_of(slot, n - 2, o_t, low, near)
+            grad_weights = dot(kv[span(n - 2, near), HEAD_DIM:], o_t, NN)
         if begin:
-            found = score_dot(n)
+            found = score_dot(n, near)
         if end:
-            grad_scores = score_gradients(slot, grad_weights, delta)
-            acc_v[:, span(n - 2)] += dot(o_scaled, exps[slot][...], NT)
+            grad_scores = score_gradients(slot, n - 2, grad_weights, delta, near)
+            acc_v[:, span(n - 2, near)] += dot(o_scaled, low, NT)
         if middle:
-            exponentials(1 - slot, n - 1)
+            exponentials(1 - slot, n - 1, near)
         if begin:
-            keep_scores(slot, n, found)
+            keep_scores(slot, n, found, near)
         if end:
-            spend(n - 2, grad_scores, inverse)
-            flush(n - 2)
+            spend(n - 2, grad_scores, inverse, near)
+            if not near:
+                flush(n - 2)
 
     def extend(c):
         turn(c)
@@ -186,29 +186,45 @@
     own_copy.wait()
     qo_copy(0).wait()
     qo_copy(1).wait()
-    stages(0, 0, middle=False, end=False)
-    stages(1, 1, end=False)
-    for c in range(whole + 1):
-        turn(c)
-
-    def step(j, carry):
-        n = 2 * j
-        qo_copy(n).wait()
-        qo_copy(n + 1).wait()
-        stages(n, 0)
-        extend(n + whole - 1)
-        stages(n + 1, 1)
-        extend(n + whole)
-        send(n - 2)
-        send(n - 1)
-        return carry
-
-    lax.fori_loop(1, blocks // 2, step, 0)
-    stages(blocks, 0, begin=False)
-    extend(blocks + whole - 1)
-    send(blocks - 2)
-    stages(blocks + 1, 1, begin=False, middle=False)
-    send(blocks - 1)
+
+    @pl.when(jnp.logical_not(place.first))
+    def _():
+        stages(0, 0, middle=False, end=False)
+        stages(1, 1, end=False)
+        for c in range(whole + 1):
+            turn(c)
+
+        def step(j, carry):
+            n = 2 * j
+            qo_copy(n).wait()
+            qo_copy(n + 1).wait()
+            stages(n, 0)
+            extend(n + whole - 1)
+            stages(n + 1, 1)
+            extend(n + whole)
+            send(n - 2)
+            send(n - 1)
+            return carry
+
+        lax.fori_loop(1, blocks // 2, step, 0)
+        stages(blocks, 0, begin=False)
+        extend(blocks + whole - 1)
+        send(blocks - 2)
+        stages(blocks + 1, 1, begin=False, middle=False)
+        send(blocks - 1)
+
+    @pl.when(place.first)
+    def _():
+        dhalo[...] = jnp.zeros_like(dhalo)
+        for n in range(blocks + 2):
+            if 2 <= n < blocks:
+                qo_copy(n).wait()
+            if n >= 2:
+                extend(whole + n - 2)
+            stages(n, n % 2, n < blocks, 1 <= n <= blocks, n >= 2, near=True)
+            if n >= 2:
+                send(n - 2)
+
     if pieces > 1:
         for j in range(pieces):
             piece_copy(j).start()
@@ -502,7 +518,7 @@
         last = h == heads - 1
         *ao, dhalo, down = attention(apart, qos[h], halos[h], own[h], members if last else 1)
         if last:
-            ao, back[h - 1] = lax.optimization_barrier((ao, back[h - 1]))
+            ao[order[WAITS]], back[h - 1] = lax.optimization_barrier((ao[order[WAITS]], back[h - 1]))
         back.append(backward(dhalo))
         outs.append(swap(ao) if last else exchange(ao[0].reshape(members, rows, -1)))
         mine.append(down)

time: 105 us -> 103 us (0.981)
  starting transfers between devices: 43 us -> 50.5 us
  Pallas kernels: 33.6 us -> 27.2 us
  waiting for transfers between devices: 24 us -> 20.9 us
    pallas_call x2, Pallas kernels: 24.3 us -> 17.9 us  [attention(): pl.pallas_call(functools.partial(attention_kernel, apart, len(qo), pieces...]
    ppermute x2, starting transfers between devices: 4.36 us -> 10.7 us  [backward(): lax.ppermute(x, 'seq', [((i + apart) % shards, i) for i in range(shards)])]
    ppermute x28, waiting for transfers between devices: 22.3 us -> 19.9 us  [swap(): out[j] = lax.ppermute(piece, ('seq', 'kvh'), [(i, i ^ j) for i in every])]
    ppermute x28, starting transfers between devices: 28.2 us -> 29.5 us  [swap(): out[j] = lax.ppermute(piece, ('seq', 'kvh'), [(i, i ^ j) for i in every])]
  transfers between devices with their start and end apart: 34 -> 34, of which waited for: 12 -> 11; matrix products, arithmetic and copies ran while one was open for 0% -> 0% of each run, Pallas kernels for 28% -> 23%
where the time goes in v7:
time: 103 us
  starting transfers between devices  50.5 us (49%)
  Pallas kernels  27.2 us (26%)
  waiting for transfers between devices  20.9 us (20%)
  local copies, waits for them, and re-layouts  3.28 us (3%)
    ppermute x28, starting transfers between devices, swap(): out[j] = lax.ppermute(piece, ('seq', 'kvh'), [(i, i ^ j) for i in every])  29.5 us
    ppermute x28, waiting for transfers between devices, swap(): out[j] = lax.ppermute(piece, ('seq', 'kvh'), [(i, i ^ j) for i in every])  19.9 us
    pallas_call x2, Pallas kernels, attention(): pl.pallas_call(functools.partial(attention_kernel, apart, len(qo), pieces...  17.9 us
    ppermute x2, starting transfers between devices, backward(): lax.ppermute(x, 'seq', [((i + apart) % shards, i) for i in range(shards)])  10.7 us
    all_to_all x2, starting transfers between devices, exchange(): lax.all_to_all(x, ('seq', 'kvh'), 0, 0, tiled=True, axis_index_groups=gro...  7.13 us
    pallas_call x2, Pallas kernels, interleave(): pl.pallas_call(functools.partial(interleave_kernel, apart, width, sets),...  5.41 us
    unnamed x48, local copies, waits for them, and re-layouts  3.28 us
    ppermute x2, starting transfers between devices, onward(): lax.ppermute(x, 'seq', [(i, (i + apart) % shards) for i in range(shards)])  3.26 us
  transfers between devices with their start and end apart: 34, of which 11 were waited for; matrix products, arithmetic and copies ran while one was open for 0% of the time, Pallas kernels for 23%

profile of v7, /device:TPU:0, one launch (start us, length us, event | category | flops | bytes accessed | tf_op | source)
XLA Modules:
  0.0 102.8 jit_solution(5018242289167104120)
XLA Ops:
  0.6 2.3 %interleave.2 = (bf16[128,512]{1,0:T(8,128)(2,1)}, bf16[128,512]{1,0:T(8,128)(2,1)}, bf16[128,512]{1,0:T(8,128)(2,1)}, bf16[128,512]{1,0:T(8,128)(2,1)}, bf16[12...) custom-call(bf16[128,2048]{1,0:T(8,128)(2,1)} %refs_0_.2, ...), custom_call_target="tpu_custom_call" | custom-call | tf_op jit(solution)/shard_map/interleave/pallas_call | solution.py:318
  2.9 3.0 %collective-permute-start.7 = (bf16[128,512]{1,0:T(8,128)(2,1)}, bf16[128,512]{1,0:T(8,128)(2,1)S(1)}, u32[]{:S(2)}, u32[]{:S(2)}) collective-permute-start(bf16[128,512]{1,0:T(8,128)(2,1)} %get-tuple-element.141), channel_id=1, source_target_pairs={{0,2},{1,3},{2,0},{3,1},{4,6},{5,7},{6,4},{7,5},{8,10},{9,11},{10,... | collective-permute-start | bytes 393224 | tf_op jit(solution)/shard_map/ppermute | solution.py:489
  5.9 1.8 %collective-permute-start = (bf16[128,512]{1,0:T(8,128)(2,1)}, bf16[128,512]{1,0:T(8,128)(2,1)S(1)}, u32[]{:S(2)}, u32[]{:S(2)}) collective-permute-start(bf16[128,512]{1,0:T(8,128)(2,1)} %get-tuple-element.126), channel_id=1, source_target_pairs={{0,5},{1,4},{2,7},{3,6},{4,1},{5,0},{6,3},{7,2},{8,13},{9,12},{10,... | collective-permute-start | bytes 393224 | tf_op jit(solution)/shard_map/ppermute | solution.py:489
  7.8 3.1 %interleave.3 = (bf16[128,512]{1,0:T(8,128)(2,1)}, bf16[128,512]{1,0:T(8,128)(2,1)}, bf16[128,512]{1,0:T(8,128)(2,1)}, bf16[128,512]{1,0:T(8,128)(2,1)}, bf16[12...) custom-call(bf16[128,4096]{1,0:T(8,128)(2,1)} %refs_0_.3, ...), custom_call_target="tpu_custom_call" | custom-call | tf_op jit(solution)/shard_map/interleave/pallas_call | solution.py:318
  11.0 2.8 %collective-permute-start.5 = (bf16[128,512]{1,0:T(8,128)(2,1)S(1)}, bf16[128,512]{1,0:T(8,128)(2,1)S(1)}, u32[]{:S(2)}, u32[]{:S(2)}) collective-permute-start(bf16[128,512]{1,0:T(8,128)(2,1)S(1)} %copy-done.23), channel_id=1, source_target_pairs={{0,6},{1,7},{2,4},{3,5},{4,2},{5,3},{6,0},{7,1},{8,14},{9,15},{10,... | collective-permute-start | bytes 393224 | tf_op jit(solution)/shard_map/ppermute | solution.py:489
  13.9 0.2 collective-permute-start.11
  14.1 6.3 %collective-permute-done.3.refs_4_ = bf16[128,512]{1,0:T(8,128)(2,1)S(1)} collective-permute-done((bf16[128,512]{1,0:T(8,128)(2,1)}, bf16[128,512]{1,0:T(8,128)(2,1)S(1)}, u32[]{:S(2)}, u32[]{:S(2)}) %collective-permute-start.3) | collective-permute-done | bytes 131104 | tf_op jit(solution)/shard_map/ppermute | solution.py:489
  20.5 0.3 assemble.1
  20.8 1.6 %collective-permute-start.14 = (bf16[1024,256]{1,0:T(8,128)(2,1)S(1)}, bf16[1024,256]{1,0:T(8,128)(2,1)S(1)}, u32[]{:S(2)}, u32[]{:S(2)}) collective-permute-start(bf16[1024,256]{1,0:T(8,128)(2,1)S(1)} %get-tuple-element.161.refs_9_), channel_id=1, source_target_pairs={{0,8},{4,12},{8,16},{12,20},{16,24},{20,28},{24,0},{28,4},{1,9},{5... | collective-permute-start | bytes 1572872 | tf_op jit(solution)/shard_map/ppermute | solution.py:494
  22.5 1.5 %collective-permute-start.4 = (bf16[128,512]{1,0:T(8,128)(2,1)S(1)}, bf16[128,512]{1,0:T(8,128)(2,1)S(1)}, u32[]{:S(2)}, u32[]{:S(2)}) collective-permute-start(bf16[128,512]{1,0:T(8,128)(2,1)S(1)} %copy-done.17), channel_id=1, source_target_pairs={{0,2},{1,3},{2,0},{3,1},{4,6},{5,7},{6,4},{7,5},{8,10},{9,11},{10,... | collective-permute-start | bytes 393224 | tf_op jit(solution)/shard_map/ppermute | solution.py:489
  24.0 1.8 %collective-permute-start.9 = (bf16[128,512]{1,0:T(8,128)(2,1)S(1)}, bf16[128,512]{1,0:T(8,128)(2,1)S(1)}, u32[]{:S(2)}, u32[]{:S(2)}) collective-permute-start(bf16[128,512]{1,0:T(8,128)(2,1)S(1)} %copy-done.15), channel_id=1, source_target_pairs={{0,5},{1,4},{2,7},{3,6},{4,1},{5,0},{6,3},{7,2},{8,13},{9,12},{10,... | collective-permute-start | bytes 393224 | tf_op jit(solution)/shard_map/ppermute | solution.py:489
  25.7 0.5 collective-permute-start.6
  26.2 1.7 %collective-permute-done.4.refs_2_ = bf16[128,512]{1,0:T(8,128)(2,1)S(1)} collective-permute-done((bf16[128,512]{1,0:T(8,128)(2,1)S(1)}, bf16[128,512]{1,0:T(8,128)(2,1)S(1)}, u32[]{:S(2)}, u32[]{:S(2)}) %collective-permute-start.4) | collective-permute-done | bytes 131104 | tf_op jit(solution)/shard_map/ppermute | solution.py:489
  27.9 1.8 %collective-permute-done.1.refs_3_ = bf16[128,512]{1,0:T(8,128)(2,1)S(1)} collective-permute-done((bf16[128,512]{1,0:T(8,128)(2,1)S(1)}, bf16[128,512]{1,0:T(8,128)(2,1)S(1)}, u32[]{:S(2)}, u32[]{:S(2)}) %collective-permute-start.1) | collective-permute-done | bytes 131104 | tf_op jit(solution)/shard_map/ppermute | solution.py:489
  29.7 1.5 %collective-permute-start.12 = (bf16[128,512]{1,0:T(8,128)(2,1)S(1)}, bf16[128,512]{1,0:T(8,128)(2,1)}, u32[]{:S(2)}, u32[]{:S(2)}) collective-permute-start(bf16[128,512]{1,0:T(8,128)(2,1)S(1)} %copy-done.9), channel_id=1, source_target_pairs={{0,6},{1,7},{2,4},{3,5},{4,2},{5,3},{6,0},{7,1},{8,14},{9,15},{10,... | collective-permute-start | bytes 393224 | tf_op jit(solution)/shard_map/ppermute | solution.py:489
  31.2 1.0 collective-permute-start.2
  32.3 3.6 %all-to-all-start.1 = ((bf16[8,128,512]{2,1,0:T(8,128)(2,1)}), bf16[8,128,512]{2,1,0:T(8,128)(2,1)S(1)}, u32[]{:S(2)}, u32[]{:S(2)}) async-start(bf16[8,128,512]{2,1,0:T(8,128)(2,1)} %get-tuple-element.164), calls=%async_computation.1 | async-start | bytes 2097152 | tf_op jit(solution)/shard_map/all_to_all | solution.py:476
  35.9 1.6 %collective-permute-start.15 = (bf16[1024,256]{1,0:T(8,128)(2,1)S(1)}, bf16[1024,256]{1,0:T(8,128)(2,1)}, u32[]{:S(2)}, u32[]{:S(2)}) collective-permute-start(bf16[1024,256]{1,0:T(8,128)(2,1)S(1)} %get-tuple-element.165.refs_2_), channel_id=1, source_target_pairs={{0,8},{4,12},{8,16},{12,20},{16,24},{20,28},{24,0},{28,4},{1,9},{5... | collective-permute-start | bytes 1572872 | tf_op jit(solution)/shard_map/ppermute | solution.py:494
  37.5 0.9 collective-permute-done.6.refs_4_
  38.4 0.8 copy-done.7
  39.2 8.6 %attention.2 = (bf16[1024,512]{1,0:T(8,128)(2,1)}, bf16[1024,256]{1,0:T(8,128)(2,1)}, f32[2,128,1024]{2,1,0:T(8,128)}) custom-call(bf16[128,512]{1,0:T(8,128)(2,1)} %get-tuple-element.123.refs_0_, bf16[128,512]{1,0:T(8,128)(2,1)} %collective-permute-done.2.refs_1_, bf16[128,512]{1,0:T(8,128)(2,1)} %copy-done.18, bf16[128,512]{1,0:T(8,128)(2,1)} %copy-done.19, ...), custom_call_target="tpu_custom_call" | custom-call | flops 10000000000 | bytes 4194304 | tf_op jit(solution)/shard_map/attention/pallas_call | solution.py:248
  47.8 5.7 %collective-permute-start.16 = (bf16[1024,256]{1,0:T(8,128)(2,1)}, bf16[1024,256]{1,0:T(8,128)(2,1)S(1)}, u32[]{:S(2)}, u32[]{:S(2)}) collective-permute-start(bf16[1024,256]{1,0:T(8,128)(2,1)} %get-tuple-element.168), channel_id=1, source_target_pairs={{8,0},{12,4},{16,8},{20,12},{24,16},{28,20},{0,24},{4,28},{9,1},{1... | collective-permute-start | bytes 1572872 | tf_op jit(solution)/shard_map/ppermute | solution.py:497
  53.5 1.0 copy-done.6
  54.5 3.6 %all-to-all-start = ((bf16[8,128,512]{2,1,0:T(8,128)(2,1)}), bf16[8,128,512]{2,1,0:T(8,128)(2,1)S(1)}, u32[]{:S(2)}, u32[]{:S(2)}) async-start(bf16[8,128,512]{2,1,0:T(8,128)(2,1)} %bitcast.2), calls=%async_computation | async-start | bytes 2097152 | tf_op jit(solution)/shard_map/all_to_all | solution.py:476
  58.1 9.3 %attention.3 = (bf16[128,512]{1,0:T(8,128)(2,1)}, bf16[128,512]{1,0:T(8,128)(2,1)}, bf16[128,512]{1,0:T(8,128)(2,1)}, bf16[128,512]{1,0:T(8,128)(2,1)}, bf16[128...) custom-call(bf16[1024,512]{1,0:T(8,128)(2,1)} %bitcast.3, ...), custom_call_target="tpu_custom_call" | custom-call | flops 10000000000 | bytes 4194304 | tf_op jit(solution)/shard_map/attention/pallas_call | solution.py:248
  67.4 5.0 %collective-permute-start.17 = (bf16[1024,256]{1,0:T(8,128)(2,1)}, bf16[1024,256]{1,0:T(8,128)(2,1)S(1)}, u32[]{:S(2)}, u32[]{:S(2)}) collective-permute-start(bf16[1024,256]{1,0:T(8,128)(2,1)} %get-tuple-element.172), channel_id=1, source_target_pairs={{8,0},{12,4},{16,8},{20,12},{24,16},{28,20},{0,24},{4,28},{9,1},{1... | collective-permute-start | bytes 1572872 | tf_op jit(solution)/shard_map/ppermute | solution.py:497
  72.4 1.9 %collective-permute-start.18 = (bf16[128,512]{1,0:T(8,128)(2,1)}, bf16[128,512]{1,0:T(8,128)(2,1)S(1)}, u32[]{:S(2)}, u32[]{:S(2)}) collective-permute-start(bf16[128,512]{1,0:T(8,128)(2,1)} %get-tuple-element.185), channel_id=1, source_target_pairs={{0,4},{1,5},{2,6},{3,7},{4,0},{5,1},{6,2},{7,3},{8,12},{9,13},{10,... | collective-permute-start | bytes 393224 | tf_op jit(solution)/shard_map/ppermute | solution.py:489
  74.3 1.5 %collective-permute-start.20 = (bf16[128,512]{1,0:T(8,128)(2,1)}, bf16[128,512]{1,0:T(8,128)(2,1)S(1)}, u32[]{:S(2)}, u32[]{:S(2)}) collective-permute-start(bf16[128,512]{1,0:T(8,128)(2,1)} %get-tuple-element.189), channel_id=1, source_target_pairs={{0,2},{1,3},{2,0},{3,1},{4,6},{5,7},{6,4},{7,5},{8,10},{9,11},{10,... | collective-permute-start | bytes 393224 | tf_op jit(solution)/shard_map/ppermute | solution.py:489
  75.7 0.4 collective-permute-start.22
  76.1 1.2 %copy-done.1 = f32[2,128,1024]{2,1,0:T(8,128)S(1)} copy-done((f32[2,128,1024]{2,1,0:T(8,128)S(1)}, f32[2,128,1024]{2,1,0:T(8,128)}, u32[]{:S(2)}) %copy-start.1) | copy-done | bytes 1048600
  77.4 0.6 settle.1
  78.1 0.2 copy-done.14
  78.3 0.3 collective-permute-start.19
  78.5 1.5 %collective-permute-done.20.refs_2_ = bf16[128,512]{1,0:T(8,128)(2,1)S(1)} collective-permute-done((bf16[128,512]{1,0:T(8,128)(2,1)}, bf16[128,512]{1,0:T(8,128)(2,1)S(1)}, u32[]{:S(2)}, u32[]{:S(2)}) %collective-permute-start.20) | collective-permute-done | bytes 131104 | tf_op jit(solution)/shard_map/ppermute | solution.py:489
  80.0 2.3 %collective-permute-start.23 = (bf16[128,512]{1,0:T(8,128)(2,1)S(1)}, bf16[128,512]{1,0:T(8,128)(2,1)S(1)}, u32[]{:S(2)}, u32[]{:S(2)}) collective-permute-start(bf16[128,512]{1,0:T(8,128)(2,1)S(1)} %copy-done.13), channel_id=1, source_target_pairs={{0,6},{1,7},{2,4},{3,5},{4,2},{5,3},{6,0},{7,1},{8,14},{9,15},{10,... | collective-permute-start | bytes 393224 | tf_op jit(solution)/shard_map/ppermute | solution.py:489
  82.3 1.1 %collective-permute-start.24 = (bf16[128,512]{1,0:T(8,128)(2,1)S(1)}, bf16[128,512]{1,0:T(8,128)(2,1)S(1)}, u32[]{:S(2)}, u32[]{:S(2)}) collective-permute-start(bf16[128,512]{1,0:T(8,128)(2,1)S(1)} %copy-done.11), channel_id=1, source_target_pairs={{0,7},{1,6},{2,5},{3,4},{4,3},{5,2},{6,1},{7,0},{8,15},{9,14},{10,... | collective-permute-start | bytes 393224 | tf_op jit(solution)/shard_map/ppermute | solution.py:489
  83.4 0.9 collective-permute-done.17.back_ref
  84.5 0.7 collective-permute-start.25
  85.2 1.2 %collective-permute-start.27 = (bf16[128,512]{1,0:T(8,128)(2,1)S(1)}, bf16[128,512]{1,0:T(8,128)(2,1)S(1)}, u32[]{:S(2)}, u32[]{:S(2)}) collective-permute-start(bf16[128,512]{1,0:T(8,128)(2,1)S(1)} %get-tuple-element.213), channel_id=1, source_target_pairs={{0,2},{1,3},{2,0},{3,1},{4,6},{5,7},{6,4},{7,5},{8,10},{9,11},{10,... | collective-permute-start | bytes 393224 | tf_op jit(solution)/shard_map/ppermute | solution.py:489
  86.4 1.5 %collective-permute-start.28 = (bf16[128,512]{1,0:T(8,128)(2,1)S(1)}, bf16[128,512]{1,0:T(8,128)(2,1)S(1)}, u32[]{:S(2)}, u32[]{:S(2)}) collective-permute-start(bf16[128,512]{1,0:T(8,128)(2,1)S(1)} %get-tuple-element.216), channel_id=1, source_target_pairs={{0,4},{1,5},{2,6},{3,7},{4,0},{5,1},{6,2},{7,3},{8,12},{9,13},{10,... | collective-permute-start | bytes 393224 | tf_op jit(solution)/shard_map/ppermute | solution.py:489
  87.8 2.8 %collective-permute-start.30 = (bf16[128,512]{1,0:T(8,128)(2,1)S(1)}, bf16[128,512]{1,0:T(8,128)(2,1)S(1)}, u32[]{:S(2)}, u32[]{:S(2)}) collective-permute-start(bf16[128,512]{1,0:T(8,128)(2,1)S(1)} %get-tuple-element.218), channel_id=1, source_target_pairs={{0,6},{1,7},{2,4},{3,5},{4,2},{5,3},{6,0},{7,1},{8,14},{9,15},{10,... | collective-permute-start | bytes 393224 | tf_op jit(solution)/shard_map/ppermute | solution.py:489
  90.6 1.0 collective-permute-done.25.refs_3_
  91.7 2.3 %collective-permute-done.27.refs_2_ = bf16[128,512]{1,0:T(8,128)(2,1)S(1)} collective-permute-done((bf16[128,512]{1,0:T(8,128)(2,1)S(1)}, bf16[128,512]{1,0:T(8,128)(2,1)S(1)}, u32[]{:S(2)}, u32[]{:S(2)}) %collective-permute-start.27) | collective-permute-done | bytes 131104 | tf_op jit(solution)/shard_map/ppermute | solution.py:489
  94.0 1.6 %collective-permute-start.31 = (bf16[128,512]{1,0:T(8,128)(2,1)S(1)}, bf16[128,512]{1,0:T(8,128)(2,1)S(1)}, u32[]{:S(2)}, u32[]{:S(2)}) collective-permute-start(bf16[128,512]{1,0:T(8,128)(2,1)S(1)} %get-tuple-element.219), channel_id=1, source_target_pairs={{0,7},{1,6},{2,5},{3,4},{4,3},{5,2},{6,1},{7,0},{8,15},{9,14},{10,... | collective-permute-start | bytes 393224 | tf_op jit(solution)/shard_map/ppermute | solution.py:489
  95.6 1.6 %spread.1 = (bf16[128,4096]{1,0:T(8,128)(2,1)}, bf16[128,4096]{1,0:T(8,128)(2,1)}) custom-call(bf16[8,128,512]{2,1,0:T(8,128)(2,1)S(1)} %all-to-all-done.x_ref, bf16[128,512]{1,0:T(8,128)(2,1)S(1)} %copy-done.2, bf16[128,512]{1,0:T(8,128)(2,1)S(1)} %collective-permute-done.19.refs_1_, bf16[128,512]{1,0:T(8,128)(2,1)S(1)} %collective-permute-done.20.refs_2_, ...), custom_call_target="tpu_custom_call" | custom-call | tf_op jit(solution)/shard_map/spread/pallas_call | solution.py:387
  97.1 0.4 collective-permute-done.30.refs_6_
  97.6 4.0 %collective-permute-done.29.refs_5_ = bf16[128,512]{1,0:T(8,128)(2,1)S(1)} collective-permute-done((bf16[128,512]{1,0:T(8,128)(2,1)S(1)}, bf16[128,512]{1,0:T(8,128)(2,1)S(1)}, u32[]{:S(2)}, u32[]{:S(2)}) %collective-permute-start.29) | collective-permute-done | bytes 131104 | tf_op jit(solution)/shard_map/ppermute | solution.py:489
  101.5 1.3 %unpack.1 = (bf16[128,2048]{1,0:T(8,128)(2,1)}, bf16[128,2048]{1,0:T(8,128)(2,1)}) custom-call(bf16[128,512]{1,0:T(8,128)(2,1)S(1)} %get-tuple-element.208.refs_0_, bf16[128,512]{1,0:T(8,128)(2,1)S(1)} %collective-permute-done.26.refs_1_, bf16[128,512]{1,0:T(8,128)(2,1)S(1)} %collective-permute-done.27.refs_2_, ...), custom_call_target="tpu_custom_call" | custom-call | tf_op jit(solution)/shard_map/unpack/pallas_call | solution.py:458
  (77 shorter events, 0.6 us)
Async XLA Ops:
  2.9 10.9 %collective-permute-start.7 = (bf16[128,512]{1,0:T(8,128)(2,1)}, bf16[128,512]{1,0:T(8,128)(2,1)S(1)}, u32[]{:S(2)}, u32[]{:S(2)}) collective-permute-start(bf16[128,512]{1,0:T(8,128)(2,1)} %get-tuple-element.141), channel_id=1, source_target_pairs={{0,2},{1,3},{2,0},{3,1},{4,6},{5,7},{6,4},{7,5},{8,10},{9,11},{10,... | collective-permute-start | bytes 393224 | tf_op jit(solution)/shard_map/ppermute | solution.py:489
  5.9 7.9 %collective-permute-start.10 = (bf16[128,512]{1,0:T(8,128)(2,1)}, bf16[128,512]{1,0:T(8,128)(2,1)S(1)}, u32[]{:S(2)}, u32[]{:S(2)}) collective-permute-start(bf16[128,512]{1,0:T(8,128)(2,1)} %get-tuple-element.147), channel_id=1, source_target_pairs={{0,3},{1,2},{2,1},{3,0},{4,7},{5,6},{6,5},{7,4},{8,11},{9,10},{10,... | collective-permute-start | bytes 393224 | tf_op jit(solution)/shard_map/ppermute | solution.py:489
  5.9 8.2 %collective-permute-start = (bf16[128,512]{1,0:T(8,128)(2,1)}, bf16[128,512]{1,0:T(8,128)(2,1)S(1)}, u32[]{:S(2)}, u32[]{:S(2)}) collective-permute-start(bf16[128,512]{1,0:T(8,128)(2,1)} %get-tuple-element.126), channel_id=1, source_target_pairs={{0,5},{1,4},{2,7},{3,6},{4,1},{5,0},{6,3},{7,2},{8,13},{9,12},{10,... | collective-permute-start | bytes 393224 | tf_op jit(solution)/shard_map/ppermute | solution.py:489
  7.7 6.1 %copy-start.22 = (bf16[128,512]{1,0:T(8,128)(2,1)S(1)}, bf16[128,512]{1,0:T(8,128)(2,1)}, u32[]{:S(2)}) copy-start(bf16[128,512]{1,0:T(8,128)(2,1)} %get-tuple-element.142) | copy-start | bytes 393220
  7.7 6.1 %copy-start.21 = (bf16[128,512]{1,0:T(8,128)(2,1)S(1)}, bf16[128,512]{1,0:T(8,128)(2,1)}, u32[]{:S(2)}) copy-start(bf16[128,512]{1,0:T(8,128)(2,1)} %get-tuple-element.148) | copy-start | bytes 393220
  7.7 12.7 %copy-start.3 = (bf16[128,512]{1,0:T(8,128)(2,1)S(1)}, bf16[128,512]{1,0:T(8,128)(2,1)}, u32[]{:S(2)}) copy-start(bf16[128,512]{1,0:T(8,128)(2,1)} %get-tuple-element.150.refs_0_) | copy-start | bytes 393220
  7.7 12.7 %collective-permute-start.3 = (bf16[128,512]{1,0:T(8,128)(2,1)}, bf16[128,512]{1,0:T(8,128)(2,1)S(1)}, u32[]{:S(2)}, u32[]{:S(2)}) collective-permute-start(bf16[128,512]{1,0:T(8,128)(2,1)} %get-tuple-element.131), channel_id=1, source_target_pairs={{0,4},{1,5},{2,6},{3,7},{4,0},{5,1},{6,2},{7,3},{8,12},{9,13},{10,... | collective-permute-start | bytes 393224 | tf_op jit(solution)/shard_map/ppermute | solution.py:489
  11.0 9.4 %collective-permute-start.5 = (bf16[128,512]{1,0:T(8,128)(2,1)S(1)}, bf16[128,512]{1,0:T(8,128)(2,1)S(1)}, u32[]{:S(2)}, u32[]{:S(2)}) collective-permute-start(bf16[128,512]{1,0:T(8,128)(2,1)S(1)} %copy-done.23), channel_id=1, source_target_pairs={{0,6},{1,7},{2,4},{3,5},{4,2},{5,3},{6,0},{7,1},{8,14},{9,15},{10,... | collective-permute-start | bytes 393224 | tf_op jit(solution)/shard_map/ppermute | solution.py:489
  13.8 6.6 %collective-permute-start.8 = (bf16[128,512]{1,0:T(8,128)(2,1)S(1)}, bf16[128,512]{1,0:T(8,128)(2,1)S(1)}, u32[]{:S(2)}, u32[]{:S(2)}) collective-permute-start(bf16[128,512]{1,0:T(8,128)(2,1)S(1)} %copy-done.22), channel_id=1, source_target_pairs={{0,7},{1,6},{2,5},{3,4},{4,3},{5,2},{6,1},{7,0},{8,15},{9,14},{10,... | collective-permute-start | bytes 393224 | tf_op jit(solution)/shard_map/ppermute | solution.py:489
  13.9 6.5 %collective-permute-start.11 = (bf16[128,512]{1,0:T(8,128)(2,1)S(1)}, bf16[128,512]{1,0:T(8,128)(2,1)S(1)}, u32[]{:S(2)}, u32[]{:S(2)}) collective-permute-start(bf16[128,512]{1,0:T(8,128)(2,1)S(1)} %copy-done.21), channel_id=1, source_target_pairs={{0,1},{1,0},{2,3},{3,2},{4,5},{5,4},{6,7},{7,6},{8,9},{9,8},{10,11... | collective-permute-start | bytes 393224 | tf_op jit(solution)/shard_map/ppermute | solution.py:489
  20.4 3.5 %copy-start.16 = (bf16[128,512]{1,0:T(8,128)(2,1)S(1)}, bf16[128,512]{1,0:T(8,128)(2,1)}, u32[]{:S(2)}) copy-start(bf16[128,512]{1,0:T(8,128)(2,1)} %get-tuple-element.127) | copy-start | bytes 393220
  20.5 5.3 %copy-start.10 = (bf16[128,512]{1,0:T(8,128)(2,1)S(1)}, bf16[128,512]{1,0:T(8,128)(2,1)}, u32[]{:S(2)}) copy-start(bf16[128,512]{1,0:T(8,128)(2,1)} %get-tuple-element.137) | copy-start | bytes 393220
  20.5 7.5 %copy-start.12 = (bf16[128,512]{1,0:T(8,128)(2,1)S(1)}, bf16[128,512]{1,0:T(8,128)(2,1)}, u32[]{:S(2)}) copy-start(bf16[128,512]{1,0:T(8,128)(2,1)} %get-tuple-element.159) | copy-start | bytes 393220
  20.5 9.3 %copy-start.9 = (bf16[128,512]{1,0:T(8,128)(2,1)S(1)}, bf16[128,512]{1,0:T(8,128)(2,1)}, u32[]{:S(2)}) copy-start(bf16[128,512]{1,0:T(8,128)(2,1)} %get-tuple-element.149) | copy-start | bytes 393220
  20.5 10.8 %copy-start.8 = (bf16[128,512]{1,0:T(8,128)(2,1)S(1)}, bf16[128,512]{1,0:T(8,128)(2,1)}, u32[]{:S(2)}) copy-start(bf16[128,512]{1,0:T(8,128)(2,1)} %get-tuple-element.128) | copy-start | bytes 393220
  20.8 11.5 %copy-start.5 = (bf16[1024,256]{1,0:T(8,128)(2,1)}, bf16[1024,256]{1,0:T(8,128)(2,1)S(1)}, u32[]{:S(2)}) copy-start(bf16[1024,256]{1,0:T(8,128)(2,1)S(1)} %get-tuple-element.161.refs_9_) | copy-start | bytes 1572868
  20.8 15.0 %copy-start.4 = (bf16[1024,256]{1,0:T(8,128)(2,1)}, bf16[1024,256]{1,0:T(8,128)(2,1)S(1)}, u32[]{:S(2)}) copy-start(bf16[1024,256]{1,0:T(8,128)(2,1)S(1)} %get-tuple-element.165.refs_2_) | copy-start | bytes 1572868
  20.8 17.5 %collective-permute-start.14 = (bf16[1024,256]{1,0:T(8,128)(2,1)S(1)}, bf16[1024,256]{1,0:T(8,128)(2,1)S(1)}, u32[]{:S(2)}, u32[]{:S(2)}) collective-permute-start(bf16[1024,256]{1,0:T(8,128)(2,1)S(1)} %get-tuple-element.161.refs_9_), channel_id=1, source_target_pairs={{0,8},{4,12},{8,16},{12,20},{16,24},{20,28},{24,0},{28,4},{1,9},{5... | collective-permute-start | bytes 1572872 | tf_op jit(solution)/shard_map/ppermute | solution.py:494
  22.5 5.5 %collective-permute-start.4 = (bf16[128,512]{1,0:T(8,128)(2,1)S(1)}, bf16[128,512]{1,0:T(8,128)(2,1)S(1)}, u32[]{:S(2)}, u32[]{:S(2)}) collective-permute-start(bf16[128,512]{1,0:T(8,128)(2,1)S(1)} %copy-done.17), channel_id=1, source_target_pairs={{0,2},{1,3},{2,0},{3,1},{4,6},{5,7},{6,4},{7,5},{8,10},{9,11},{10,... | collective-permute-start | bytes 393224 | tf_op jit(solution)/shard_map/ppermute | solution.py:489
  24.0 5.8 %collective-permute-start.1 = (bf16[128,512]{1,0:T(8,128)(2,1)S(1)}, bf16[128,512]{1,0:T(8,128)(2,1)S(1)}, u32[]{:S(2)}, u32[]{:S(2)}) collective-permute-start(bf16[128,512]{1,0:T(8,128)(2,1)S(1)} %copy-done.16), channel_id=1, source_target_pairs={{0,3},{1,2},{2,1},{3,0},{4,7},{5,6},{6,5},{7,4},{8,11},{9,10},{10,... | collective-permute-start | bytes 393224 | tf_op jit(solution)/shard_map/ppermute | solution.py:489
  24.0 7.3 %collective-permute-start.9 = (bf16[128,512]{1,0:T(8,128)(2,1)S(1)}, bf16[128,512]{1,0:T(8,128)(2,1)S(1)}, u32[]{:S(2)}, u32[]{:S(2)}) collective-permute-start(bf16[128,512]{1,0:T(8,128)(2,1)S(1)} %copy-done.15), channel_id=1, source_target_pairs={{0,5},{1,4},{2,7},{3,6},{4,1},{5,0},{6,3},{7,2},{8,13},{9,12},{10,... | collective-permute-start | bytes 393224 | tf_op jit(solution)/shard_map/ppermute | solution.py:489
  25.7 12.6 %collective-permute-start.6 = (bf16[128,512]{1,0:T(8,128)(2,1)S(1)}, bf16[128,512]{1,0:T(8,128)(2,1)}, u32[]{:S(2)}, u32[]{:S(2)}) collective-permute-start(bf16[128,512]{1,0:T(8,128)(2,1)S(1)} %copy-done.10), channel_id=1, source_target_pairs={{0,4},{1,5},{2,6},{3,7},{4,0},{5,1},{6,2},{7,3},{8,12},{9,13},{10,... | collective-permute-start | bytes 393224 | tf_op jit(solution)/shard_map/ppermute | solution.py:489
  27.9 4.3 %copy-start.18 = (bf16[128,512]{1,0:T(8,128)(2,1)}, bf16[128,512]{1,0:T(8,128)(2,1)S(1)}, u32[]{:S(2)}) copy-start(bf16[128,512]{1,0:T(8,128)(2,1)S(1)} %collective-permute-done.4.refs_2_) | copy-start | bytes 393220
  27.9 7.9 %collective-permute-start.13 = (bf16[128,512]{1,0:T(8,128)(2,1)S(1)}, bf16[128,512]{1,0:T(8,128)(2,1)}, u32[]{:S(2)}, u32[]{:S(2)}) collective-permute-start(bf16[128,512]{1,0:T(8,128)(2,1)S(1)} %copy-done.12), channel_id=1, source_target_pairs={{0,7},{1,6},{2,5},{3,4},{4,3},{5,2},{6,1},{7,0},{8,15},{9,14},{10,... | collective-permute-start | bytes 393224 | tf_op jit(solution)/shard_map/ppermute | solution.py:489
  29.7 8.6 %collective-permute-start.12 = (bf16[128,512]{1,0:T(8,128)(2,1)S(1)}, bf16[128,512]{1,0:T(8,128)(2,1)}, u32[]{:S(2)}, u32[]{:S(2)}) collective-permute-start(bf16[128,512]{1,0:T(8,128)(2,1)S(1)} %copy-done.9), channel_id=1, source_target_pairs={{0,6},{1,7},{2,4},{3,5},{4,2},{5,3},{6,0},{7,1},{8,14},{9,15},{10,... | collective-permute-start | bytes 393224 | tf_op jit(solution)/shard_map/ppermute | solution.py:489
  31.2 7.1 %collective-permute-start.2 = (bf16[128,512]{1,0:T(8,128)(2,1)S(1)}, bf16[128,512]{1,0:T(8,128)(2,1)}, u32[]{:S(2)}, u32[]{:S(2)}) collective-permute-start(bf16[128,512]{1,0:T(8,128)(2,1)S(1)} %copy-done.8), channel_id=1, source_target_pairs={{0,1},{1,0},{2,3},{3,2},{4,5},{5,4},{6,7},{7,6},{8,9},{9,8},{10,11... | collective-permute-start | bytes 393224 | tf_op jit(solution)/shard_map/ppermute | solution.py:489
  32.3 21.3 %all-to-all-start.1 = ((bf16[8,128,512]{2,1,0:T(8,128)(2,1)}), bf16[8,128,512]{2,1,0:T(8,128)(2,1)S(1)}, u32[]{:S(2)}, u32[]{:S(2)}) async-start(bf16[8,128,512]{2,1,0:T(8,128)(2,1)} %get-tuple-element.164), calls=%async_computation.1 | async-start | bytes 2097152 | tf_op jit(solution)/shard_map/all_to_all | solution.py:476
  35.9 22.2 %collective-permute-start.15 = (bf16[1024,256]{1,0:T(8,128)(2,1)S(1)}, bf16[1024,256]{1,0:T(8,128)(2,1)}, u32[]{:S(2)}, u32[]{:S(2)}) collective-permute-start(bf16[1024,256]{1,0:T(8,128)(2,1)S(1)} %get-tuple-element.165.refs_2_), channel_id=1, source_target_pairs={{0,8},{4,12},{8,16},{12,20},{16,24},{20,28},{24,0},{28,4},{1,9},{5... | collective-permute-start | bytes 1572872 | tf_op jit(solution)/shard_map/ppermute | solution.py:494
  47.8 28.0 %collective-permute-start.16 = (bf16[1024,256]{1,0:T(8,128)(2,1)}, bf16[1024,256]{1,0:T(8,128)(2,1)S(1)}, u32[]{:S(2)}, u32[]{:S(2)}) collective-permute-start(bf16[1024,256]{1,0:T(8,128)(2,1)} %get-tuple-element.168), channel_id=1, source_target_pairs={{8,0},{12,4},{16,8},{20,12},{24,16},{28,20},{0,24},{4,28},{9,1},{1... | collective-permute-start | bytes 1572872 | tf_op jit(solution)/shard_map/ppermute | solution.py:497
  54.5 30.0 %all-to-all-start = ((bf16[8,128,512]{2,1,0:T(8,128)(2,1)}), bf16[8,128,512]{2,1,0:T(8,128)(2,1)S(1)}, u32[]{:S(2)}, u32[]{:S(2)}) async-start(bf16[8,128,512]{2,1,0:T(8,128)(2,1)} %bitcast.2), calls=%async_computation | async-start | bytes 2097152 | tf_op jit(solution)/shard_map/all_to_all | solution.py:476
  58.1 18.1 %copy-start = (f32[2,128,1024]{2,1,0:T(8,128)S(1)}, f32[2,128,1024]{2,1,0:T(8,128)}, u32[]{:S(2)}) copy-start(f32[2,128,1024]{2,1,0:T(8,128)} %get-tuple-element.163.own0) | copy-start | bytes 3145732
  67.4 17.0 %collective-permute-start.17 = (bf16[1024,256]{1,0:T(8,128)(2,1)}, bf16[1024,256]{1,0:T(8,128)(2,1)S(1)}, u32[]{:S(2)}, u32[]{:S(2)}) collective-permute-start(bf16[1024,256]{1,0:T(8,128)(2,1)} %get-tuple-element.172), channel_id=1, source_target_pairs={{8,0},{12,4},{16,8},{20,12},{24,16},{28,20},{0,24},{4,28},{9,1},{1... | collective-permute-start | bytes 1572872 | tf_op jit(solution)/shard_map/ppermute | solution.py:497
  72.4 5.7 %collective-permute-start.18 = (bf16[128,512]{1,0:T(8,128)(2,1)}, bf16[128,512]{1,0:T(8,128)(2,1)S(1)}, u32[]{:S(2)}, u32[]{:S(2)}) collective-permute-start(bf16[128,512]{1,0:T(8,128)(2,1)} %get-tuple-element.185), channel_id=1, source_target_pairs={{0,4},{1,5},{2,6},{3,7},{4,0},{5,1},{6,2},{7,3},{8,12},{9,13},{10,... | collective-permute-start | bytes 393224 | tf_op jit(solution)/shard_map/ppermute | solution.py:489
  74.3 5.7 %collective-permute-start.20 = (bf16[128,512]{1,0:T(8,128)(2,1)}, bf16[128,512]{1,0:T(8,128)(2,1)S(1)}, u32[]{:S(2)}, u32[]{:S(2)}) collective-permute-start(bf16[128,512]{1,0:T(8,128)(2,1)} %get-tuple-element.189), channel_id=1, source_target_pairs={{0,2},{1,3},{2,0},{3,1},{4,6},{5,7},{6,4},{7,5},{8,10},{9,11},{10,... | collective-permute-start | bytes 393224 | tf_op jit(solution)/shard_map/ppermute | solution.py:489
  75.7 6.6 %collective-permute-start.21 = (bf16[128,512]{1,0:T(8,128)(2,1)}, bf16[128,512]{1,0:T(8,128)(2,1)S(1)}, u32[]{:S(2)}, u32[]{:S(2)}) collective-permute-start(bf16[128,512]{1,0:T(8,128)(2,1)} %get-tuple-element.192), channel_id=1, source_target_pairs={{0,3},{1,2},{2,1},{3,0},{4,7},{5,6},{6,5},{7,4},{8,11},{9,10},{10,... | collective-permute-start | bytes 393224 | tf_op jit(solution)/shard_map/ppermute | solution.py:489
  75.7 8.8 %collective-permute-start.22 = (bf16[128,512]{1,0:T(8,128)(2,1)}, bf16[128,512]{1,0:T(8,128)(2,1)S(1)}, u32[]{:S(2)}, u32[]{:S(2)}) collective-permute-start(bf16[128,512]{1,0:T(8,128)(2,1)} %get-tuple-element.198), channel_id=1, source_target_pairs={{0,5},{1,4},{2,7},{3,6},{4,1},{5,0},{6,3},{7,2},{8,13},{9,12},{10,... | collective-permute-start | bytes 393224 | tf_op jit(solution)/shard_map/ppermute | solution.py:489
  77.4 5.0 %copy-start.11 = (bf16[128,512]{1,0:T(8,128)(2,1)S(1)}, bf16[128,512]{1,0:T(8,128)(2,1)}, u32[]{:S(2)}) copy-start(bf16[128,512]{1,0:T(8,128)(2,1)} %get-tuple-element.204) | copy-start | bytes 393220
  78.3 8.1 %collective-permute-start.19 = (bf16[128,512]{1,0:T(8,128)(2,1)S(1)}, bf16[128,512]{1,0:T(8,128)(2,1)S(1)}, u32[]{:S(2)}, u32[]{:S(2)}) collective-permute-start(bf16[128,512]{1,0:T(8,128)(2,1)S(1)} %copy-done.14), channel_id=1, source_target_pairs={{0,1},{1,0},{2,3},{3,2},{4,5},{5,4},{6,7},{7,6},{8,9},{9,8},{10,11... | collective-permute-start | bytes 393224 | tf_op jit(solution)/shard_map/ppermute | solution.py:489
  80.0 6.4 %collective-permute-start.23 = (bf16[128,512]{1,0:T(8,128)(2,1)S(1)}, bf16[128,512]{1,0:T(8,128)(2,1)S(1)}, u32[]{:S(2)}, u32[]{:S(2)}) collective-permute-start(bf16[128,512]{1,0:T(8,128)(2,1)S(1)} %copy-done.13), channel_id=1, source_target_pairs={{0,6},{1,7},{2,4},{3,5},{4,2},{5,3},{6,0},{7,1},{8,14},{9,15},{10,... | collective-permute-start | bytes 393224 | tf_op jit(solution)/shard_map/ppermute | solution.py:489
  82.3 8.3 %collective-permute-start.24 = (bf16[128,512]{1,0:T(8,128)(2,1)S(1)}, bf16[128,512]{1,0:T(8,128)(2,1)S(1)}, u32[]{:S(2)}, u32[]{:S(2)}) collective-permute-start(bf16[128,512]{1,0:T(8,128)(2,1)S(1)} %copy-done.11), channel_id=1, source_target_pairs={{0,7},{1,6},{2,5},{3,4},{4,3},{5,2},{6,1},{7,0},{8,15},{9,14},{10,... | collective-permute-start | bytes 393224 | tf_op jit(solution)/shard_map/ppermute | solution.py:489
  84.4 11.2 %copy-start.2 = (bf16[128,512]{1,0:T(8,128)(2,1)S(1)}, bf16[128,512]{1,0:T(8,128)(2,1)}, u32[]{:S(2)}) copy-start(bf16[128,512]{1,0:T(8,128)(2,1)} %get-tuple-element.182.refs_0_) | copy-start | bytes 393220
  84.5 7.1 %collective-permute-start.25 = (bf16[128,512]{1,0:T(8,128)(2,1)S(1)}, bf16[128,512]{1,0:T(8,128)(2,1)S(1)}, u32[]{:S(2)}, u32[]{:S(2)}) collective-permute-start(bf16[128,512]{1,0:T(8,128)(2,1)S(1)} %get-tuple-element.210), channel_id=1, source_target_pairs={{0,3},{1,2},{2,1},{3,0},{4,7},{5,6},{6,5},{7,4},{8,11},{9,10},{10,... | collective-permute-start | bytes 393224 | tf_op jit(solution)/shard_map/ppermute | solution.py:489
  85.2 8.8 %collective-permute-start.27 = (bf16[128,512]{1,0:T(8,128)(2,1)S(1)}, bf16[128,512]{1,0:T(8,128)(2,1)S(1)}, u32[]{:S(2)}, u32[]{:S(2)}) collective-permute-start(bf16[128,512]{1,0:T(8,128)(2,1)S(1)} %get-tuple-element.213), channel_id=1, source_target_pairs={{0,2},{1,3},{2,0},{3,1},{4,6},{5,7},{6,4},{7,5},{8,10},{9,11},{10,... | collective-permute-start | bytes 393224 | tf_op jit(solution)/shard_map/ppermute | solution.py:489
  86.4 10.8 %collective-permute-start.28 = (bf16[128,512]{1,0:T(8,128)(2,1)S(1)}, bf16[128,512]{1,0:T(8,128)(2,1)S(1)}, u32[]{:S(2)}, u32[]{:S(2)}) collective-permute-start(bf16[128,512]{1,0:T(8,128)(2,1)S(1)} %get-tuple-element.216), channel_id=1, source_target_pairs={{0,4},{1,5},{2,6},{3,7},{4,0},{5,1},{6,2},{7,3},{8,12},{9,13},{10,... | collective-permute-start | bytes 393224 | tf_op jit(solution)/shard_map/ppermute | solution.py:489
  87.8 9.7 %collective-permute-start.30 = (bf16[128,512]{1,0:T(8,128)(2,1)S(1)}, bf16[128,512]{1,0:T(8,128)(2,1)S(1)}, u32[]{:S(2)}, u32[]{:S(2)}) collective-permute-start(bf16[128,512]{1,0:T(8,128)(2,1)S(1)} %get-tuple-element.218), channel_id=1, source_target_pairs={{0,6},{1,7},{2,4},{3,5},{4,2},{5,3},{6,0},{7,1},{8,14},{9,15},{10,... | collective-permute-start | bytes 393224 | tf_op jit(solution)/shard_map/ppermute | solution.py:489
  90.6 10.9 %collective-permute-start.29 = (bf16[128,512]{1,0:T(8,128)(2,1)S(1)}, bf16[128,512]{1,0:T(8,128)(2,1)S(1)}, u32[]{:S(2)}, u32[]{:S(2)}) collective-permute-start(bf16[128,512]{1,0:T(8,128)(2,1)S(1)} %get-tuple-element.217), channel_id=1, source_target_pairs={{0,5},{1,4},{2,7},{3,6},{4,1},{5,0},{6,3},{7,2},{8,13},{9,12},{10,... | collective-permute-start | bytes 393224 | tf_op jit(solution)/shard_map/ppermute | solution.py:489
  91.6 9.9 %collective-permute-start.26 = (bf16[128,512]{1,0:T(8,128)(2,1)S(1)}, bf16[128,512]{1,0:T(8,128)(2,1)S(1)}, u32[]{:S(2)}, u32[]{:S(2)}) collective-permute-start(bf16[128,512]{1,0:T(8,128)(2,1)S(1)} %get-tuple-element.211), channel_id=1, source_target_pairs={{0,1},{1,0},{2,3},{3,2},{4,5},{5,4},{6,7},{7,6},{8,9},{9,8},{10,11... | collective-permute-start | bytes 393224 | tf_op jit(solution)/shard_map/ppermute | solution.py:489
  94.0 7.5 %collective-permute-start.31 = (bf16[128,512]{1,0:T(8,128)(2,1)S(1)}, bf16[128,512]{1,0:T(8,128)(2,1)S(1)}, u32[]{:S(2)}, u32[]{:S(2)}) collective-permute-start(bf16[128,512]{1,0:T(8,128)(2,1)S(1)} %get-tuple-element.219), channel_id=1, source_target_pairs={{0,7},{1,6},{2,5},{3,4},{4,3},{5,2},{6,1},{7,0},{8,15},{9,14},{10,... | collective-permute-start | bytes 393224 | tf_op jit(solution)/shard_map/ppermute | solution.py:489
  (10 other events, 18.9 us)

commit v8 on v7

--- a/solution.py
+++ b/solution.py
@@ -493,8 +493,8 @@
     def onward(x):
         return lax.ppermute(x, "seq", [(i, (i + apart) % shards) for i in range(shards)])
 
-    def backward(x):
-        return lax.ppermute(x, "seq", [((i + apart) % shards, i) for i in range(shards)])
+    def backward(x, wrap):
+        return lax.ppermute(x, "seq", [((i + apart) % shards, i) for i in range(shards if wrap else shards - apart)])
 
     stride = heads * HEAD_DIM
     kv_parts = [(n, h * HEAD_DIM, stride) for h in range(heads) for n in range(2)]
@@ -519,7 +519,7 @@
         *ao, dhalo, down = attention(apart, qos[h], halos[h], own[h], members if last else 1)
         if last:
             ao[order[WAITS]], back[h - 1] = lax.optimization_barrier((ao[order[WAITS]], back[h - 1]))
-        back.append(backward(dhalo))
+        back.append(backward(dhalo, not last))
         outs.append(swap(ao) if last else exchange(ao[0].reshape(members, rows, -1)))
         mine.append(down)
     total = add(apart, *settle(mine, back[0]), back[1], members)

time: 103 us -> 102 us (level)
  starting transfers between devices: 50.5 us -> 47 us
  waiting for transfers between devices: 20.9 us -> 23.5 us
    ppermute x2, starting transfers between devices: 10.7 us -> 7.03 us  [backward(): lax.ppermute(x, 'seq', [((i + apart) % shards, i) for i in range(shards i...]
    ppermute x2, waiting for transfers between devices: 0.94 us -> 4.37 us  [backward(): lax.ppermute(x, 'seq', [((i + apart) % shards, i) for i in range(shards i...]
  transfers between devices with their start and end apart: 34 -> 34, of which waited for: 11 -> 10; matrix products, arithmetic and copies ran while one was open for 0% -> 0% of each run, Pallas kernels for 23% -> 23%
where the time goes in v8:
time: 102 us
  starting transfers between devices  47 us (46%)
  Pallas kernels  27.2 us (27%)
  waiting for transfers between devices  23.5 us (23%)
  local copies, waits for them, and re-layouts  3.07 us (3%)
    ppermute x28, starting transfers between devices, swap(): out[j] = lax.ppermute(piece, ('seq', 'kvh'), [(i, i ^ j) for i in every])  29.5 us
    ppermute x28, waiting for transfers between devices, swap(): out[j] = lax.ppermute(piece, ('seq', 'kvh'), [(i, i ^ j) for i in every])  19.1 us
    pallas_call x2, Pallas kernels, attention(): pl.pallas_call(functools.partial(attention_kernel, apart, len(qo), pieces...  17.9 us
    all_to_all x2, starting transfers between devices, exchange(): lax.all_to_all(x, ('seq', 'kvh'), 0, 0, tiled=True, axis_index_groups=gro...  7.13 us
    ppermute x2, starting transfers between devices, backward(): lax.ppermute(x, 'seq', [((i + apart) % shards, i) for i in range(shards i...  7.03 us
    pallas_call x2, Pallas kernels, interleave(): pl.pallas_call(functools.partial(interleave_kernel, apart, width, sets),...  5.41 us
    ppermute x2, waiting for transfers between devices, backward(): lax.ppermute(x, 'seq', [((i + apart) % shards, i) for i in range(shards i...  4.37 us
    ppermute x2, starting transfers between devices, onward(): lax.ppermute(x, 'seq', [(i, (i + apart) % shards) for i in range(shards)])  3.26 us
  transfers between devices with their start and end apart: 34, of which 10 were waited for; matrix products, arithmetic and copies ran while one was open for 0% of the time, Pallas kernels for 23%

profile of v8, /device:TPU:0, one launch (start us, length us, event | category | flops | bytes accessed | tf_op | source)
XLA Modules:
  0.0 101.6 jit_solution(12728544436134332306)
XLA Ops:
  0.6 2.3 %interleave.2 = (bf16[128,512]{1,0:T(8,128)(2,1)}, bf16[128,512]{1,0:T(8,128)(2,1)}, bf16[128,512]{1,0:T(8,128)(2,1)}, bf16[128,512]{1,0:T(8,128)(2,1)}, bf16[12...) custom-call(bf16[128,2048]{1,0:T(8,128)(2,1)} %refs_0_.2, ...), custom_call_target="tpu_custom_call" | custom-call | tf_op jit(solution)/shard_map/interleave/pallas_call | solution.py:318
  2.9 3.0 %collective-permute-start.7 = (bf16[128,512]{1,0:T(8,128)(2,1)}, bf16[128,512]{1,0:T(8,128)(2,1)S(1)}, u32[]{:S(2)}, u32[]{:S(2)}) collective-permute-start(bf16[128,512]{1,0:T(8,128)(2,1)} %get-tuple-element.141), channel_id=1, source_target_pairs={{0,2},{1,3},{2,0},{3,1},{4,6},{5,7},{6,4},{7,5},{8,10},{9,11},{10,... | collective-permute-start | bytes 393224 | tf_op jit(solution)/shard_map/ppermute | solution.py:489
  5.9 1.8 %collective-permute-start = (bf16[128,512]{1,0:T(8,128)(2,1)}, bf16[128,512]{1,0:T(8,128)(2,1)S(1)}, u32[]{:S(2)}, u32[]{:S(2)}) collective-permute-start(bf16[128,512]{1,0:T(8,128)(2,1)} %get-tuple-element.126), channel_id=1, source_target_pairs={{0,5},{1,4},{2,7},{3,6},{4,1},{5,0},{6,3},{7,2},{8,13},{9,12},{10,... | collective-permute-start | bytes 393224 | tf_op jit(solution)/shard_map/ppermute | solution.py:489
  7.8 3.1 %interleave.3 = (bf16[128,512]{1,0:T(8,128)(2,1)}, bf16[128,512]{1,0:T(8,128)(2,1)}, bf16[128,512]{1,0:T(8,128)(2,1)}, bf16[128,512]{1,0:T(8,128)(2,1)}, bf16[12...) custom-call(bf16[128,4096]{1,0:T(8,128)(2,1)} %refs_0_.3, ...), custom_call_target="tpu_custom_call" | custom-call | tf_op jit(solution)/shard_map/interleave/pallas_call | solution.py:318
  11.0 2.8 %collective-permute-start.5 = (bf16[128,512]{1,0:T(8,128)(2,1)S(1)}, bf16[128,512]{1,0:T(8,128)(2,1)S(1)}, u32[]{:S(2)}, u32[]{:S(2)}) collective-permute-start(bf16[128,512]{1,0:T(8,128)(2,1)S(1)} %copy-done.23), channel_id=1, source_target_pairs={{0,6},{1,7},{2,4},{3,5},{4,2},{5,3},{6,0},{7,1},{8,14},{9,15},{10,... | collective-permute-start | bytes 393224 | tf_op jit(solution)/shard_map/ppermute | solution.py:489
  13.9 0.2 collective-permute-start.11
  14.1 6.3 %collective-permute-done.3.refs_4_ = bf16[128,512]{1,0:T(8,128)(2,1)S(1)} collective-permute-done((bf16[128,512]{1,0:T(8,128)(2,1)}, bf16[128,512]{1,0:T(8,128)(2,1)S(1)}, u32[]{:S(2)}, u32[]{:S(2)}) %collective-permute-start.3) | collective-permute-done | bytes 131104 | tf_op jit(solution)/shard_map/ppermute | solution.py:489
  20.5 0.3 assemble.1
  20.8 1.6 %collective-permute-start.14 = (bf16[1024,256]{1,0:T(8,128)(2,1)S(1)}, bf16[1024,256]{1,0:T(8,128)(2,1)S(1)}, u32[]{:S(2)}, u32[]{:S(2)}) collective-permute-start(bf16[1024,256]{1,0:T(8,128)(2,1)S(1)} %get-tuple-element.161.refs_9_), channel_id=1, source_target_pairs={{0,8},{4,12},{8,16},{12,20},{16,24},{20,28},{24,0},{28,4},{1,9},{5... | collective-permute-start | bytes 1572872 | tf_op jit(solution)/shard_map/ppermute | solution.py:494
  22.5 1.5 %collective-permute-start.4 = (bf16[128,512]{1,0:T(8,128)(2,1)S(1)}, bf16[128,512]{1,0:T(8,128)(2,1)S(1)}, u32[]{:S(2)}, u32[]{:S(2)}) collective-permute-start(bf16[128,512]{1,0:T(8,128)(2,1)S(1)} %copy-done.17), channel_id=1, source_target_pairs={{0,2},{1,3},{2,0},{3,1},{4,6},{5,7},{6,4},{7,5},{8,10},{9,11},{10,... | collective-permute-start | bytes 393224 | tf_op jit(solution)/shard_map/ppermute | solution.py:489
  24.0 1.8 %collective-permute-start.9 = (bf16[128,512]{1,0:T(8,128)(2,1)S(1)}, bf16[128,512]{1,0:T(8,128)(2,1)S(1)}, u32[]{:S(2)}, u32[]{:S(2)}) collective-permute-start(bf16[128,512]{1,0:T(8,128)(2,1)S(1)} %copy-done.15), channel_id=1, source_target_pairs={{0,5},{1,4},{2,7},{3,6},{4,1},{5,0},{6,3},{7,2},{8,13},{9,12},{10,... | collective-permute-start | bytes 393224 | tf_op jit(solution)/shard_map/ppermute | solution.py:489
  25.7 0.5 collective-permute-start.6
  26.2 1.7 %collective-permute-done.4.refs_2_ = bf16[128,512]{1,0:T(8,128)(2,1)S(1)} collective-permute-done((bf16[128,512]{1,0:T(8,128)(2,1)S(1)}, bf16[128,512]{1,0:T(8,128)(2,1)S(1)}, u32[]{:S(2)}, u32[]{:S(2)}) %collective-permute-start.4) | collective-permute-done | bytes 131104 | tf_op jit(solution)/shard_map/ppermute | solution.py:489
  27.9 1.8 %collective-permute-done.1.refs_3_ = bf16[128,512]{1,0:T(8,128)(2,1)S(1)} collective-permute-done((bf16[128,512]{1,0:T(8,128)(2,1)S(1)}, bf16[128,512]{1,0:T(8,128)(2,1)S(1)}, u32[]{:S(2)}, u32[]{:S(2)}) %collective-permute-start.1) | collective-permute-done | bytes 131104 | tf_op jit(solution)/shard_map/ppermute | solution.py:489
  29.7 1.5 %collective-permute-start.12 = (bf16[128,512]{1,0:T(8,128)(2,1)S(1)}, bf16[128,512]{1,0:T(8,128)(2,1)}, u32[]{:S(2)}, u32[]{:S(2)}) collective-permute-start(bf16[128,512]{1,0:T(8,128)(2,1)S(1)} %copy-done.9), channel_id=1, source_target_pairs={{0,6},{1,7},{2,4},{3,5},{4,2},{5,3},{6,0},{7,1},{8,14},{9,15},{10,... | collective-permute-start | bytes 393224 | tf_op jit(solution)/shard_map/ppermute | solution.py:489
  31.2 1.0 collective-permute-start.2
  32.3 3.6 %all-to-all-start.1 = ((bf16[8,128,512]{2,1,0:T(8,128)(2,1)}), bf16[8,128,512]{2,1,0:T(8,128)(2,1)S(1)}, u32[]{:S(2)}, u32[]{:S(2)}) async-start(bf16[8,128,512]{2,1,0:T(8,128)(2,1)} %get-tuple-element.164), calls=%async_computation.1 | async-start | bytes 2097152 | tf_op jit(solution)/shard_map/all_to_all | solution.py:476
  35.9 1.6 %collective-permute-start.15 = (bf16[1024,256]{1,0:T(8,128)(2,1)S(1)}, bf16[1024,256]{1,0:T(8,128)(2,1)}, u32[]{:S(2)}, u32[]{:S(2)}) collective-permute-start(bf16[1024,256]{1,0:T(8,128)(2,1)S(1)} %get-tuple-element.165.refs_2_), channel_id=1, source_target_pairs={{0,8},{4,12},{8,16},{12,20},{16,24},{20,28},{24,0},{28,4},{1,9},{5... | collective-permute-start | bytes 1572872 | tf_op jit(solution)/shard_map/ppermute | solution.py:494
  37.5 0.9 collective-permute-done.6.refs_4_
  38.4 0.8 copy-done.7
  39.2 8.6 %attention.2 = (bf16[1024,512]{1,0:T(8,128)(2,1)}, bf16[1024,256]{1,0:T(8,128)(2,1)}, f32[2,128,1024]{2,1,0:T(8,128)}) custom-call(bf16[128,512]{1,0:T(8,128)(2,1)} %get-tuple-element.123.refs_0_, bf16[128,512]{1,0:T(8,128)(2,1)} %collective-permute-done.2.refs_1_, bf16[128,512]{1,0:T(8,128)(2,1)} %copy-done.18, bf16[128,512]{1,0:T(8,128)(2,1)} %copy-done.19, ...), custom_call_target="tpu_custom_call" | custom-call | flops 10000000000 | bytes 4194304 | tf_op jit(solution)/shard_map/attention/pallas_call | solution.py:248
  47.8 5.7 %collective-permute-start.16 = (bf16[1024,256]{1,0:T(8,128)(2,1)}, bf16[1024,256]{1,0:T(8,128)(2,1)S(1)}, u32[]{:S(2)}, u32[]{:S(2)}) collective-permute-start(bf16[1024,256]{1,0:T(8,128)(2,1)} %get-tuple-element.168), channel_id=1, source_target_pairs={{8,0},{12,4},{16,8},{20,12},{24,16},{28,20},{0,24},{4,28},{9,1},{1... | collective-permute-start | bytes 1572872 | tf_op jit(solution)/shard_map/ppermute | solution.py:497
  53.5 1.0 copy-done.6
  54.5 3.6 %all-to-all-start = ((bf16[8,128,512]{2,1,0:T(8,128)(2,1)}), bf16[8,128,512]{2,1,0:T(8,128)(2,1)S(1)}, u32[]{:S(2)}, u32[]{:S(2)}) async-start(bf16[8,128,512]{2,1,0:T(8,128)(2,1)} %bitcast.2), calls=%async_computation | async-start | bytes 2097152 | tf_op jit(solution)/shard_map/all_to_all | solution.py:476
  58.1 9.3 %attention.3 = (bf16[128,512]{1,0:T(8,128)(2,1)}, bf16[128,512]{1,0:T(8,128)(2,1)}, bf16[128,512]{1,0:T(8,128)(2,1)}, bf16[128,512]{1,0:T(8,128)(2,1)}, bf16[128...) custom-call(bf16[1024,512]{1,0:T(8,128)(2,1)} %bitcast.3, ...), custom_call_target="tpu_custom_call" | custom-call | flops 10000000000 | bytes 4194304 | tf_op jit(solution)/shard_map/attention/pallas_call | solution.py:248
  67.4 1.3 %collective-permute-start.17 = (bf16[1024,256]{1,0:T(8,128)(2,1)}, bf16[1024,256]{1,0:T(8,128)(2,1)S(1)}, u32[]{:S(2)}, u32[]{:S(2)}) collective-permute-start(bf16[1024,256]{1,0:T(8,128)(2,1)} %get-tuple-element.172), channel_id=1, source_target_pairs={{8,0},{12,4},{16,8},{20,12},{24,16},{28,20},{9,1},{13,5},{17,9},{2... | collective-permute-start | bytes 1572872 | tf_op jit(solution)/shard_map/ppermute | solution.py:497
  68.7 2.0 %collective-permute-start.18 = (bf16[128,512]{1,0:T(8,128)(2,1)}, bf16[128,512]{1,0:T(8,128)(2,1)S(1)}, u32[]{:S(2)}, u32[]{:S(2)}) collective-permute-start(bf16[128,512]{1,0:T(8,128)(2,1)} %get-tuple-element.185), channel_id=1, source_target_pairs={{0,4},{1,5},{2,6},{3,7},{4,0},{5,1},{6,2},{7,3},{8,12},{9,13},{10,... | collective-permute-start | bytes 393224 | tf_op jit(solution)/shard_map/ppermute | solution.py:489
  70.7 1.5 %collective-permute-start.20 = (bf16[128,512]{1,0:T(8,128)(2,1)}, bf16[128,512]{1,0:T(8,128)(2,1)S(1)}, u32[]{:S(2)}, u32[]{:S(2)}) collective-permute-start(bf16[128,512]{1,0:T(8,128)(2,1)} %get-tuple-element.189), channel_id=1, source_target_pairs={{0,2},{1,3},{2,0},{3,1},{4,6},{5,7},{6,4},{7,5},{8,10},{9,11},{10,... | collective-permute-start | bytes 393224 | tf_op jit(solution)/shard_map/ppermute | solution.py:489
  72.2 0.4 collective-permute-start.22
  72.6 1.2 %copy-done.1 = f32[2,128,1024]{2,1,0:T(8,128)S(1)} copy-done((f32[2,128,1024]{2,1,0:T(8,128)S(1)}, f32[2,128,1024]{2,1,0:T(8,128)}, u32[]{:S(2)}) %copy-start.1) | copy-done | bytes 1048600
  73.8 0.6 settle.1
  74.4 1.8 %collective-permute-done.18.refs_4_ = bf16[128,512]{1,0:T(8,128)(2,1)S(1)} collective-permute-done((bf16[128,512]{1,0:T(8,128)(2,1)}, bf16[128,512]{1,0:T(8,128)(2,1)S(1)}, u32[]{:S(2)}, u32[]{:S(2)}) %collective-permute-start.18) | collective-permute-done | bytes 131104 | tf_op jit(solution)/shard_map/ppermute | solution.py:489
  76.3 0.7 collective-permute-done.20.refs_2_
  77.0 1.7 %collective-permute-start.23 = (bf16[128,512]{1,0:T(8,128)(2,1)S(1)}, bf16[128,512]{1,0:T(8,128)(2,1)S(1)}, u32[]{:S(2)}, u32[]{:S(2)}) collective-permute-start(bf16[128,512]{1,0:T(8,128)(2,1)S(1)} %copy-done.13), channel_id=1, source_target_pairs={{0,6},{1,7},{2,4},{3,5},{4,2},{5,3},{6,0},{7,1},{8,14},{9,15},{10,... | collective-permute-start | bytes 393224 | tf_op jit(solution)/shard_map/ppermute | solution.py:489
  78.7 1.4 %collective-permute-start.24 = (bf16[128,512]{1,0:T(8,128)(2,1)S(1)}, bf16[128,512]{1,0:T(8,128)(2,1)S(1)}, u32[]{:S(2)}, u32[]{:S(2)}) collective-permute-start(bf16[128,512]{1,0:T(8,128)(2,1)S(1)} %copy-done.11), channel_id=1, source_target_pairs={{0,7},{1,6},{2,5},{3,4},{4,3},{5,2},{6,1},{7,0},{8,15},{9,14},{10,... | collective-permute-start | bytes 393224 | tf_op jit(solution)/shard_map/ppermute | solution.py:489
  80.2 4.4 %collective-permute-done.17.back_ref = bf16[1024,256]{1,0:T(8,128)(2,1)S(1)} collective-permute-done((bf16[1024,256]{1,0:T(8,128)(2,1)}, bf16[1024,256]{1,0:T(8,128)(2,1)S(1)}, u32[]{:S(2)}, u32[]{:S(2)}) %collective-permute-start.17) | collective-permute-done | bytes 524320 | tf_op jit(solution)/shard_map/ppermute | solution.py:497
  84.7 1.0 collective-permute-start.25
  85.6 0.9 collective-permute-start.27
  86.5 1.5 %collective-permute-start.28 = (bf16[128,512]{1,0:T(8,128)(2,1)S(1)}, bf16[128,512]{1,0:T(8,128)(2,1)S(1)}, u32[]{:S(2)}, u32[]{:S(2)}) collective-permute-start(bf16[128,512]{1,0:T(8,128)(2,1)S(1)} %get-tuple-element.216), channel_id=1, source_target_pairs={{0,4},{1,5},{2,6},{3,7},{4,0},{5,1},{6,2},{7,3},{8,12},{9,13},{10,... | collective-permute-start | bytes 393224 | tf_op jit(solution)/shard_map/ppermute | solution.py:489
  88.0 1.2 %collective-permute-start.30 = (bf16[128,512]{1,0:T(8,128)(2,1)S(1)}, bf16[128,512]{1,0:T(8,128)(2,1)S(1)}, u32[]{:S(2)}, u32[]{:S(2)}) collective-permute-start(bf16[128,512]{1,0:T(8,128)(2,1)S(1)} %get-tuple-element.218), channel_id=1, source_target_pairs={{0,6},{1,7},{2,4},{3,5},{4,2},{5,3},{6,0},{7,1},{8,14},{9,15},{10,... | collective-permute-start | bytes 393224 | tf_op jit(solution)/shard_map/ppermute | solution.py:489
  89.1 1.1 %collective-permute-start.29 = (bf16[128,512]{1,0:T(8,128)(2,1)S(1)}, bf16[128,512]{1,0:T(8,128)(2,1)S(1)}, u32[]{:S(2)}, u32[]{:S(2)}) collective-permute-start(bf16[128,512]{1,0:T(8,128)(2,1)S(1)} %get-tuple-element.217), channel_id=1, source_target_pairs={{0,5},{1,4},{2,7},{3,6},{4,1},{5,0},{6,3},{7,2},{8,13},{9,12},{10,... | collective-permute-start | bytes 393224 | tf_op jit(solution)/shard_map/ppermute | solution.py:489
  90.3 0.6 collective-permute-start.26
  90.9 2.7 %collective-permute-done.27.refs_2_ = bf16[128,512]{1,0:T(8,128)(2,1)S(1)} collective-permute-done((bf16[128,512]{1,0:T(8,128)(2,1)S(1)}, bf16[128,512]{1,0:T(8,128)(2,1)S(1)}, u32[]{:S(2)}, u32[]{:S(2)}) %collective-permute-start.27) | collective-permute-done | bytes 131104 | tf_op jit(solution)/shard_map/ppermute | solution.py:489
  93.6 2.1 %collective-permute-start.31 = (bf16[128,512]{1,0:T(8,128)(2,1)S(1)}, bf16[128,512]{1,0:T(8,128)(2,1)S(1)}, u32[]{:S(2)}, u32[]{:S(2)}) collective-permute-start(bf16[128,512]{1,0:T(8,128)(2,1)S(1)} %get-tuple-element.219), channel_id=1, source_target_pairs={{0,7},{1,6},{2,5},{3,4},{4,3},{5,2},{6,1},{7,0},{8,15},{9,14},{10,... | collective-permute-start | bytes 393224 | tf_op jit(solution)/shard_map/ppermute | solution.py:489
  95.7 1.6 %spread.1 = (bf16[128,4096]{1,0:T(8,128)(2,1)}, bf16[128,4096]{1,0:T(8,128)(2,1)}) custom-call(bf16[8,128,512]{2,1,0:T(8,128)(2,1)S(1)} %all-to-all-done.x_ref, bf16[128,512]{1,0:T(8,128)(2,1)S(1)} %copy-done.2, bf16[128,512]{1,0:T(8,128)(2,1)S(1)} %collective-permute-done.19.refs_1_, bf16[128,512]{1,0:T(8,128)(2,1)S(1)} %collective-permute-done.20.refs_2_, ...), custom_call_target="tpu_custom_call" | custom-call | tf_op jit(solution)/shard_map/spread/pallas_call | solution.py:387
  97.2 0.1 collective-permute-done.30.refs_6_
  97.4 3.0 %collective-permute-done.29.refs_5_ = bf16[128,512]{1,0:T(8,128)(2,1)S(1)} collective-permute-done((bf16[128,512]{1,0:T(8,128)(2,1)S(1)}, bf16[128,512]{1,0:T(8,128)(2,1)S(1)}, u32[]{:S(2)}, u32[]{:S(2)}) %collective-permute-start.29) | collective-permute-done | bytes 131104 | tf_op jit(solution)/shard_map/ppermute | solution.py:489
  100.4 1.3 %unpack.1 = (bf16[128,2048]{1,0:T(8,128)(2,1)}, bf16[128,2048]{1,0:T(8,128)(2,1)}) custom-call(bf16[128,512]{1,0:T(8,128)(2,1)S(1)} %get-tuple-element.208.refs_0_, bf16[128,512]{1,0:T(8,128)(2,1)S(1)} %collective-permute-done.26.refs_1_, bf16[128,512]{1,0:T(8,128)(2,1)S(1)} %collective-permute-done.27.refs_2_, ...), custom_call_target="tpu_custom_call" | custom-call | tf_op jit(solution)/shard_map/unpack/pallas_call | solution.py:458
  (77 shorter events, 0.4 us)
Async XLA Ops:
  2.9 10.9 %collective-permute-start.7 = (bf16[128,512]{1,0:T(8,128)(2,1)}, bf16[128,512]{1,0:T(8,128)(2,1)S(1)}, u32[]{:S(2)}, u32[]{:S(2)}) collective-permute-start(bf16[128,512]{1,0:T(8,128)(2,1)} %get-tuple-element.141), channel_id=1, source_target_pairs={{0,2},{1,3},{2,0},{3,1},{4,6},{5,7},{6,4},{7,5},{8,10},{9,11},{10,... | collective-permute-start | bytes 393224 | tf_op jit(solution)/shard_map/ppermute | solution.py:489
  5.9 7.9 %collective-permute-start.10 = (bf16[128,512]{1,0:T(8,128)(2,1)}, bf16[128,512]{1,0:T(8,128)(2,1)S(1)}, u32[]{:S(2)}, u32[]{:S(2)}) collective-permute-start(bf16[128,512]{1,0:T(8,128)(2,1)} %get-tuple-element.147), channel_id=1, source_target_pairs={{0,3},{1,2},{2,1},{3,0},{4,7},{5,6},{6,5},{7,4},{8,11},{9,10},{10,... | collective-permute-start | bytes 393224 | tf_op jit(solution)/shard_map/ppermute | solution.py:489
  5.9 8.2 %collective-permute-start = (bf16[128,512]{1,0:T(8,128)(2,1)}, bf16[128,512]{1,0:T(8,128)(2,1)S(1)}, u32[]{:S(2)}, u32[]{:S(2)}) collective-permute-start(bf16[128,512]{1,0:T(8,128)(2,1)} %get-tuple-element.126), channel_id=1, source_target_pairs={{0,5},{1,4},{2,7},{3,6},{4,1},{5,0},{6,3},{7,2},{8,13},{9,12},{10,... | collective-permute-start | bytes 393224 | tf_op jit(solution)/shard_map/ppermute | solution.py:489
  7.7 6.1 %copy-start.22 = (bf16[128,512]{1,0:T(8,128)(2,1)S(1)}, bf16[128,512]{1,0:T(8,128)(2,1)}, u32[]{:S(2)}) copy-start(bf16[128,512]{1,0:T(8,128)(2,1)} %get-tuple-element.142) | copy-start | bytes 393220
  7.7 6.1 %copy-start.21 = (bf16[128,512]{1,0:T(8,128)(2,1)S(1)}, bf16[128,512]{1,0:T(8,128)(2,1)}, u32[]{:S(2)}) copy-start(bf16[128,512]{1,0:T(8,128)(2,1)} %get-tuple-element.148) | copy-start | bytes 393220
  7.7 12.7 %copy-start.3 = (bf16[128,512]{1,0:T(8,128)(2,1)S(1)}, bf16[128,512]{1,0:T(8,128)(2,1)}, u32[]{:S(2)}) copy-start(bf16[128,512]{1,0:T(8,128)(2,1)} %get-tuple-element.150.refs_0_) | copy-start | bytes 393220
  7.7 12.7 %collective-permute-start.3 = (bf16[128,512]{1,0:T(8,128)(2,1)}, bf16[128,512]{1,0:T(8,128)(2,1)S(1)}, u32[]{:S(2)}, u32[]{:S(2)}) collective-permute-start(bf16[128,512]{1,0:T(8,128)(2,1)} %get-tuple-element.131), channel_id=1, source_target_pairs={{0,4},{1,5},{2,6},{3,7},{4,0},{5,1},{6,2},{7,3},{8,12},{9,13},{10,... | collective-permute-start | bytes 393224 | tf_op jit(solution)/shard_map/ppermute | solution.py:489
  11.0 9.4 %collective-permute-start.5 = (bf16[128,512]{1,0:T(8,128)(2,1)S(1)}, bf16[128,512]{1,0:T(8,128)(2,1)S(1)}, u32[]{:S(2)}, u32[]{:S(2)}) collective-permute-start(bf16[128,512]{1,0:T(8,128)(2,1)S(1)} %copy-done.23), channel_id=1, source_target_pairs={{0,6},{1,7},{2,4},{3,5},{4,2},{5,3},{6,0},{7,1},{8,14},{9,15},{10,... | collective-permute-start | bytes 393224 | tf_op jit(solution)/shard_map/ppermute | solution.py:489
  13.8 6.6 %collective-permute-start.8 = (bf16[128,512]{1,0:T(8,128)(2,1)S(1)}, bf16[128,512]{1,0:T(8,128)(2,1)S(1)}, u32[]{:S(2)}, u32[]{:S(2)}) collective-permute-start(bf16[128,512]{1,0:T(8,128)(2,1)S(1)} %copy-done.22), channel_id=1, source_target_pairs={{0,7},{1,6},{2,5},{3,4},{4,3},{5,2},{6,1},{7,0},{8,15},{9,14},{10,... | collective-permute-start | bytes 393224 | tf_op jit(solution)/shard_map/ppermute | solution.py:489
  13.9 6.5 %collective-permute-start.11 = (bf16[128,512]{1,0:T(8,128)(2,1)S(1)}, bf16[128,512]{1,0:T(8,128)(2,1)S(1)}, u32[]{:S(2)}, u32[]{:S(2)}) collective-permute-start(bf16[128,512]{1,0:T(8,128)(2,1)S(1)} %copy-done.21), channel_id=1, source_target_pairs={{0,1},{1,0},{2,3},{3,2},{4,5},{5,4},{6,7},{7,6},{8,9},{9,8},{10,11... | collective-permute-start | bytes 393224 | tf_op jit(solution)/shard_map/ppermute | solution.py:489
  20.4 3.5 %copy-start.16 = (bf16[128,512]{1,0:T(8,128)(2,1)S(1)}, bf16[128,512]{1,0:T(8,128)(2,1)}, u32[]{:S(2)}) copy-start(bf16[128,512]{1,0:T(8,128)(2,1)} %get-tuple-element.127) | copy-start | bytes 393220
  20.5 5.3 %copy-start.10 = (bf16[128,512]{1,0:T(8,128)(2,1)S(1)}, bf16[128,512]{1,0:T(8,128)(2,1)}, u32[]{:S(2)}) copy-start(bf16[128,512]{1,0:T(8,128)(2,1)} %get-tuple-element.137) | copy-start | bytes 393220
  20.5 7.5 %copy-start.12 = (bf16[128,512]{1,0:T(8,128)(2,1)S(1)}, bf16[128,512]{1,0:T(8,128)(2,1)}, u32[]{:S(2)}) copy-start(bf16[128,512]{1,0:T(8,128)(2,1)} %get-tuple-element.159) | copy-start | bytes 393220
  20.5 9.3 %copy-start.9 = (bf16[128,512]{1,0:T(8,128)(2,1)S(1)}, bf16[128,512]{1,0:T(8,128)(2,1)}, u32[]{:S(2)}) copy-start(bf16[128,512]{1,0:T(8,128)(2,1)} %get-tuple-element.149) | copy-start | bytes 393220
  20.5 10.8 %copy-start.8 = (bf16[128,512]{1,0:T(8,128)(2,1)S(1)}, bf16[128,512]{1,0:T(8,128)(2,1)}, u32[]{:S(2)}) copy-start(bf16[128,512]{1,0:T(8,128)(2,1)} %get-tuple-element.128) | copy-start | bytes 393220
  20.8 11.5 %copy-start.5 = (bf16[1024,256]{1,0:T(8,128)(2,1)}, bf16[1024,256]{1,0:T(8,128)(2,1)S(1)}, u32[]{:S(2)}) copy-start(bf16[1024,256]{1,0:T(8,128)(2,1)S(1)} %get-tuple-element.161.refs_9_) | copy-start | bytes 1572868
  20.8 15.0 %copy-start.4 = (bf16[1024,256]{1,0:T(8,128)(2,1)}, bf16[1024,256]{1,0:T(8,128)(2,1)S(1)}, u32[]{:S(2)}) copy-start(bf16[1024,256]{1,0:T(8,128)(2,1)S(1)} %get-tuple-element.165.refs_2_) | copy-start | bytes 1572868
  20.8 17.5 %collective-permute-start.14 = (bf16[1024,256]{1,0:T(8,128)(2,1)S(1)}, bf16[1024,256]{1,0:T(8,128)(2,1)S(1)}, u32[]{:S(2)}, u32[]{:S(2)}) collective-permute-start(bf16[1024,256]{1,0:T(8,128)(2,1)S(1)} %get-tuple-element.161.refs_9_), channel_id=1, source_target_pairs={{0,8},{4,12},{8,16},{12,20},{16,24},{20,28},{24,0},{28,4},{1,9},{5... | collective-permute-start | bytes 1572872 | tf_op jit(solution)/shard_map/ppermute | solution.py:494
  22.5 5.5 %collective-permute-start.4 = (bf16[128,512]{1,0:T(8,128)(2,1)S(1)}, bf16[128,512]{1,0:T(8,128)(2,1)S(1)}, u32[]{:S(2)}, u32[]{:S(2)}) collective-permute-start(bf16[128,512]{1,0:T(8,128)(2,1)S(1)} %copy-done.17), channel_id=1, source_target_pairs={{0,2},{1,3},{2,0},{3,1},{4,6},{5,7},{6,4},{7,5},{8,10},{9,11},{10,... | collective-permute-start | bytes 393224 | tf_op jit(solution)/shard_map/ppermute | solution.py:489
  24.0 5.8 %collective-permute-start.1 = (bf16[128,512]{1,0:T(8,128)(2,1)S(1)}, bf16[128,512]{1,0:T(8,128)(2,1)S(1)}, u32[]{:S(2)}, u32[]{:S(2)}) collective-permute-start(bf16[128,512]{1,0:T(8,128)(2,1)S(1)} %copy-done.16), channel_id=1, source_target_pairs={{0,3},{1,2},{2,1},{3,0},{4,7},{5,6},{6,5},{7,4},{8,11},{9,10},{10,... | collective-permute-start | bytes 393224 | tf_op jit(solution)/shard_map/ppermute | solution.py:489
  24.0 7.3 %collective-permute-start.9 = (bf16[128,512]{1,0:T(8,128)(2,1)S(1)}, bf16[128,512]{1,0:T(8,128)(2,1)S(1)}, u32[]{:S(2)}, u32[]{:S(2)}) collective-permute-start(bf16[128,512]{1,0:T(8,128)(2,1)S(1)} %copy-done.15), channel_id=1, source_target_pairs={{0,5},{1,4},{2,7},{3,6},{4,1},{5,0},{6,3},{7,2},{8,13},{9,12},{10,... | collective-permute-start | bytes 393224 | tf_op jit(solution)/shard_map/ppermute | solution.py:489
  25.7 12.6 %collective-permute-start.6 = (bf16[128,512]{1,0:T(8,128)(2,1)S(1)}, bf16[128,512]{1,0:T(8,128)(2,1)}, u32[]{:S(2)}, u32[]{:S(2)}) collective-permute-start(bf16[128,512]{1,0:T(8,128)(2,1)S(1)} %copy-done.10), channel_id=1, source_target_pairs={{0,4},{1,5},{2,6},{3,7},{4,0},{5,1},{6,2},{7,3},{8,12},{9,13},{10,... | collective-permute-start | bytes 393224 | tf_op jit(solution)/shard_map/ppermute | solution.py:489
  27.9 4.3 %copy-start.18 = (bf16[128,512]{1,0:T(8,128)(2,1)}, bf16[128,512]{1,0:T(8,128)(2,1)S(1)}, u32[]{:S(2)}) copy-start(bf16[128,512]{1,0:T(8,128)(2,1)S(1)} %collective-permute-done.4.refs_2_) | copy-start | bytes 393220
  27.9 7.9 %collective-permute-start.13 = (bf16[128,512]{1,0:T(8,128)(2,1)S(1)}, bf16[128,512]{1,0:T(8,128)(2,1)}, u32[]{:S(2)}, u32[]{:S(2)}) collective-permute-start(bf16[128,512]{1,0:T(8,128)(2,1)S(1)} %copy-done.12), channel_id=1, source_target_pairs={{0,7},{1,6},{2,5},{3,4},{4,3},{5,2},{6,1},{7,0},{8,15},{9,14},{10,... | collective-permute-start | bytes 393224 | tf_op jit(solution)/shard_map/ppermute | solution.py:489
  29.7 8.6 %collective-permute-start.12 = (bf16[128,512]{1,0:T(8,128)(2,1)S(1)}, bf16[128,512]{1,0:T(8,128)(2,1)}, u32[]{:S(2)}, u32[]{:S(2)}) collective-permute-start(bf16[128,512]{1,0:T(8,128)(2,1)S(1)} %copy-done.9), channel_id=1, source_target_pairs={{0,6},{1,7},{2,4},{3,5},{4,2},{5,3},{6,0},{7,1},{8,14},{9,15},{10,... | collective-permute-start | bytes 393224 | tf_op jit(solution)/shard_map/ppermute | solution.py:489
  31.2 7.1 %collective-permute-start.2 = (bf16[128,512]{1,0:T(8,128)(2,1)S(1)}, bf16[128,512]{1,0:T(8,128)(2,1)}, u32[]{:S(2)}, u32[]{:S(2)}) collective-permute-start(bf16[128,512]{1,0:T(8,128)(2,1)S(1)} %copy-done.8), channel_id=1, source_target_pairs={{0,1},{1,0},{2,3},{3,2},{4,5},{5,4},{6,7},{7,6},{8,9},{9,8},{10,11... | collective-permute-start | bytes 393224 | tf_op jit(solution)/shard_map/ppermute | solution.py:489
  32.3 21.3 %all-to-all-start.1 = ((bf16[8,128,512]{2,1,0:T(8,128)(2,1)}), bf16[8,128,512]{2,1,0:T(8,128)(2,1)S(1)}, u32[]{:S(2)}, u32[]{:S(2)}) async-start(bf16[8,128,512]{2,1,0:T(8,128)(2,1)} %get-tuple-element.164), calls=%async_computation.1 | async-start | bytes 2097152 | tf_op jit(solution)/shard_map/all_to_all | solution.py:476
  35.9 22.2 %collective-permute-start.15 = (bf16[1024,256]{1,0:T(8,128)(2,1)S(1)}, bf16[1024,256]{1,0:T(8,128)(2,1)}, u32[]{:S(2)}, u32[]{:S(2)}) collective-permute-start(bf16[1024,256]{1,0:T(8,128)(2,1)S(1)} %get-tuple-element.165.refs_2_), channel_id=1, source_target_pairs={{0,8},{4,12},{8,16},{12,20},{16,24},{20,28},{24,0},{28,4},{1,9},{5... | collective-permute-start | bytes 1572872 | tf_op jit(solution)/shard_map/ppermute | solution.py:494
  47.8 24.4 %collective-permute-start.16 = (bf16[1024,256]{1,0:T(8,128)(2,1)}, bf16[1024,256]{1,0:T(8,128)(2,1)S(1)}, u32[]{:S(2)}, u32[]{:S(2)}) collective-permute-start(bf16[1024,256]{1,0:T(8,128)(2,1)} %get-tuple-element.168), channel_id=1, source_target_pairs={{8,0},{12,4},{16,8},{20,12},{24,16},{28,20},{0,24},{4,28},{9,1},{1... | collective-permute-start | bytes 1572872 | tf_op jit(solution)/shard_map/ppermute | solution.py:497
  54.5 30.2 %all-to-all-start = ((bf16[8,128,512]{2,1,0:T(8,128)(2,1)}), bf16[8,128,512]{2,1,0:T(8,128)(2,1)S(1)}, u32[]{:S(2)}, u32[]{:S(2)}) async-start(bf16[8,128,512]{2,1,0:T(8,128)(2,1)} %bitcast.2), calls=%async_computation | async-start | bytes 2097152 | tf_op jit(solution)/shard_map/all_to_all | solution.py:476
  58.1 14.5 %copy-start = (f32[2,128,1024]{2,1,0:T(8,128)S(1)}, f32[2,128,1024]{2,1,0:T(8,128)}, u32[]{:S(2)}) copy-start(f32[2,128,1024]{2,1,0:T(8,128)} %get-tuple-element.163.own0) | copy-start | bytes 3145732
  67.4 17.1 %collective-permute-start.17 = (bf16[1024,256]{1,0:T(8,128)(2,1)}, bf16[1024,256]{1,0:T(8,128)(2,1)S(1)}, u32[]{:S(2)}, u32[]{:S(2)}) collective-permute-start(bf16[1024,256]{1,0:T(8,128)(2,1)} %get-tuple-element.172), channel_id=1, source_target_pairs={{8,0},{12,4},{16,8},{20,12},{24,16},{28,20},{9,1},{13,5},{17,9},{2... | collective-permute-start | bytes 1572872 | tf_op jit(solution)/shard_map/ppermute | solution.py:497
  68.7 7.6 %collective-permute-start.18 = (bf16[128,512]{1,0:T(8,128)(2,1)}, bf16[128,512]{1,0:T(8,128)(2,1)S(1)}, u32[]{:S(2)}, u32[]{:S(2)}) collective-permute-start(bf16[128,512]{1,0:T(8,128)(2,1)} %get-tuple-element.185), channel_id=1, source_target_pairs={{0,4},{1,5},{2,6},{3,7},{4,0},{5,1},{6,2},{7,3},{8,12},{9,13},{10,... | collective-permute-start | bytes 393224 | tf_op jit(solution)/shard_map/ppermute | solution.py:489
  70.7 6.3 %collective-permute-start.20 = (bf16[128,512]{1,0:T(8,128)(2,1)}, bf16[128,512]{1,0:T(8,128)(2,1)S(1)}, u32[]{:S(2)}, u32[]{:S(2)}) collective-permute-start(bf16[128,512]{1,0:T(8,128)(2,1)} %get-tuple-element.189), channel_id=1, source_target_pairs={{0,2},{1,3},{2,0},{3,1},{4,6},{5,7},{6,4},{7,5},{8,10},{9,11},{10,... | collective-permute-start | bytes 393224 | tf_op jit(solution)/shard_map/ppermute | solution.py:489
  72.2 6.6 %collective-permute-start.21 = (bf16[128,512]{1,0:T(8,128)(2,1)}, bf16[128,512]{1,0:T(8,128)(2,1)S(1)}, u32[]{:S(2)}, u32[]{:S(2)}) collective-permute-start(bf16[128,512]{1,0:T(8,128)(2,1)} %get-tuple-element.192), channel_id=1, source_target_pairs={{0,3},{1,2},{2,1},{3,0},{4,7},{5,6},{6,5},{7,4},{8,11},{9,10},{10,... | collective-permute-start | bytes 393224 | tf_op jit(solution)/shard_map/ppermute | solution.py:489
  72.2 12.5 %collective-permute-start.22 = (bf16[128,512]{1,0:T(8,128)(2,1)}, bf16[128,512]{1,0:T(8,128)(2,1)S(1)}, u32[]{:S(2)}, u32[]{:S(2)}) collective-permute-start(bf16[128,512]{1,0:T(8,128)(2,1)} %get-tuple-element.198), channel_id=1, source_target_pairs={{0,5},{1,4},{2,7},{3,6},{4,1},{5,0},{6,3},{7,2},{8,13},{9,12},{10,... | collective-permute-start | bytes 393224 | tf_op jit(solution)/shard_map/ppermute | solution.py:489
  73.8 4.9 %copy-start.11 = (bf16[128,512]{1,0:T(8,128)(2,1)S(1)}, bf16[128,512]{1,0:T(8,128)(2,1)}, u32[]{:S(2)}) copy-start(bf16[128,512]{1,0:T(8,128)(2,1)} %get-tuple-element.204) | copy-start | bytes 393220
  76.3 10.2 %collective-permute-start.19 = (bf16[128,512]{1,0:T(8,128)(2,1)S(1)}, bf16[128,512]{1,0:T(8,128)(2,1)S(1)}, u32[]{:S(2)}, u32[]{:S(2)}) collective-permute-start(bf16[128,512]{1,0:T(8,128)(2,1)S(1)} %copy-done.14), channel_id=1, source_target_pairs={{0,1},{1,0},{2,3},{3,2},{4,5},{5,4},{6,7},{7,6},{8,9},{9,8},{10,11... | collective-permute-start | bytes 393224 | tf_op jit(solution)/shard_map/ppermute | solution.py:489
  77.0 9.5 %collective-permute-start.23 = (bf16[128,512]{1,0:T(8,128)(2,1)S(1)}, bf16[128,512]{1,0:T(8,128)(2,1)S(1)}, u32[]{:S(2)}, u32[]{:S(2)}) collective-permute-start(bf16[128,512]{1,0:T(8,128)(2,1)S(1)} %copy-done.13), channel_id=1, source_target_pairs={{0,6},{1,7},{2,4},{3,5},{4,2},{5,3},{6,0},{7,1},{8,14},{9,15},{10,... | collective-permute-start | bytes 393224 | tf_op jit(solution)/shard_map/ppermute | solution.py:489
  78.7 10.4 %collective-permute-start.24 = (bf16[128,512]{1,0:T(8,128)(2,1)S(1)}, bf16[128,512]{1,0:T(8,128)(2,1)S(1)}, u32[]{:S(2)}, u32[]{:S(2)}) collective-permute-start(bf16[128,512]{1,0:T(8,128)(2,1)S(1)} %copy-done.11), channel_id=1, source_target_pairs={{0,7},{1,6},{2,5},{3,4},{4,3},{5,2},{6,1},{7,0},{8,15},{9,14},{10,... | collective-permute-start | bytes 393224 | tf_op jit(solution)/shard_map/ppermute | solution.py:489
  84.5 11.1 %copy-start.2 = (bf16[128,512]{1,0:T(8,128)(2,1)S(1)}, bf16[128,512]{1,0:T(8,128)(2,1)}, u32[]{:S(2)}) copy-start(bf16[128,512]{1,0:T(8,128)(2,1)} %get-tuple-element.182.refs_0_) | copy-start | bytes 393220
  84.7 5.6 %collective-permute-start.25 = (bf16[128,512]{1,0:T(8,128)(2,1)S(1)}, bf16[128,512]{1,0:T(8,128)(2,1)S(1)}, u32[]{:S(2)}, u32[]{:S(2)}) collective-permute-start(bf16[128,512]{1,0:T(8,128)(2,1)S(1)} %get-tuple-element.210), channel_id=1, source_target_pairs={{0,3},{1,2},{2,1},{3,0},{4,7},{5,6},{6,5},{7,4},{8,11},{9,10},{10,... | collective-permute-start | bytes 393224 | tf_op jit(solution)/shard_map/ppermute | solution.py:489
  85.6 7.9 %collective-permute-start.27 = (bf16[128,512]{1,0:T(8,128)(2,1)S(1)}, bf16[128,512]{1,0:T(8,128)(2,1)S(1)}, u32[]{:S(2)}, u32[]{:S(2)}) collective-permute-start(bf16[128,512]{1,0:T(8,128)(2,1)S(1)} %get-tuple-element.213), channel_id=1, source_target_pairs={{0,2},{1,3},{2,0},{3,1},{4,6},{5,7},{6,4},{7,5},{8,10},{9,11},{10,... | collective-permute-start | bytes 393224 | tf_op jit(solution)/shard_map/ppermute | solution.py:489
  86.5 10.7 %collective-permute-start.28 = (bf16[128,512]{1,0:T(8,128)(2,1)S(1)}, bf16[128,512]{1,0:T(8,128)(2,1)S(1)}, u32[]{:S(2)}, u32[]{:S(2)}) collective-permute-start(bf16[128,512]{1,0:T(8,128)(2,1)S(1)} %get-tuple-element.216), channel_id=1, source_target_pairs={{0,4},{1,5},{2,6},{3,7},{4,0},{5,1},{6,2},{7,3},{8,12},{9,13},{10,... | collective-permute-start | bytes 393224 | tf_op jit(solution)/shard_map/ppermute | solution.py:489
  88.0 9.4 %collective-permute-start.30 = (bf16[128,512]{1,0:T(8,128)(2,1)S(1)}, bf16[128,512]{1,0:T(8,128)(2,1)S(1)}, u32[]{:S(2)}, u32[]{:S(2)}) collective-permute-start(bf16[128,512]{1,0:T(8,128)(2,1)S(1)} %get-tuple-element.218), channel_id=1, source_target_pairs={{0,6},{1,7},{2,4},{3,5},{4,2},{5,3},{6,0},{7,1},{8,14},{9,15},{10,... | collective-permute-start | bytes 393224 | tf_op jit(solution)/shard_map/ppermute | solution.py:489
  89.1 11.2 %collective-permute-start.29 = (bf16[128,512]{1,0:T(8,128)(2,1)S(1)}, bf16[128,512]{1,0:T(8,128)(2,1)S(1)}, u32[]{:S(2)}, u32[]{:S(2)}) collective-permute-start(bf16[128,512]{1,0:T(8,128)(2,1)S(1)} %get-tuple-element.217), channel_id=1, source_target_pairs={{0,5},{1,4},{2,7},{3,6},{4,1},{5,0},{6,3},{7,2},{8,13},{9,12},{10,... | collective-permute-start | bytes 393224 | tf_op jit(solution)/shard_map/ppermute | solution.py:489
  90.3 10.1 %collective-permute-start.26 = (bf16[128,512]{1,0:T(8,128)(2,1)S(1)}, bf16[128,512]{1,0:T(8,128)(2,1)S(1)}, u32[]{:S(2)}, u32[]{:S(2)}) collective-permute-start(bf16[128,512]{1,0:T(8,128)(2,1)S(1)} %get-tuple-element.211), channel_id=1, source_target_pairs={{0,1},{1,0},{2,3},{3,2},{4,5},{5,4},{6,7},{7,6},{8,9},{9,8},{10,11... | collective-permute-start | bytes 393224 | tf_op jit(solution)/shard_map/ppermute | solution.py:489
  93.6 6.8 %collective-permute-start.31 = (bf16[128,512]{1,0:T(8,128)(2,1)S(1)}, bf16[128,512]{1,0:T(8,128)(2,1)S(1)}, u32[]{:S(2)}, u32[]{:S(2)}) collective-permute-start(bf16[128,512]{1,0:T(8,128)(2,1)S(1)} %get-tuple-element.219), channel_id=1, source_target_pairs={{0,7},{1,6},{2,5},{3,4},{4,3},{5,2},{6,1},{7,0},{8,15},{9,14},{10,... | collective-permute-start | bytes 393224 | tf_op jit(solution)/shard_map/ppermute | solution.py:489
  (10 other events, 21.0 us)

commit v9 on v8

--- a/solution.py
+++ b/solution.py
@@ -287,18 +287,23 @@
     loads = [pltpu.make_async_copy(arrays[n], fetched[n], in_sem.at[n]) for n in range(2)]
     for load in loads:
         load.start()
-    for load in loads:
-        load.wait()
+    arrived = set()
     stores = []
     taken = 0
     for k, (split, parts) in enumerate(sets):
-        for g in range(groups):
-            source = place.member ^ g if split else g
-            for n, (which, start, stride) in enumerate(parts):
-                at = source * stride + start
+        to = 0
+        for which, start, stride, *size in parts:
+            span = size[0] if size else width
+            if which not in arrived:
+                loads[which].wait()
+                arrived.add(which)
+            for g in range(groups):
+                at = (place.member ^ g if split else g) * stride + start
                 if split:
                     at = pl.multiple_of(at, HEAD_DIM)
-                staged[k][g, :, n * width : (n + 1) * width] = fetched[which][:, pl.ds(at, width)]
+                staged[k][g, :, to : to + span] = fetched[which][:, pl.ds(at, span)]
+            to += span
+        for g in range(groups):
             out = outs[taken + g] if split else outs[taken].at[g]
             stores.append(pltpu.make_async_copy(staged[k].at[g], out, out_sem.at[k, g]))
             stores[-1].start()

time: 102 us -> 103 us (level)
  starting transfers between devices: 47 us -> 48.2 us
  waiting for transfers between devices: 23.5 us -> 22.3 us
    ppermute x28, waiting for transfers between devices: 19.1 us -> 17.7 us  [swap(): out[j] = lax.ppermute(piece, ('seq', 'kvh'), [(i, i ^ j) for i in every])]
    ppermute x28, starting transfers between devices: 29.5 us -> 30.6 us  [swap(): out[j] = lax.ppermute(piece, ('seq', 'kvh'), [(i, i ^ j) for i in every])]
where the time goes in v9:
time: 103 us; the launch traced here: 102 us
  starting transfers between devices  48.2 us (47%)
  Pallas kernels  27.4 us (27%)
  waiting for transfers between devices  22.3 us (22%)
  local copies, waits for them, and re-layouts  3.38 us (3%)
    ppermute x28, starting transfers between devices, swap(): out[j] = lax.ppermute(piece, ('seq', 'kvh'), [(i, i ^ j) for i in every])  30.6 us
    pallas_call x2, Pallas kernels, attention(): pl.pallas_call(functools.partial(attention_kernel, apart, len(qo), pieces...  17.9 us
    ppermute x28, waiting for transfers between devices, swap(): out[j] = lax.ppermute(piece, ('seq', 'kvh'), [(i, i ^ j) for i in every])  17.7 us
    all_to_all x2, starting transfers between devices, exchange(): lax.all_to_all(x, ('seq', 'kvh'), 0, 0, tiled=True, axis_index_groups=gro...  7.19 us
    ppermute x2, starting transfers between devices, backward(): lax.ppermute(x, 'seq', [((i + apart) % shards, i) for i in range(shards i...  7.03 us
    pallas_call x2, Pallas kernels, interleave(): pl.pallas_call(functools.partial(interleave_kernel, apart, width, sets),...  5.63 us
    ppermute x2, waiting for transfers between devices, backward(): lax.ppermute(x, 'seq', [((i + apart) % shards, i) for i in range(shards i...  4.62 us
    unnamed x48, local copies, waits for them, and re-layouts  3.38 us
  transfers between devices with their start and end apart: 34, of which 10 were waited for; matrix products, arithmetic and copies ran while one was open for 0% of the time, Pallas kernels for 23%

profile of v9, /device:TPU:0, one launch (start us, length us, event | category | flops | bytes accessed | tf_op | source)
XLA Modules:
  0.0 102.2 jit_solution(16923664296719303165)
XLA Ops:
  0.6 2.5 %interleave.2 = (bf16[128,512]{1,0:T(8,128)(2,1)}, bf16[128,512]{1,0:T(8,128)(2,1)}, bf16[128,512]{1,0:T(8,128)(2,1)}, bf16[128,512]{1,0:T(8,128)(2,1)}, bf16[12...) custom-call(bf16[128,2048]{1,0:T(8,128)(2,1)} %refs_0_.2, ...), custom_call_target="tpu_custom_call" | custom-call | tf_op jit(solution)/shard_map/interleave/pallas_call | solution.py:323
  3.1 3.0 %collective-permute-start.7 = (bf16[128,512]{1,0:T(8,128)(2,1)}, bf16[128,512]{1,0:T(8,128)(2,1)S(1)}, u32[]{:S(2)}, u32[]{:S(2)}) collective-permute-start(bf16[128,512]{1,0:T(8,128)(2,1)} %get-tuple-element.141), channel_id=1, source_target_pairs={{0,2},{1,3},{2,0},{3,1},{4,6},{5,7},{6,4},{7,5},{8,10},{9,11},{10,... | collective-permute-start | bytes 393224 | tf_op jit(solution)/shard_map/ppermute | solution.py:494
  6.1 1.8 %collective-permute-start = (bf16[128,512]{1,0:T(8,128)(2,1)}, bf16[128,512]{1,0:T(8,128)(2,1)S(1)}, u32[]{:S(2)}, u32[]{:S(2)}) collective-permute-start(bf16[128,512]{1,0:T(8,128)(2,1)} %get-tuple-element.126), channel_id=1, source_target_pairs={{0,5},{1,4},{2,7},{3,6},{4,1},{5,0},{6,3},{7,2},{8,13},{9,12},{10,... | collective-permute-start | bytes 393224 | tf_op jit(solution)/shard_map/ppermute | solution.py:494
  8.0 3.2 %interleave.3 = (bf16[128,512]{1,0:T(8,128)(2,1)}, bf16[128,512]{1,0:T(8,128)(2,1)}, bf16[128,512]{1,0:T(8,128)(2,1)}, bf16[128,512]{1,0:T(8,128)(2,1)}, bf16[12...) custom-call(bf16[128,4096]{1,0:T(8,128)(2,1)} %refs_0_.3, ...), custom_call_target="tpu_custom_call" | custom-call | tf_op jit(solution)/shard_map/interleave/pallas_call | solution.py:323
  11.2 2.8 %collective-permute-start.5 = (bf16[128,512]{1,0:T(8,128)(2,1)S(1)}, bf16[128,512]{1,0:T(8,128)(2,1)S(1)}, u32[]{:S(2)}, u32[]{:S(2)}) collective-permute-start(bf16[128,512]{1,0:T(8,128)(2,1)S(1)} %copy-done.23), channel_id=1, source_target_pairs={{0,6},{1,7},{2,4},{3,5},{4,2},{5,3},{6,0},{7,1},{8,14},{9,15},{10,... | collective-permute-start | bytes 393224 | tf_op jit(solution)/shard_map/ppermute | solution.py:494
  14.3 6.2 %collective-permute-done.3.refs_4_ = bf16[128,512]{1,0:T(8,128)(2,1)S(1)} collective-permute-done((bf16[128,512]{1,0:T(8,128)(2,1)}, bf16[128,512]{1,0:T(8,128)(2,1)S(1)}, u32[]{:S(2)}, u32[]{:S(2)}) %collective-permute-start.3) | collective-permute-done | bytes 131104 | tf_op jit(solution)/shard_map/ppermute | solution.py:494
  20.7 0.3 assemble.1
  21.0 1.6 %collective-permute-start.14 = (bf16[1024,256]{1,0:T(8,128)(2,1)S(1)}, bf16[1024,256]{1,0:T(8,128)(2,1)S(1)}, u32[]{:S(2)}, u32[]{:S(2)}) collective-permute-start(bf16[1024,256]{1,0:T(8,128)(2,1)S(1)} %get-tuple-element.161.refs_9_), channel_id=1, source_target_pairs={{0,8},{4,12},{8,16},{12,20},{16,24},{20,28},{24,0},{28,4},{1,9},{5... | collective-permute-start | bytes 1572872 | tf_op jit(solution)/shard_map/ppermute | solution.py:499
  22.6 1.5 %collective-permute-start.4 = (bf16[128,512]{1,0:T(8,128)(2,1)S(1)}, bf16[128,512]{1,0:T(8,128)(2,1)S(1)}, u32[]{:S(2)}, u32[]{:S(2)}) collective-permute-start(bf16[128,512]{1,0:T(8,128)(2,1)S(1)} %copy-done.17), channel_id=1, source_target_pairs={{0,2},{1,3},{2,0},{3,1},{4,6},{5,7},{6,4},{7,5},{8,10},{9,11},{10,... | collective-permute-start | bytes 393224 | tf_op jit(solution)/shard_map/ppermute | solution.py:494
  24.1 1.7 %collective-permute-start.9 = (bf16[128,512]{1,0:T(8,128)(2,1)S(1)}, bf16[128,512]{1,0:T(8,128)(2,1)S(1)}, u32[]{:S(2)}, u32[]{:S(2)}) collective-permute-start(bf16[128,512]{1,0:T(8,128)(2,1)S(1)} %copy-done.15), channel_id=1, source_target_pairs={{0,5},{1,4},{2,7},{3,6},{4,1},{5,0},{6,3},{7,2},{8,13},{9,12},{10,... | collective-permute-start | bytes 393224 | tf_op jit(solution)/shard_map/ppermute | solution.py:494
  25.9 0.5 collective-permute-start.6
  26.4 1.7 %collective-permute-done.4.refs_2_ = bf16[128,512]{1,0:T(8,128)(2,1)S(1)} collective-permute-done((bf16[128,512]{1,0:T(8,128)(2,1)S(1)}, bf16[128,512]{1,0:T(8,128)(2,1)S(1)}, u32[]{:S(2)}, u32[]{:S(2)}) %collective-permute-start.4) | collective-permute-done | bytes 131104 | tf_op jit(solution)/shard_map/ppermute | solution.py:494
  28.1 1.0 collective-permute-start.13
  29.1 0.9 collective-permute-done.1.refs_3_
  29.9 2.2 %collective-permute-start.12 = (bf16[128,512]{1,0:T(8,128)(2,1)S(1)}, bf16[128,512]{1,0:T(8,128)(2,1)}, u32[]{:S(2)}, u32[]{:S(2)}) collective-permute-start(bf16[128,512]{1,0:T(8,128)(2,1)S(1)} %copy-done.9), channel_id=1, source_target_pairs={{0,6},{1,7},{2,4},{3,5},{4,2},{5,3},{6,0},{7,1},{8,14},{9,15},{10,... | collective-permute-start | bytes 393224 | tf_op jit(solution)/shard_map/ppermute | solution.py:494
  32.1 0.3 collective-permute-start.2
  32.5 0.3 copy-done.20
  32.8 3.6 %all-to-all-start.1 = ((bf16[8,128,512]{2,1,0:T(8,128)(2,1)}), bf16[8,128,512]{2,1,0:T(8,128)(2,1)S(1)}, u32[]{:S(2)}, u32[]{:S(2)}) async-start(bf16[8,128,512]{2,1,0:T(8,128)(2,1)} %get-tuple-element.164), calls=%async_computation.1 | async-start | bytes 2097152 | tf_op jit(solution)/shard_map/all_to_all | solution.py:481
  36.4 1.7 %collective-permute-start.15 = (bf16[1024,256]{1,0:T(8,128)(2,1)S(1)}, bf16[1024,256]{1,0:T(8,128)(2,1)}, u32[]{:S(2)}, u32[]{:S(2)}) collective-permute-start(bf16[1024,256]{1,0:T(8,128)(2,1)S(1)} %get-tuple-element.165.refs_2_), channel_id=1, source_target_pairs={{0,8},{4,12},{8,16},{12,20},{16,24},{20,28},{24,0},{28,4},{1,9},{5... | collective-permute-start | bytes 1572872 | tf_op jit(solution)/shard_map/ppermute | solution.py:499
  38.1 0.4 collective-permute-done.6.refs_4_
  38.5 0.8 copy-done.7
  39.3 8.6 %attention.2 = (bf16[1024,512]{1,0:T(8,128)(2,1)}, bf16[1024,256]{1,0:T(8,128)(2,1)}, f32[2,128,1024]{2,1,0:T(8,128)}) custom-call(bf16[128,512]{1,0:T(8,128)(2,1)} %get-tuple-element.123.refs_0_, bf16[128,512]{1,0:T(8,128)(2,1)} %collective-permute-done.2.refs_1_, bf16[128,512]{1,0:T(8,128)(2,1)} %copy-done.18, bf16[128,512]{1,0:T(8,128)(2,1)} %copy-done.19, ...), custom_call_target="tpu_custom_call" | custom-call | flops 10000000000 | bytes 4194304 | tf_op jit(solution)/shard_map/attention/pallas_call | solution.py:248
  47.9 5.7 %collective-permute-start.16 = (bf16[1024,256]{1,0:T(8,128)(2,1)}, bf16[1024,256]{1,0:T(8,128)(2,1)S(1)}, u32[]{:S(2)}, u32[]{:S(2)}) collective-permute-start(bf16[1024,256]{1,0:T(8,128)(2,1)} %get-tuple-element.168), channel_id=1, source_target_pairs={{8,0},{12,4},{16,8},{20,12},{24,16},{28,20},{0,24},{4,28},{9,1},{1... | collective-permute-start | bytes 1572872 | tf_op jit(solution)/shard_map/ppermute | solution.py:502
  53.7 1.0 copy-done.6
  54.7 3.6 %all-to-all-start = ((bf16[8,128,512]{2,1,0:T(8,128)(2,1)}), bf16[8,128,512]{2,1,0:T(8,128)(2,1)S(1)}, u32[]{:S(2)}, u32[]{:S(2)}) async-start(bf16[8,128,512]{2,1,0:T(8,128)(2,1)} %bitcast.2), calls=%async_computation | async-start | bytes 2097152 | tf_op jit(solution)/shard_map/all_to_all | solution.py:481
  58.3 9.3 %attention.3 = (bf16[128,512]{1,0:T(8,128)(2,1)}, bf16[128,512]{1,0:T(8,128)(2,1)}, bf16[128,512]{1,0:T(8,128)(2,1)}, bf16[128,512]{1,0:T(8,128)(2,1)}, bf16[128...) custom-call(bf16[1024,512]{1,0:T(8,128)(2,1)} %bitcast.3, ...), custom_call_target="tpu_custom_call" | custom-call | flops 10000000000 | bytes 4194304 | tf_op jit(solution)/shard_map/attention/pallas_call | solution.py:248
  67.6 1.3 %collective-permute-start.17 = (bf16[1024,256]{1,0:T(8,128)(2,1)}, bf16[1024,256]{1,0:T(8,128)(2,1)S(1)}, u32[]{:S(2)}, u32[]{:S(2)}) collective-permute-start(bf16[1024,256]{1,0:T(8,128)(2,1)} %get-tuple-element.172), channel_id=1, source_target_pairs={{8,0},{12,4},{16,8},{20,12},{24,16},{28,20},{9,1},{13,5},{17,9},{2... | collective-permute-start | bytes 1572872 | tf_op jit(solution)/shard_map/ppermute | solution.py:502
  68.9 2.1 %collective-permute-start.18 = (bf16[128,512]{1,0:T(8,128)(2,1)}, bf16[128,512]{1,0:T(8,128)(2,1)S(1)}, u32[]{:S(2)}, u32[]{:S(2)}) collective-permute-start(bf16[128,512]{1,0:T(8,128)(2,1)} %get-tuple-element.185), channel_id=1, source_target_pairs={{0,4},{1,5},{2,6},{3,7},{4,0},{5,1},{6,2},{7,3},{8,12},{9,13},{10,... | collective-permute-start | bytes 393224 | tf_op jit(solution)/shard_map/ppermute | solution.py:494
  71.0 1.5 %collective-permute-start.20 = (bf16[128,512]{1,0:T(8,128)(2,1)}, bf16[128,512]{1,0:T(8,128)(2,1)S(1)}, u32[]{:S(2)}, u32[]{:S(2)}) collective-permute-start(bf16[128,512]{1,0:T(8,128)(2,1)} %get-tuple-element.189), channel_id=1, source_target_pairs={{0,2},{1,3},{2,0},{3,1},{4,6},{5,7},{6,4},{7,5},{8,10},{9,11},{10,... | collective-permute-start | bytes 393224 | tf_op jit(solution)/shard_map/ppermute | solution.py:494
  72.5 0.4 collective-permute-start.22
  72.9 1.2 %copy-done.1 = f32[2,128,1024]{2,1,0:T(8,128)S(1)} copy-done((f32[2,128,1024]{2,1,0:T(8,128)S(1)}, f32[2,128,1024]{2,1,0:T(8,128)}, u32[]{:S(2)}) %copy-start.1) | copy-done | bytes 1048600
  74.1 0.6 settle.1
  74.7 1.9 %collective-permute-done.18.refs_4_ = bf16[128,512]{1,0:T(8,128)(2,1)S(1)} collective-permute-done((bf16[128,512]{1,0:T(8,128)(2,1)}, bf16[128,512]{1,0:T(8,128)(2,1)S(1)}, u32[]{:S(2)}, u32[]{:S(2)}) %collective-permute-start.18) | collective-permute-done | bytes 131104 | tf_op jit(solution)/shard_map/ppermute | solution.py:494
  76.6 0.7 collective-permute-done.20.refs_2_
  77.3 1.7 %collective-permute-start.23 = (bf16[128,512]{1,0:T(8,128)(2,1)S(1)}, bf16[128,512]{1,0:T(8,128)(2,1)S(1)}, u32[]{:S(2)}, u32[]{:S(2)}) collective-permute-start(bf16[128,512]{1,0:T(8,128)(2,1)S(1)} %copy-done.13), channel_id=1, source_target_pairs={{0,6},{1,7},{2,4},{3,5},{4,2},{5,3},{6,0},{7,1},{8,14},{9,15},{10,... | collective-permute-start | bytes 393224 | tf_op jit(solution)/shard_map/ppermute | solution.py:494
  79.1 1.4 %collective-permute-start.24 = (bf16[128,512]{1,0:T(8,128)(2,1)S(1)}, bf16[128,512]{1,0:T(8,128)(2,1)S(1)}, u32[]{:S(2)}, u32[]{:S(2)}) collective-permute-start(bf16[128,512]{1,0:T(8,128)(2,1)S(1)} %copy-done.11), channel_id=1, source_target_pairs={{0,7},{1,6},{2,5},{3,4},{4,3},{5,2},{6,1},{7,0},{8,15},{9,14},{10,... | collective-permute-start | bytes 393224 | tf_op jit(solution)/shard_map/ppermute | solution.py:494
  80.5 4.6 %collective-permute-done.17.back_ref = bf16[1024,256]{1,0:T(8,128)(2,1)S(1)} collective-permute-done((bf16[1024,256]{1,0:T(8,128)(2,1)}, bf16[1024,256]{1,0:T(8,128)(2,1)S(1)}, u32[]{:S(2)}, u32[]{:S(2)}) %collective-permute-start.17) | collective-permute-done | bytes 524320 | tf_op jit(solution)/shard_map/ppermute | solution.py:502
  85.2 1.0 collective-permute-start.25
  86.2 0.8 collective-permute-start.27
  87.1 1.5 %collective-permute-start.28 = (bf16[128,512]{1,0:T(8,128)(2,1)S(1)}, bf16[128,512]{1,0:T(8,128)(2,1)S(1)}, u32[]{:S(2)}, u32[]{:S(2)}) collective-permute-start(bf16[128,512]{1,0:T(8,128)(2,1)S(1)} %get-tuple-element.216), channel_id=1, source_target_pairs={{0,4},{1,5},{2,6},{3,7},{4,0},{5,1},{6,2},{7,3},{8,12},{9,13},{10,... | collective-permute-start | bytes 393224 | tf_op jit(solution)/shard_map/ppermute | solution.py:494
  88.6 1.2 %collective-permute-start.30 = (bf16[128,512]{1,0:T(8,128)(2,1)S(1)}, bf16[128,512]{1,0:T(8,128)(2,1)S(1)}, u32[]{:S(2)}, u32[]{:S(2)}) collective-permute-start(bf16[128,512]{1,0:T(8,128)(2,1)S(1)} %get-tuple-element.218), channel_id=1, source_target_pairs={{0,6},{1,7},{2,4},{3,5},{4,2},{5,3},{6,0},{7,1},{8,14},{9,15},{10,... | collective-permute-start | bytes 393224 | tf_op jit(solution)/shard_map/ppermute | solution.py:494
  89.7 1.1 %collective-permute-start.29 = (bf16[128,512]{1,0:T(8,128)(2,1)S(1)}, bf16[128,512]{1,0:T(8,128)(2,1)S(1)}, u32[]{:S(2)}, u32[]{:S(2)}) collective-permute-start(bf16[128,512]{1,0:T(8,128)(2,1)S(1)} %get-tuple-element.217), channel_id=1, source_target_pairs={{0,5},{1,4},{2,7},{3,6},{4,1},{5,0},{6,3},{7,2},{8,13},{9,12},{10,... | collective-permute-start | bytes 393224 | tf_op jit(solution)/shard_map/ppermute | solution.py:494
  90.9 0.6 collective-permute-start.26
  91.4 2.7 %collective-permute-done.27.refs_2_ = bf16[128,512]{1,0:T(8,128)(2,1)S(1)} collective-permute-done((bf16[128,512]{1,0:T(8,128)(2,1)S(1)}, bf16[128,512]{1,0:T(8,128)(2,1)S(1)}, u32[]{:S(2)}, u32[]{:S(2)}) %collective-permute-start.27) | collective-permute-done | bytes 131104 | tf_op jit(solution)/shard_map/ppermute | solution.py:494
  94.1 2.1 %collective-permute-start.31 = (bf16[128,512]{1,0:T(8,128)(2,1)S(1)}, bf16[128,512]{1,0:T(8,128)(2,1)S(1)}, u32[]{:S(2)}, u32[]{:S(2)}) collective-permute-start(bf16[128,512]{1,0:T(8,128)(2,1)S(1)} %get-tuple-element.219), channel_id=1, source_target_pairs={{0,7},{1,6},{2,5},{3,4},{4,3},{5,2},{6,1},{7,0},{8,15},{9,14},{10,... | collective-permute-start | bytes 393224 | tf_op jit(solution)/shard_map/ppermute | solution.py:494
  96.2 1.6 %spread.1 = (bf16[128,4096]{1,0:T(8,128)(2,1)}, bf16[128,4096]{1,0:T(8,128)(2,1)}) custom-call(bf16[8,128,512]{2,1,0:T(8,128)(2,1)S(1)} %all-to-all-done.x_ref, bf16[128,512]{1,0:T(8,128)(2,1)S(1)} %copy-done.2, bf16[128,512]{1,0:T(8,128)(2,1)S(1)} %collective-permute-done.19.refs_1_, bf16[128,512]{1,0:T(8,128)(2,1)S(1)} %collective-permute-done.20.refs_2_, ...), custom_call_target="tpu_custom_call" | custom-call | tf_op jit(solution)/shard_map/spread/pallas_call | solution.py:392
  97.9 3.0 %collective-permute-done.29.refs_5_ = bf16[128,512]{1,0:T(8,128)(2,1)S(1)} collective-permute-done((bf16[128,512]{1,0:T(8,128)(2,1)S(1)}, bf16[128,512]{1,0:T(8,128)(2,1)S(1)}, u32[]{:S(2)}, u32[]{:S(2)}) %collective-permute-start.29) | collective-permute-done | bytes 131104 | tf_op jit(solution)/shard_map/ppermute | solution.py:494
  100.9 1.3 %unpack.1 = (bf16[128,2048]{1,0:T(8,128)(2,1)}, bf16[128,2048]{1,0:T(8,128)(2,1)}) custom-call(bf16[128,512]{1,0:T(8,128)(2,1)S(1)} %get-tuple-element.208.refs_0_, bf16[128,512]{1,0:T(8,128)(2,1)S(1)} %collective-permute-done.26.refs_1_, bf16[128,512]{1,0:T(8,128)(2,1)S(1)} %collective-permute-done.27.refs_2_, ...), custom_call_target="tpu_custom_call" | custom-call | tf_op jit(solution)/shard_map/unpack/pallas_call | solution.py:463
  (77 shorter events, 0.9 us)
Async XLA Ops:
  3.1 11.0 %collective-permute-start.7 = (bf16[128,512]{1,0:T(8,128)(2,1)}, bf16[128,512]{1,0:T(8,128)(2,1)S(1)}, u32[]{:S(2)}, u32[]{:S(2)}) collective-permute-start(bf16[128,512]{1,0:T(8,128)(2,1)} %get-tuple-element.141), channel_id=1, source_target_pairs={{0,2},{1,3},{2,0},{3,1},{4,6},{5,7},{6,4},{7,5},{8,10},{9,11},{10,... | collective-permute-start | bytes 393224 | tf_op jit(solution)/shard_map/ppermute | solution.py:494
  6.1 8.0 %collective-permute-start.10 = (bf16[128,512]{1,0:T(8,128)(2,1)}, bf16[128,512]{1,0:T(8,128)(2,1)S(1)}, u32[]{:S(2)}, u32[]{:S(2)}) collective-permute-start(bf16[128,512]{1,0:T(8,128)(2,1)} %get-tuple-element.147), channel_id=1, source_target_pairs={{0,3},{1,2},{2,1},{3,0},{4,7},{5,6},{6,5},{7,4},{8,11},{9,10},{10,... | collective-permute-start | bytes 393224 | tf_op jit(solution)/shard_map/ppermute | solution.py:494
  6.1 8.2 %collective-permute-start = (bf16[128,512]{1,0:T(8,128)(2,1)}, bf16[128,512]{1,0:T(8,128)(2,1)S(1)}, u32[]{:S(2)}, u32[]{:S(2)}) collective-permute-start(bf16[128,512]{1,0:T(8,128)(2,1)} %get-tuple-element.126), channel_id=1, source_target_pairs={{0,5},{1,4},{2,7},{3,6},{4,1},{5,0},{6,3},{7,2},{8,13},{9,12},{10,... | collective-permute-start | bytes 393224 | tf_op jit(solution)/shard_map/ppermute | solution.py:494
  7.9 6.2 %copy-start.22 = (bf16[128,512]{1,0:T(8,128)(2,1)S(1)}, bf16[128,512]{1,0:T(8,128)(2,1)}, u32[]{:S(2)}) copy-start(bf16[128,512]{1,0:T(8,128)(2,1)} %get-tuple-element.142) | copy-start | bytes 393220
  7.9 6.2 %copy-start.21 = (bf16[128,512]{1,0:T(8,128)(2,1)S(1)}, bf16[128,512]{1,0:T(8,128)(2,1)}, u32[]{:S(2)}) copy-start(bf16[128,512]{1,0:T(8,128)(2,1)} %get-tuple-element.148) | copy-start | bytes 393220
  7.9 12.7 %copy-start.3 = (bf16[128,512]{1,0:T(8,128)(2,1)S(1)}, bf16[128,512]{1,0:T(8,128)(2,1)}, u32[]{:S(2)}) copy-start(bf16[128,512]{1,0:T(8,128)(2,1)} %get-tuple-element.150.refs_0_) | copy-start | bytes 393220
  7.9 12.7 %collective-permute-start.3 = (bf16[128,512]{1,0:T(8,128)(2,1)}, bf16[128,512]{1,0:T(8,128)(2,1)S(1)}, u32[]{:S(2)}, u32[]{:S(2)}) collective-permute-start(bf16[128,512]{1,0:T(8,128)(2,1)} %get-tuple-element.131), channel_id=1, source_target_pairs={{0,4},{1,5},{2,6},{3,7},{4,0},{5,1},{6,2},{7,3},{8,12},{9,13},{10,... | collective-permute-start | bytes 393224 | tf_op jit(solution)/shard_map/ppermute | solution.py:494
  11.2 9.4 %collective-permute-start.5 = (bf16[128,512]{1,0:T(8,128)(2,1)S(1)}, bf16[128,512]{1,0:T(8,128)(2,1)S(1)}, u32[]{:S(2)}, u32[]{:S(2)}) collective-permute-start(bf16[128,512]{1,0:T(8,128)(2,1)S(1)} %copy-done.23), channel_id=1, source_target_pairs={{0,6},{1,7},{2,4},{3,5},{4,2},{5,3},{6,0},{7,1},{8,14},{9,15},{10,... | collective-permute-start | bytes 393224 | tf_op jit(solution)/shard_map/ppermute | solution.py:494
  14.1 6.5 %collective-permute-start.8 = (bf16[128,512]{1,0:T(8,128)(2,1)S(1)}, bf16[128,512]{1,0:T(8,128)(2,1)S(1)}, u32[]{:S(2)}, u32[]{:S(2)}) collective-permute-start(bf16[128,512]{1,0:T(8,128)(2,1)S(1)} %copy-done.22), channel_id=1, source_target_pairs={{0,7},{1,6},{2,5},{3,4},{4,3},{5,2},{6,1},{7,0},{8,15},{9,14},{10,... | collective-permute-start | bytes 393224 | tf_op jit(solution)/shard_map/ppermute | solution.py:494
  14.1 6.5 %collective-permute-start.11 = (bf16[128,512]{1,0:T(8,128)(2,1)S(1)}, bf16[128,512]{1,0:T(8,128)(2,1)S(1)}, u32[]{:S(2)}, u32[]{:S(2)}) collective-permute-start(bf16[128,512]{1,0:T(8,128)(2,1)S(1)} %copy-done.21), channel_id=1, source_target_pairs={{0,1},{1,0},{2,3},{3,2},{4,5},{5,4},{6,7},{7,6},{8,9},{9,8},{10,11... | collective-permute-start | bytes 393224 | tf_op jit(solution)/shard_map/ppermute | solution.py:494
  20.6 3.5 %copy-start.16 = (bf16[128,512]{1,0:T(8,128)(2,1)S(1)}, bf16[128,512]{1,0:T(8,128)(2,1)}, u32[]{:S(2)}) copy-start(bf16[128,512]{1,0:T(8,128)(2,1)} %get-tuple-element.127) | copy-start | bytes 393220
  20.6 5.3 %copy-start.10 = (bf16[128,512]{1,0:T(8,128)(2,1)S(1)}, bf16[128,512]{1,0:T(8,128)(2,1)}, u32[]{:S(2)}) copy-start(bf16[128,512]{1,0:T(8,128)(2,1)} %get-tuple-element.137) | copy-start | bytes 393220
  20.6 7.5 %copy-start.12 = (bf16[128,512]{1,0:T(8,128)(2,1)S(1)}, bf16[128,512]{1,0:T(8,128)(2,1)}, u32[]{:S(2)}) copy-start(bf16[128,512]{1,0:T(8,128)(2,1)} %get-tuple-element.159) | copy-start | bytes 393220
  20.6 9.3 %copy-start.9 = (bf16[128,512]{1,0:T(8,128)(2,1)S(1)}, bf16[128,512]{1,0:T(8,128)(2,1)}, u32[]{:S(2)}) copy-start(bf16[128,512]{1,0:T(8,128)(2,1)} %get-tuple-element.149) | copy-start | bytes 393220
  20.7 11.5 %copy-start.8 = (bf16[128,512]{1,0:T(8,128)(2,1)S(1)}, bf16[128,512]{1,0:T(8,128)(2,1)}, u32[]{:S(2)}) copy-start(bf16[128,512]{1,0:T(8,128)(2,1)} %get-tuple-element.128) | copy-start | bytes 393220
  21.0 11.5 %copy-start.5 = (bf16[1024,256]{1,0:T(8,128)(2,1)}, bf16[1024,256]{1,0:T(8,128)(2,1)S(1)}, u32[]{:S(2)}) copy-start(bf16[1024,256]{1,0:T(8,128)(2,1)S(1)} %get-tuple-element.161.refs_9_) | copy-start | bytes 1572868
  21.0 15.4 %copy-start.4 = (bf16[1024,256]{1,0:T(8,128)(2,1)}, bf16[1024,256]{1,0:T(8,128)(2,1)S(1)}, u32[]{:S(2)}) copy-start(bf16[1024,256]{1,0:T(8,128)(2,1)S(1)} %get-tuple-element.165.refs_2_) | copy-start | bytes 1572868
  21.0 17.5 %collective-permute-start.14 = (bf16[1024,256]{1,0:T(8,128)(2,1)S(1)}, bf16[1024,256]{1,0:T(8,128)(2,1)S(1)}, u32[]{:S(2)}, u32[]{:S(2)}) collective-permute-start(bf16[1024,256]{1,0:T(8,128)(2,1)S(1)} %get-tuple-element.161.refs_9_), channel_id=1, source_target_pairs={{0,8},{4,12},{8,16},{12,20},{16,24},{20,28},{24,0},{28,4},{1,9},{5... | collective-permute-start | bytes 1572872 | tf_op jit(solution)/shard_map/ppermute | solution.py:499
  22.6 5.5 %collective-permute-start.4 = (bf16[128,512]{1,0:T(8,128)(2,1)S(1)}, bf16[128,512]{1,0:T(8,128)(2,1)S(1)}, u32[]{:S(2)}, u32[]{:S(2)}) collective-permute-start(bf16[128,512]{1,0:T(8,128)(2,1)S(1)} %copy-done.17), channel_id=1, source_target_pairs={{0,2},{1,3},{2,0},{3,1},{4,6},{5,7},{6,4},{7,5},{8,10},{9,11},{10,... | collective-permute-start | bytes 393224 | tf_op jit(solution)/shard_map/ppermute | solution.py:494
  24.1 5.8 %collective-permute-start.1 = (bf16[128,512]{1,0:T(8,128)(2,1)S(1)}, bf16[128,512]{1,0:T(8,128)(2,1)S(1)}, u32[]{:S(2)}, u32[]{:S(2)}) collective-permute-start(bf16[128,512]{1,0:T(8,128)(2,1)S(1)} %copy-done.16), channel_id=1, source_target_pairs={{0,3},{1,2},{2,1},{3,0},{4,7},{5,6},{6,5},{7,4},{8,11},{9,10},{10,... | collective-permute-start | bytes 393224 | tf_op jit(solution)/shard_map/ppermute | solution.py:494
  24.1 8.0 %collective-permute-start.9 = (bf16[128,512]{1,0:T(8,128)(2,1)S(1)}, bf16[128,512]{1,0:T(8,128)(2,1)S(1)}, u32[]{:S(2)}, u32[]{:S(2)}) collective-permute-start(bf16[128,512]{1,0:T(8,128)(2,1)S(1)} %copy-done.15), channel_id=1, source_target_pairs={{0,5},{1,4},{2,7},{3,6},{4,1},{5,0},{6,3},{7,2},{8,13},{9,12},{10,... | collective-permute-start | bytes 393224 | tf_op jit(solution)/shard_map/ppermute | solution.py:494
  25.9 12.7 %collective-permute-start.6 = (bf16[128,512]{1,0:T(8,128)(2,1)S(1)}, bf16[128,512]{1,0:T(8,128)(2,1)}, u32[]{:S(2)}, u32[]{:S(2)}) collective-permute-start(bf16[128,512]{1,0:T(8,128)(2,1)S(1)} %copy-done.10), channel_id=1, source_target_pairs={{0,4},{1,5},{2,6},{3,7},{4,0},{5,1},{6,2},{7,3},{8,12},{9,13},{10,... | collective-permute-start | bytes 393224 | tf_op jit(solution)/shard_map/ppermute | solution.py:494
  28.1 4.4 %copy-start.18 = (bf16[128,512]{1,0:T(8,128)(2,1)}, bf16[128,512]{1,0:T(8,128)(2,1)S(1)}, u32[]{:S(2)}) copy-start(bf16[128,512]{1,0:T(8,128)(2,1)S(1)} %collective-permute-done.4.refs_2_) | copy-start | bytes 393220
  28.1 8.3 %collective-permute-start.13 = (bf16[128,512]{1,0:T(8,128)(2,1)S(1)}, bf16[128,512]{1,0:T(8,128)(2,1)}, u32[]{:S(2)}, u32[]{:S(2)}) collective-permute-start(bf16[128,512]{1,0:T(8,128)(2,1)S(1)} %copy-done.12), channel_id=1, source_target_pairs={{0,7},{1,6},{2,5},{3,4},{4,3},{5,2},{6,1},{7,0},{8,15},{9,14},{10,... | collective-permute-start | bytes 393224 | tf_op jit(solution)/shard_map/ppermute | solution.py:494
  29.9 8.6 %collective-permute-start.12 = (bf16[128,512]{1,0:T(8,128)(2,1)S(1)}, bf16[128,512]{1,0:T(8,128)(2,1)}, u32[]{:S(2)}, u32[]{:S(2)}) collective-permute-start(bf16[128,512]{1,0:T(8,128)(2,1)S(1)} %copy-done.9), channel_id=1, source_target_pairs={{0,6},{1,7},{2,4},{3,5},{4,2},{5,3},{6,0},{7,1},{8,14},{9,15},{10,... | collective-permute-start | bytes 393224 | tf_op jit(solution)/shard_map/ppermute | solution.py:494
  32.1 6.4 %collective-permute-start.2 = (bf16[128,512]{1,0:T(8,128)(2,1)S(1)}, bf16[128,512]{1,0:T(8,128)(2,1)}, u32[]{:S(2)}, u32[]{:S(2)}) collective-permute-start(bf16[128,512]{1,0:T(8,128)(2,1)S(1)} %copy-done.8), channel_id=1, source_target_pairs={{0,1},{1,0},{2,3},{3,2},{4,5},{5,4},{6,7},{7,6},{8,9},{9,8},{10,11... | collective-permute-start | bytes 393224 | tf_op jit(solution)/shard_map/ppermute | solution.py:494
  32.8 20.9 %all-to-all-start.1 = ((bf16[8,128,512]{2,1,0:T(8,128)(2,1)}), bf16[8,128,512]{2,1,0:T(8,128)(2,1)S(1)}, u32[]{:S(2)}, u32[]{:S(2)}) async-start(bf16[8,128,512]{2,1,0:T(8,128)(2,1)} %get-tuple-element.164), calls=%async_computation.1 | async-start | bytes 2097152 | tf_op jit(solution)/shard_map/all_to_all | solution.py:481
  36.4 21.9 %collective-permute-start.15 = (bf16[1024,256]{1,0:T(8,128)(2,1)S(1)}, bf16[1024,256]{1,0:T(8,128)(2,1)}, u32[]{:S(2)}, u32[]{:S(2)}) collective-permute-start(bf16[1024,256]{1,0:T(8,128)(2,1)S(1)} %get-tuple-element.165.refs_2_), channel_id=1, source_target_pairs={{0,8},{4,12},{8,16},{12,20},{16,24},{20,28},{24,0},{28,4},{1,9},{5... | collective-permute-start | bytes 1572872 | tf_op jit(solution)/shard_map/ppermute | solution.py:499
  47.9 24.5 %collective-permute-start.16 = (bf16[1024,256]{1,0:T(8,128)(2,1)}, bf16[1024,256]{1,0:T(8,128)(2,1)S(1)}, u32[]{:S(2)}, u32[]{:S(2)}) collective-permute-start(bf16[1024,256]{1,0:T(8,128)(2,1)} %get-tuple-element.168), channel_id=1, source_target_pairs={{8,0},{12,4},{16,8},{20,12},{24,16},{28,20},{0,24},{4,28},{9,1},{1... | collective-permute-start | bytes 1572872 | tf_op jit(solution)/shard_map/ppermute | solution.py:502
  54.7 30.6 %all-to-all-start = ((bf16[8,128,512]{2,1,0:T(8,128)(2,1)}), bf16[8,128,512]{2,1,0:T(8,128)(2,1)S(1)}, u32[]{:S(2)}, u32[]{:S(2)}) async-start(bf16[8,128,512]{2,1,0:T(8,128)(2,1)} %bitcast.2), calls=%async_computation | async-start | bytes 2097152 | tf_op jit(solution)/shard_map/all_to_all | solution.py:481
  58.3 14.5 %copy-start = (f32[2,128,1024]{2,1,0:T(8,128)S(1)}, f32[2,128,1024]{2,1,0:T(8,128)}, u32[]{:S(2)}) copy-start(f32[2,128,1024]{2,1,0:T(8,128)} %get-tuple-element.163.own0) | copy-start | bytes 3145732
  67.6 17.5 %collective-permute-start.17 = (bf16[1024,256]{1,0:T(8,128)(2,1)}, bf16[1024,256]{1,0:T(8,128)(2,1)S(1)}, u32[]{:S(2)}, u32[]{:S(2)}) collective-permute-start(bf16[1024,256]{1,0:T(8,128)(2,1)} %get-tuple-element.172), channel_id=1, source_target_pairs={{8,0},{12,4},{16,8},{20,12},{24,16},{28,20},{9,1},{13,5},{17,9},{2... | collective-permute-start | bytes 1572872 | tf_op jit(solution)/shard_map/ppermute | solution.py:502
  68.9 7.6 %collective-permute-start.18 = (bf16[128,512]{1,0:T(8,128)(2,1)}, bf16[128,512]{1,0:T(8,128)(2,1)S(1)}, u32[]{:S(2)}, u32[]{:S(2)}) collective-permute-start(bf16[128,512]{1,0:T(8,128)(2,1)} %get-tuple-element.185), channel_id=1, source_target_pairs={{0,4},{1,5},{2,6},{3,7},{4,0},{5,1},{6,2},{7,3},{8,12},{9,13},{10,... | collective-permute-start | bytes 393224 | tf_op jit(solution)/shard_map/ppermute | solution.py:494
  71.0 6.3 %collective-permute-start.20 = (bf16[128,512]{1,0:T(8,128)(2,1)}, bf16[128,512]{1,0:T(8,128)(2,1)S(1)}, u32[]{:S(2)}, u32[]{:S(2)}) collective-permute-start(bf16[128,512]{1,0:T(8,128)(2,1)} %get-tuple-element.189), channel_id=1, source_target_pairs={{0,2},{1,3},{2,0},{3,1},{4,6},{5,7},{6,4},{7,5},{8,10},{9,11},{10,... | collective-permute-start | bytes 393224 | tf_op jit(solution)/shard_map/ppermute | solution.py:494
  72.5 6.6 %collective-permute-start.21 = (bf16[128,512]{1,0:T(8,128)(2,1)}, bf16[128,512]{1,0:T(8,128)(2,1)S(1)}, u32[]{:S(2)}, u32[]{:S(2)}) collective-permute-start(bf16[128,512]{1,0:T(8,128)(2,1)} %get-tuple-element.192), channel_id=1, source_target_pairs={{0,3},{1,2},{2,1},{3,0},{4,7},{5,6},{6,5},{7,4},{8,11},{9,10},{10,... | collective-permute-start | bytes 393224 | tf_op jit(solution)/shard_map/ppermute | solution.py:494
  72.5 12.7 %collective-permute-start.22 = (bf16[128,512]{1,0:T(8,128)(2,1)}, bf16[128,512]{1,0:T(8,128)(2,1)S(1)}, u32[]{:S(2)}, u32[]{:S(2)}) collective-permute-start(bf16[128,512]{1,0:T(8,128)(2,1)} %get-tuple-element.198), channel_id=1, source_target_pairs={{0,5},{1,4},{2,7},{3,6},{4,1},{5,0},{6,3},{7,2},{8,13},{9,12},{10,... | collective-permute-start | bytes 393224 | tf_op jit(solution)/shard_map/ppermute | solution.py:494
  74.1 5.0 %copy-start.11 = (bf16[128,512]{1,0:T(8,128)(2,1)S(1)}, bf16[128,512]{1,0:T(8,128)(2,1)}, u32[]{:S(2)}) copy-start(bf16[128,512]{1,0:T(8,128)(2,1)} %get-tuple-element.204) | copy-start | bytes 393220
  76.6 10.5 %collective-permute-start.19 = (bf16[128,512]{1,0:T(8,128)(2,1)S(1)}, bf16[128,512]{1,0:T(8,128)(2,1)S(1)}, u32[]{:S(2)}, u32[]{:S(2)}) collective-permute-start(bf16[128,512]{1,0:T(8,128)(2,1)S(1)} %copy-done.14), channel_id=1, source_target_pairs={{0,1},{1,0},{2,3},{3,2},{4,5},{5,4},{6,7},{7,6},{8,9},{9,8},{10,11... | collective-permute-start | bytes 393224 | tf_op jit(solution)/shard_map/ppermute | solution.py:494
  77.3 9.7 %collective-permute-start.23 = (bf16[128,512]{1,0:T(8,128)(2,1)S(1)}, bf16[128,512]{1,0:T(8,128)(2,1)S(1)}, u32[]{:S(2)}, u32[]{:S(2)}) collective-permute-start(bf16[128,512]{1,0:T(8,128)(2,1)S(1)} %copy-done.13), channel_id=1, source_target_pairs={{0,6},{1,7},{2,4},{3,5},{4,2},{5,3},{6,0},{7,1},{8,14},{9,15},{10,... | collective-permute-start | bytes 393224 | tf_op jit(solution)/shard_map/ppermute | solution.py:494
  79.1 10.6 %collective-permute-start.24 = (bf16[128,512]{1,0:T(8,128)(2,1)S(1)}, bf16[128,512]{1,0:T(8,128)(2,1)S(1)}, u32[]{:S(2)}, u32[]{:S(2)}) collective-permute-start(bf16[128,512]{1,0:T(8,128)(2,1)S(1)} %copy-done.11), channel_id=1, source_target_pairs={{0,7},{1,6},{2,5},{3,4},{4,3},{5,2},{6,1},{7,0},{8,15},{9,14},{10,... | collective-permute-start | bytes 393224 | tf_op jit(solution)/shard_map/ppermute | solution.py:494
  85.1 11.1 %copy-start.2 = (bf16[128,512]{1,0:T(8,128)(2,1)S(1)}, bf16[128,512]{1,0:T(8,128)(2,1)}, u32[]{:S(2)}) copy-start(bf16[128,512]{1,0:T(8,128)(2,1)} %get-tuple-element.182.refs_0_) | copy-start | bytes 393220
  85.2 5.6 %collective-permute-start.25 = (bf16[128,512]{1,0:T(8,128)(2,1)S(1)}, bf16[128,512]{1,0:T(8,128)(2,1)S(1)}, u32[]{:S(2)}, u32[]{:S(2)}) collective-permute-start(bf16[128,512]{1,0:T(8,128)(2,1)S(1)} %get-tuple-element.210), channel_id=1, source_target_pairs={{0,3},{1,2},{2,1},{3,0},{4,7},{5,6},{6,5},{7,4},{8,11},{9,10},{10,... | collective-permute-start | bytes 393224 | tf_op jit(solution)/shard_map/ppermute | solution.py:494
  86.2 7.9 %collective-permute-start.27 = (bf16[128,512]{1,0:T(8,128)(2,1)S(1)}, bf16[128,512]{1,0:T(8,128)(2,1)S(1)}, u32[]{:S(2)}, u32[]{:S(2)}) collective-permute-start(bf16[128,512]{1,0:T(8,128)(2,1)S(1)} %get-tuple-element.213), channel_id=1, source_target_pairs={{0,2},{1,3},{2,0},{3,1},{4,6},{5,7},{6,4},{7,5},{8,10},{9,11},{10,... | collective-permute-start | bytes 393224 | tf_op jit(solution)/shard_map/ppermute | solution.py:494
  87.1 10.7 %collective-permute-start.28 = (bf16[128,512]{1,0:T(8,128)(2,1)S(1)}, bf16[128,512]{1,0:T(8,128)(2,1)S(1)}, u32[]{:S(2)}, u32[]{:S(2)}) collective-permute-start(bf16[128,512]{1,0:T(8,128)(2,1)S(1)} %get-tuple-element.216), channel_id=1, source_target_pairs={{0,4},{1,5},{2,6},{3,7},{4,0},{5,1},{6,2},{7,3},{8,12},{9,13},{10,... | collective-permute-start | bytes 393224 | tf_op jit(solution)/shard_map/ppermute | solution.py:494
  88.6 9.4 %collective-permute-start.30 = (bf16[128,512]{1,0:T(8,128)(2,1)S(1)}, bf16[128,512]{1,0:T(8,128)(2,1)S(1)}, u32[]{:S(2)}, u32[]{:S(2)}) collective-permute-start(bf16[128,512]{1,0:T(8,128)(2,1)S(1)} %get-tuple-element.218), channel_id=1, source_target_pairs={{0,6},{1,7},{2,4},{3,5},{4,2},{5,3},{6,0},{7,1},{8,14},{9,15},{10,... | collective-permute-start | bytes 393224 | tf_op jit(solution)/shard_map/ppermute | solution.py:494
  89.7 11.2 %collective-permute-start.29 = (bf16[128,512]{1,0:T(8,128)(2,1)S(1)}, bf16[128,512]{1,0:T(8,128)(2,1)S(1)}, u32[]{:S(2)}, u32[]{:S(2)}) collective-permute-start(bf16[128,512]{1,0:T(8,128)(2,1)S(1)} %get-tuple-element.217), channel_id=1, source_target_pairs={{0,5},{1,4},{2,7},{3,6},{4,1},{5,0},{6,3},{7,2},{8,13},{9,12},{10,... | collective-permute-start | bytes 393224 | tf_op jit(solution)/shard_map/ppermute | solution.py:494
  90.9 10.0 %collective-permute-start.26 = (bf16[128,512]{1,0:T(8,128)(2,1)S(1)}, bf16[128,512]{1,0:T(8,128)(2,1)S(1)}, u32[]{:S(2)}, u32[]{:S(2)}) collective-permute-start(bf16[128,512]{1,0:T(8,128)(2,1)S(1)} %get-tuple-element.211), channel_id=1, source_target_pairs={{0,1},{1,0},{2,3},{3,2},{4,5},{5,4},{6,7},{7,6},{8,9},{9,8},{10,11... | collective-permute-start | bytes 393224 | tf_op jit(solution)/shard_map/ppermute | solution.py:494
  94.1 6.8 %collective-permute-start.31 = (bf16[128,512]{1,0:T(8,128)(2,1)S(1)}, bf16[128,512]{1,0:T(8,128)(2,1)S(1)}, u32[]{:S(2)}, u32[]{:S(2)}) collective-permute-start(bf16[128,512]{1,0:T(8,128)(2,1)S(1)} %get-tuple-element.219), channel_id=1, source_target_pairs={{0,7},{1,6},{2,5},{3,4},{4,3},{5,2},{6,1},{7,0},{8,15},{9,14},{10,... | collective-permute-start | bytes 393224 | tf_op jit(solution)/shard_map/ppermute | solution.py:494
  (10 other events, 20.8 us)
